TPU v7x, 32 devices: a whole 2x2x4 slice. The times are simulated.
32 devices in a mesh: grp: 2 (over y), hh: 4 (over z), per: 2 (over x), st: 2 (over core).
Axes of the slice: x: 2, y: 2, z: 4, core: 2. Of those that a mesh axis runs over, the one named last changes fastest.
Arguments:
- earnings: float32 [3072, 16], P(('hh', 'per')), may hold values from -5.4 to 5.4
- starts: int32 [3072], P(('hh', 'per')), may hold values from 0 to 12, as said below
- lengths: int32 [3072], P(('hh', 'per')), may hold values from 4 to 16
- block_count: int32 [8], P(('hh', 'per')), may hold values from 0 to 3, as said below
- trans_logits: bfloat16 [32, 256, 256], P(('grp', 'per', 'st')), parts along dimension 0, may hold values from -4 to 4
- init_logits: float32 [512], P('grp'), parts along dimension 0, may hold values from -4 to 4
- state_mean: float32 [512], P('grp'), parts along dimension 0, may hold values from -4 to 4
- log_sd: float32 [512], P('grp'), parts along dimension 0, may hold values from 0 to 1
Outputs:
- trans_grad: float32 [32, 256, 256], P(('grp', 'per'), 'hh', 'st'), parts along dimension 0
- mean_loglik: float32 [2], P('grp'), parts along dimension 0
There are 2 independent parts, one for each index of `grp`. A program takes and returns all parts, laid end to end along the dimension named above; an argument that names none is the same for every part. Nothing has to cross between parts.
Inputs may be any that keep to these rules, and one draw needn't show every extreme that they name: starts[h] + lengths[h] <= 16. Exactly 1 device hold 3 blocks and as many hold 2; the counts sum to 8. Only the first block_count[d] blocks of device d's 3 slots hold households; the entries of the other slots are to be ignored.
All inputs are finite; a program needn't handle non-finite values.
Results may differ from a plain program's by a relative error of at most 0.00055.
Values may be sent and summed in bfloat16 or wider, within the bound.
No kernel may reach another device: no remote copies, remote signals or barrier semaphores. Data moves between devices by JAX's collectives and lax.ppermute only.
A program may use at most 64 MiB of HBM per device.

v0:
```python
import jax
import jax.numpy as jnp
from jax import lax
from jax.sharding import PartitionSpec as P

HB = 128


top_precision = lax.Precision.HIGHEST


def emission(column, state_mean, log_sd):
    z_score = (column[:, None] - state_mean[None, :]) / jnp.exp(log_sd)[None, :]
    return jnp.exp(-0.5 * z_score * z_score - log_sd[None, :])


def per_device(
    earnings, starts, lengths, block_count, trans_logits, init_logits, state_mean, log_sd
):
    num_states = init_logits.shape[0]
    num_periods = earnings.shape[1]
    slot_rows = earnings.shape[0]
    group_size = lax.axis_size(("hh", "per"))
    core_count = lax.axis_size("st")
    half_states = num_states // core_count
    lead_state = lax.axis_index("st") * half_states
    whole_logits = lax.all_gather(trans_logits, ("per", "st"), axis=0, tiled=True)
    raised = jnp.exp(whole_logits.astype(jnp.float32))
    trans_probs = raised / jnp.sum(raised, axis=2, keepdims=True)
    raised_first = jnp.exp(init_logits)
    first_probs = raised_first / jnp.sum(raised_first)
    source_rows = slot_rows // group_size
    count_out = jnp.broadcast_to(block_count.reshape(1, 1), (1, group_size))
    got_earn, got_start, got_len, got_count = (
        lax.all_to_all(
            earnings.reshape(source_rows, group_size, num_periods),
            ("hh", "per"),
            split_axis=1,
            concat_axis=1,
            tiled=True,
        ),
        lax.all_to_all(
            starts.reshape(source_rows, group_size),
            ("hh", "per"),
            split_axis=1,
            concat_axis=1,
            tiled=True,
        ),
        lax.all_to_all(
            lengths.reshape(source_rows, group_size),
            ("hh", "per"),
            split_axis=1,
            concat_axis=1,
            tiled=True,
        ),
        lax.all_to_all(count_out, ("hh", "per"), split_axis=1, concat_axis=1, tiled=True),
    )
    per_source = got_count[0] * (HB // group_size)
    ends_at = jnp.cumsum(per_source)
    target_ids = jnp.arange(HB, dtype=jnp.int32)
    before_mask = ends_at[None, :] <= target_ids[:, None]
    source_ids = jnp.sum(before_mask.astype(jnp.int32), axis=1)
    begins_at = jnp.sum(jnp.where(before_mask, per_source[None, :], 0), axis=1)
    pick_ids = (target_ids - begins_at) * group_size + source_ids
    rows_earn = jnp.take(got_earn.reshape(source_rows * group_size, num_periods), pick_ids, axis=0)
    rows_start = jnp.take(got_start.reshape(source_rows * group_size), pick_ids)
    rows_len = jnp.take(got_len.reshape(source_rows * group_size), pick_ids)
    row_live = jnp.ones((HB,), dtype=bool)
    years_local = jnp.sum(jnp.where(row_live, rows_len, 0)).astype(jnp.float32)
    row_total_count = rows_earn.shape[0]
    columns = rows_earn.T
    period_ids = jnp.arange(num_periods, dtype=jnp.int32)

    def observed(step_now):
        return row_live & (step_now >= rows_start) & (step_now < rows_start + rows_len)

    def forward(prev_alpha, inputs):
        matrix, column, step_now = inputs
        fresh_start = (step_now <= rows_start)[:, None]
        moved_mass = jnp.dot(
            prev_alpha, matrix, precision=top_precision, preferred_element_type=jnp.float32
        )
        joint_mass = jnp.where(fresh_start, first_probs[None, :], moved_mass) * emission(
            column, state_mean, log_sd
        )
        seen_now = observed(step_now)
        scale_now = jnp.where(seen_now, jnp.sum(joint_mass, axis=1), 1.0)
        new_alpha = jnp.where(seen_now[:, None], joint_mass / scale_now[:, None], prev_alpha)
        return (new_alpha, (new_alpha, scale_now))

    start_alpha = jnp.broadcast_to(first_probs[None, :], (row_total_count, num_states))
    _, (alphas, scales) = lax.scan(forward, start_alpha, (trans_probs, columns, period_ids))

    def carry_of(back_now, column, scale_now, step_now):
        seen_now = observed(step_now)
        return jnp.where(
            seen_now[:, None],
            emission(column, state_mean, log_sd) * back_now / scale_now[:, None],
            0.0,
        )

    def backward(carry_now, inputs):
        matrix, alpha_prev, column_prev, scale_prev, step_now = inputs
        moving = row_live & (step_now > rows_start) & (step_now < rows_start + rows_len)
        weights = jnp.where(moving[:, None], alpha_prev, 0.0)
        own_carry = lax.dynamic_slice_in_dim(carry_now, lead_state, half_states, 1)
        grad_term = lax.dot_general(
            weights,
            own_carry,
            (((0,), (0,)), ((), ())),
            precision=top_precision,
            preferred_element_type=jnp.float32,
        )
        pulled = lax.dot_general(
            carry_now,
            matrix,
            (((1,), (1,)), ((), ())),
            precision=top_precision,
            preferred_element_type=jnp.float32,
        )
        back_now = jnp.where(moving[:, None], pulled, 1.0)
        return (carry_of(back_now, column_prev, scale_prev, step_now - 1), grad_term)

    ones_back = jnp.ones((row_total_count, num_states), jnp.float32)
    last_carry = carry_of(
        ones_back, columns[num_periods - 1], scales[num_periods - 1], num_periods - 1
    )
    _, grad_terms = lax.scan(
        backward,
        last_carry,
        (trans_probs[1:], alphas[:-1], columns[:-1], scales[:-1], period_ids[1:]),
        reverse=True,
    )
    zero_first = jnp.zeros((1,) + grad_terms.shape[1:], jnp.float32)
    partial_counts = jnp.concatenate([zero_first, grad_terms], axis=0)
    loglik_local = jnp.sum(jnp.log(scales))
    summed = lax.psum_scatter(partial_counts, "hh", scatter_dimension=1, tiled=True)
    summed = lax.psum_scatter(summed, "per", scatter_dimension=0, tiled=True)
    loglik_share = loglik_local / core_count
    years_share = years_local / core_count
    period_block = summed.shape[0]
    row_block_size = summed.shape[1]
    local_probs = lax.dynamic_slice(
        trans_probs,
        (lax.axis_index("per") * period_block, lax.axis_index("hh") * row_block_size, lead_state),
        (period_block, row_block_size, half_states),
    )
    weighted = local_probs * summed
    row_total, loglik_core, years_core = lax.psum(
        (jnp.sum(weighted, axis=2), loglik_share, years_share), "st"
    )
    loglik_all, years_all = lax.psum((loglik_core, years_core), ("hh", "per"))
    factor = float(num_states * num_states * num_periods) / years_all
    trans_grad = factor * (weighted - local_probs * row_total[:, :, None])
    mean_loglik = jnp.reshape(loglik_all / years_all, (1,))
    return (trans_grad, mean_loglik)


def solution(mesh):
    placed = (
        P(("hh", "per"), None),
        P(("hh", "per")),
        P(("hh", "per")),
        P(("hh", "per")),
        P(("grp", "per", "st"), None, None),
        P("grp"),
        P("grp"),
        P("grp"),
    )
    return jax.shard_map(
        per_device,
        mesh=mesh,
        in_specs=placed,
        out_specs=(P(("grp", "per"), "hh", "st"), P("grp")),
        check_vma=False,
    )
```

profile of v0, /device:TPU:0, one launch (start us, length us, event | category | flops | bytes accessed | tf_op | source)
XLA Modules:
  0.0 299.1 jit_solution(5646740172056218741)
XLA Ops:
  9.1 7.3 %all-to-all-start.1 = ((s32[1,8,1]{2,0,1:T(1,128)}), s32[1,8,1]{2,0,1:T(1,128)S(1)}, u32[]{:S(2)}, u32[]{:S(2)}) async-start(s32[1,8,1]{2,0,1:T(1,128)} %broadcast_in_dim.209), calls=%async_computation.1 | async-start | bytes 8192 | tf_op jit(solution)/shard_map/all_to_all | solution.py:56
  21.8 1.3 exponential_reduce_fusion
  23.0 1.2 exponential_divide_fusion
  24.3 6.0 %all-to-all-start = ((s32[48,8,1]{0,2,1:T(1,128)}), s32[48,8,1]{0,2,1:T(1,128)S(1)}, u32[]{:S(2)}, u32[]{:S(2)}) async-start(s32[48,8,1]{0,2,1:T(1,128)} %copy.34), calls=%async_computation | async-start | bytes 8192 | tf_op jit(solution)/shard_map/all_to_all | solution.py:49
  30.8 5.9 %all-to-all-done = s32[48,8,1]{0,2,1:T(1,128)S(1)} async-done(((s32[48,8,1]{0,2,1:T(1,128)}), s32[48,8,1]{0,2,1:T(1,128)S(1)}, u32[]{:S(2)}, u32[]{:S(2)}) %all-to-all-start) | async-done | bytes 1568 | tf_op jit(solution)/shard_map/all_to_all | solution.py:49
  36.7 3.3 %all-to-all-start.2 = ((s32[48,8,1]{0,2,1:T(1,128)}), s32[48,8,1]{0,2,1:T(1,128)S(1)}, u32[]{:S(2)}, u32[]{:S(2)}) async-start(s32[48,8,1]{0,2,1:T(1,128)} %copy.36), calls=%async_computation.2 | async-start | bytes 8192 | tf_op jit(solution)/shard_map/all_to_all | solution.py:42
  40.2 6.2 %all-to-all-done.2 = s32[48,8,1]{0,2,1:T(1,128)S(1)} async-done(((s32[48,8,1]{0,2,1:T(1,128)}), s32[48,8,1]{0,2,1:T(1,128)S(1)}, u32[]{:S(2)}, u32[]{:S(2)}) %all-to-all-start.2) | async-done | bytes 1568 | tf_op jit(solution)/shard_map/all_to_all | solution.py:42
  46.4 3.3 %all-to-all-start.3 = ((f32[8,1,768]{2,1,0:T(1,128)}), f32[8,1,768]{2,1,0:T(1,128)S(1)}, u32[]{:S(2)}, u32[]{:S(2)}) async-start(f32[8,1,768]{2,1,0:T(1,128)} %reshape.291), calls=%async_computation.3 | async-start | bytes 49152 | tf_op jit(solution)/shard_map/all_to_all | solution.py:35
  49.9 1.3 gather_fusion.1
  51.2 1.3 gather_fusion.2
  52.5 3.8 %all-to-all-done.3 = f32[8,1,768]{2,1,0:T(1,128)S(1)} async-done(((f32[8,1,768]{2,1,0:T(1,128)}), f32[8,1,768]{2,1,0:T(1,128)S(1)}, u32[]{:S(2)}, u32[]{:S(2)}) %all-to-all-start.3) | async-done | bytes 24608 | tf_op jit(solution)/shard_map/all_to_all | solution.py:35
  58.8 2.4 fusion.28
  62.2 2.3 slice.36
  65.4 68.4 %while.34 = (s32[]{:T(128)}, f32[128,256]{0,1:T(8,128)S(1)}, f32[16,128,256]{1,2,0:T(8,128)S(1)}, f32[16,128]{1,0:T(8,128)S(1)}, s32[16]{0:T(128)S(1)}, /*index=...) while((s32[]{:T(128)}, f32[128,256]{0,1:T(8,128)S(1)}, ...), condition=%wide.region_10.12_spmd, body=%wide.region_8.11_spmd.sunk | while | flops 100992000 | bytes 1062457 | solution.py:92
  66.6 1.6 fusion.54
  70.9 1.6 fusion.54
  75.2 1.6 fusion.54
  79.5 1.6 fusion.54
  83.7 1.6 fusion.54
  88.0 1.6 fusion.54
  92.3 1.6 fusion.54
  96.6 1.6 fusion.54
  100.8 1.6 fusion.54
  105.1 1.6 fusion.54
  109.4 1.6 fusion.54
  113.7 1.6 fusion.54
  117.9 1.6 fusion.54
  122.2 1.6 fusion.54
  126.5 1.6 fusion.54
  130.8 1.6 fusion.54
  133.8 1.5 slice.27
  135.7 67.4 %while.35 = (s32[]{:T(128)}, f32[128,256]{0,1:T(8,128)S(1)}, f32[15,256,128]{2,1,0:T(8,128)S(1)}, s32[15]{0:T(128)S(1)}, s32[128]{0:T(128)S(1)}, /*index=5*/s32[...) while((s32[]{:T(128)}, f32[128,256]{0,1:T(8,128)S(1)}, ...), condition=%wide.region_12.14_spmd, body=%wide.region_11.13_spmd.sunk | while | flops 151323392 | bytes 1124049 | solution.py:128
  137.6 1.2 fusion.61
  138.8 1.3 fusion.60
  142.1 1.2 fusion.61
  143.3 1.3 fusion.60
  146.6 1.2 fusion.61
  147.8 1.3 fusion.60
  151.1 1.2 fusion.61
  152.3 1.3 fusion.60
  155.5 1.2 fusion.61
  156.8 1.3 fusion.60
  160.0 1.2 fusion.61
  161.3 1.3 fusion.60
  164.5 1.2 fusion.61
  165.7 1.3 fusion.60
  169.0 1.2 fusion.61
  170.2 1.3 fusion.60
  174.7 1.3 fusion.60
  179.2 1.3 fusion.60
  182.5 1.2 fusion.61
  183.7 1.3 fusion.60
  188.2 1.3 fusion.60
  191.5 1.2 fusion.61
  192.7 1.3 fusion.60
  196.0 1.2 fusion.61
  197.2 1.3 fusion.60
  201.7 1.3 fusion.60
  203.0 1.6 concatenate.3
  204.7 41.5 %reduce-scatter.3.cloned.1.call-done = f32[16,64,128]{2,1,0:T(8,128)} async-done(((f32[16,256,128]{2,1,0:T(8,128)}), f32[16,64,128]{2,1,0:T(8,128)}) %reduce-scatter.3.cloned.1.call-update) | async-done | bytes 524304 | tf_op jit(solution)/shard_map/reduce_scatter | solution.py:137
  248.8 13.7 %reduce-scatter.5.cloned.1.call-done = f32[8,64,128]{2,1,0:T(8,128)} async-done(((f32[16,64,128]{2,1,0:T(8,128)}), f32[8,64,128]{2,1,0:T(8,128)}) %reduce-scatter.5.cloned.1.call-update) | async-done | bytes 262160 | tf_op jit(solution)/shard_map/reduce_scatter | solution.py:138
  263.6 3.0 %all-reduce.2 = (f32[8,64]{1,0:T(8,128)S(1)}, f32[]{:T(128)}, f32[]{:T(128)}) all-reduce(f32[8,64]{1,0:T(8,128)S(1)} %fusion.33, f32[]{:T(128)S(6)} %div.140, f32[]{:T(128)S(6)} %div.151), channel_id=1, replica_groups=mesh['grp'=2,'hh'=4,'per'=2,'st'=2] {'st'}, use_global_device_ids=true, to_apply=%region_16.18 | all-reduce | flops 514 | bytes 4112 | tf_op jit(solution)/shard_map/psum | solution.py:149
  266.7 21.0 %all-reduce.1 = (f32[]{:T(128)}, f32[]{:T(128)}) all-reduce(f32[]{:T(128)} %get-tuple-element.712, f32[]{:T(128)} %get-tuple-element.713), channel_id=1, replica_groups=mesh['grp'=2,'hh'=4,'per'=2,'st'=2] {'hh','per'}, use_global_device_ids=true, to_apply=%region_5.7 | all-reduce | flops 2 | bytes 16 | tf_op jit(solution)/shard_map/psum | solution.py:152
  289.6 1.9 subtract_multiply_fusion
  (235 shorter events, 80.4 us)
Async XLA Ops:
  7.2 51.7 %all-gather.2.cloned.1.call-start = ((), (), s32[]{:S(2)}) async-start(), calls=%async_computation.6 | async-start | bytes 2621440 | tf_op jit(solution)/shard_map/all_gather | solution.py:27
  9.1 15.1 %all-to-all-start.1 = ((s32[1,8,1]{2,0,1:T(1,128)}), s32[1,8,1]{2,0,1:T(1,128)S(1)}, u32[]{:S(2)}, u32[]{:S(2)}) async-start(s32[1,8,1]{2,0,1:T(1,128)} %broadcast_in_dim.209), calls=%async_computation.1 | async-start | bytes 8192 | tf_op jit(solution)/shard_map/all_to_all | solution.py:56
  24.3 12.5 %all-to-all-start = ((s32[48,8,1]{0,2,1:T(1,128)}), s32[48,8,1]{0,2,1:T(1,128)S(1)}, u32[]{:S(2)}, u32[]{:S(2)}) async-start(s32[48,8,1]{0,2,1:T(1,128)} %copy.34), calls=%async_computation | async-start | bytes 8192 | tf_op jit(solution)/shard_map/all_to_all | solution.py:49
  36.7 9.7 %all-to-all-start.2 = ((s32[48,8,1]{0,2,1:T(1,128)}), s32[48,8,1]{0,2,1:T(1,128)S(1)}, u32[]{:S(2)}, u32[]{:S(2)}) async-start(s32[48,8,1]{0,2,1:T(1,128)} %copy.36), calls=%async_computation.2 | async-start | bytes 8192 | tf_op jit(solution)/shard_map/all_to_all | solution.py:42
  46.4 9.9 %all-to-all-start.3 = ((f32[8,1,768]{2,1,0:T(1,128)}), f32[8,1,768]{2,1,0:T(1,128)S(1)}, u32[]{:S(2)}, u32[]{:S(2)}) async-start(f32[8,1,768]{2,1,0:T(1,128)} %reshape.291), calls=%async_computation.3 | async-start | bytes 49152 | tf_op jit(solution)/shard_map/all_to_all | solution.py:35
  49.7 196.5 %reduce-scatter.3.cloned.1.call-start = ((), (), s32[]{:S(2)}) async-start(), calls=%async_computation.7 | async-start | bytes 2621440 | tf_op jit(solution)/shard_map/reduce_scatter | solution.py:137
  58.8 2.4 copy-start.1
  62.1 3.1 %copy-start = (f32[16,256,256]{2,1,0:T(8,128)}, f32[16,256,256]{2,1,0:T(8,128)S(1)}, u32[]{:S(2)}) copy-start(f32[16,256,256]{2,1,0:T(8,128)S(1)} %fusion.27) | copy-start | bytes 12582916
  62.1 3.2 %copy-start.2 = (f32[256]{0:T(256)S(1)}, f32[256]{0:T(256)}, u32[]{:S(2)}) copy-start(f32[256]{0:T(256)} %param.21) | copy-start | bytes 3076
  62.1 3.2 %copy-start.3 = (f32[256]{0:T(256)S(1)}, f32[256]{0:T(256)}, u32[]{:S(2)}) copy-start(f32[256]{0:T(256)} %param.20) | copy-start | bytes 3076
  204.6 57.9 %reduce-scatter.5.cloned.1.call-start = ((), (), s32[]{:S(2)}) async-start(), calls=%async_computation.8 | async-start | bytes 786432 | tf_op jit(solution)/shard_map/reduce_scatter | solution.py:138
Sparse Core Ops, SparseCore 0:
  9.6 25.3 all-gather.1
  204.7 41.4 reduce-scatter.2
  248.5 13.8 reduce-scatter.4
where the time goes:
time: 302 us; the launch traced here: 299 us
  waiting for transfers between devices  71.9 us (24%)
  matrix products  63.4 us (21%)
  other arithmetic  53.2 us (18%)
  local copies, waits for them, and re-layouts  36.2 us (12%)
  blocking collectives  24.1 us (8%)
  starting transfers between devices  20 us (7%)
  between operations  19 us (6%)
  loops' own time  11.4 us (4%)
    reduce_scatter x1, waiting for transfers between devices, per_device(): lax.psum_scatter(partial_counts, 'hh', scatter_dimension=1, tiled=True)  41.5 us
    dot_general x16, matrix products, forward(): jnp.dot(prev_alpha, matrix, precision=top_precision, preferred_element_ty...  25.6 us
    psum x1, blocking collectives, per_device(): loglik_all, years_all = lax.psum((loglik_core, years_core), ('hh', 'per'))  21 us
    select_n x32, other arithmetic, forward(): scale_now = jnp.where(seen_now, jnp.sum(joint_mass, axis=1), 1.0)  20.9 us
    dot_general x15, matrix products, backward(): lax.dot_general(carry_now, matrix, (((1,), (1,)), ((), ())), precision=to...  20 us
    dot_general x15, matrix products, backward(): lax.dot_general(weights, own_carry, (((0,), (0,)), ((), ())), precision=t...  17.8 us
    reduce_scatter x1, waiting for transfers between devices, per_device(): summed = lax.psum_scatter(summed, 'per', scatter_dimension=0, tiled=True)  13.7 us
    another operation x1, loops' own time, per_device(): lax.scan(backward, last_carry, (trans_probs[1:], alphas[:-1], columns[:-1...  10.6 us
  transfers between devices with their start and end apart: 7, of which 5 were waited for; matrix products, arithmetic and copies ran while one was open for 5% of the time, Pallas kernels for 0%

commit v1 on v0

v1 whole, which is shorter than its diff:
```python
import functools

import jax
import jax.numpy as jnp
from jax import lax
from jax.experimental import pallas as pl
from jax.experimental.pallas import tpu as pltpu
from jax.sharding import PartitionSpec as P

HB = 128
LANES = 128
F32 = jnp.float32
BF16 = jnp.bfloat16
LOG2E = 1.4426950408889634
LN2 = 0.6931471805599453
VMEM_LIMIT = 40 * 1024 * 1024


def vmem():
    return pl.BlockSpec(memory_space=pltpu.VMEM)


def smem():
    return pl.BlockSpec(memory_space=pltpu.SMEM)


def params():
    return pltpu.CompilerParams(vmem_limit_bytes=VMEM_LIMIT)


def pack_kernel(count_ref, earn_ref, start_ref, len_ref, out_ref):
    periods, rows = earn_ref.shape
    live = lax.broadcasted_iota(jnp.int32, (1, rows), 1) < count_ref[0] * HB
    code = jnp.where(live, start_ref[...] * (2 * periods) + len_ref[...], -1)
    out_ref[:periods, :] = earn_ref[...]
    out_ref[periods:, :] = jnp.broadcast_to(code.astype(F32), (8, rows))


def prep_kernel(
    ids_ref, own_ref, other_ref, init_ref, mean_ref, sd_ref, first_mat, second_mat, row_probs, consts, scratch
):
    core, forward_first, row_begin = ids_ref[0], ids_ref[1], ids_ref[2]
    part, states, _ = own_ref.shape
    rows = row_probs.shape[1]

    def column(row):
        return jnp.broadcast_to(row, (LANES, states)).T

    raised = jnp.exp(init_ref[...])
    consts[0] = column(raised / jnp.sum(raised, axis=1, keepdims=True))
    consts[1] = column(mean_ref[...])
    consts[2] = column((-0.5 * LOG2E) * jnp.exp(-2.0 * sd_ref[...]))
    consts[3] = column(-LOG2E * sd_ref[...])

    def put(ref, at, value):
        high = value.astype(BF16)
        ref[at, :states, :] = high
        ref[at, states:, :] = (value - high.astype(F32)).astype(BF16)

    for source, ref in ((core, own_ref), (1 - core, other_ref)):

        @pl.loop(0, part)
        def _(i):
            at = source * part + i
            lifted = jnp.exp(ref[i].astype(F32))
            probs = lifted / jnp.sum(lifted, axis=1, keepdims=True)
            scratch[...] = probs
            row_probs[at] = scratch[pl.ds(pl.multiple_of(row_begin, rows), rows), :]
            turned = probs.T

            @pl.when(forward_first == 1)
            def _():
                put(first_mat, at, turned)
                put(second_mat, at, probs)

            @pl.when(forward_first == 0)
            def _():
                put(first_mat, at, probs)
                put(second_mat, at, turned)


def emission(sel_ref, consts, step_now, cols):
    gap = sel_ref[step_now, :1, cols] - consts[1]
    power = gap * gap * consts[2] + consts[3]
    top = jnp.max(power, axis=0, keepdims=True)
    return jnp.exp2(power - top), top


def spans(sel_ref, periods, cols):
    begin = sel_ref[periods, :1, cols]
    return begin, begin + sel_ref[periods + 1, :1, cols]


def run_forward(lead, mat, hist, sel_ref, consts, ab_ref, weights_ref, counts_ref, row_begin):
    steps, states, width = hist.shape
    periods = sel_ref.shape[0] - 3

    def body(k, carry):
        inverse, loglik = carry
        step_now = lead + k
        step_f = step_now.astype(F32)
        if counts_ref is None:
            hist[k] = ab_ref[...]
        else:
            rows = weights_ref.shape[0]
            own_alpha = ab_ref[pl.ds(pl.multiple_of(row_begin, rows), rows), :].astype(F32)
        product = jnp.dot(mat[k], ab_ref[...], preferred_element_type=F32)
        new_inverse, new_loglik = [], []
        for q in range(width // LANES):
            cols = slice(q * LANES, (q + 1) * LANES)
            begin, end = spans(sel_ref, periods, cols)
            moved = (product[:states, cols] + product[states:, cols]) * inverse[:, cols]
            if counts_ref is not None:
                total = jnp.sum(moved * hist[k, :, cols].astype(F32), axis=0, keepdims=True)
                moving = (step_f > begin) & (step_f < end)
                weight = jnp.where(moving, inverse[:, cols] / total, 0.0)
                weights_ref[:, cols] = (own_alpha[:, cols] * weight).astype(BF16)
            emit, top = emission(sel_ref, consts, step_now, cols)
            joint = jnp.where(step_f <= begin, consts[0], moved) * emit
            scale = jnp.sum(joint, axis=0, keepdims=True)
            seen = (step_f >= begin) & (step_f < end)
            new_loglik.append(loglik[:, cols] + jnp.where(seen, jnp.log(scale) + top * LN2, 0.0))
            new_inverse.append(1.0 / scale)
            ab_ref[:, cols] = joint.astype(BF16)
        if counts_ref is not None:
            counts_ref[k] += lax.dot_general(
                weights_ref[...], hist[k], (((1,), (1,)), ((), ())), preferred_element_type=F32
            )
        return jnp.concatenate(new_inverse, axis=1), jnp.concatenate(new_loglik, axis=1)

    inverse = 1.0 / jnp.sum(ab_ref[...].astype(F32), axis=0, keepdims=True)
    _, loglik = lax.fori_loop(0, steps, body, (inverse, jnp.zeros((1, width), F32)))
    return jnp.sum(loglik, axis=1, keepdims=True)


def run_backward(lead, mat, hist, sel_ref, consts, back_ref, ub_ref, weights_ref, counts_ref, row_begin):
    steps, states, width = hist.shape
    periods = sel_ref.shape[0] - 3

    def body(j, carry):
        k = steps - 1 - j
        step_now = lead + k
        step_f = step_now.astype(F32)
        shrink = []
        for q in range(width // LANES):
            cols = slice(q * LANES, (q + 1) * LANES)
            emit, _ = emission(sel_ref, consts, step_now, cols)
            carried = emit * back_ref[:, cols]
            shrink.append(1.0 / jnp.sum(carried, axis=0, keepdims=True))
            ub_ref[:, cols] = carried.astype(BF16)
        if counts_ref is None:
            hist[k] = ub_ref[...]
        product = jnp.dot(mat[k], ub_ref[...], preferred_element_type=F32)
        if counts_ref is not None:
            rows = weights_ref.shape[0]
            own_alpha = hist[k, pl.ds(pl.multiple_of(row_begin, rows), rows), :].astype(F32)
        for q in range(width // LANES):
            cols = slice(q * LANES, (q + 1) * LANES)
            begin, end = spans(sel_ref, periods, cols)
            moving = (step_f > begin) & (step_f < end)
            pulled = (product[:states, cols] + product[states:, cols]) * shrink[q]
            if counts_ref is not None:
                total = jnp.sum(pulled * hist[k, :, cols].astype(F32), axis=0, keepdims=True)
                weight = jnp.where(moving, shrink[q] / total, 0.0)
                weights_ref[:, cols] = (own_alpha[:, cols] * weight).astype(BF16)
            back_ref[:, cols] = jnp.where(moving, pulled, 1.0)
        if counts_ref is not None:
            counts_ref[k] += lax.dot_general(
                weights_ref[...], ub_ref[...], (((1,), (1,)), ((), ())), preferred_element_type=F32
            )
        return carry

    lax.fori_loop(0, steps, body, 0)


def first_kernel(direct, resume, group, chunks, *refs):
    refs = list(refs)
    ids_ref = refs.pop(0)
    gathered = [refs.pop(0) for _ in range(group)] if direct else [refs.pop(0)]
    mat, consts = refs.pop(0), refs.pop(0)
    state_in = refs.pop(0) if resume else None
    hist, state_out, sel_ref, ll_ref, ab_ref, back_ref = refs[:6]
    core, forward_first, lead, me, cores = ids_ref[0], ids_ref[1], ids_ref[3], ids_ref[4], ids_ref[5]
    chunk = pl.program_id(0) if chunks > 1 else 0
    steps, states, width = hist.shape
    periods = sel_ref.shape[0] - 3
    if direct:
        all_rows = refs[6]
        for r, ref in enumerate(gathered):
            all_rows[lax.rem(me + group - r, group)] = ref[...]
    else:
        all_rows = gathered[0]
    slots = all_rows.shape[2] // HB
    picks = width // HB
    base = 2.0 * periods
    pieces = (periods + 8) // 8

    def scan_source(d, carry):
        rank, years, picked = carry
        for slot in range(slots):
            cols = slice(slot * HB, (slot + 1) * HB)
            code = all_rows[d, periods:, cols]
            live = code >= 0.0
            begin = jnp.floor(code * (1.0 / base))
            years = years + jnp.where(live, code - begin * base, 0.0)
            block = [all_rows[d, 8 * p : 8 * p + 8, cols] for p in range(pieces)]
            fresh = []
            for q in range(picks):
                target = (chunk * picks + q) * cores + core
                hit = live & (rank == target)
                fresh.append([jnp.where(hit, new, old) for new, old in zip(block, picked[q])])
            picked = fresh
            rank = rank + live.astype(jnp.int32)
        return rank, years, picked

    zero = jnp.zeros((8, HB), F32)
    carry = (jnp.zeros((8, HB), jnp.int32), zero, [[zero] * pieces for _ in range(picks)])
    if group <= 8:
        for d in range(group):
            carry = scan_source(d, carry)
    else:
        carry = lax.fori_loop(0, group, scan_source, carry)
    _, years, picked = carry
    years = jnp.sum(years, axis=1, keepdims=True)
    for q in range(picks):
        cols = slice(q * HB, (q + 1) * HB)
        for p in range(pieces - 1):
            for i in range(8):
                sel_ref[8 * p + i, :, cols] = jnp.broadcast_to(picked[q][p][i : i + 1], (8, HB))
        begin = jnp.floor(picked[q][pieces - 1] * (1.0 / base))
        sel_ref[periods, :, cols] = begin
        sel_ref[periods + 1, :, cols] = picked[q][pieces - 1] - begin * base
        sel_ref[periods + 2, :, cols] = jnp.broadcast_to(years, (8, HB))

    @pl.when(chunk == 0)
    def _():
        ll_ref[...] = jnp.zeros_like(ll_ref)

    @pl.when(forward_first == 1)
    def _():
        if resume:
            ab_ref[...] = state_in[...]
        else:
            for q in range(width // LANES):
                ab_ref[:, q * LANES : (q + 1) * LANES] = consts[0].astype(BF16)
        loglik = run_forward(lead, mat, hist, sel_ref, consts, ab_ref, None, None, None)
        ll_ref[...] += jnp.broadcast_to(loglik, ll_ref.shape)
        state_out[...] = ab_ref[...]

    @pl.when(forward_first == 0)
    def _():
        if resume:
            back_ref[...] = state_in[...].astype(F32)
        else:
            back_ref[...] = jnp.ones_like(back_ref)
        run_backward(lead, mat, hist, sel_ref, consts, back_ref, ab_ref, None, None, None)
        state_out[...] = back_ref[...].astype(BF16)


def second_kernel(
    extend, chunks, ids_ref, sel_ref, mat, consts, hist, state_in, row_probs, ll_in, mine_ref, other_ref, ll_ref, *refs
):
    ab_ref, back_ref, weights_ref, counts_ref = refs[-4:]
    core, forward_first, row_begin, lead = ids_ref[0], ids_ref[1], ids_ref[2], ids_ref[3]
    chunk = pl.program_id(0) if chunks > 1 else 0
    steps, rows, half = mine_ref.shape
    states = hist.shape[1]
    periods = sel_ref.shape[0] - 3

    @pl.when(chunk == 0)
    def _():
        counts_ref[...] = jnp.zeros_like(counts_ref)
        ll_ref[...] = ll_in[...]

    @pl.when(forward_first == 0)
    def _():
        ab_ref[...] = state_in[...]
        loglik = run_forward(lead, mat, hist, sel_ref, consts, ab_ref, weights_ref, counts_ref, row_begin)
        ll_ref[...] += jnp.broadcast_to(loglik, ll_ref.shape)
        if extend:
            refs[0][...] = ab_ref[...]

    @pl.when(forward_first == 1)
    def _():
        back_ref[...] = state_in[...].astype(F32)
        run_backward(
            lead, mat, hist, sel_ref, consts, back_ref, ab_ref, weights_ref, counts_ref, row_begin
        )
        if extend:
            refs[0][...] = back_ref[...].astype(BF16)

    @pl.when(chunk == chunks - 1)
    def _():
        years = sel_ref[periods + 2, :1, :LANES]
        factor = float(states * states * periods) / years
        ll_ref[...] = ll_ref[...] / years
        for k in range(steps):
            probs = row_probs[k]
            weighted = probs * counts_ref[k]
            grad = weighted - probs * jnp.sum(weighted, axis=1, keepdims=True)
            for side in range(2):
                piece = grad[:, side * half : (side + 1) * half] * factor[:, :half]

                @pl.when(core == side)
                def _():
                    mine_ref[k] = piece

                @pl.when(core != side)
                def _():
                    other_ref[k] = piece


def per_device(
    earnings, starts, lengths, block_count, trans_logits, init_logits, state_mean, log_sd
):
    slot_rows, periods = earnings.shape
    states = init_logits.shape[0]
    group = lax.axis_size(("hh", "per"))
    sides = lax.axis_size("per")
    cores = lax.axis_size("st")
    part = trans_logits.shape[0]
    steps = part * cores
    rows = states // lax.axis_size("hh")
    half = states // cores
    households = group * HB // cores
    width = min(4 * HB, households)
    chunks = households // width
    direct = group <= 8
    me = lax.axis_index(("hh", "per"))
    side = lax.axis_index("per")
    core = lax.axis_index("st")
    forward_first = (2 * side < sides).astype(jnp.int32)
    ids = jnp.stack(
        [core, forward_first, lax.axis_index("hh") * rows, side * steps, me, jnp.int32(cores)]
    ).astype(jnp.int32)

    packed = pl.pallas_call(
        pack_kernel,
        out_shape=jax.ShapeDtypeStruct((periods + 8, slot_rows), F32),
        in_specs=[smem(), vmem(), vmem(), vmem()],
        out_specs=vmem(),
        name="pack",
    )(block_count, earnings.T, starts.reshape(1, slot_rows), lengths.reshape(1, slot_rows))
    swap = [(0, 1), (1, 0)]
    other_logits = lax.ppermute(trans_logits, "st", swap)
    if direct:
        gathered = [packed] + [
            lax.ppermute(packed, ("hh", "per"), [(i, (i + r) % group) for i in range(group)])
            for r in range(1, group)
        ]
    else:
        gathered = [lax.all_gather(packed, ("hh", "per"), axis=0)]

    shaped = jax.ShapeDtypeStruct
    first_mat, second_mat, row_probs, consts = pl.pallas_call(
        prep_kernel,
        out_shape=[
            shaped((steps, 2 * states, states), BF16),
            shaped((steps, 2 * states, states), BF16),
            shaped((steps, rows, states), F32),
            shaped((4, states, LANES), F32),
        ],
        in_specs=[smem()] + [vmem()] * 5,
        out_specs=[vmem()] * 4,
        scratch_shapes=[pltpu.VMEM((states, states), F32)],
        compiler_params=params(),
        name="prep",
    )(
        ids, trans_logits, other_logits,
        init_logits.reshape(1, states), state_mean.reshape(1, states), log_sd.reshape(1, states),
    )

    def whole(shape):
        if chunks == 1:
            return vmem()
        return pl.BlockSpec(shape, lambda g: (0,) * len(shape))

    def lanes(*lead):
        if chunks == 1:
            return vmem()
        return pl.BlockSpec(lead + (width,), lambda g: (0,) * len(lead) + (g,))

    hist_shape = shaped((steps, states, households), BF16)
    state_shape = shaped((states, households), BF16)
    sel_shape = shaped((periods + 3, 8, households), F32)
    ll_shape = shaped((8, LANES), F32)
    mat_spec = whole((steps, 2 * states, states))
    const_spec = whole((4, states, LANES))

    def first_pass(state_in):
        resume = state_in is not None
        scratch = [pltpu.VMEM((states, width), BF16), pltpu.VMEM((states, width), F32)]
        if direct:
            scratch.append(pltpu.VMEM((group, periods + 8, slot_rows), F32))
        return pl.pallas_call(
            functools.partial(first_kernel, direct, resume, group, chunks),
            grid=(chunks,) if chunks > 1 else (),
            out_shape=[hist_shape, state_shape, sel_shape, ll_shape],
            in_specs=[smem()]
            + [whole(x.shape) for x in gathered]
            + [mat_spec, const_spec]
            + ([lanes(states)] if resume else []),
            out_specs=[lanes(steps, states), lanes(states), lanes(periods + 3, 8), whole((8, LANES))],
            scratch_shapes=scratch,
            compiler_params=params(),
            name="first_pass",
        )(ids, *gathered, first_mat, consts, *([state_in] if resume else []))

    grad_shape = shaped((steps, rows, half), F32)

    def second_pass(state_in, hist, sel, loglik, extend):
        return pl.pallas_call(
            functools.partial(second_kernel, extend, chunks),
            grid=(chunks,) if chunks > 1 else (),
            out_shape=[grad_shape, grad_shape, ll_shape] + ([state_shape] if extend else []),
            in_specs=[
                smem(), lanes(periods + 3, 8), mat_spec, const_spec, lanes(steps, states), lanes(states),
                whole((steps, rows, states)), whole((8, LANES)),
            ],
            out_specs=[whole((steps, rows, half)), whole((steps, rows, half)), whole((8, LANES))]
            + ([lanes(states)] if extend else []),
            scratch_shapes=[
                pltpu.VMEM((states, width), BF16),
                pltpu.VMEM((states, width), F32),
                pltpu.VMEM((rows, width), BF16),
                pltpu.VMEM((steps, rows, states), F32),
            ],
            compiler_params=params(),
            name="second_pass",
        )(ids, sel, second_mat, consts, hist, state_in, row_probs, loglik)

    def hand_over(state, stage):
        moves = [(stage, stage + 1), (sides - 1 - stage, sides - 2 - stage)]
        return lax.ppermute(state, "per", moves)

    if sides == 2:
        hist, state, sel, loglik = first_pass(None)
        mine, other, loglik = second_pass(hand_over(state, 0), hist, sel, loglik, False)
    else:
        kept = [jnp.zeros(x.shape, x.dtype) for x in (hist_shape, state_shape, sel_shape, ll_shape)]
        done = [jnp.zeros(x.shape, x.dtype) for x in (grad_shape, grad_shape, ll_shape, state_shape)]
        state = None
        for stage in range(sides):
            active = (side == stage) | (side == sides - 1 - stage)
            if stage < sides // 2:
                kept = lax.cond(active, lambda x, kept: list(first_pass(x)), lambda x, kept: kept, state, kept)
                state = kept[1]
            else:
                done = lax.cond(
                    active,
                    lambda x, done: list(second_pass(x, kept[0], kept[2], kept[3], True)),
                    lambda x, done: done,
                    state,
                    done,
                )
                state = done[3]
            if stage < sides - 1:
                state = hand_over(state, stage)
        mine, other, loglik, _ = done
    received = lax.ppermute(other, "st", swap)
    trans_grad = mine + received
    if sides == 2:
        pairs = [(i, j) for i in range(sides) for j in range(cores)]
        total = loglik
        for flip in range(1, 4):
            moves = [(n, n ^ flip) for n in range(len(pairs))]
            total = total + lax.ppermute(loglik, ("per", "st"), moves)
    else:
        total = lax.psum(loglik, ("per", "st"))
    return (trans_grad, total[0, :1])


def solution(mesh):
    placed = (
        P(("hh", "per"), None),
        P(("hh", "per")),
        P(("hh", "per")),
        P(("hh", "per")),
        P(("grp", "per", "st"), None, None),
        P("grp"),
        P("grp"),
        P("grp"),
    )
    return jax.shard_map(
        per_device,
        mesh=mesh,
        in_specs=placed,
        out_specs=(P(("grp", "per"), "hh", "st"), P("grp")),
        check_vma=False,
    )
```

time: 302 us -> 51.3 us (0.17)
  waiting for transfers between devices: 71.9 us -> 7.91 us
  matrix products: 63.4 us -> 0 us
  other arithmetic: 53.2 us -> 0.74 us
  local copies, waits for them, and re-layouts: 36.2 us -> 6.96 us
  blocking collectives: 24.1 us -> 0 us
  between operations: 19 us -> 1.37 us
  Pallas kernels: 0 us -> 15.4 us
  loops' own time: 11.4 us -> 0 us
    dot_general x46 -> x0, matrix products: 63.4 us -> none  [the longest x16 25.6 us: forward(): jnp.dot(prev_alpha, matrix, precision=top_precision, preferred_element_ty...]
    reduce_scatter x2 -> x0, waiting for transfers between devices: 55.2 us -> none  [the longest x1 41.5 us: per_device(): lax.psum_scatter(partial_counts, 'hh', scatter_dimension=1, tiled=True)]
    psum x2 -> x0, blocking collectives: 24.1 us -> none  [the longest x1 21 us: per_device(): loglik_all, years_all = lax.psum((loglik_core, years_core), ('hh', 'per'))]
    select_n x35 -> x0, other arithmetic: 21.2 us -> none  [the longest x32 20.9 us: forward(): scale_now = jnp.where(seen_now, jnp.sum(joint_mass, axis=1), 1.0)]
    all_to_all x4 -> x0, starting transfers between devices: 19.8 us -> none  [the longest x1 7.25 us: per_device(): lax.all_to_all(count_out, ('hh', 'per'), split_axis=1, concat_axis=1, til...]
    ppermute x0 -> x13, starting transfers between devices: none -> 18.5 us  [the longest x7 11.3 us: per_device(): lax.ppermute(packed, ('hh', 'per'), [(i, (i + r) % group) for i in range(...]
    dynamic_slice x31 -> x0, local copies, waits for them, and re-layouts: 18.2 us -> none  [the longest x16 9.38 us: per_device(): lax.scan(forward, start_alpha, (trans_probs, columns, period_ids))]
    all_to_all x4 -> x0, waiting for transfers between devices: 15.9 us -> none  [the longest x1 6.21 us: per_device(): lax.all_to_all(starts.reshape(source_rows, group_size), ('hh', 'per'), sp...]
  transfers between devices with their start and end apart: 7 -> 13, of which waited for: 5 -> 4; matrix products, arithmetic and copies ran while one was open for 5% -> 6% of each run, Pallas kernels for 0% -> 9%
where the time goes in v1:
time: 51.3 us; the launch traced here: 50.9 us
  starting transfers between devices  18.5 us (36%)
  Pallas kernels  15.4 us (30%)
  waiting for transfers between devices  7.91 us (15%)
  local copies, waits for them, and re-layouts  6.96 us (14%)
  between operations  1.37 us (3%)
  other arithmetic  0.74 us (1%)
    ppermute x7, starting transfers between devices, per_device(): lax.ppermute(packed, ('hh', 'per'), [(i, (i + r) % group) for i in range(...  11.3 us
    pallas_call x1, Pallas kernels, second_pass(): pl.pallas_call(functools.partial(second_kernel, extend, chunks), grid=(ch...  6.89 us
    ppermute x1, waiting for transfers between devices, hand_over(): return lax.ppermute(state, 'per', moves)  4.57 us
    ppermute x1, starting transfers between devices, hand_over(): return lax.ppermute(state, 'per', moves)  4.54 us
    pallas_call x1, Pallas kernels, first_pass(): pl.pallas_call(functools.partial(first_kernel, direct, resume, group, chu...  3.97 us
    unnamed x10, local copies, waits for them, and re-layouts  3.84 us
    pallas_call x1, Pallas kernels, per_device(): pl.pallas_call(prep_kernel, out_shape=[shaped((steps, 2 * states, states)...  3.16 us
    ppermute x3, waiting for transfers between devices, per_device(): total = total + lax.ppermute(loglik, ('per', 'st'), moves)  2.61 us
  transfers between devices with their start and end apart: 13, of which 4 were waited for; matrix products, arithmetic and copies ran while one was open for 6% of the time, Pallas kernels for 9%

profile of v1, /device:TPU:0, one launch (start us, length us, event | category | flops | bytes accessed | tf_op | source)
XLA Modules:
  0.0 50.9 jit_solution(8705358874593710226)
XLA Ops:
  0.6 0.5 %collective-permute-start.7 = (bf16[4,256,256]{2,1,0:T(8,128)(2,1)}, bf16[4,256,256]{2,1,0:T(8,128)(2,1)S(1)}, u32[]{:S(2)}, u32[]{:S(2)}) collective-permute-start(bf16[4,256,256]{2,1,0:T(8,128)(2,1)} %own_ref.1), channel_id=1, source_target_pairs={{0,1},{1,0},{2,3},{3,2},{4,5},{5,4},{6,7},{7,6},{8,9},{9,8},{10,11... | collective-permute-start | bytes 1572872 | tf_op jit(solution)/shard_map/ppermute | solution.py:345
  1.8 1.3 %reshape.19.start_ref = s32[1,384]{1,0:T(1,128)} reshape(s32[384]{0:T(512)} %param.9) | data formatting | bytes 3072 | tf_op jit(solution)/shard_map/reshape | solution.py:343
  3.1 1.2 %reshape.20.len_ref = s32[1,384]{1,0:T(1,128)} reshape(s32[384]{0:T(512)} %param.10) | data formatting | bytes 3072 | tf_op jit(solution)/shard_map/reshape | solution.py:343
  4.3 1.4 %pack.1.refs_1_ = f32[24,384]{1,0:T(8,128)} custom-call(s32[1]{0:T(128)S(6)} %copy.10.count_ref, f32[16,384]{1,0:T(8,128)} %bitcast.13, s32[1,384]{1,0:T(1,128)} %reshape.19.start_ref, s32[1,384]{1,0:T(1,128)} %reshape.20.len_ref), custom_call_target="tpu_custom_call" | custom-call | tf_op jit(solution)/shard_map/pack/pallas_call | solution.py:337
  5.7 5.5 %collective-permute-start.6 = (f32[24,384]{1,0:T(8,128)}, f32[24,384]{1,0:T(8,128)S(1)}, u32[]{:S(2)}, u32[]{:S(2)}) collective-permute-start(f32[24,384]{1,0:T(8,128)} %pack.1.refs_1_), channel_id=1, source_target_pairs={{0,14},{2,0},{4,2},{6,4},{8,6},{10,8},{12,10},{14,12},{1,15},{3,1}... | collective-permute-start | bytes 110600 | tf_op jit(solution)/shard_map/ppermute | solution.py:348
  11.2 0.4 collective-permute-start.5
  11.7 0.0 collective-permute-start.4
  11.7 3.0 %collective-permute-start.3 = (f32[24,384]{1,0:T(8,128)}, f32[24,384]{1,0:T(8,128)S(1)}, u32[]{:S(2)}, u32[]{:S(2)}) collective-permute-start(f32[24,384]{1,0:T(8,128)} %pack.1.refs_1_), channel_id=1, source_target_pairs={{0,8},{2,10},{4,12},{6,14},{8,0},{10,2},{12,4},{14,6},{1,9},{3,11}... | collective-permute-start | bytes 110600 | tf_op jit(solution)/shard_map/ppermute | solution.py:348
  14.7 0.0 collective-permute-done.6.refs_8_
  14.7 0.0 collective-permute-start.2
  14.7 0.7 %collective-permute-done.5.refs_7_ = f32[24,384]{1,0:T(8,128)S(1)} collective-permute-done((f32[24,384]{1,0:T(8,128)}, f32[24,384]{1,0:T(8,128)S(1)}, u32[]{:S(2)}, u32[]{:S(2)}) %collective-permute-start.5) | collective-permute-done | bytes 36896 | tf_op jit(solution)/shard_map/ppermute | solution.py:348
  15.4 1.1 %collective-permute-start.1 = (f32[24,384]{1,0:T(8,128)}, f32[24,384]{1,0:T(8,128)S(1)}, u32[]{:S(2)}, u32[]{:S(2)}) collective-permute-start(f32[24,384]{1,0:T(8,128)} %pack.1.refs_1_), channel_id=1, source_target_pairs={{0,4},{2,6},{4,8},{6,10},{8,12},{10,14},{12,0},{14,2},{1,5},{3,7},... | collective-permute-start | bytes 110600 | tf_op jit(solution)/shard_map/ppermute | solution.py:348
  16.5 0.0 collective-permute-done.7.other_ref
  16.5 1.1 %collective-permute-start = (f32[24,384]{1,0:T(8,128)}, f32[24,384]{1,0:T(8,128)S(1)}, u32[]{:S(2)}, u32[]{:S(2)}) collective-permute-start(f32[24,384]{1,0:T(8,128)} %pack.1.refs_1_), channel_id=1, source_target_pairs={{0,2},{2,4},{4,6},{6,8},{8,10},{10,12},{12,14},{14,0},{1,3},{3,5},... | collective-permute-start | bytes 110600 | tf_op jit(solution)/shard_map/ppermute | solution.py:348
  17.6 0.1 stack.27.ids_ref.refs_0_
  17.7 0.0 copy-start
  17.7 1.0 %copy-done = bf16[4,256,256]{2,1,0:T(8,128)(2,1)S(1)} copy-done((bf16[4,256,256]{2,1,0:T(8,128)(2,1)S(1)}, bf16[4,256,256]{2,1,0:T(8,128)(2,1)}, u32[]{:S(2)}) %copy-start) | copy-done | bytes 524312
  18.8 0.0 copy-start.2
  18.8 0.7 %copy-done.2 = f32[256]{0:T(256)S(1)} copy-done((f32[256]{0:T(256)S(1)}, f32[256]{0:T(256)}, u32[]{:S(2)}) %copy-start.2) | copy-done | bytes 1048
  19.5 0.0 copy-start.3
  19.5 0.7 %copy-done.3 = f32[256]{0:T(256)S(1)} copy-done((f32[256]{0:T(256)S(1)}, f32[256]{0:T(256)}, u32[]{:S(2)}) %copy-start.3) | copy-done | bytes 1048
  20.1 0.0 copy-start.4
  20.1 0.7 %copy-done.4 = f32[256]{0:T(256)S(1)} copy-done((f32[256]{0:T(256)S(1)}, f32[256]{0:T(256)}, u32[]{:S(2)}) %copy-start.4) | copy-done | bytes 1048
  20.8 3.2 %prep.1 = (bf16[8,512,256]{2,1,0:T(8,128)(2,1)S(1)}, bf16[8,512,256]{2,1,0:T(8,128)(2,1)S(1)}, f32[8,64,256]{2,1,0:T(8,128)S(1)}, f32[4,256,128]{2,1,0:T(8,128)S(1)}) custom-call(s32[6]{0:T(128)S(1)} %stack.27.ids_ref.refs_0_, bf16[4,256,256]{2,1,0:T(8,128)(2,1)S(1)} %copy-done, bf16[4,256,256]{2,1,0:T(8,128)(2,1)S(1)} %collective-permute-done.7.other_ref, ...), custom_call_target="tpu_custom_call" | custom-call | tf_op jit(solution)/shard_map/prep/pallas_call | solution.py:355
  24.0 0.0 collective-permute-done.4.refs_6_
  24.0 0.0 collective-permute-done.3.refs_5_
  24.0 0.0 collective-permute-done.2.refs_4_
  24.0 0.0 collective-permute-done.1.refs_3_
  24.0 0.0 collective-permute-done.refs_2_
  24.0 0.0 copy-start.1
  24.0 0.8 %copy-done.1 = f32[24,384]{1,0:T(8,128)S(1)} copy-done((f32[24,384]{1,0:T(8,128)S(1)}, f32[24,384]{1,0:T(8,128)}, u32[]{:S(2)}) %copy-start.1) | copy-done | bytes 36888
  24.8 4.0 %first_pass.1 = (bf16[8,256,512]{2,1,0:T(8,128)(2,1)S(1)}, bf16[256,512]{1,0:T(8,128)(2,1)S(1)}, f32[19,8,512]{2,1,0:T(8,128)S(1)}, f32[8,128]{1,0:T(8,128)S(1)}) custom-call(s32[6]{0:T(128)S(1)} %stack.27.ids_ref.refs_0_, f32[24,384]{1,0:T(8,128)S(1)} %copy-done.1, f32[24,384]{1,0:T(8,128)S(1)} %collective-permute-done.refs_2_, ...), custom_call_target="tpu_custom_call" | custom-call | tf_op jit(solution)/shard_map/first_pass/pallas_call | solution.py:395
  28.8 4.5 %collective-permute-start.8 = (bf16[256,512]{1,0:T(8,128)(2,1)S(1)}, bf16[256,512]{1,0:T(8,128)(2,1)S(1)}, u32[]{:S(2)}, u32[]{:S(2)}) collective-permute-start(bf16[256,512]{1,0:T(8,128)(2,1)S(1)} %get-tuple-element.18), channel_id=1, source_target_pairs={{0,2},{2,0},{1,3},{3,1},{4,6},{6,4},{5,7},{7,5},{8,10},{10,8},{9,1... | collective-permute-start | bytes 786440 | tf_op jit(solution)/shard_map/ppermute | solution.py:434
  33.3 4.6 %collective-permute-done.8.state_in = bf16[256,512]{1,0:T(8,128)(2,1)S(1)} collective-permute-done((bf16[256,512]{1,0:T(8,128)(2,1)S(1)}, bf16[256,512]{1,0:T(8,128)(2,1)S(1)}, u32[]{:S(2)}, u32[]{:S(2)}) %collective-permute-start.8) | collective-permute-done | bytes 262176 | tf_op jit(solution)/shard_map/ppermute | solution.py:434
  37.9 6.9 %second_pass.1 = (f32[8,64,128]{2,1,0:T(8,128)S(1)}, f32[8,64,128]{2,1,0:T(8,128)S(1)}, f32[8,128]{1,0:T(8,128)S(1)}) custom-call(s32[6]{0:T(128)S(1)} %stack.27.ids_ref.refs_0_, f32[19,8,512]{2,1,0:T(8,128)S(1)} %get-tuple-element.15.sel_ref, bf16[8,512,256]{2,1,0:T(8,128)(2,1)S(1)} %get-tuple-element.16.mat, ...), custom_call_target="tpu_custom_call" | custom-call | tf_op jit(solution)/shard_map/second_pass/pallas_call | solution.py:412
  44.8 0.1 collective-permute-start.9
  44.9 1.1 %collective-permute-start.12 = (f32[8,128]{1,0:T(8,128)S(1)}, f32[8,128]{1,0:T(8,128)S(1)}, u32[]{:S(2)}, u32[]{:S(2)}) collective-permute-start(f32[8,128]{1,0:T(8,128)S(1)} %get-tuple-element.23), channel_id=1, source_target_pairs={{0,3},{1,2},{2,1},{3,0},{4,7},{5,6},{6,5},{7,4},{8,11},{9,10},{10,... | collective-permute-start | bytes 12296 | tf_op jit(solution)/shard_map/ppermute | solution.py:467
  46.0 1.0 %collective-permute-start.11 = (f32[8,128]{1,0:T(8,128)S(1)}, f32[8,128]{1,0:T(8,128)S(1)}, u32[]{:S(2)}, u32[]{:S(2)}) collective-permute-start(f32[8,128]{1,0:T(8,128)S(1)} %get-tuple-element.23), channel_id=1, source_target_pairs={{0,2},{1,3},{2,0},{3,1},{4,6},{5,7},{6,4},{7,5},{8,10},{9,11},{10,... | collective-permute-start | bytes 12296 | tf_op jit(solution)/shard_map/ppermute | solution.py:467
  47.0 0.0 collective-permute-start.10
  47.0 1.0 %collective-permute-done.12 = f32[8,128]{1,0:T(8,128)S(1)} collective-permute-done((f32[8,128]{1,0:T(8,128)S(1)}, f32[8,128]{1,0:T(8,128)S(1)}, u32[]{:S(2)}, u32[]{:S(2)}) %collective-permute-start.12) | collective-permute-done | bytes 4128 | tf_op jit(solution)/shard_map/ppermute | solution.py:467
  48.0 1.7 %collective-permute-done.11 = f32[8,128]{1,0:T(8,128)S(1)} collective-permute-done((f32[8,128]{1,0:T(8,128)S(1)}, f32[8,128]{1,0:T(8,128)S(1)}, u32[]{:S(2)}, u32[]{:S(2)}) %collective-permute-start.11) | collective-permute-done | bytes 4128 | tf_op jit(solution)/shard_map/ppermute | solution.py:467
  49.6 0.0 collective-permute-done.10
  49.6 0.5 %slice.3 = f32[1,1]{1,0:T(1,128)} slice(f32[8,128]{1,0:T(8,128)S(1)} %add_add_fusion), slice={[0:1], [0:1]} | slice | bytes 8 | tf_op jit(solution)/shard_map/slice | solution.py:470
  50.1 0.0 collective-permute-done.9
  50.1 0.7 %add.16 = f32[8,64,128]{2,1,0:T(8,128)} add(f32[8,64,128]{2,1,0:T(8,128)S(1)} %get-tuple-element.21, f32[8,64,128]{2,1,0:T(8,128)S(1)} %collective-permute-done.9) | non-fusion elementwise | flops 65536 | bytes 786432 | tf_op jit(solution)/shard_map/add | solution.py:461
  (1 shorter events, 0.0 us)
Async XLA Ops:
  0.6 15.9 %collective-permute-start.7 = (bf16[4,256,256]{2,1,0:T(8,128)(2,1)}, bf16[4,256,256]{2,1,0:T(8,128)(2,1)S(1)}, u32[]{:S(2)}, u32[]{:S(2)}) collective-permute-start(bf16[4,256,256]{2,1,0:T(8,128)(2,1)} %own_ref.1), channel_id=1, source_target_pairs={{0,1},{1,0},{2,3},{3,2},{4,5},{5,4},{6,7},{7,6},{8,9},{9,8},{10,11... | collective-permute-start | bytes 1572872 | tf_op jit(solution)/shard_map/ppermute | solution.py:345
  5.7 9.0 %collective-permute-start.6 = (f32[24,384]{1,0:T(8,128)}, f32[24,384]{1,0:T(8,128)S(1)}, u32[]{:S(2)}, u32[]{:S(2)}) collective-permute-start(f32[24,384]{1,0:T(8,128)} %pack.1.refs_1_), channel_id=1, source_target_pairs={{0,14},{2,0},{4,2},{6,4},{8,6},{10,8},{12,10},{14,12},{1,15},{3,1}... | collective-permute-start | bytes 110600 | tf_op jit(solution)/shard_map/ppermute | solution.py:348
  11.2 4.2 %collective-permute-start.5 = (f32[24,384]{1,0:T(8,128)}, f32[24,384]{1,0:T(8,128)S(1)}, u32[]{:S(2)}, u32[]{:S(2)}) collective-permute-start(f32[24,384]{1,0:T(8,128)} %pack.1.refs_1_), channel_id=1, source_target_pairs={{0,12},{2,14},{4,0},{6,2},{8,4},{10,6},{12,8},{14,10},{1,13},{3,15... | collective-permute-start | bytes 110600 | tf_op jit(solution)/shard_map/ppermute | solution.py:348
  11.7 12.3 %collective-permute-start.4 = (f32[24,384]{1,0:T(8,128)}, f32[24,384]{1,0:T(8,128)S(1)}, u32[]{:S(2)}, u32[]{:S(2)}) collective-permute-start(f32[24,384]{1,0:T(8,128)} %pack.1.refs_1_), channel_id=1, source_target_pairs={{0,10},{2,12},{4,14},{6,0},{8,2},{10,4},{12,6},{14,8},{1,11},{3,13... | collective-permute-start | bytes 110600 | tf_op jit(solution)/shard_map/ppermute | solution.py:348
  11.7 12.3 %collective-permute-start.3 = (f32[24,384]{1,0:T(8,128)}, f32[24,384]{1,0:T(8,128)S(1)}, u32[]{:S(2)}, u32[]{:S(2)}) collective-permute-start(f32[24,384]{1,0:T(8,128)} %pack.1.refs_1_), channel_id=1, source_target_pairs={{0,8},{2,10},{4,12},{6,14},{8,0},{10,2},{12,4},{14,6},{1,9},{3,11}... | collective-permute-start | bytes 110600 | tf_op jit(solution)/shard_map/ppermute | solution.py:348
  14.7 9.3 %collective-permute-start.2 = (f32[24,384]{1,0:T(8,128)}, f32[24,384]{1,0:T(8,128)S(1)}, u32[]{:S(2)}, u32[]{:S(2)}) collective-permute-start(f32[24,384]{1,0:T(8,128)} %pack.1.refs_1_), channel_id=1, source_target_pairs={{0,6},{2,8},{4,10},{6,12},{8,14},{10,0},{12,2},{14,4},{1,7},{3,9},... | collective-permute-start | bytes 110600 | tf_op jit(solution)/shard_map/ppermute | solution.py:348
  15.4 8.6 %collective-permute-start.1 = (f32[24,384]{1,0:T(8,128)}, f32[24,384]{1,0:T(8,128)S(1)}, u32[]{:S(2)}, u32[]{:S(2)}) collective-permute-start(f32[24,384]{1,0:T(8,128)} %pack.1.refs_1_), channel_id=1, source_target_pairs={{0,4},{2,6},{4,8},{6,10},{8,12},{10,14},{12,0},{14,2},{1,5},{3,7},... | collective-permute-start | bytes 110600 | tf_op jit(solution)/shard_map/ppermute | solution.py:348
  16.5 7.5 %collective-permute-start = (f32[24,384]{1,0:T(8,128)}, f32[24,384]{1,0:T(8,128)S(1)}, u32[]{:S(2)}, u32[]{:S(2)}) collective-permute-start(f32[24,384]{1,0:T(8,128)} %pack.1.refs_1_), channel_id=1, source_target_pairs={{0,2},{2,4},{4,6},{6,8},{8,10},{10,12},{12,14},{14,0},{1,3},{3,5},... | collective-permute-start | bytes 110600 | tf_op jit(solution)/shard_map/ppermute | solution.py:348
  17.7 1.0 %copy-start = (bf16[4,256,256]{2,1,0:T(8,128)(2,1)S(1)}, bf16[4,256,256]{2,1,0:T(8,128)(2,1)}, u32[]{:S(2)}) copy-start(bf16[4,256,256]{2,1,0:T(8,128)(2,1)} %own_ref.1) | copy-start | bytes 1572868
  18.8 0.7 %copy-start.2 = (f32[256]{0:T(256)S(1)}, f32[256]{0:T(256)}, u32[]{:S(2)}) copy-start(f32[256]{0:T(256)} %param.13) | copy-start | bytes 3076
  19.5 0.7 %copy-start.3 = (f32[256]{0:T(256)S(1)}, f32[256]{0:T(256)}, u32[]{:S(2)}) copy-start(f32[256]{0:T(256)} %param.14) | copy-start | bytes 3076
  20.1 0.7 %copy-start.4 = (f32[256]{0:T(256)S(1)}, f32[256]{0:T(256)}, u32[]{:S(2)}) copy-start(f32[256]{0:T(256)} %param.15) | copy-start | bytes 3076
  24.0 0.8 %copy-start.1 = (f32[24,384]{1,0:T(8,128)S(1)}, f32[24,384]{1,0:T(8,128)}, u32[]{:S(2)}) copy-start(f32[24,384]{1,0:T(8,128)} %pack.1.refs_1_) | copy-start | bytes 110596
  28.8 9.1 %collective-permute-start.8 = (bf16[256,512]{1,0:T(8,128)(2,1)S(1)}, bf16[256,512]{1,0:T(8,128)(2,1)S(1)}, u32[]{:S(2)}, u32[]{:S(2)}) collective-permute-start(bf16[256,512]{1,0:T(8,128)(2,1)S(1)} %get-tuple-element.18), channel_id=1, source_target_pairs={{0,2},{2,0},{1,3},{3,1},{4,6},{6,4},{5,7},{7,5},{8,10},{10,8},{9,1... | collective-permute-start | bytes 786440 | tf_op jit(solution)/shard_map/ppermute | solution.py:434
  44.8 5.4 %collective-permute-start.9 = (f32[8,64,128]{2,1,0:T(8,128)S(1)}, f32[8,64,128]{2,1,0:T(8,128)S(1)}, u32[]{:S(2)}, u32[]{:S(2)}) collective-permute-start(f32[8,64,128]{2,1,0:T(8,128)S(1)} %get-tuple-element.22), channel_id=1, source_target_pairs={{0,1},{1,0},{2,3},{3,2},{4,5},{5,4},{6,7},{7,6},{8,9},{9,8},{10,11... | collective-permute-start | bytes 786440 | tf_op jit(solution)/shard_map/ppermute | solution.py:460
  44.9 3.1 %collective-permute-start.12 = (f32[8,128]{1,0:T(8,128)S(1)}, f32[8,128]{1,0:T(8,128)S(1)}, u32[]{:S(2)}, u32[]{:S(2)}) collective-permute-start(f32[8,128]{1,0:T(8,128)S(1)} %get-tuple-element.23), channel_id=1, source_target_pairs={{0,3},{1,2},{2,1},{3,0},{4,7},{5,6},{6,5},{7,4},{8,11},{9,10},{10,... | collective-permute-start | bytes 12296 | tf_op jit(solution)/shard_map/ppermute | solution.py:467
  46.0 3.6 %collective-permute-start.11 = (f32[8,128]{1,0:T(8,128)S(1)}, f32[8,128]{1,0:T(8,128)S(1)}, u32[]{:S(2)}, u32[]{:S(2)}) collective-permute-start(f32[8,128]{1,0:T(8,128)S(1)} %get-tuple-element.23), channel_id=1, source_target_pairs={{0,2},{1,3},{2,0},{3,1},{4,6},{5,7},{6,4},{7,5},{8,10},{9,11},{10,... | collective-permute-start | bytes 12296 | tf_op jit(solution)/shard_map/ppermute | solution.py:467
  47.0 2.6 %collective-permute-start.10 = (f32[8,128]{1,0:T(8,128)S(1)}, f32[8,128]{1,0:T(8,128)S(1)}, u32[]{:S(2)}, u32[]{:S(2)}) collective-permute-start(f32[8,128]{1,0:T(8,128)S(1)} %get-tuple-element.23), channel_id=1, source_target_pairs={{0,1},{1,0},{2,3},{3,2},{4,5},{5,4},{6,7},{7,6},{8,9},{9,8},{10,11... | collective-permute-start | bytes 12296 | tf_op jit(solution)/shard_map/ppermute | solution.py:467

commit v2 on v1

v2 whole, which is shorter than its diff:
```python
import functools

import jax
import jax.numpy as jnp
from jax import lax
from jax.experimental import pallas as pl
from jax.experimental.pallas import tpu as pltpu
from jax.sharding import PartitionSpec as P

HB = 128
LANES = 128
HALF = HB // 2
SEEN = 16.0
F32 = jnp.float32
BF16 = jnp.bfloat16
LOG2E = 1.4426950408889634
LN2 = 0.6931471805599453
VMEM_LIMIT = 40 * 1024 * 1024
EXTRA = 16


def vmem():
    return pl.BlockSpec(memory_space=pltpu.VMEM)


def smem():
    return pl.BlockSpec(memory_space=pltpu.SMEM)


def anywhere():
    return pl.BlockSpec(memory_space=pl.ANY)


def params():
    return pltpu.CompilerParams(vmem_limit_bytes=VMEM_LIMIT)


def tiles(width):
    return [slice(q, q + LANES) for q in range(0, width, LANES)]


def pack_kernel(ids_ref, count_ref, earn_any, start_any, len_any, out_ref, earn_ref, start_ref, len_ref, sems):
    copies = [
        pltpu.make_async_copy(src, dst, sems.at[i])
        for i, (src, dst) in enumerate(((earn_any, earn_ref), (start_any, start_ref), (len_any, len_ref)))
    ]
    for copy in copies:
        copy.start()
    for copy in copies:
        copy.wait()
    periods, slot_rows = earn_ref.shape
    core = ids_ref[0]
    low_lane = lax.broadcasted_iota(jnp.int32, (periods // 2, HB), 1) < HALF
    time = lax.broadcasted_iota(jnp.int32, (periods, HB), 0)
    for slot in range(slot_rows // HB):
        cols = slice(slot * HB, (slot + 1) * HB)
        begin = start_ref[slot : slot + 1, :]
        seen = (time >= begin) & (time < begin + len_ref[slot : slot + 1, :])
        live = slot < count_ref[0]
        shift = jnp.where(live, jnp.where(seen, SEEN, 0.0), -SEEN)
        value = earn_ref[:, cols] + shift
        early, late = value[: periods // 2], value[periods // 2 :]
        turned = pltpu.roll(jnp.where(core == 0, late, early), HALF, 1)
        packed = jnp.where(low_lane, jnp.where(core == 0, early, turned), jnp.where(core == 0, turned, late))
        for to in range(out_ref.shape[0]):
            out_ref[to, :, cols] = packed


def prep_kernel(
    ids_ref, own_any, other_ref, init_any, mean_any, sd_any,
    first_mat, second_mat, row_probs, consts, scratch, own_ref, init_ref, mean_ref, sd_ref, sems,
):
    pairs = ((own_any, own_ref), (init_any, init_ref), (mean_any, mean_ref), (sd_any, sd_ref))
    copies = [pltpu.make_async_copy(src, dst, sems.at[i]) for i, (src, dst) in enumerate(pairs)]
    for copy in copies:
        copy.start()
    for copy in copies:
        copy.wait()
    core, forward_first, row_begin = ids_ref[0], ids_ref[1], ids_ref[2]
    part, states, _ = own_ref.shape
    rows = row_probs.shape[1]

    def column(row):
        return jnp.broadcast_to(row, (LANES, states)).T

    raised = jnp.exp(init_ref[...])
    start = raised / jnp.sum(raised, axis=1, keepdims=True)
    consts[0] = column(start)
    consts[1] = column(mean_ref[...])
    consts[2] = column((-0.5 * LOG2E) * jnp.exp(-2.0 * sd_ref[...]))
    consts[3] = column(-LOG2E * sd_ref[...])
    start_high = start.astype(BF16).astype(F32)
    row = lax.broadcasted_iota(jnp.int32, (EXTRA, states), 0)
    start_rows = jnp.where(row == 0, start_high, jnp.where(row == 1, start - start_high, 0.0)).astype(BF16)

    def put(ref, at, value):
        high = value.astype(BF16)
        ref[at, :states, :] = high
        ref[at, states : 2 * states, :] = (value - high.astype(F32)).astype(BF16)

    for source, ref in ((core, own_ref), (1 - core, other_ref)):

        @pl.loop(0, part)
        def _(i):
            at = source * part + i
            lifted = jnp.exp(ref[i].astype(F32))
            probs = lifted / jnp.sum(lifted, axis=1, keepdims=True)
            scratch[...] = probs
            row_probs[at] = scratch[pl.ds(pl.multiple_of(row_begin, rows), rows), :]
            turned = probs.T
            first_mat[at, 2 * states :, :] = start_rows

            @pl.when(forward_first == 1)
            def _():
                put(first_mat, at, turned)
                put(second_mat, at, probs)

            @pl.when(forward_first == 0)
            def _():
                put(first_mat, at, probs)
                put(second_mat, at, turned)


def emission(sel_ref, consts, step_now, cols):
    gap = sel_ref[0, step_now, :1, cols] - consts[1]
    power = gap * gap * consts[2] + consts[3]
    top = jnp.max(power, axis=0, keepdims=True)
    return jnp.exp2(power - top), top


def is_moving(sel_ref, step_now, cols):
    return sel_ref[1, step_now, :1, cols] > 0.5


def is_seen(sel_ref, step_now, cols):
    return sel_ref[2, step_now, :1, cols] > 0.5


def column_sum(x):
    return jnp.sum(x, axis=0, keepdims=True)


def own_rows(row_begin, rows):
    return pl.ds(pl.multiple_of(row_begin, rows), rows)


def outer_sum(weights_ref, carried):
    return lax.dot_general(weights_ref[...], carried, (((1,), (1,)), ((), ())), preferred_element_type=F32)


def run_forward(lead, mat, hist, sel_ref, consts, ab_ref, logs, second=None):
    steps, states, width = hist.shape
    cuts = tiles(width)
    inverse = [1.0 / column_sum(ab_ref[:, cols].astype(F32)) for cols in cuts]
    for k in range(steps):
        step_now = lead + k
        if second is None:
            hist[k] = ab_ref[...]
        else:
            weights_ref, counts_ref, row_begin = second
            own_alpha = ab_ref[own_rows(row_begin, weights_ref.shape[0]), :].astype(F32)
        product = jnp.dot(mat[k, : 2 * states, :], ab_ref[...], preferred_element_type=F32)
        for q, cols in enumerate(cuts):
            moved = (product[:states, cols] + product[states:, cols]) * inverse[q]
            moving = is_moving(sel_ref, step_now, cols)
            if second is not None:
                total = column_sum(moved * hist[k, :, cols].astype(F32))
                weight = jnp.where(moving, inverse[q] / total, 0.0)
                weights_ref[:, cols] = (own_alpha[:, cols] * weight).astype(BF16)
            emit, top = emission(sel_ref, consts, step_now, cols)
            joint = jnp.where(moving, moved, consts[0]) * emit
            scale = column_sum(joint)
            if second is None:
                seen = is_seen(sel_ref, step_now, cols)
                logs[q] = logs[q] + jnp.where(seen, jnp.log(scale) + top * LN2, 0.0)
            inverse[q] = 1.0 / scale
            ab_ref[:, cols] = joint.astype(BF16)
        if second is not None:
            counts_ref[k] += outer_sum(weights_ref, hist[k])
    return logs


def run_backward(lead, mat, hist, sel_ref, consts, back_ref, ub_ref, logs, second=None):
    steps, states, width = hist.shape
    cuts = tiles(width)
    for k in reversed(range(steps)):
        step_now = lead + k
        shrink = []
        for q, cols in enumerate(cuts):
            emit, top = emission(sel_ref, consts, step_now, cols)
            carried = emit * back_ref[:, cols]
            size = column_sum(carried)
            if second is None:
                seen = is_seen(sel_ref, step_now, cols)
                logs[q] = logs[q] + jnp.where(seen, jnp.log(size) + top * LN2, 0.0)
            shrink.append(1.0 / size)
            ub_ref[:, cols] = carried.astype(BF16)
        if second is None:
            hist[k] = ub_ref[...]
        else:
            weights_ref, counts_ref, row_begin = second
            own_alpha = hist[k, own_rows(row_begin, weights_ref.shape[0]), :].astype(F32)
        product = jnp.dot(mat[k], ub_ref[...], preferred_element_type=F32)
        for q, cols in enumerate(cuts):
            moving = is_moving(sel_ref, step_now, cols)
            pulled = (product[:states, cols] + product[states : 2 * states, cols]) * shrink[q]
            if second is None:
                seen = is_seen(sel_ref, step_now, cols)
                begun = column_sum(product[2 * states :, cols]) * shrink[q]
                rest = jnp.where(seen, begun, back_ref[:, cols])
            else:
                total = column_sum(pulled * hist[k, :, cols].astype(F32))
                weight = jnp.where(moving, shrink[q] / total, 0.0)
                weights_ref[:, cols] = (own_alpha[:, cols] * weight).astype(BF16)
                rest = 1.0
            back_ref[:, cols] = jnp.where(moving, pulled, rest)
        if second is not None:
            counts_ref[k] += outer_sum(weights_ref, ub_ref[...])
    return logs


def put_state(state_out, values, logs):
    states = state_out.shape[0] - EXTRA
    state_out[:states, :] = values
    for q, cols in enumerate(tiles(state_out.shape[1])):
        high = logs[q].astype(BF16).astype(F32)
        middle = (logs[q] - high).astype(BF16).astype(F32)
        row = lax.broadcasted_iota(jnp.int32, (EXTRA, LANES), 0)
        piece = jnp.where(
            row == 0, high, jnp.where(row == 1, middle, jnp.where(row == 2, logs[q] - high - middle, 0.0))
        )
        state_out[states:, cols] = piece.astype(BF16)


def state_logs(state_ref):
    states = state_ref.shape[0] - EXTRA
    return [column_sum(state_ref[states:, cols].astype(F32)) for cols in tiles(state_ref.shape[1])]


def first_kernel(resume, grids, part, ids_ref, rows_ref, mat, consts, *refs):
    state_in = refs[0] if resume else None
    hist, state_out, sel_ref, ab_ref, back_ref = refs[-5:]
    forward_first, lead = ids_ref[1], ids_ref[3]
    chunk = part * grids + (pl.program_id(0) if grids > 1 else 0)
    steps, states, width = hist.shape
    cuts = tiles(width)
    group, half_periods, slot_rows = rows_ref.shape
    tops = 2 * len(cuts)

    def scan_source(d, carry):
        rank, picked = carry
        for slot in range(slot_rows // HB):
            block = rows_ref[d, :, slot * HB : (slot + 1) * HB]
            live = block > -0.5 * SEEN
            picked = [jnp.where(live & (rank == chunk * tops + i), block, old) for i, old in enumerate(picked)]
            rank = rank + live.astype(jnp.int32)
        return rank, picked

    carry = (jnp.zeros((half_periods, HB), jnp.int32), [jnp.zeros((half_periods, HB), F32)] * tops)
    if group <= 8:
        for d in range(group):
            carry = scan_source(d, carry)
    else:
        carry = lax.fori_loop(0, group, scan_source, carry)
    low_lane = lax.broadcasted_iota(jnp.int32, (half_periods, HB), 1) < HALF
    for q, cols in enumerate(cuts):
        left, right = carry[1][2 * q], carry[1][2 * q + 1]
        before = jnp.zeros((1, HB), F32)
        for late in range(2):
            value = (
                jnp.where(low_lane, pltpu.roll(left, HALF, 1), right)
                if late
                else jnp.where(low_lane, left, pltpu.roll(right, HALF, 1))
            )
            seen = value > 0.5 * SEEN
            earn = jnp.where(seen, value - SEEN, value)
            seen = seen.astype(F32)
            for i in range(half_periods):
                at = late * half_periods + i
                now = seen[i : i + 1]
                sel_ref[0, at, :, cols] = jnp.broadcast_to(earn[i : i + 1], (8, HB))
                sel_ref[1, at, :, cols] = jnp.broadcast_to(now * before, (8, HB))
                sel_ref[2, at, :, cols] = jnp.broadcast_to(now, (8, HB))
                before = now
    zeros = [jnp.zeros((1, LANES), F32) for _ in cuts]

    @pl.when(forward_first == 1)
    def _():
        if resume:
            ab_ref[...] = state_in[:states, :]
        else:
            for cols in cuts:
                ab_ref[:, cols] = consts[0].astype(BF16)
        logs = state_logs(state_in) if resume else list(zeros)
        logs = run_forward(lead, mat, hist, sel_ref, consts, ab_ref, logs)
        put_state(state_out, ab_ref[...], logs)

    @pl.when(forward_first == 0)
    def _():
        if resume:
            back_ref[...] = state_in[:states, :].astype(F32)
        else:
            back_ref[...] = jnp.ones_like(back_ref)
        logs = state_logs(state_in) if resume else list(zeros)
        logs = run_backward(lead, mat, hist, sel_ref, consts, back_ref, ab_ref, logs)
        put_state(state_out, back_ref[...].astype(BF16), logs)


def second_kernel(resume, last, extend, grids, *refs):
    refs = list(refs)
    ids_ref, sel_ref, mat, consts, hist, own_state, state_in = (refs.pop(0) for _ in range(7))
    counts_in, sums_in = (refs.pop(0), refs.pop(0)) if resume else (None, None)
    row_probs = refs.pop(0) if last else None
    mine_ref, other_ref = (refs.pop(0), refs.pop(0)) if last else (None, None)
    counts_out, sums_out = (None, None) if last else (refs.pop(0), refs.pop(0))
    state_out = refs.pop(0) if extend else None
    ab_ref, back_ref, weights_ref = refs[:3]
    counts_ref, sums_ref = refs[3:] if last else (counts_out, sums_out)
    core, forward_first, row_begin, lead = ids_ref[0], ids_ref[1], ids_ref[2], ids_ref[3]
    chunk = pl.program_id(0) if grids > 1 else 0
    steps, states, width = hist.shape
    second = (weights_ref, counts_ref, row_begin)

    @pl.when(chunk == 0)
    def _():
        if resume:
            counts_ref[...] = counts_in[...]
            sums_ref[...] = sums_in[...]
        else:
            counts_ref[...] = jnp.zeros_like(counts_ref)
            sums_ref[...] = jnp.zeros_like(sums_ref)

    def add_sums(alpha_ref, other_state):
        total = jnp.zeros((1, LANES), F32)
        years = jnp.zeros((8, LANES), F32)
        for cols, here, there in zip(tiles(width), state_logs(alpha_ref), state_logs(other_state)):
            alpha = alpha_ref[:states, cols].astype(F32)
            meet = column_sum(alpha * other_state[:states, cols].astype(F32))
            total += here + there + jnp.log(meet / column_sum(alpha))
            years += jnp.sum(sel_ref[2, :, :, cols], axis=0)
        total = jnp.broadcast_to(jnp.sum(total, axis=1, keepdims=True), (1, LANES))
        years = jnp.broadcast_to(jnp.sum(years[:1], axis=1, keepdims=True), (1, LANES))
        row = lax.broadcasted_iota(jnp.int32, (8, LANES), 0)
        sums_ref[...] += jnp.where(row == 0, total, jnp.where(row == 1, years, 0.0))

    zeros = [jnp.zeros((1, LANES), F32) for _ in tiles(width)]

    @pl.when(forward_first == 0)
    def _():
        add_sums(state_in, own_state)
        ab_ref[...] = state_in[:states, :]
        run_forward(lead, mat, hist, sel_ref, consts, ab_ref, list(zeros), second)
        if extend:
            put_state(state_out, ab_ref[...], zeros)

    @pl.when(forward_first == 1)
    def _():
        add_sums(own_state, state_in)
        back_ref[...] = state_in[:states, :].astype(F32)
        run_backward(lead, mat, hist, sel_ref, consts, back_ref, ab_ref, list(zeros), second)
        if extend:
            put_state(state_out, back_ref[...].astype(BF16), zeros)

    if last:

        @pl.when(chunk == grids - 1)
        def _():
            rows = counts_ref.shape[1]
            for k in range(steps):
                probs = row_probs[k]
                weighted = probs * counts_ref[k]
                grad = weighted - probs * jnp.sum(weighted, axis=1, keepdims=True)
                for side in range(2):
                    piece = grad[:, side * LANES : (side + 1) * LANES]
                    at = slice(k * rows, (k + 1) * rows)

                    @pl.when(core == side)
                    def _():
                        mine_ref[at, :] = piece

                    @pl.when(core != side)
                    def _():
                        other_ref[at, :] = piece

            mine_ref[steps * rows :, :] = sums_ref[...]
            other_ref[steps * rows :, :] = sums_ref[...]


def finish_kernel(scale, mine_ref, other_ref, grad_ref, mean_ref):
    count = grad_ref.shape[0]
    total = mine_ref[count : count + 1, :] + other_ref[count : count + 1, :]
    years = mine_ref[count + 1 : count + 2, :] + other_ref[count + 1 : count + 2, :]
    grad_ref[...] = (mine_ref[:count, :] + other_ref[:count, :]) * (scale / years)
    mean_ref[0] = (total / years)[0, 0]


def per_device(
    earnings, starts, lengths, block_count, trans_logits, init_logits, state_mean, log_sd
):
    slot_rows, periods = earnings.shape
    states = init_logits.shape[0]
    group = lax.axis_size(("hh", "per"))
    sides = lax.axis_size("per")
    cores = lax.axis_size("st")
    part = trans_logits.shape[0]
    steps = part * cores
    rows = states // lax.axis_size("hh")
    households = group * HB // cores
    parts = 2 if households <= 4 * HB else 1
    share = households // parts
    width = min(2 * HB, share)
    grids = share // width
    side = lax.axis_index("per")
    core = lax.axis_index("st")
    forward_first = (2 * side < sides).astype(jnp.int32)
    ids = jnp.stack([core, forward_first, lax.axis_index("hh") * rows, side * steps]).astype(jnp.int32)
    shaped = jax.ShapeDtypeStruct
    dma = pltpu.SemaphoreType.DMA

    swap = [(0, 1), (1, 0)]
    other_logits = lax.ppermute(trans_logits, "st", swap)
    packed = pl.pallas_call(
        pack_kernel,
        out_shape=shaped((group, periods // 2, slot_rows), F32),
        in_specs=[smem(), smem(), anywhere(), anywhere(), anywhere()],
        out_specs=vmem(),
        scratch_shapes=[
            pltpu.VMEM((periods, slot_rows), F32),
            pltpu.VMEM((slot_rows // HB, HB), jnp.int32),
            pltpu.VMEM((slot_rows // HB, HB), jnp.int32),
            dma((3,)),
        ],
        name="pack",
    )(ids, block_count, earnings.T, starts.reshape(-1, HB), lengths.reshape(-1, HB))
    gathered = lax.all_to_all(packed, ("hh", "per"), split_axis=0, concat_axis=0, tiled=True)

    first_mat, second_mat, row_probs, consts = pl.pallas_call(
        prep_kernel,
        out_shape=[
            shaped((steps, 2 * states + EXTRA, states), BF16),
            shaped((steps, 2 * states, states), BF16),
            shaped((steps, rows, states), F32),
            shaped((4, states, LANES), F32),
        ],
        in_specs=[smem(), anywhere(), vmem(), anywhere(), anywhere(), anywhere()],
        out_specs=[vmem()] * 4,
        scratch_shapes=[
            pltpu.VMEM((states, states), F32),
            pltpu.VMEM(trans_logits.shape, BF16),
            pltpu.VMEM((1, states), F32),
            pltpu.VMEM((1, states), F32),
            pltpu.VMEM((1, states), F32),
            dma((4,)),
        ],
        compiler_params=params(),
        name="prep",
    )(
        ids, trans_logits, other_logits,
        init_logits.reshape(1, states), state_mean.reshape(1, states), log_sd.reshape(1, states),
    )

    def whole(*shape):
        if grids == 1:
            return vmem()
        return pl.BlockSpec(shape, lambda g: (0,) * len(shape))

    def lanes(*lead):
        if grids == 1:
            return vmem()
        return pl.BlockSpec(lead + (width,), lambda g: (0,) * len(lead) + (g,))

    grid = (grids,) if grids > 1 else ()
    hist_shape = shaped((steps, states, share), BF16)
    state_shape = shaped((states + EXTRA, share), BF16)
    sel_shape = shaped((3, periods, 8, share), F32)
    swap_shape = shaped((steps * rows + 8, LANES), F32)
    counts_shape = shaped((steps, rows, states), F32)
    sums_shape = shaped((8, LANES), F32)
    hist_spec, state_spec, sel_spec = lanes(steps, states), lanes(states + EXTRA), lanes(3, periods, 8)
    const_spec = whole(4, states, LANES)

    def first_pass(index, state_in):
        resume = state_in is not None
        return pl.pallas_call(
            functools.partial(first_kernel, resume, grids, index),
            grid=grid,
            out_shape=[hist_shape, state_shape, sel_shape],
            in_specs=[smem(), whole(*gathered.shape), whole(*first_mat.shape), const_spec]
            + [state_spec] * resume,
            out_specs=[hist_spec, state_spec, sel_spec],
            scratch_shapes=[pltpu.VMEM((states, width), BF16), pltpu.VMEM((states, width), F32)],
            compiler_params=params(),
            name="first_pass",
        )(ids, gathered, first_mat, consts, *([state_in] if resume else []))

    def second_pass(kept, state_in, sums_in, last, extend):
        hist, own_state, sel = kept
        resume = sums_in is not None
        scratch = [
            pltpu.VMEM((states, width), BF16),
            pltpu.VMEM((states, width), F32),
            pltpu.VMEM((rows, width), BF16),
        ]
        counts_spec, sums_spec = whole(*counts_shape.shape), whole(*sums_shape.shape)
        if last:
            out_shape = [swap_shape] * 2
            scratch += [pltpu.VMEM(counts_shape.shape, F32), pltpu.VMEM(sums_shape.shape, F32)]
        else:
            out_shape = [counts_shape, sums_shape]
        out_specs = [whole(*x.shape) for x in out_shape]
        if extend:
            out_shape, out_specs = out_shape + [state_shape], out_specs + [state_spec]
        return pl.pallas_call(
            functools.partial(second_kernel, resume, last, extend, grids),
            grid=grid,
            out_shape=out_shape,
            in_specs=[smem(), sel_spec, whole(*second_mat.shape), const_spec, hist_spec, state_spec, state_spec]
            + [counts_spec, sums_spec] * resume
            + [whole(*row_probs.shape)] * last,
            out_specs=out_specs,
            scratch_shapes=scratch,
            compiler_params=params(),
            name="second_pass",
        )(
            ids, sel, second_mat, consts, hist, own_state, state_in,
            *(sums_in if resume else []),
            *([row_probs] if last else []),
        )

    def hand_over(state, stage):
        moves = [(stage, stage + 1), (sides - 1 - stage, sides - 2 - stage)]
        return lax.ppermute(state, "per", moves)

    if sides == 2:
        kept = [first_pass(index, None) for index in range(parts)]
        arrived = [hand_over(each[1], 0) for each in kept]
        sums = None
        for index in range(parts):
            sums = second_pass(kept[index], arrived[index], sums, index == parts - 1, False)
        mine, other = sums
    else:
        kept = [jnp.zeros(x.shape, x.dtype) for x in (hist_shape, state_shape, sel_shape)]
        done = [jnp.zeros(x.shape, x.dtype) for x in (swap_shape, swap_shape, state_shape)]
        state = None
        for stage in range(sides):
            active = (side == stage) | (side == sides - 1 - stage)
            if stage < sides // 2:
                kept = lax.cond(
                    active, lambda x, kept: list(first_pass(0, x)), lambda x, kept: kept, state, kept
                )
                state = kept[1]
            else:
                done = lax.cond(
                    active,
                    lambda x, done: list(second_pass(kept, x, None, True, True)),
                    lambda x, done: done,
                    state,
                    done,
                )
                state = done[2]
            if stage < sides - 1:
                state = hand_over(state, stage)
        mine, other, _ = done
        total = jnp.where(side == sides // 2, mine[steps * rows], 0.0)
        total = lax.psum(total, "per")
        mine = mine.at[steps * rows].set(total)
        other = other.at[steps * rows].set(total)
    received = lax.ppermute(other, "st", swap)
    trans_grad, mean_loglik = pl.pallas_call(
        functools.partial(finish_kernel, float(states * states * periods)),
        out_shape=[shaped((steps * rows, LANES), F32), shaped((1,), F32)],
        in_specs=[vmem(), vmem()],
        out_specs=[vmem(), smem()],
        name="finish",
    )(mine, received)
    return (trans_grad.reshape(steps, rows, LANES), mean_loglik)


def solution(mesh):
    placed = (
        P(("hh", "per"), None),
        P(("hh", "per")),
        P(("hh", "per")),
        P(("hh", "per")),
        P(("grp", "per", "st"), None, None),
        P("grp"),
        P("grp"),
        P("grp"),
    )
    return jax.shard_map(
        per_device,
        mesh=mesh,
        in_specs=placed,
        out_specs=(P(("grp", "per"), "hh", "st"), P("grp")),
        check_vma=False,
    )
```

time: 51.3 us -> 46 us (0.90)
  starting transfers between devices: 18.5 us -> 10.6 us
  Pallas kernels: 15.4 us -> 21.2 us
  waiting for transfers between devices: 7.91 us -> 2.51 us
  local copies, waits for them, and re-layouts: 6.96 us -> 9.03 us
    ppermute x10 -> x0, starting transfers between devices: 13.4 us -> none  [the longest x7 11.3 us: per_device(): lax.ppermute(packed, ('hh', 'per'), [(i, (i + r) % group) for i in range(...]
    all_to_all x0 -> x1, starting transfers between devices: none -> 6.83 us  [per_device(): lax.all_to_all(packed, ('hh', 'per'), split_axis=0, concat_axis=0, tiled=...]
    pallas_call x4 -> x7, Pallas kernels: 15.4 us -> 21.2 us  [the longest x2 7.99 us: second_pass(): pl.pallas_call(functools.partial(second_kernel, resume, last, extend, gri...]
    unnamed x10 -> x26, local copies, waits for them, and re-layouts: 3.84 us -> 9.03 us
    ppermute x1 -> x2, waiting for transfers between devices: 4.57 us -> 0.96 us  [hand_over(): return lax.ppermute(state, 'per', moves)]
    ppermute x10 -> x0, waiting for transfers between devices: 3.33 us -> none  [the longest x3 2.61 us: per_device(): total = total + lax.ppermute(loglik, ('per', 'st'), moves)]
    reshape x2 -> x0, local copies, waits for them, and re-layouts: 2.52 us -> none  [the longest x1 1.27 us: per_device(): starts.reshape(1, slot_rows)]
    ppermute x1, waiting for transfers between devices: 0.01 us -> 1.54 us  [per_device(): received = lax.ppermute(other, 'st', swap)]
  transfers between devices with their start and end apart: 13 -> 5, of which waited for: 4 -> 3; matrix products, arithmetic and copies ran while one was open for 6% -> 1% of each run, Pallas kernels for 9% -> 27%
where the time goes in v2:
time: 46 us; the launch traced here: 45.5 us
  Pallas kernels  21.2 us (46%)
  starting transfers between devices  10.6 us (23%)
  local copies, waits for them, and re-layouts  9.03 us (20%)
  waiting for transfers between devices  2.51 us (5%)
  between operations  1.53 us (3%)
  other arithmetic  0.67 us (1%)
    unnamed x26, local copies, waits for them, and re-layouts  9.03 us
    pallas_call x2, Pallas kernels, second_pass(): pl.pallas_call(functools.partial(second_kernel, resume, last, extend, gri...  7.99 us
    all_to_all x1, starting transfers between devices, per_device(): lax.all_to_all(packed, ('hh', 'per'), split_axis=0, concat_axis=0, tiled=...  6.83 us
    pallas_call x2, Pallas kernels, first_pass(): pl.pallas_call(functools.partial(first_kernel, resume, grids, index), gri...  6.02 us
    ppermute x2, starting transfers between devices, hand_over(): return lax.ppermute(state, 'per', moves)  3.25 us
    pallas_call x1, Pallas kernels, per_device(): pl.pallas_call(prep_kernel, out_shape=[shaped((steps, 2 * states + EXTRA,...  3.22 us
    pallas_call x1, Pallas kernels, per_device(): pl.pallas_call(pack_kernel, out_shape=shaped((group, periods // 2, slot_r...  2.15 us
    pallas_call x1, Pallas kernels, per_device(): pl.pallas_call(functools.partial(finish_kernel, float(states * states * p...  1.79 us
  transfers between devices with their start and end apart: 5, of which 3 were waited for; matrix products, arithmetic and copies ran while one was open for 1% of the time, Pallas kernels for 27%

profile of v2, /device:TPU:0, one launch (start us, length us, event | category | flops | bytes accessed | tf_op | source)
XLA Modules:
  0.0 45.5 jit_solution(8893414306804107492)
XLA Ops:
  0.6 0.5 %collective-permute-start = (bf16[4,256,256]{2,1,0:T(8,128)(2,1)}, bf16[4,256,256]{2,1,0:T(8,128)(2,1)S(1)}, u32[]{:S(2)}, u32[]{:S(2)}) collective-permute-start(bf16[4,256,256]{2,1,0:T(8,128)(2,1)} %own_any.1), channel_id=1, source_target_pairs={{0,1},{1,0},{2,3},{3,2},{4,5},{5,4},{6,7},{7,6},{8,9},{9,8},{10,11... | collective-permute-start | bytes 1572872 | tf_op jit(solution)/shard_map/ppermute | solution.py:421
  1.8 0.7 %pad_add_fusion.ids_ref.refs_0_ = s32[4]{0:T(128)} fusion(s32[1]{0:T(128)} %bitcast.3, s32[1]{0:T(128)} %bitcast.2, s32[1]{0:T(128)} %bitcast.1, s32[1]{0:T(128)} %bitcast), kind=kLoop, calls=%fused_computation | loop fusion | flops 12 | bytes 32 | tf_op jit(solution)/shard_map/stack | solution.py:416
  2.5 2.1 %pack.1 = f32[8,8,384]{2,1,0:T(8,128)} custom-call(s32[4]{0:T(128)} %pad_add_fusion.ids_ref.refs_0_, s32[1]{0:T(128)S(6)} %copy.10.count_ref, f32[16,384]{1,0:T(8,128)} %bitcast.14, s32[3,128]{1,0:T(4,128)} %bitcast.15, s32[3,128]{1,0:T(4,128)} %bitcast.16), custom_call_target="tpu_custom_call" | custom-call | tf_op jit(solution)/shard_map/pack/pallas_call | solution.py:422
  4.6 6.8 %all-to-all-start = ((f32[8,8,384]{2,1,0:T(8,128)}), f32[8,8,384]{2,1,0:T(8,128)S(1)}, u32[]{:S(2)}, u32[]{:S(2)}) async-start(f32[8,8,384]{2,1,0:T(8,128)} %pack.1), calls=%async_computation | async-start | bytes 196608 | tf_op jit(solution)/shard_map/all_to_all | solution.py:435
  11.5 0.0 collective-permute-done.other_ref
  11.5 0.0 copy-start.3
  11.5 0.8 %copy-done.3 = bf16[4,256,256]{2,1,0:T(8,128)(2,1)} copy-done((bf16[4,256,256]{2,1,0:T(8,128)(2,1)}, bf16[4,256,256]{2,1,0:T(8,128)(2,1)S(1)}, u32[]{:S(2)}) %copy-start.3) | copy-done | bytes 524312
  12.3 0.0 copy-start.2
  12.3 1.0 %copy-done.2 = bf16[4,256,256]{2,1,0:T(8,128)(2,1)S(1)} copy-done((bf16[4,256,256]{2,1,0:T(8,128)(2,1)S(1)}, bf16[4,256,256]{2,1,0:T(8,128)(2,1)}, u32[]{:S(2)}) %copy-start.2) | copy-done | bytes 524312
  13.3 0.0 copy-start.4
  13.3 1.0 %copy-done.4 = bf16[4,256,256]{2,1,0:T(8,128)(2,1)S(1)} copy-done((bf16[4,256,256]{2,1,0:T(8,128)(2,1)S(1)}, bf16[4,256,256]{2,1,0:T(8,128)(2,1)}, u32[]{:S(2)}) %copy-start.4) | copy-done | bytes 524312
  14.4 0.0 copy-start.6
  14.4 0.7 %copy-done.6 = s32[4]{0:T(128)S(1)} copy-done((s32[4]{0:T(128)S(1)}, s32[4]{0:T(128)}, u32[]{:S(2)}) %copy-start.6) | copy-done | bytes 40
  15.0 0.0 copy-start.9
  15.0 0.7 %copy-done.9 = f32[256]{0:T(256)S(1)} copy-done((f32[256]{0:T(256)S(1)}, f32[256]{0:T(256)}, u32[]{:S(2)}) %copy-start.9) | copy-done | bytes 1048
  15.7 0.0 copy-start.10
  15.7 0.7 %copy-done.10 = f32[256]{0:T(256)S(1)} copy-done((f32[256]{0:T(256)S(1)}, f32[256]{0:T(256)}, u32[]{:S(2)}) %copy-start.10) | copy-done | bytes 1048
  16.4 0.0 copy-start.11
  16.4 0.7 %copy-done.11 = f32[256]{0:T(256)S(1)} copy-done((f32[256]{0:T(256)S(1)}, f32[256]{0:T(256)}, u32[]{:S(2)}) %copy-start.11) | copy-done | bytes 1048
  17.1 3.2 %prep.1 = (bf16[8,528,256]{2,1,0:T(8,128)(2,1)S(1)}, bf16[8,512,256]{2,1,0:T(8,128)(2,1)S(1)}, f32[8,64,256]{2,1,0:T(8,128)S(1)}, f32[4,256,128]{2,1,0:T(8,128)S(1)}) custom-call(s32[4]{0:T(128)S(1)} %copy-done.6, bf16[4,256,256]{2,1,0:T(8,128)(2,1)S(1)} %copy-done.2, bf16[4,256,256]{2,1,0:T(8,128)(2,1)S(1)} %copy-done.4, f32[1,256]{1,0:T(1,128)S(1)} %bitcast.11, ...), custom_call_target="tpu_custom_call" | custom-call | tf_op jit(solution)/shard_map/prep/pallas_call | solution.py:437
  20.3 0.0 copy-start
  20.3 1.3 %copy-done = bf16[8,512,256]{2,1,0:T(8,128)(2,1)} copy-done((bf16[8,512,256]{2,1,0:T(8,128)(2,1)}, bf16[8,512,256]{2,1,0:T(8,128)(2,1)S(1)}, u32[]{:S(2)}) %copy-start) | copy-done | bytes 2097176
  21.6 0.0 all-to-all-done.rows_ref
  21.7 0.0 copy-start.7
  21.7 0.7 %copy-done.7 = s32[4]{0:T(128)S(1)} copy-done((s32[4]{0:T(128)S(1)}, s32[4]{0:T(128)}, u32[]{:S(2)}) %copy-start.7) | copy-done | bytes 40
  22.3 0.0 copy-start.1
  22.3 3.0 %first_pass.3 = (bf16[8,256,256]{2,1,0:T(8,128)(2,1)S(1)}, bf16[272,256]{1,0:T(8,128)(2,1)S(1)}, f32[3,16,8,256]{3,2,1,0:T(8,128)S(1)}) custom-call(s32[4]{0:T(128)S(1)} %copy-done.7, f32[8,8,384]{2,1,0:T(8,128)S(1)} %all-to-all-done.rows_ref, bf16[8,528,256]{2,1,0:T(8,128)(2,1)S(1)} %get-tuple-element.18.mat, ...), custom_call_target="tpu_custom_call" | custom-call | tf_op jit(solution)/shard_map/first_pass/pallas_call | solution.py:484
  25.4 2.7 %collective-permute-start.2 = (bf16[272,256]{1,0:T(8,128)(2,1)S(1)}, bf16[272,256]{1,0:T(8,128)(2,1)S(1)}, u32[]{:S(2)}, u32[]{:S(2)}) collective-permute-start(bf16[272,256]{1,0:T(8,128)(2,1)S(1)} %get-tuple-element.26.refs_5_), channel_id=1, source_target_pairs={{0,2},{2,0},{1,3},{3,1},{4,6},{6,4},{5,7},{7,5},{8,10},{10,8},{9,1... | collective-permute-start | bytes 417800 | tf_op jit(solution)/shard_map/ppermute | solution.py:532
  28.0 3.0 %first_pass.2 = (bf16[8,256,256]{2,1,0:T(8,128)(2,1)S(1)}, bf16[272,256]{1,0:T(8,128)(2,1)S(1)}, f32[3,16,8,256]{3,2,1,0:T(8,128)S(1)}) custom-call(s32[4]{0:T(128)S(1)} %copy-done.7, f32[8,8,384]{2,1,0:T(8,128)S(1)} %all-to-all-done.rows_ref, bf16[8,528,256]{2,1,0:T(8,128)(2,1)S(1)} %get-tuple-element.18.mat, ...), custom_call_target="tpu_custom_call" | custom-call | tf_op jit(solution)/shard_map/first_pass/pallas_call | solution.py:484
  31.0 0.6 %collective-permute-start.1 = (bf16[272,256]{1,0:T(8,128)(2,1)S(1)}, bf16[272,256]{1,0:T(8,128)(2,1)S(1)}, u32[]{:S(2)}, u32[]{:S(2)}) collective-permute-start(bf16[272,256]{1,0:T(8,128)(2,1)S(1)} %get-tuple-element.23.refs_5_), channel_id=1, source_target_pairs={{0,2},{2,0},{1,3},{3,1},{4,6},{6,4},{5,7},{7,5},{8,10},{10,8},{9,1... | collective-permute-start | bytes 417800 | tf_op jit(solution)/shard_map/ppermute | solution.py:532
  31.6 0.2 collective-permute-done.2.refs_6_
  31.8 0.0 copy-done.1
  31.8 0.0 copy-start.8
  31.8 3.7 %second_pass.2 = (f32[8,64,256]{2,1,0:T(8,128)S(1)}, f32[8,128]{1,0:T(8,128)S(1)}) custom-call(s32[4]{0:T(128)S(1)} %copy-done.7, f32[3,16,8,256]{3,2,1,0:T(8,128)S(1)} %get-tuple-element.24.refs_1_, bf16[8,512,256]{2,1,0:T(8,128)(2,1)S(1)} %copy-done.1, f32[4,256,128]{2,1,0:T(8,128)S(1)} %get-tuple-element.19.consts.refs_3_, ...), custom_call_target="tpu_custom_call" | custom-call | tf_op jit(solution)/shard_map/second_pass/pallas_call | solution.py:513
  35.5 0.8 %collective-permute-done.1.refs_6_ = bf16[272,256]{1,0:T(8,128)(2,1)S(1)} collective-permute-done((bf16[272,256]{1,0:T(8,128)(2,1)S(1)}, bf16[272,256]{1,0:T(8,128)(2,1)S(1)}, u32[]{:S(2)}, u32[]{:S(2)}) %collective-permute-start.1) | collective-permute-done | bytes 139296 | tf_op jit(solution)/shard_map/ppermute | solution.py:532
  36.3 0.0 copy-done.8
  36.3 4.3 %second_pass.3 = (f32[520,128]{1,0:T(8,128)S(1)}, f32[520,128]{1,0:T(8,128)S(1)}) custom-call(s32[4]{0:T(128)S(1)} %copy-done.8, f32[3,16,8,256]{3,2,1,0:T(8,128)S(1)} %get-tuple-element.20.refs_1_, bf16[8,512,256]{2,1,0:T(8,128)(2,1)S(1)} %copy-done.1, f32[4,256,128]{2,1,0:T(8,128)S(1)} %get-tuple-element.19.consts.refs_3_, ...), custom_call_target="tpu_custom_call" | custom-call | tf_op jit(solution)/shard_map/second_pass/pallas_call | solution.py:513
  40.6 0.0 copy-start.5
  40.6 0.7 %copy-done.5 = f32[520,128]{1,0:T(8,128)} copy-done((f32[520,128]{1,0:T(8,128)}, f32[520,128]{1,0:T(8,128)S(1)}, u32[]{:S(2)}) %copy-start.5) | copy-done | bytes 266264
  41.3 0.0 collective-permute-start.3
  41.3 1.5 %collective-permute-done.3.other_ref = f32[520,128]{1,0:T(8,128)S(1)} collective-permute-done((f32[520,128]{1,0:T(8,128)S(1)}, f32[520,128]{1,0:T(8,128)S(1)}, u32[]{:S(2)}, u32[]{:S(2)}) %collective-permute-start.3) | collective-permute-done | bytes 266272 | tf_op jit(solution)/shard_map/ppermute | solution.py:568
  42.9 0.0 copy-start.12
  42.9 0.7 %copy-done.12 = f32[520,128]{1,0:T(8,128)} copy-done((f32[520,128]{1,0:T(8,128)}, f32[520,128]{1,0:T(8,128)S(1)}, u32[]{:S(2)}) %copy-start.12) | copy-done | bytes 266264
  43.6 1.8 %finish.1 = (f32[512,128]{1,0:T(8,128)}, f32[1]{0:T(128)}) custom-call(f32[520,128]{1,0:T(8,128)} %copy-done.5, f32[520,128]{1,0:T(8,128)} %copy-done.12), custom_call_target="tpu_custom_call" | custom-call | tf_op jit(solution)/shard_map/finish/pallas_call | solution.py:569
Async XLA Ops:
  0.6 10.8 %collective-permute-start = (bf16[4,256,256]{2,1,0:T(8,128)(2,1)}, bf16[4,256,256]{2,1,0:T(8,128)(2,1)S(1)}, u32[]{:S(2)}, u32[]{:S(2)}) collective-permute-start(bf16[4,256,256]{2,1,0:T(8,128)(2,1)} %own_any.1), channel_id=1, source_target_pairs={{0,1},{1,0},{2,3},{3,2},{4,5},{5,4},{6,7},{7,6},{8,9},{9,8},{10,11... | collective-permute-start | bytes 1572872 | tf_op jit(solution)/shard_map/ppermute | solution.py:421
  4.6 17.0 %all-to-all-start = ((f32[8,8,384]{2,1,0:T(8,128)}), f32[8,8,384]{2,1,0:T(8,128)S(1)}, u32[]{:S(2)}, u32[]{:S(2)}) async-start(f32[8,8,384]{2,1,0:T(8,128)} %pack.1), calls=%async_computation | async-start | bytes 196608 | tf_op jit(solution)/shard_map/all_to_all | solution.py:435
  11.5 0.8 %copy-start.3 = (bf16[4,256,256]{2,1,0:T(8,128)(2,1)}, bf16[4,256,256]{2,1,0:T(8,128)(2,1)S(1)}, u32[]{:S(2)}) copy-start(bf16[4,256,256]{2,1,0:T(8,128)(2,1)S(1)} %collective-permute-done.other_ref) | copy-start | bytes 1572868
  12.3 1.0 %copy-start.2 = (bf16[4,256,256]{2,1,0:T(8,128)(2,1)S(1)}, bf16[4,256,256]{2,1,0:T(8,128)(2,1)}, u32[]{:S(2)}) copy-start(bf16[4,256,256]{2,1,0:T(8,128)(2,1)} %own_any.1) | copy-start | bytes 1572868
  13.3 1.0 %copy-start.4 = (bf16[4,256,256]{2,1,0:T(8,128)(2,1)S(1)}, bf16[4,256,256]{2,1,0:T(8,128)(2,1)}, u32[]{:S(2)}) copy-start(bf16[4,256,256]{2,1,0:T(8,128)(2,1)} %copy-done.3) | copy-start | bytes 1572868
  14.4 0.7 %copy-start.6 = (s32[4]{0:T(128)S(1)}, s32[4]{0:T(128)}, u32[]{:S(2)}) copy-start(s32[4]{0:T(128)} %pad_add_fusion.ids_ref.refs_0_) | copy-start | bytes 52
  15.0 0.7 %copy-start.9 = (f32[256]{0:T(256)S(1)}, f32[256]{0:T(256)}, u32[]{:S(2)}) copy-start(f32[256]{0:T(256)} %param.13) | copy-start | bytes 3076
  15.7 0.7 %copy-start.10 = (f32[256]{0:T(256)S(1)}, f32[256]{0:T(256)}, u32[]{:S(2)}) copy-start(f32[256]{0:T(256)} %param.14) | copy-start | bytes 3076
  16.4 0.7 %copy-start.11 = (f32[256]{0:T(256)S(1)}, f32[256]{0:T(256)}, u32[]{:S(2)}) copy-start(f32[256]{0:T(256)} %param.15) | copy-start | bytes 3076
  20.3 1.3 %copy-start = (bf16[8,512,256]{2,1,0:T(8,128)(2,1)}, bf16[8,512,256]{2,1,0:T(8,128)(2,1)S(1)}, u32[]{:S(2)}) copy-start(bf16[8,512,256]{2,1,0:T(8,128)(2,1)S(1)} %get-tuple-element.21.refs_2_) | copy-start | bytes 6291460
  21.7 0.7 %copy-start.7 = (s32[4]{0:T(128)S(1)}, s32[4]{0:T(128)}, u32[]{:S(2)}) copy-start(s32[4]{0:T(128)} %pad_add_fusion.ids_ref.refs_0_) | copy-start | bytes 52
  22.3 9.4 %copy-start.1 = (bf16[8,512,256]{2,1,0:T(8,128)(2,1)S(1)}, bf16[8,512,256]{2,1,0:T(8,128)(2,1)}, u32[]{:S(2)}) copy-start(bf16[8,512,256]{2,1,0:T(8,128)(2,1)} %copy-done) | copy-start | bytes 6291460
  25.4 6.4 %collective-permute-start.2 = (bf16[272,256]{1,0:T(8,128)(2,1)S(1)}, bf16[272,256]{1,0:T(8,128)(2,1)S(1)}, u32[]{:S(2)}, u32[]{:S(2)}) collective-permute-start(bf16[272,256]{1,0:T(8,128)(2,1)S(1)} %get-tuple-element.26.refs_5_), channel_id=1, source_target_pairs={{0,2},{2,0},{1,3},{3,1},{4,6},{6,4},{5,7},{7,5},{8,10},{10,8},{9,1... | collective-permute-start | bytes 417800 | tf_op jit(solution)/shard_map/ppermute | solution.py:532
  31.0 5.3 %collective-permute-start.1 = (bf16[272,256]{1,0:T(8,128)(2,1)S(1)}, bf16[272,256]{1,0:T(8,128)(2,1)S(1)}, u32[]{:S(2)}, u32[]{:S(2)}) collective-permute-start(bf16[272,256]{1,0:T(8,128)(2,1)S(1)} %get-tuple-element.23.refs_5_), channel_id=1, source_target_pairs={{0,2},{2,0},{1,3},{3,1},{4,6},{6,4},{5,7},{7,5},{8,10},{10,8},{9,1... | collective-permute-start | bytes 417800 | tf_op jit(solution)/shard_map/ppermute | solution.py:532
  31.8 4.5 %copy-start.8 = (s32[4]{0:T(128)S(1)}, s32[4]{0:T(128)}, u32[]{:S(2)}) copy-start(s32[4]{0:T(128)} %pad_add_fusion.ids_ref.refs_0_) | copy-start | bytes 52
  40.6 0.7 %copy-start.5 = (f32[520,128]{1,0:T(8,128)}, f32[520,128]{1,0:T(8,128)S(1)}, u32[]{:S(2)}) copy-start(f32[520,128]{1,0:T(8,128)S(1)} %get-tuple-element.30.mine_ref) | copy-start | bytes 798724
  41.3 1.5 %collective-permute-start.3 = (f32[520,128]{1,0:T(8,128)S(1)}, f32[520,128]{1,0:T(8,128)S(1)}, u32[]{:S(2)}, u32[]{:S(2)}) collective-permute-start(f32[520,128]{1,0:T(8,128)S(1)} %get-tuple-element.31), channel_id=1, source_target_pairs={{0,1},{1,0},{2,3},{3,2},{4,5},{5,4},{6,7},{7,6},{8,9},{9,8},{10,11... | collective-permute-start | bytes 798728 | tf_op jit(solution)/shard_map/ppermute | solution.py:568
  42.9 0.7 %copy-start.12 = (f32[520,128]{1,0:T(8,128)}, f32[520,128]{1,0:T(8,128)S(1)}, u32[]{:S(2)}) copy-start(f32[520,128]{1,0:T(8,128)S(1)} %collective-permute-done.3.other_ref) | copy-start | bytes 798724

commit v3 on v2

--- a/solution.py
+++ b/solution.py
@@ -15,7 +15,6 @@
 BF16 = jnp.bfloat16
 LOG2E = 1.4426950408889634
 LN2 = 0.6931471805599453
-VMEM_LIMIT = 40 * 1024 * 1024
 EXTRA = 16
 
 
@@ -27,19 +26,27 @@
     return pl.BlockSpec(memory_space=pltpu.SMEM)
 
 
-def anywhere():
-    return pl.BlockSpec(memory_space=pl.ANY)
-
-
-def params():
-    return pltpu.CompilerParams(vmem_limit_bytes=VMEM_LIMIT)
+def hbm():
+    return pl.BlockSpec(memory_space=pltpu.HBM)
+
+
+def params(mebibytes):
+    return pltpu.CompilerParams(vmem_limit_bytes=mebibytes * 1024 * 1024)
+
+
+def core_index():
+    return lax.axis_index("st")
+
+
+def is_forward_first():
+    return 2 * lax.axis_index("per") < lax.axis_size("per")
 
 
 def tiles(width):
     return [slice(q, q + LANES) for q in range(0, width, LANES)]
 
 
-def pack_kernel(ids_ref, count_ref, earn_any, start_any, len_any, out_ref, earn_ref, start_ref, len_ref, sems):
+def pack_kernel(count_ref, earn_any, start_any, len_any, out_ref, earn_ref, start_ref, len_ref, sems):
     copies = [
         pltpu.make_async_copy(src, dst, sems.at[i])
         for i, (src, dst) in enumerate(((earn_any, earn_ref), (start_any, start_ref), (len_any, len_ref)))
@@ -49,7 +56,7 @@
     for copy in copies:
         copy.wait()
     periods, slot_rows = earn_ref.shape
-    core = ids_ref[0]
+    core = core_index()
     low_lane = lax.broadcasted_iota(jnp.int32, (periods // 2, HB), 1) < HALF
     time = lax.broadcasted_iota(jnp.int32, (periods, HB), 0)
     for slot in range(slot_rows // HB):
@@ -67,7 +74,7 @@
 
 
 def prep_kernel(
-    ids_ref, own_any, other_ref, init_any, mean_any, sd_any,
+    own_any, other_ref, init_any, mean_any, sd_any,
     first_mat, second_mat, row_probs, consts, scratch, own_ref, init_ref, mean_ref, sd_ref, sems,
 ):
     pairs = ((own_any, own_ref), (init_any, init_ref), (mean_any, mean_ref), (sd_any, sd_ref))
@@ -76,9 +83,9 @@
         copy.start()
     for copy in copies:
         copy.wait()
-    core, forward_first, row_begin = ids_ref[0], ids_ref[1], ids_ref[2]
     part, states, _ = own_ref.shape
     rows = row_probs.shape[1]
+    core, forward_first, row_begin = core_index(), is_forward_first(), lax.axis_index("hh") * rows
 
     def column(row):
         return jnp.broadcast_to(row, (LANES, states)).T
@@ -110,12 +117,12 @@
             turned = probs.T
             first_mat[at, 2 * states :, :] = start_rows
 
-            @pl.when(forward_first == 1)
+            @pl.when(forward_first)
             def _():
                 put(first_mat, at, turned)
                 put(second_mat, at, probs)
 
-            @pl.when(forward_first == 0)
+            @pl.when(jnp.logical_not(forward_first))
             def _():
                 put(first_mat, at, probs)
                 put(second_mat, at, turned)
@@ -159,9 +166,9 @@
         else:
             weights_ref, counts_ref, row_begin = second
             own_alpha = ab_ref[own_rows(row_begin, weights_ref.shape[0]), :].astype(F32)
-        product = jnp.dot(mat[k, : 2 * states, :], ab_ref[...], preferred_element_type=F32)
         for q, cols in enumerate(cuts):
-            moved = (product[:states, cols] + product[states:, cols]) * inverse[q]
+            product = jnp.dot(mat[k, : 2 * states, :], ab_ref[:, cols], preferred_element_type=F32)
+            moved = (product[:states] + product[states:]) * inverse[q]
             moving = is_moving(sel_ref, step_now, cols)
             if second is not None:
                 total = column_sum(moved * hist[k, :, cols].astype(F32))
@@ -200,13 +207,13 @@
         else:
             weights_ref, counts_ref, row_begin = second
             own_alpha = hist[k, own_rows(row_begin, weights_ref.shape[0]), :].astype(F32)
-        product = jnp.dot(mat[k], ub_ref[...], preferred_element_type=F32)
         for q, cols in enumerate(cuts):
+            product = jnp.dot(mat[k], ub_ref[:, cols], preferred_element_type=F32)
             moving = is_moving(sel_ref, step_now, cols)
-            pulled = (product[:states, cols] + product[states : 2 * states, cols]) * shrink[q]
+            pulled = (product[:states] + product[states : 2 * states]) * shrink[q]
             if second is None:
                 seen = is_seen(sel_ref, step_now, cols)
-                begun = column_sum(product[2 * states :, cols]) * shrink[q]
+                begun = column_sum(product[2 * states :]) * shrink[q]
                 rest = jnp.where(seen, begun, back_ref[:, cols])
             else:
                 total = column_sum(pulled * hist[k, :, cols].astype(F32))
@@ -237,12 +244,12 @@
     return [column_sum(state_ref[states:, cols].astype(F32)) for cols in tiles(state_ref.shape[1])]
 
 
-def first_kernel(resume, grids, part, ids_ref, rows_ref, mat, consts, *refs):
+def first_kernel(resume, grids, part, rows_ref, mat, consts, *refs):
     state_in = refs[0] if resume else None
     hist, state_out, sel_ref, ab_ref, back_ref = refs[-5:]
-    forward_first, lead = ids_ref[1], ids_ref[3]
     chunk = part * grids + (pl.program_id(0) if grids > 1 else 0)
     steps, states, width = hist.shape
+    forward_first, lead = is_forward_first(), lax.axis_index("per") * steps
     cuts = tiles(width)
     group, half_periods, slot_rows = rows_ref.shape
     tops = 2 * len(cuts)
@@ -284,7 +291,7 @@
                 before = now
     zeros = [jnp.zeros((1, LANES), F32) for _ in cuts]
 
-    @pl.when(forward_first == 1)
+    @pl.when(forward_first)
     def _():
         if resume:
             ab_ref[...] = state_in[:states, :]
@@ -295,7 +302,7 @@
         logs = run_forward(lead, mat, hist, sel_ref, consts, ab_ref, logs)
         put_state(state_out, ab_ref[...], logs)
 
-    @pl.when(forward_first == 0)
+    @pl.when(jnp.logical_not(forward_first))
     def _():
         if resume:
             back_ref[...] = state_in[:states, :].astype(F32)
@@ -308,7 +315,7 @@
 
 def second_kernel(resume, last, extend, grids, *refs):
     refs = list(refs)
-    ids_ref, sel_ref, mat, consts, hist, own_state, state_in = (refs.pop(0) for _ in range(7))
+    sel_ref, mat, consts, hist, own_state, state_in = (refs.pop(0) for _ in range(6))
     counts_in, sums_in = (refs.pop(0), refs.pop(0)) if resume else (None, None)
     row_probs = refs.pop(0) if last else None
     mine_ref, other_ref = (refs.pop(0), refs.pop(0)) if last else (None, None)
@@ -316,9 +323,11 @@
     state_out = refs.pop(0) if extend else None
     ab_ref, back_ref, weights_ref = refs[:3]
     counts_ref, sums_ref = refs[3:] if last else (counts_out, sums_out)
-    core, forward_first, row_begin, lead = ids_ref[0], ids_ref[1], ids_ref[2], ids_ref[3]
     chunk = pl.program_id(0) if grids > 1 else 0
     steps, states, width = hist.shape
+    core, forward_first = core_index(), is_forward_first()
+    row_begin = lax.axis_index("hh") * counts_ref.shape[1]
+    lead = lax.axis_index("per") * steps
     second = (weights_ref, counts_ref, row_begin)
 
     @pl.when(chunk == 0)
@@ -345,7 +354,7 @@
 
     zeros = [jnp.zeros((1, LANES), F32) for _ in tiles(width)]
 
-    @pl.when(forward_first == 0)
+    @pl.when(jnp.logical_not(forward_first))
     def _():
         add_sums(state_in, own_state)
         ab_ref[...] = state_in[:states, :]
@@ -353,7 +362,7 @@
         if extend:
             put_state(state_out, ab_ref[...], zeros)
 
-    @pl.when(forward_first == 1)
+    @pl.when(forward_first)
     def _():
         add_sums(own_state, state_in)
         back_ref[...] = state_in[:states, :].astype(F32)
@@ -411,9 +420,6 @@
     width = min(2 * HB, share)
     grids = share // width
     side = lax.axis_index("per")
-    core = lax.axis_index("st")
-    forward_first = (2 * side < sides).astype(jnp.int32)
-    ids = jnp.stack([core, forward_first, lax.axis_index("hh") * rows, side * steps]).astype(jnp.int32)
     shaped = jax.ShapeDtypeStruct
     dma = pltpu.SemaphoreType.DMA
 
@@ -422,7 +428,7 @@
     packed = pl.pallas_call(
         pack_kernel,
         out_shape=shaped((group, periods // 2, slot_rows), F32),
-        in_specs=[smem(), smem(), anywhere(), anywhere(), anywhere()],
+        in_specs=[smem(), hbm(), hbm(), hbm()],
         out_specs=vmem(),
         scratch_shapes=[
             pltpu.VMEM((periods, slot_rows), F32),
@@ -430,8 +436,9 @@
             pltpu.VMEM((slot_rows // HB, HB), jnp.int32),
             dma((3,)),
         ],
+        compiler_params=params(4),
         name="pack",
-    )(ids, block_count, earnings.T, starts.reshape(-1, HB), lengths.reshape(-1, HB))
+    )(block_count, earnings.T, starts.reshape(-1, HB), lengths.reshape(-1, HB))
     gathered = lax.all_to_all(packed, ("hh", "per"), split_axis=0, concat_axis=0, tiled=True)
 
     first_mat, second_mat, row_probs, consts = pl.pallas_call(
@@ -442,7 +449,7 @@
             shaped((steps, rows, states), F32),
             shaped((4, states, LANES), F32),
         ],
-        in_specs=[smem(), anywhere(), vmem(), anywhere(), anywhere(), anywhere()],
+        in_specs=[hbm(), vmem(), hbm(), hbm(), hbm()],
         out_specs=[vmem()] * 4,
         scratch_shapes=[
             pltpu.VMEM((states, states), F32),
@@ -452,10 +459,10 @@
             pltpu.VMEM((1, states), F32),
             dma((4,)),
         ],
-        compiler_params=params(),
+        compiler_params=params(8),
         name="prep",
     )(
-        ids, trans_logits, other_logits,
+        trans_logits, other_logits,
         init_logits.reshape(1, states), state_mean.reshape(1, states), log_sd.reshape(1, states),
     )
 
@@ -485,13 +492,13 @@
             functools.partial(first_kernel, resume, grids, index),
             grid=grid,
             out_shape=[hist_shape, state_shape, sel_shape],
-            in_specs=[smem(), whole(*gathered.shape), whole(*first_mat.shape), const_spec]
+            in_specs=[whole(*gathered.shape), whole(*first_mat.shape), const_spec]
             + [state_spec] * resume,
             out_specs=[hist_spec, state_spec, sel_spec],
             scratch_shapes=[pltpu.VMEM((states, width), BF16), pltpu.VMEM((states, width), F32)],
-            compiler_params=params(),
+            compiler_params=params(8 if grids == 1 else 32),
             name="first_pass",
-        )(ids, gathered, first_mat, consts, *([state_in] if resume else []))
+        )(gathered, first_mat, consts, *([state_in] if resume else []))
 
     def second_pass(kept, state_in, sums_in, last, extend):
         hist, own_state, sel = kept
@@ -514,15 +521,15 @@
             functools.partial(second_kernel, resume, last, extend, grids),
             grid=grid,
             out_shape=out_shape,
-            in_specs=[smem(), sel_spec, whole(*second_mat.shape), const_spec, hist_spec, state_spec, state_spec]
+            in_specs=[sel_spec, whole(*second_mat.shape), const_spec, hist_spec, state_spec, state_spec]
             + [counts_spec, sums_spec] * resume
             + [whole(*row_probs.shape)] * last,
             out_specs=out_specs,
             scratch_shapes=scratch,
-            compiler_params=params(),
+            compiler_params=params(8 if grids == 1 else 32),
             name="second_pass",
         )(
-            ids, sel, second_mat, consts, hist, own_state, state_in,
+            sel, second_mat, consts, hist, own_state, state_in,
             *(sums_in if resume else []),
             *([row_probs] if last else []),
         )
@@ -571,6 +578,7 @@
         out_shape=[shaped((steps * rows, LANES), F32), shaped((1,), F32)],
         in_specs=[vmem(), vmem()],
         out_specs=[vmem(), smem()],
+        compiler_params=params(4),
         name="finish",
     )(mine, received)
     return (trans_grad.reshape(steps, rows, LANES), mean_loglik)

time: 46 us -> 40.2 us (0.87)
  Pallas kernels: 21.2 us -> 16.5 us
  local copies, waits for them, and re-layouts: 9.03 us -> 8.33 us
  other arithmetic: 0.67 us -> 0 us
  waiting for transfers between devices: 2.51 us -> 3.14 us
    pallas_call x1, Pallas kernels: 2.15 us -> 0.76 us  [per_device(): pl.pallas_call(pack_kernel, out_shape=shaped((group, periods // 2, slot_r...]
    pallas_call x1, Pallas kernels: 1.79 us -> 0.75 us  [per_device(): pl.pallas_call(functools.partial(finish_kernel, float(states * states * p...]
    pallas_call x2, Pallas kernels: 7.99 us -> 7.1 us  [second_pass(): pl.pallas_call(functools.partial(second_kernel, resume, last, extend, gri...]
    pallas_call x2, Pallas kernels: 6.02 us -> 5.17 us  [first_pass(): pl.pallas_call(functools.partial(first_kernel, resume, grids, index), gri...]
    unnamed x26 -> x22, local copies, waits for them, and re-layouts: 9.03 us -> 8.33 us
    another operation x1 -> x0, other arithmetic: 0.67 us -> none  [per_device(): jnp.stack([core, forward_first, lax.axis_index('hh') * rows, side * steps])]
    ppermute x2, waiting for transfers between devices: 0.96 us -> 1.61 us  [hand_over(): return lax.ppermute(state, 'per', moves)]
    pallas_call x1, Pallas kernels: 3.22 us -> 2.68 us  [per_device(): pl.pallas_call(prep_kernel, out_shape=[shaped((steps, 2 * states + EXTRA,...]
  transfers between devices with their start and end apart: 5 -> 5, of which waited for: 3 -> 3; matrix products, arithmetic and copies ran while one was open for 1% -> 0% of each run, Pallas kernels for 27% -> 23%
where the time goes in v3:
time: 40.2 us; the launch traced here: 39.7 us
  Pallas kernels  16.5 us (41%)
  starting transfers between devices  10.3 us (26%)
  local copies, waits for them, and re-layouts  8.33 us (21%)
  waiting for transfers between devices  3.14 us (8%)
  between operations  1.54 us (4%)
    unnamed x22, local copies, waits for them, and re-layouts  8.33 us
    pallas_call x2, Pallas kernels, second_pass(): pl.pallas_call(functools.partial(second_kernel, resume, last, extend, gri...  7.1 us
    all_to_all x1, starting transfers between devices, per_device(): lax.all_to_all(packed, ('hh', 'per'), split_axis=0, concat_axis=0, tiled=...  6.82 us
    pallas_call x2, Pallas kernels, first_pass(): pl.pallas_call(functools.partial(first_kernel, resume, grids, index), gri...  5.17 us
    ppermute x2, starting transfers between devices, hand_over(): return lax.ppermute(state, 'per', moves)  2.85 us
    pallas_call x1, Pallas kernels, per_device(): pl.pallas_call(prep_kernel, out_shape=[shaped((steps, 2 * states + EXTRA,...  2.68 us
    ppermute x2, waiting for transfers between devices, hand_over(): return lax.ppermute(state, 'per', moves)  1.61 us
    ppermute x1, waiting for transfers between devices, per_device(): received = lax.ppermute(other, 'st', swap)  1.53 us
  transfers between devices with their start and end apart: 5, of which 3 were waited for; matrix products, arithmetic and copies ran while one was open for 0% of the time, Pallas kernels for 23%

profile of v3, /device:TPU:0, one launch (start us, length us, event | category | flops | bytes accessed | tf_op | source)
XLA Modules:
  0.0 39.7 jit_solution(18148271751750015702)
XLA Ops:
  0.6 0.5 %collective-permute-start = (bf16[4,256,256]{2,1,0:T(8,128)(2,1)}, bf16[4,256,256]{2,1,0:T(8,128)(2,1)S(1)}, u32[]{:S(2)}, u32[]{:S(2)}) collective-permute-start(bf16[4,256,256]{2,1,0:T(8,128)(2,1)} %own_any.1), channel_id=1, source_target_pairs={{0,1},{1,0},{2,3},{3,2},{4,5},{5,4},{6,7},{7,6},{8,9},{9,8},{10,11... | collective-permute-start | bytes 1572872 | tf_op jit(solution)/shard_map/ppermute | solution.py:427
  1.8 0.0 copy-start.5
  1.8 0.7 %copy-done.5 = f32[384,16]{0,1:T(8,128)S(1)} copy-done((f32[384,16]{0,1:T(8,128)S(1)}, f32[384,16]{0,1:T(8,128)}, u32[]{:S(2)}) %copy-start.5) | copy-done | bytes 24600
  2.5 0.0 copy-start.6
  2.5 0.7 %copy-done.6 = s32[384]{0:T(512)S(1)} copy-done((s32[384]{0:T(512)S(1)}, s32[384]{0:T(512)}, u32[]{:S(2)}) %copy-start.6) | copy-done | bytes 1560
  3.2 0.0 copy-start.7
  3.2 0.7 %copy-done.7 = s32[384]{0:T(512)S(1)} copy-done((s32[384]{0:T(512)S(1)}, s32[384]{0:T(512)}, u32[]{:S(2)}) %copy-start.7) | copy-done | bytes 1560
  3.9 0.8 %pack.1 = f32[8,8,384]{2,1,0:T(8,128)} custom-call(s32[1]{0:T(128)S(6)} %copy.10.count_ref, f32[16,384]{1,0:T(8,128)S(1)} %bitcast.7, s32[3,128]{1,0:T(4,128)S(1)} %bitcast.8, s32[3,128]{1,0:T(4,128)S(1)} %bitcast.9), custom_call_target="tpu_custom_call" | custom-call | tf_op jit(solution)/shard_map/pack/pallas_call | solution.py:428
  4.7 6.8 %all-to-all-start = ((f32[8,8,384]{2,1,0:T(8,128)}), f32[8,8,384]{2,1,0:T(8,128)S(1)}, u32[]{:S(2)}, u32[]{:S(2)}) async-start(f32[8,8,384]{2,1,0:T(8,128)} %pack.1), calls=%async_computation | async-start | bytes 196608 | tf_op jit(solution)/shard_map/all_to_all | solution.py:442
  11.5 0.0 collective-permute-done.other_ref
  11.5 0.0 copy-start.3
  11.5 0.8 %copy-done.3 = bf16[4,256,256]{2,1,0:T(8,128)(2,1)} copy-done((bf16[4,256,256]{2,1,0:T(8,128)(2,1)}, bf16[4,256,256]{2,1,0:T(8,128)(2,1)S(1)}, u32[]{:S(2)}) %copy-start.3) | copy-done | bytes 524312
  12.3 0.0 copy-start.2
  12.3 1.0 %copy-done.2 = bf16[4,256,256]{2,1,0:T(8,128)(2,1)S(1)} copy-done((bf16[4,256,256]{2,1,0:T(8,128)(2,1)S(1)}, bf16[4,256,256]{2,1,0:T(8,128)(2,1)}, u32[]{:S(2)}) %copy-start.2) | copy-done | bytes 524312
  13.4 0.0 copy-start.4
  13.4 1.0 %copy-done.4 = bf16[4,256,256]{2,1,0:T(8,128)(2,1)S(1)} copy-done((bf16[4,256,256]{2,1,0:T(8,128)(2,1)S(1)}, bf16[4,256,256]{2,1,0:T(8,128)(2,1)}, u32[]{:S(2)}) %copy-start.4) | copy-done | bytes 524312
  14.4 0.0 copy-start.8
  14.4 0.7 %copy-done.8 = f32[256]{0:T(256)S(1)} copy-done((f32[256]{0:T(256)S(1)}, f32[256]{0:T(256)}, u32[]{:S(2)}) %copy-start.8) | copy-done | bytes 1048
  15.1 0.0 copy-start.9
  15.1 0.7 %copy-done.9 = f32[256]{0:T(256)S(1)} copy-done((f32[256]{0:T(256)S(1)}, f32[256]{0:T(256)}, u32[]{:S(2)}) %copy-start.9) | copy-done | bytes 1048
  15.8 0.0 copy-start.10
  15.8 0.7 %copy-done.10 = f32[256]{0:T(256)S(1)} copy-done((f32[256]{0:T(256)S(1)}, f32[256]{0:T(256)}, u32[]{:S(2)}) %copy-start.10) | copy-done | bytes 1048
  16.4 2.7 %prep.1 = (bf16[8,528,256]{2,1,0:T(8,128)(2,1)S(1)}, bf16[8,512,256]{2,1,0:T(8,128)(2,1)S(1)}, f32[8,64,256]{2,1,0:T(8,128)S(1)}, f32[4,256,128]{2,1,0:T(8,128)S(1)}) custom-call(bf16[4,256,256]{2,1,0:T(8,128)(2,1)S(1)} %copy-done.2, bf16[4,256,256]{2,1,0:T(8,128)(2,1)S(1)} %copy-done.4, f32[1,256]{1,0:T(1,128)S(1)} %bitcast.10, f32[1,256]{1,0:T(1,128)S(1)} %bitcast.11, ...), custom_call_target="tpu_custom_call" | custom-call | tf_op jit(solution)/shard_map/prep/pallas_call | solution.py:444
  19.1 0.0 copy-start
  19.1 1.3 %copy-done = bf16[8,512,256]{2,1,0:T(8,128)(2,1)} copy-done((bf16[8,512,256]{2,1,0:T(8,128)(2,1)}, bf16[8,512,256]{2,1,0:T(8,128)(2,1)S(1)}, u32[]{:S(2)}) %copy-start) | copy-done | bytes 2097176
  20.5 0.0 all-to-all-done.rows_ref
  20.5 0.0 copy-start.1
  20.5 2.6 %first_pass.3 = (bf16[8,256,256]{2,1,0:T(8,128)(2,1)S(1)}, bf16[272,256]{1,0:T(8,128)(2,1)S(1)}, f32[3,16,8,256]{3,2,1,0:T(8,128)S(1)}) custom-call(f32[8,8,384]{2,1,0:T(8,128)S(1)} %all-to-all-done.rows_ref, bf16[8,528,256]{2,1,0:T(8,128)(2,1)S(1)} %get-tuple-element.18.mat, f32[4,256,128]{2,1,0:T(8,128)S(1)} %get-tuple-element.19.consts.refs_2_), custom_call_target="tpu_custom_call" | custom-call | tf_op jit(solution)/shard_map/first_pass/pallas_call | solution.py:491
  23.0 2.5 %collective-permute-start.2 = (bf16[272,256]{1,0:T(8,128)(2,1)S(1)}, bf16[272,256]{1,0:T(8,128)(2,1)S(1)}, u32[]{:S(2)}, u32[]{:S(2)}) collective-permute-start(bf16[272,256]{1,0:T(8,128)(2,1)S(1)} %get-tuple-element.26.refs_4_), channel_id=1, source_target_pairs={{0,2},{2,0},{1,3},{3,1},{4,6},{6,4},{5,7},{7,5},{8,10},{10,8},{9,1... | collective-permute-start | bytes 417800 | tf_op jit(solution)/shard_map/ppermute | solution.py:539
  25.5 2.6 %first_pass.2 = (bf16[8,256,256]{2,1,0:T(8,128)(2,1)S(1)}, bf16[272,256]{1,0:T(8,128)(2,1)S(1)}, f32[3,16,8,256]{3,2,1,0:T(8,128)S(1)}) custom-call(f32[8,8,384]{2,1,0:T(8,128)S(1)} %all-to-all-done.rows_ref, bf16[8,528,256]{2,1,0:T(8,128)(2,1)S(1)} %get-tuple-element.18.mat, f32[4,256,128]{2,1,0:T(8,128)S(1)} %get-tuple-element.19.consts.refs_2_), custom_call_target="tpu_custom_call" | custom-call | tf_op jit(solution)/shard_map/first_pass/pallas_call | solution.py:491
  28.1 0.4 collective-permute-start.1
  28.5 0.8 %collective-permute-done.2.refs_5_ = bf16[272,256]{1,0:T(8,128)(2,1)S(1)} collective-permute-done((bf16[272,256]{1,0:T(8,128)(2,1)S(1)}, bf16[272,256]{1,0:T(8,128)(2,1)S(1)}, u32[]{:S(2)}, u32[]{:S(2)}) %collective-permute-start.2) | collective-permute-done | bytes 139296 | tf_op jit(solution)/shard_map/ppermute | solution.py:539
  29.3 0.0 copy-done.1
  29.3 3.3 %second_pass.2 = (f32[8,64,256]{2,1,0:T(8,128)S(1)}, f32[8,128]{1,0:T(8,128)S(1)}) custom-call(f32[3,16,8,256]{3,2,1,0:T(8,128)S(1)} %get-tuple-element.24.refs_0_, bf16[8,512,256]{2,1,0:T(8,128)(2,1)S(1)} %copy-done.1, f32[4,256,128]{2,1,0:T(8,128)S(1)} %get-tuple-element.19.consts.refs_2_, bf16[8,256,256]{2,1,0:T(8,128)(2,1)S(1)} %get-tuple-element.25.refs_3_, ...), custom_call_target="tpu_custom_call" | custom-call | tf_op jit(solution)/shard_map/second_pass/pallas_call | solution.py:520
  32.6 0.8 %collective-permute-done.1.refs_5_ = bf16[272,256]{1,0:T(8,128)(2,1)S(1)} collective-permute-done((bf16[272,256]{1,0:T(8,128)(2,1)S(1)}, bf16[272,256]{1,0:T(8,128)(2,1)S(1)}, u32[]{:S(2)}, u32[]{:S(2)}) %collective-permute-start.1) | collective-permute-done | bytes 139296 | tf_op jit(solution)/shard_map/ppermute | solution.py:539
  33.4 3.8 %second_pass.3 = (f32[520,128]{1,0:T(8,128)S(1)}, f32[520,128]{1,0:T(8,128)S(1)}) custom-call(f32[3,16,8,256]{3,2,1,0:T(8,128)S(1)} %get-tuple-element.20.refs_0_, bf16[8,512,256]{2,1,0:T(8,128)(2,1)S(1)} %copy-done.1, f32[4,256,128]{2,1,0:T(8,128)S(1)} %get-tuple-element.19.consts.refs_2_, bf16[8,256,256]{2,1,0:T(8,128)(2,1)S(1)} %get-tuple-element.22.refs_3_, ...), custom_call_target="tpu_custom_call" | custom-call | tf_op jit(solution)/shard_map/second_pass/pallas_call | solution.py:520
  37.2 0.1 collective-permute-start.3
  37.3 1.5 %collective-permute-done.3.other_ref = f32[520,128]{1,0:T(8,128)S(1)} collective-permute-done((f32[520,128]{1,0:T(8,128)S(1)}, f32[520,128]{1,0:T(8,128)S(1)}, u32[]{:S(2)}, u32[]{:S(2)}) %collective-permute-start.3) | collective-permute-done | bytes 266272 | tf_op jit(solution)/shard_map/ppermute | solution.py:575
  38.8 0.8 %finish.1 = (f32[512,128]{1,0:T(8,128)}, f32[1]{0:T(128)}) custom-call(f32[520,128]{1,0:T(8,128)S(1)} %get-tuple-element.30.mine_ref, f32[520,128]{1,0:T(8,128)S(1)} %collective-permute-done.3.other_ref), custom_call_target="tpu_custom_call" | custom-call | tf_op jit(solution)/shard_map/finish/pallas_call | solution.py:576
Async XLA Ops:
  0.6 10.9 %collective-permute-start = (bf16[4,256,256]{2,1,0:T(8,128)(2,1)}, bf16[4,256,256]{2,1,0:T(8,128)(2,1)S(1)}, u32[]{:S(2)}, u32[]{:S(2)}) collective-permute-start(bf16[4,256,256]{2,1,0:T(8,128)(2,1)} %own_any.1), channel_id=1, source_target_pairs={{0,1},{1,0},{2,3},{3,2},{4,5},{5,4},{6,7},{7,6},{8,9},{9,8},{10,11... | collective-permute-start | bytes 1572872 | tf_op jit(solution)/shard_map/ppermute | solution.py:427
  1.8 0.7 %copy-start.5 = (f32[384,16]{0,1:T(8,128)S(1)}, f32[384,16]{0,1:T(8,128)}, u32[]{:S(2)}) copy-start(f32[384,16]{0,1:T(8,128)} %param.8) | copy-start | bytes 73732
  2.5 0.7 %copy-start.6 = (s32[384]{0:T(512)S(1)}, s32[384]{0:T(512)}, u32[]{:S(2)}) copy-start(s32[384]{0:T(512)} %param.9) | copy-start | bytes 4612
  3.2 0.7 %copy-start.7 = (s32[384]{0:T(512)S(1)}, s32[384]{0:T(512)}, u32[]{:S(2)}) copy-start(s32[384]{0:T(512)} %param.10) | copy-start | bytes 4612
  4.7 15.8 %all-to-all-start = ((f32[8,8,384]{2,1,0:T(8,128)}), f32[8,8,384]{2,1,0:T(8,128)S(1)}, u32[]{:S(2)}, u32[]{:S(2)}) async-start(f32[8,8,384]{2,1,0:T(8,128)} %pack.1), calls=%async_computation | async-start | bytes 196608 | tf_op jit(solution)/shard_map/all_to_all | solution.py:442
  11.5 0.8 %copy-start.3 = (bf16[4,256,256]{2,1,0:T(8,128)(2,1)}, bf16[4,256,256]{2,1,0:T(8,128)(2,1)S(1)}, u32[]{:S(2)}) copy-start(bf16[4,256,256]{2,1,0:T(8,128)(2,1)S(1)} %collective-permute-done.other_ref) | copy-start | bytes 1572868
  12.3 1.0 %copy-start.2 = (bf16[4,256,256]{2,1,0:T(8,128)(2,1)S(1)}, bf16[4,256,256]{2,1,0:T(8,128)(2,1)}, u32[]{:S(2)}) copy-start(bf16[4,256,256]{2,1,0:T(8,128)(2,1)} %own_any.1) | copy-start | bytes 1572868
  13.4 1.0 %copy-start.4 = (bf16[4,256,256]{2,1,0:T(8,128)(2,1)S(1)}, bf16[4,256,256]{2,1,0:T(8,128)(2,1)}, u32[]{:S(2)}) copy-start(bf16[4,256,256]{2,1,0:T(8,128)(2,1)} %copy-done.3) | copy-start | bytes 1572868
  14.4 0.7 %copy-start.8 = (f32[256]{0:T(256)S(1)}, f32[256]{0:T(256)}, u32[]{:S(2)}) copy-start(f32[256]{0:T(256)} %param.13) | copy-start | bytes 3076
  15.1 0.7 %copy-start.9 = (f32[256]{0:T(256)S(1)}, f32[256]{0:T(256)}, u32[]{:S(2)}) copy-start(f32[256]{0:T(256)} %param.14) | copy-start | bytes 3076
  15.8 0.7 %copy-start.10 = (f32[256]{0:T(256)S(1)}, f32[256]{0:T(256)}, u32[]{:S(2)}) copy-start(f32[256]{0:T(256)} %param.15) | copy-start | bytes 3076
  19.1 1.3 %copy-start = (bf16[8,512,256]{2,1,0:T(8,128)(2,1)}, bf16[8,512,256]{2,1,0:T(8,128)(2,1)S(1)}, u32[]{:S(2)}) copy-start(bf16[8,512,256]{2,1,0:T(8,128)(2,1)S(1)} %get-tuple-element.21.refs_1_) | copy-start | bytes 6291460
  20.5 8.8 %copy-start.1 = (bf16[8,512,256]{2,1,0:T(8,128)(2,1)S(1)}, bf16[8,512,256]{2,1,0:T(8,128)(2,1)}, u32[]{:S(2)}) copy-start(bf16[8,512,256]{2,1,0:T(8,128)(2,1)} %copy-done) | copy-start | bytes 6291460
  23.0 6.2 %collective-permute-start.2 = (bf16[272,256]{1,0:T(8,128)(2,1)S(1)}, bf16[272,256]{1,0:T(8,128)(2,1)S(1)}, u32[]{:S(2)}, u32[]{:S(2)}) collective-permute-start(bf16[272,256]{1,0:T(8,128)(2,1)S(1)} %get-tuple-element.26.refs_4_), channel_id=1, source_target_pairs={{0,2},{2,0},{1,3},{3,1},{4,6},{6,4},{5,7},{7,5},{8,10},{10,8},{9,1... | collective-permute-start | bytes 417800 | tf_op jit(solution)/shard_map/ppermute | solution.py:539
  28.1 5.3 %collective-permute-start.1 = (bf16[272,256]{1,0:T(8,128)(2,1)S(1)}, bf16[272,256]{1,0:T(8,128)(2,1)S(1)}, u32[]{:S(2)}, u32[]{:S(2)}) collective-permute-start(bf16[272,256]{1,0:T(8,128)(2,1)S(1)} %get-tuple-element.23.refs_4_), channel_id=1, source_target_pairs={{0,2},{2,0},{1,3},{3,1},{4,6},{6,4},{5,7},{7,5},{8,10},{10,8},{9,1... | collective-permute-start | bytes 417800 | tf_op jit(solution)/shard_map/ppermute | solution.py:539
  37.2 1.6 %collective-permute-start.3 = (f32[520,128]{1,0:T(8,128)S(1)}, f32[520,128]{1,0:T(8,128)S(1)}, u32[]{:S(2)}, u32[]{:S(2)}) collective-permute-start(f32[520,128]{1,0:T(8,128)S(1)} %get-tuple-element.31), channel_id=1, source_target_pairs={{0,1},{1,0},{2,3},{3,2},{4,5},{5,4},{6,7},{7,6},{8,9},{9,8},{10,11... | collective-permute-start | bytes 798728 | tf_op jit(solution)/shard_map/ppermute | solution.py:575

commit v4 on v3

--- a/solution.py
+++ b/solution.py
@@ -46,15 +46,25 @@
     return [slice(q, q + LANES) for q in range(0, width, LANES)]
 
 
-def pack_kernel(count_ref, earn_any, start_any, len_any, out_ref, earn_ref, start_ref, len_ref, sems):
-    copies = [
-        pltpu.make_async_copy(src, dst, sems.at[i])
-        for i, (src, dst) in enumerate(((earn_any, earn_ref), (start_any, start_ref), (len_any, len_ref)))
-    ]
+def fetch(pairs, sems):
+    copies = [pltpu.make_async_copy(src, dst, sems.at[i]) for i, (src, dst) in enumerate(pairs)]
     for copy in copies:
         copy.start()
     for copy in copies:
         copy.wait()
+
+
+def pack_kernel(
+    count_any, earn_any, start_any, len_any, init_any, mean_any, sd_any, out_ref, vec_ref,
+    count_ref, earn_ref, start_ref, len_ref, init_ref, mean_ref, sd_ref, sems,
+):
+    fetch(
+        (
+            (count_any, count_ref), (earn_any, earn_ref), (start_any, start_ref), (len_any, len_ref),
+            (init_any, init_ref), (mean_any, mean_ref), (sd_any, sd_ref),
+        ),
+        sems,
+    )
     periods, slot_rows = earn_ref.shape
     core = core_index()
     low_lane = lax.broadcasted_iota(jnp.int32, (periods // 2, HB), 1) < HALF
@@ -69,63 +79,81 @@
         early, late = value[: periods // 2], value[periods // 2 :]
         turned = pltpu.roll(jnp.where(core == 0, late, early), HALF, 1)
         packed = jnp.where(low_lane, jnp.where(core == 0, early, turned), jnp.where(core == 0, turned, late))
-        for to in range(out_ref.shape[0]):
-            out_ref[to, :, cols] = packed
-
-
-def prep_kernel(
-    own_any, other_ref, init_any, mean_any, sd_any,
-    first_mat, second_mat, row_probs, consts, scratch, own_ref, init_ref, mean_ref, sd_ref, sems,
-):
-    pairs = ((own_any, own_ref), (init_any, init_ref), (mean_any, mean_ref), (sd_any, sd_ref))
-    copies = [pltpu.make_async_copy(src, dst, sems.at[i]) for i, (src, dst) in enumerate(pairs)]
-    for copy in copies:
-        copy.start()
-    for copy in copies:
-        copy.wait()
-    part, states, _ = own_ref.shape
-    rows = row_probs.shape[1]
-    core, forward_first, row_begin = core_index(), is_forward_first(), lax.axis_index("hh") * rows
-
-    def column(row):
-        return jnp.broadcast_to(row, (LANES, states)).T
-
+        if len(out_ref.shape) == 2:
+            out_ref[:, cols] = packed
+        else:
+            for to in range(out_ref.shape[0]):
+                out_ref[to, :, cols] = packed
     raised = jnp.exp(init_ref[...])
     start = raised / jnp.sum(raised, axis=1, keepdims=True)
-    consts[0] = column(start)
-    consts[1] = column(mean_ref[...])
-    consts[2] = column((-0.5 * LOG2E) * jnp.exp(-2.0 * sd_ref[...]))
-    consts[3] = column(-LOG2E * sd_ref[...])
+    row = lax.broadcasted_iota(jnp.int32, vec_ref.shape, 0)
+    power = (-0.5 * LOG2E) * jnp.exp(-2.0 * sd_ref[...])
+    vec_ref[...] = jnp.where(
+        row == 0, start, jnp.where(row == 1, mean_ref[...], jnp.where(row == 2, power, -LOG2E * sd_ref[...]))
+    )
+
+
+def join_kernel(*refs):
+    out_ref = refs[-1]
+    here = lax.axis_index("hh")
+    for r, ref in enumerate(refs[:-2]):
+        out_ref[here ^ r] = ref[...]
+
+
+def put(ref, at, value):
+    states = value.shape[0]
+    high = value.astype(BF16)
+    ref[at, :states, :] = high
+    ref[at, states : 2 * states, :] = (value - high.astype(F32)).astype(BF16)
+
+
+def fill_periods(mat, row_probs, scratch, turned_pass, sources):
+    for source, ref in sources:
+
+        @pl.loop(0, ref.shape[0])
+        def _(i):
+            at = source * ref.shape[0] + i
+            lifted = jnp.exp(ref[i].astype(F32))
+            probs = lifted * (1.0 / jnp.sum(lifted, axis=1, keepdims=True))
+            if row_probs is not None:
+                rows = row_probs.shape[1]
+                scratch[...] = probs
+                row_probs[at] = scratch[own_rows(lax.axis_index("hh") * rows, rows), :]
+
+            @pl.when(turned_pass)
+            def _():
+                put(mat, at, probs.T)
+
+            @pl.when(jnp.logical_not(turned_pass))
+            def _():
+                put(mat, at, probs)
+
+
+def prep_own_kernel(own_any, vec_any, mat, consts, own_ref, vec_ref, sems):
+    fetch(((own_any, own_ref), (vec_any, vec_ref)), sems)
+    states = own_ref.shape[1]
+    for i in range(4):
+        consts[i] = jnp.broadcast_to(vec_ref[i : i + 1, :], (LANES, states)).T
+    start = vec_ref[:1, :]
     start_high = start.astype(BF16).astype(F32)
     row = lax.broadcasted_iota(jnp.int32, (EXTRA, states), 0)
     start_rows = jnp.where(row == 0, start_high, jnp.where(row == 1, start - start_high, 0.0)).astype(BF16)
-
-    def put(ref, at, value):
-        high = value.astype(BF16)
-        ref[at, :states, :] = high
-        ref[at, states : 2 * states, :] = (value - high.astype(F32)).astype(BF16)
-
-    for source, ref in ((core, own_ref), (1 - core, other_ref)):
-
-        @pl.loop(0, part)
-        def _(i):
-            at = source * part + i
-            lifted = jnp.exp(ref[i].astype(F32))
-            probs = lifted / jnp.sum(lifted, axis=1, keepdims=True)
-            scratch[...] = probs
-            row_probs[at] = scratch[pl.ds(pl.multiple_of(row_begin, rows), rows), :]
-            turned = probs.T
-            first_mat[at, 2 * states :, :] = start_rows
-
-            @pl.when(forward_first)
-            def _():
-                put(first_mat, at, turned)
-                put(second_mat, at, probs)
-
-            @pl.when(jnp.logical_not(forward_first))
-            def _():
-                put(first_mat, at, probs)
-                put(second_mat, at, turned)
+    for k in range(mat.shape[0]):
+        mat[k, 2 * states :, :] = start_rows
+    fill_periods(mat, None, None, is_forward_first(), ((core_index(), own_ref),))
+
+
+def prep_other_kernel(other_any, rows_any, mat_in, mat, other_ref, sems):
+    fetch(((other_any, other_ref),), sems)
+    fill_periods(mat, None, None, is_forward_first(), ((1 - core_index(), other_ref),))
+
+
+def prep_second_kernel(own_any, other_any, state_any, mat, row_probs, scratch, own_ref, other_ref, sems):
+    fetch(((own_any, own_ref), (other_any, other_ref)), sems)
+    core = core_index()
+    fill_periods(
+        mat, row_probs, scratch, jnp.logical_not(is_forward_first()), ((core, own_ref), (1 - core, other_ref))
+    )
 
 
 def emission(sel_ref, consts, step_now, cols):
@@ -244,7 +272,11 @@
     return [column_sum(state_ref[states:, cols].astype(F32)) for cols in tiles(state_ref.shape[1])]
 
 
-def first_kernel(resume, grids, part, rows_ref, mat, consts, *refs):
+def first_kernel(resume, grids, part, near, *refs):
+    refs = list(refs)
+    rows_ref = refs.pop(0)
+    rows_other = refs.pop(0) if near else None
+    mat, consts = refs.pop(0), refs.pop(0)
     state_in = refs[0] if resume else None
     hist, state_out, sel_ref, ab_ref, back_ref = refs[-5:]
     chunk = part * grids + (pl.program_id(0) if grids > 1 else 0)
@@ -257,15 +289,20 @@
     def scan_source(d, carry):
         rank, picked = carry
         for slot in range(slot_rows // HB):
-            block = rows_ref[d, :, slot * HB : (slot + 1) * HB]
+            cols = slice(slot * HB, (slot + 1) * HB)
+            if near:
+                here = lax.axis_index("per") == d // group
+                block = jnp.where(here, rows_ref[d % group, :, cols], rows_other[d % group, :, cols])
+            else:
+                block = rows_ref[d, :, cols]
             live = block > -0.5 * SEEN
             picked = [jnp.where(live & (rank == chunk * tops + i), block, old) for i, old in enumerate(picked)]
             rank = rank + live.astype(jnp.int32)
         return rank, picked
 
     carry = (jnp.zeros((half_periods, HB), jnp.int32), [jnp.zeros((half_periods, HB), F32)] * tops)
-    if group <= 8:
-        for d in range(group):
+    if near:
+        for d in range(2 * group):
             carry = scan_source(d, carry)
     else:
         carry = lax.fori_loop(0, group, scan_source, carry)
@@ -423,48 +460,82 @@
     shaped = jax.ShapeDtypeStruct
     dma = pltpu.SemaphoreType.DMA
 
+    along = lax.axis_size("hh")
+    near = sides == 2 and along <= 8 and along & (along - 1) == 0
+
     swap = [(0, 1), (1, 0)]
     other_logits = lax.ppermute(trans_logits, "st", swap)
-    packed = pl.pallas_call(
+    row_shape = (periods // 2, slot_rows)
+    vec_row = pltpu.VMEM((1, states), F32)
+    packed, vectors = pl.pallas_call(
         pack_kernel,
-        out_shape=shaped((group, periods // 2, slot_rows), F32),
-        in_specs=[smem(), hbm(), hbm(), hbm()],
-        out_specs=vmem(),
+        out_shape=[shaped(row_shape if near else (group,) + row_shape, F32), shaped((8, states), F32)],
+        in_specs=[hbm()] * 7,
+        out_specs=[vmem()] * 2,
         scratch_shapes=[
+            pltpu.SMEM((1,), jnp.int32),
             pltpu.VMEM((periods, slot_rows), F32),
             pltpu.VMEM((slot_rows // HB, HB), jnp.int32),
             pltpu.VMEM((slot_rows // HB, HB), jnp.int32),
-            dma((3,)),
+            vec_row,
+            vec_row,
+            vec_row,
+            dma((7,)),
         ],
-        compiler_params=params(4),
         name="pack",
-    )(block_count, earnings.T, starts.reshape(-1, HB), lengths.reshape(-1, HB))
-    gathered = lax.all_to_all(packed, ("hh", "per"), split_axis=0, concat_axis=0, tiled=True)
-
-    first_mat, second_mat, row_probs, consts = pl.pallas_call(
-        prep_kernel,
-        out_shape=[
-            shaped((steps, 2 * states + EXTRA, states), BF16),
-            shaped((steps, 2 * states, states), BF16),
-            shaped((steps, rows, states), F32),
-            shaped((4, states, LANES), F32),
-        ],
-        in_specs=[hbm(), vmem(), hbm(), hbm(), hbm()],
-        out_specs=[vmem()] * 4,
-        scratch_shapes=[
-            pltpu.VMEM((states, states), F32),
-            pltpu.VMEM(trans_logits.shape, BF16),
-            pltpu.VMEM((1, states), F32),
-            pltpu.VMEM((1, states), F32),
-            pltpu.VMEM((1, states), F32),
-            dma((4,)),
-        ],
-        compiler_params=params(8),
-        name="prep",
     )(
-        trans_logits, other_logits,
+        block_count, earnings.T, starts.reshape(-1, HB), lengths.reshape(-1, HB),
         init_logits.reshape(1, states), state_mean.reshape(1, states), log_sd.reshape(1, states),
     )
+    first_shape = shaped((steps, 2 * states + EXTRA, states), BF16)
+    half_logits = pltpu.VMEM(trans_logits.shape, BF16)
+    first_mat, consts = pl.pallas_call(
+        prep_own_kernel,
+        out_shape=[first_shape, shaped((4, states, LANES), F32)],
+        in_specs=[hbm()] * 2,
+        out_specs=[vmem()] * 2,
+        scratch_shapes=[half_logits, pltpu.VMEM((8, states), F32), dma((2,))],
+        compiler_params=params(4),
+        name="prep_own",
+    )(trans_logits, vectors)
+    if near:
+        pieces = [packed] + [
+            lax.ppermute(packed, "hh", [(i, i ^ r) for i in range(along)]) for r in range(1, along)
+        ]
+        joined = pl.pallas_call(
+            join_kernel,
+            out_shape=shaped((along,) + row_shape, F32),
+            in_specs=[vmem()] * along + [hbm()],
+            out_specs=vmem(),
+            compiler_params=params(2),
+            name="join",
+        )(*pieces, consts)
+        gathered = [joined, lax.ppermute(joined, "per", swap)]
+    else:
+        gathered = [lax.all_to_all(packed, ("hh", "per"), split_axis=0, concat_axis=0, tiled=True)]
+        joined = gathered[0]
+
+    first_mat = pl.pallas_call(
+        prep_other_kernel,
+        out_shape=first_shape,
+        in_specs=[hbm(), hbm(), vmem()],
+        out_specs=vmem(),
+        scratch_shapes=[half_logits, dma((1,))],
+        input_output_aliases={2: 0},
+        compiler_params=params(4),
+        name="prep_other",
+    )(other_logits, joined, first_mat)
+
+    def prep_second(after):
+        return pl.pallas_call(
+            prep_second_kernel,
+            out_shape=[shaped((steps, 2 * states, states), BF16), shaped((steps, rows, states), F32)],
+            in_specs=[hbm()] * 3,
+            out_specs=[vmem()] * 2,
+            scratch_shapes=[pltpu.VMEM((states, states), F32), half_logits, half_logits, dma((2,))],
+            compiler_params=params(4),
+            name="prep_second",
+        )(trans_logits, other_logits, after)
 
     def whole(*shape):
         if grids == 1:
@@ -489,16 +560,16 @@
     def first_pass(index, state_in):
         resume = state_in is not None
         return pl.pallas_call(
-            functools.partial(first_kernel, resume, grids, index),
+            functools.partial(first_kernel, resume, grids, index, near),
             grid=grid,
             out_shape=[hist_shape, state_shape, sel_shape],
-            in_specs=[whole(*gathered.shape), whole(*first_mat.shape), const_spec]
+            in_specs=[whole(*x.shape) for x in gathered + [first_mat]] + [const_spec]
             + [state_spec] * resume,
             out_specs=[hist_spec, state_spec, sel_spec],
             scratch_shapes=[pltpu.VMEM((states, width), BF16), pltpu.VMEM((states, width), F32)],
             compiler_params=params(8 if grids == 1 else 32),
             name="first_pass",
-        )(gathered, first_mat, consts, *([state_in] if resume else []))
+        )(*gathered, first_mat, consts, *([state_in] if resume else []))
 
     def second_pass(kept, state_in, sums_in, last, extend):
         hist, own_state, sel = kept
@@ -541,6 +612,7 @@
     if sides == 2:
         kept = [first_pass(index, None) for index in range(parts)]
         arrived = [hand_over(each[1], 0) for each in kept]
+        second_mat, row_probs = prep_second(kept[-1][1])
         sums = None
         for index in range(parts):
             sums = second_pass(kept[index], arrived[index], sums, index == parts - 1, False)
@@ -548,6 +620,7 @@
     else:
         kept = [jnp.zeros(x.shape, x.dtype) for x in (hist_shape, state_shape, sel_shape)]
         done = [jnp.zeros(x.shape, x.dtype) for x in (swap_shape, swap_shape, state_shape)]
+        second_mat, row_probs = prep_second(joined)
         state = None
         for stage in range(sides):
             active = (side == stage) | (side == sides - 1 - stage)

time: 40.2 us -> 38.4 us (0.955)
  local copies, waits for them, and re-layouts: 8.33 us -> 2.45 us
  waiting for transfers between devices: 3.14 us -> 5.59 us
  Pallas kernels: 16.5 us -> 18.7 us
  starting transfers between devices: 10.3 us -> 9.76 us
    all_to_all x1 -> x0, starting transfers between devices: 6.82 us -> none  [per_device(): lax.all_to_all(packed, ('hh', 'per'), split_axis=0, concat_axis=0, tiled=...]
    ppermute x0 -> x4, starting transfers between devices: none -> 6.73 us  [the longest x3 5.24 us: per_device(): lax.ppermute(packed, 'hh', [(i, i ^ r) for i in range(along)])]
    unnamed x22 -> x8, local copies, waits for them, and re-layouts: 8.33 us -> 2.45 us
    ppermute x0 -> x4, waiting for transfers between devices: none -> 4.05 us  [the longest x3 2.6 us: per_device(): lax.ppermute(packed, 'hh', [(i, i ^ r) for i in range(along)])]
    pallas_call x4 -> x7, Pallas kernels: 8.62 us -> 10.8 us  [the longest x2 5.27 us: first_pass(): pl.pallas_call(functools.partial(first_kernel, resume, grids, index, near...]
    ppermute x2, waiting for transfers between devices: 1.61 us -> 0.01 us  [hand_over(): return lax.ppermute(state, 'per', moves)]
    ppermute x2, starting transfers between devices: 2.85 us -> 2.44 us  [hand_over(): return lax.ppermute(state, 'per', moves)]
  transfers between devices with their start and end apart: 5 -> 8, of which waited for: 3 -> 3; matrix products, arithmetic and copies ran while one was open for 0% -> 0% of each run, Pallas kernels for 23% -> 30%
where the time goes in v4:
time: 38.4 us; the launch traced here: 38 us
  Pallas kernels  18.7 us (49%)
  starting transfers between devices  9.76 us (25%)
  waiting for transfers between devices  5.59 us (15%)
  local copies, waits for them, and re-layouts  2.45 us (6%)
  between operations  1.56 us (4%)
    pallas_call x2, Pallas kernels, second_pass(): pl.pallas_call(functools.partial(second_kernel, resume, last, extend, gri...  7.15 us
    pallas_call x2, Pallas kernels, first_pass(): pl.pallas_call(functools.partial(first_kernel, resume, grids, index, near...  5.27 us
    ppermute x3, starting transfers between devices, per_device(): lax.ppermute(packed, 'hh', [(i, i ^ r) for i in range(along)])  5.24 us
    ppermute x3, waiting for transfers between devices, per_device(): lax.ppermute(packed, 'hh', [(i, i ^ r) for i in range(along)])  2.6 us
    unnamed x8, local copies, waits for them, and re-layouts  2.45 us
    ppermute x2, starting transfers between devices, hand_over(): return lax.ppermute(state, 'per', moves)  2.44 us
    ppermute x1, waiting for transfers between devices, per_device(): received = lax.ppermute(other, 'st', swap)  1.53 us
    pallas_call x1, Pallas kernels, per_device(): pl.pallas_call(pack_kernel, out_shape=[shaped(row_shape if near else (gro...  1.52 us
  transfers between devices with their start and end apart: 8, of which 3 were waited for; matrix products, arithmetic and copies ran while one was open for 0% of the time, Pallas kernels for 30%

profile of v4, /device:TPU:0, one launch (start us, length us, event | category | flops | bytes accessed | tf_op | source)
XLA Modules:
  0.0 38.0 jit_solution(2213901238029029106)
XLA Ops:
  0.6 0.5 %collective-permute-start.4 = (bf16[4,256,256]{2,1,0:T(8,128)(2,1)}, bf16[4,256,256]{2,1,0:T(8,128)(2,1)S(1)}, u32[]{:S(2)}, u32[]{:S(2)}) collective-permute-start(bf16[4,256,256]{2,1,0:T(8,128)(2,1)} %own_any.3), channel_id=1, source_target_pairs={{0,1},{1,0},{2,3},{3,2},{4,5},{5,4},{6,7},{7,6},{8,9},{9,8},{10,11... | collective-permute-start | bytes 1572872 | tf_op jit(solution)/shard_map/ppermute | solution.py:467
  1.8 1.5 %pack.1 = (f32[8,384]{1,0:T(8,128)}, f32[8,256]{1,0:T(8,128)}) custom-call(s32[1]{0:T(128)S(6)} %copy.12.count_any, f32[16,384]{1,0:T(8,128)} %bitcast.7, s32[3,128]{1,0:T(4,128)} %bitcast.8, s32[3,128]{1,0:T(4,128)} %bitcast.9, f32[1,256]{1,0:T(1,128)} %bitcast.10, f32[1,256]{1,0:T(1,128)} %bitcast.11, f32[1,256]{1,0:T(1,128)} %bitcast.12), custom_call_target="tpu_custom_call" | custom-call | tf_op jit(solution)/shard_map/pack/pallas_call | solution.py:470
  3.3 2.6 %collective-permute-start = (f32[8,384]{1,0:T(8,128)}, f32[8,384]{1,0:T(8,128)S(1)}, u32[]{:S(2)}, u32[]{:S(2)}) collective-permute-start(f32[8,384]{1,0:T(8,128)} %get-tuple-element.20.refs_0_), channel_id=1, source_target_pairs={{0,4},{4,0},{8,12},{12,8},{1,5},{5,1},{9,13},{13,9},{2,6},{6,2},{1... | collective-permute-start | bytes 36872 | tf_op jit(solution)/shard_map/ppermute | solution.py:503
  6.0 2.6 %collective-permute-start.1 = (f32[8,384]{1,0:T(8,128)}, f32[8,384]{1,0:T(8,128)S(1)}, u32[]{:S(2)}, u32[]{:S(2)}) collective-permute-start(f32[8,384]{1,0:T(8,128)} %get-tuple-element.20.refs_0_), channel_id=1, source_target_pairs={{0,8},{4,12},{8,0},{12,4},{1,9},{5,13},{9,1},{13,5},{2,10},{6,14},... | collective-permute-start | bytes 36872 | tf_op jit(solution)/shard_map/ppermute | solution.py:503
  8.6 0.0 collective-permute-start.2
  8.6 0.0 copy-start
  8.6 1.0 %copy-done = bf16[4,256,256]{2,1,0:T(8,128)(2,1)S(1)} copy-done((bf16[4,256,256]{2,1,0:T(8,128)(2,1)S(1)}, bf16[4,256,256]{2,1,0:T(8,128)(2,1)}, u32[]{:S(2)}) %copy-start) | copy-done | bytes 524312
  9.6 0.0 copy-start.3
  9.6 0.7 %copy-done.3 = f32[8,256]{1,0:T(8,128)S(1)} copy-done((f32[8,256]{1,0:T(8,128)S(1)}, f32[8,256]{1,0:T(8,128)}, u32[]{:S(2)}) %copy-start.3) | copy-done | bytes 8216
  10.3 1.3 %prep_own.1 = (bf16[8,528,256]{2,1,0:T(8,128)(2,1)S(1)}, f32[4,256,128]{2,1,0:T(8,128)S(1)}) custom-call(bf16[4,256,256]{2,1,0:T(8,128)(2,1)S(1)} %copy-done, f32[8,256]{1,0:T(8,128)S(1)} %copy-done.3), custom_call_target="tpu_custom_call" | custom-call | tf_op jit(solution)/shard_map/prep_own/pallas_call | solution.py:492
  11.6 0.0 collective-permute-done.refs_1_
  11.7 0.0 collective-permute-done.1.refs_2_
  11.7 2.6 %collective-permute-done.2.refs_3_ = f32[8,384]{1,0:T(8,128)S(1)} collective-permute-done((f32[8,384]{1,0:T(8,128)}, f32[8,384]{1,0:T(8,128)S(1)}, u32[]{:S(2)}, u32[]{:S(2)}) %collective-permute-start.2) | collective-permute-done | bytes 12320 | tf_op jit(solution)/shard_map/ppermute | solution.py:503
  14.3 0.0 copy-start.2
  14.3 0.7 %copy-done.2 = f32[8,384]{1,0:T(8,128)S(1)} copy-done((f32[8,384]{1,0:T(8,128)S(1)}, f32[8,384]{1,0:T(8,128)}, u32[]{:S(2)}) %copy-start.2) | copy-done | bytes 12312
  15.0 1.5 %collective-permute-start.3 = (f32[4,8,384]{2,1,0:T(8,128)S(1)}, f32[4,8,384]{2,1,0:T(8,128)S(1)}, u32[]{:S(2)}, u32[]{:S(2)}) collective-permute-start(f32[4,8,384]{2,1,0:T(8,128)S(1)} %join.1.rows_any.refs_0_), channel_id=1, source_target_pairs={{0,2},{2,0},{1,3},{3,1},{4,6},{6,4},{5,7},{7,5},{8,10},{10,8},{9,1... | collective-permute-start | bytes 147464 | tf_op jit(solution)/shard_map/ppermute | solution.py:513
  16.5 0.0 collective-permute-done.4.other_any
  16.5 1.1 %prep_other.1.refs_2_ = bf16[8,528,256]{2,1,0:T(8,128)(2,1)S(1)} custom-call(bf16[4,256,256]{2,1,0:T(8,128)(2,1)S(1)} %collective-permute-done.4.other_any, f32[4,8,384]{2,1,0:T(8,128)S(1)} %join.1.rows_any.refs_0_, bf16[8,528,256]{2,1,0:T(8,128)(2,1)S(1)} %get-tuple-element.23.mat_in), custom_call_target="tpu_custom_call", output_to_operand_aliasing={{}: (2, {})} | custom-call | tf_op jit(solution)/shard_map/prep_other/pallas_call | solution.py:518
  17.6 0.0 copy-start.1
  17.6 1.5 %collective-permute-done.3.refs_1_ = f32[4,8,384]{2,1,0:T(8,128)S(1)} collective-permute-done((f32[4,8,384]{2,1,0:T(8,128)S(1)}, f32[4,8,384]{2,1,0:T(8,128)S(1)}, u32[]{:S(2)}, u32[]{:S(2)}) %collective-permute-start.3) | collective-permute-done | bytes 49184 | tf_op jit(solution)/shard_map/ppermute | solution.py:513
  19.1 2.6 %first_pass.3 = (bf16[8,256,256]{2,1,0:T(8,128)(2,1)S(1)}, bf16[272,256]{1,0:T(8,128)(2,1)S(1)}, f32[3,16,8,256]{3,2,1,0:T(8,128)S(1)}) custom-call(f32[4,8,384]{2,1,0:T(8,128)S(1)} %join.1.rows_any.refs_0_, f32[4,8,384]{2,1,0:T(8,128)S(1)} %collective-permute-done.3.refs_1_, bf16[8,528,256]{2,1,0:T(8,128)(2,1)S(1)} %prep_other.1.refs_2_, ...), custom_call_target="tpu_custom_call" | custom-call | tf_op jit(solution)/shard_map/first_pass/pallas_call | solution.py:562
  21.7 1.8 %collective-permute-start.6 = (bf16[272,256]{1,0:T(8,128)(2,1)S(1)}, bf16[272,256]{1,0:T(8,128)(2,1)S(1)}, u32[]{:S(2)}, u32[]{:S(2)}) collective-permute-start(bf16[272,256]{1,0:T(8,128)(2,1)S(1)} %get-tuple-element.30.refs_4_), channel_id=1, source_target_pairs={{0,2},{2,0},{1,3},{3,1},{4,6},{6,4},{5,7},{7,5},{8,10},{10,8},{9,1... | collective-permute-start | bytes 417800 | tf_op jit(solution)/shard_map/ppermute | solution.py:610
  23.6 2.6 %first_pass.2 = (bf16[8,256,256]{2,1,0:T(8,128)(2,1)S(1)}, bf16[272,256]{1,0:T(8,128)(2,1)S(1)}, f32[3,16,8,256]{3,2,1,0:T(8,128)S(1)}) custom-call(f32[4,8,384]{2,1,0:T(8,128)S(1)} %join.1.rows_any.refs_0_, f32[4,8,384]{2,1,0:T(8,128)S(1)} %collective-permute-done.3.refs_1_, bf16[8,528,256]{2,1,0:T(8,128)(2,1)S(1)} %prep_other.1.refs_2_, ...), custom_call_target="tpu_custom_call" | custom-call | tf_op jit(solution)/shard_map/first_pass/pallas_call | solution.py:562
  26.2 0.6 %collective-permute-start.5 = (bf16[272,256]{1,0:T(8,128)(2,1)S(1)}, bf16[272,256]{1,0:T(8,128)(2,1)S(1)}, u32[]{:S(2)}, u32[]{:S(2)}) collective-permute-start(bf16[272,256]{1,0:T(8,128)(2,1)S(1)} %get-tuple-element.25.state_any.refs_4_), channel_id=1, source_target_pairs={{0,2},{2,0},{1,3},{3,1},{4,6},{6,4},{5,7},{7,5},{8,10},{10,8},{9,1... | collective-permute-start | bytes 417800 | tf_op jit(solution)/shard_map/ppermute | solution.py:610
  26.8 0.0 copy-done.1
  26.8 1.5 %prep_second.1 = (bf16[8,512,256]{2,1,0:T(8,128)(2,1)S(1)}, f32[8,64,256]{2,1,0:T(8,128)S(1)}) custom-call(bf16[4,256,256]{2,1,0:T(8,128)(2,1)S(1)} %copy-done.1, bf16[4,256,256]{2,1,0:T(8,128)(2,1)S(1)} %collective-permute-done.4.other_any, bf16[272,256]{1,0:T(8,128)(2,1)S(1)} %get-tuple-element.25.state_any.refs_4_), custom_call_target="tpu_custom_call" | custom-call | tf_op jit(solution)/shard_map/prep_second/pallas_call | solution.py:530
  28.3 0.0 collective-permute-done.6.refs_5_
  28.3 3.3 %second_pass.2 = (f32[8,64,256]{2,1,0:T(8,128)S(1)}, f32[8,128]{1,0:T(8,128)S(1)}) custom-call(f32[3,16,8,256]{3,2,1,0:T(8,128)S(1)} %get-tuple-element.28.refs_0_, bf16[8,512,256]{2,1,0:T(8,128)(2,1)S(1)} %get-tuple-element.26.refs_1_, f32[4,256,128]{2,1,0:T(8,128)S(1)} %get-tuple-element.22.refs_4_.refs_3_.refs_2_, ...), custom_call_target="tpu_custom_call" | custom-call | tf_op jit(solution)/shard_map/second_pass/pallas_call | solution.py:591
  31.6 0.0 collective-permute-done.5.refs_5_
  31.7 3.8 %second_pass.3 = (f32[520,128]{1,0:T(8,128)S(1)}, f32[520,128]{1,0:T(8,128)S(1)}) custom-call(f32[3,16,8,256]{3,2,1,0:T(8,128)S(1)} %get-tuple-element.24.refs_0_, bf16[8,512,256]{2,1,0:T(8,128)(2,1)S(1)} %get-tuple-element.26.refs_1_, f32[4,256,128]{2,1,0:T(8,128)S(1)} %get-tuple-element.22.refs_4_.refs_3_.refs_2_, ...), custom_call_target="tpu_custom_call" | custom-call | tf_op jit(solution)/shard_map/second_pass/pallas_call | solution.py:591
  35.5 0.1 collective-permute-start.7
  35.6 1.5 %collective-permute-done.7.other_ref = f32[520,128]{1,0:T(8,128)S(1)} collective-permute-done((f32[520,128]{1,0:T(8,128)S(1)}, f32[520,128]{1,0:T(8,128)S(1)}, u32[]{:S(2)}, u32[]{:S(2)}) %collective-permute-start.7) | collective-permute-done | bytes 266272 | tf_op jit(solution)/shard_map/ppermute | solution.py:648
  37.1 0.8 %finish.1 = (f32[512,128]{1,0:T(8,128)}, f32[1]{0:T(128)}) custom-call(f32[520,128]{1,0:T(8,128)S(1)} %get-tuple-element.34.mine_ref, f32[520,128]{1,0:T(8,128)S(1)} %collective-permute-done.7.other_ref), custom_call_target="tpu_custom_call" | custom-call | tf_op jit(solution)/shard_map/finish/pallas_call | solution.py:649
  (1 shorter events, 0.0 us)
Async XLA Ops:
  0.6 15.8 %collective-permute-start.4 = (bf16[4,256,256]{2,1,0:T(8,128)(2,1)}, bf16[4,256,256]{2,1,0:T(8,128)(2,1)S(1)}, u32[]{:S(2)}, u32[]{:S(2)}) collective-permute-start(bf16[4,256,256]{2,1,0:T(8,128)(2,1)} %own_any.3), channel_id=1, source_target_pairs={{0,1},{1,0},{2,3},{3,2},{4,5},{5,4},{6,7},{7,6},{8,9},{9,8},{10,11... | collective-permute-start | bytes 1572872 | tf_op jit(solution)/shard_map/ppermute | solution.py:467
  3.3 8.3 %collective-permute-start = (f32[8,384]{1,0:T(8,128)}, f32[8,384]{1,0:T(8,128)S(1)}, u32[]{:S(2)}, u32[]{:S(2)}) collective-permute-start(f32[8,384]{1,0:T(8,128)} %get-tuple-element.20.refs_0_), channel_id=1, source_target_pairs={{0,4},{4,0},{8,12},{12,8},{1,5},{5,1},{9,13},{13,9},{2,6},{6,2},{1... | collective-permute-start | bytes 36872 | tf_op jit(solution)/shard_map/ppermute | solution.py:503
  6.0 5.7 %collective-permute-start.1 = (f32[8,384]{1,0:T(8,128)}, f32[8,384]{1,0:T(8,128)S(1)}, u32[]{:S(2)}, u32[]{:S(2)}) collective-permute-start(f32[8,384]{1,0:T(8,128)} %get-tuple-element.20.refs_0_), channel_id=1, source_target_pairs={{0,8},{4,12},{8,0},{12,4},{1,9},{5,13},{9,1},{13,5},{2,10},{6,14},... | collective-permute-start | bytes 36872 | tf_op jit(solution)/shard_map/ppermute | solution.py:503
  8.6 5.7 %collective-permute-start.2 = (f32[8,384]{1,0:T(8,128)}, f32[8,384]{1,0:T(8,128)S(1)}, u32[]{:S(2)}, u32[]{:S(2)}) collective-permute-start(f32[8,384]{1,0:T(8,128)} %get-tuple-element.20.refs_0_), channel_id=1, source_target_pairs={{0,12},{4,8},{8,4},{12,0},{1,13},{5,9},{9,5},{13,1},{2,14},{6,10},... | collective-permute-start | bytes 36872 | tf_op jit(solution)/shard_map/ppermute | solution.py:503
  8.6 1.0 %copy-start = (bf16[4,256,256]{2,1,0:T(8,128)(2,1)S(1)}, bf16[4,256,256]{2,1,0:T(8,128)(2,1)}, u32[]{:S(2)}) copy-start(bf16[4,256,256]{2,1,0:T(8,128)(2,1)} %own_any.3) | copy-start | bytes 1572868
  9.6 0.7 %copy-start.3 = (f32[8,256]{1,0:T(8,128)S(1)}, f32[8,256]{1,0:T(8,128)}, u32[]{:S(2)}) copy-start(f32[8,256]{1,0:T(8,128)} %get-tuple-element.21.vec_any) | copy-start | bytes 24580
  14.3 0.7 %copy-start.2 = (f32[8,384]{1,0:T(8,128)S(1)}, f32[8,384]{1,0:T(8,128)}, u32[]{:S(2)}) copy-start(f32[8,384]{1,0:T(8,128)} %get-tuple-element.20.refs_0_) | copy-start | bytes 36868
  15.0 4.1 %collective-permute-start.3 = (f32[4,8,384]{2,1,0:T(8,128)S(1)}, f32[4,8,384]{2,1,0:T(8,128)S(1)}, u32[]{:S(2)}, u32[]{:S(2)}) collective-permute-start(f32[4,8,384]{2,1,0:T(8,128)S(1)} %join.1.rows_any.refs_0_), channel_id=1, source_target_pairs={{0,2},{2,0},{1,3},{3,1},{4,6},{6,4},{5,7},{7,5},{8,10},{10,8},{9,1... | collective-permute-start | bytes 147464 | tf_op jit(solution)/shard_map/ppermute | solution.py:513
  17.6 9.2 %copy-start.1 = (bf16[4,256,256]{2,1,0:T(8,128)(2,1)S(1)}, bf16[4,256,256]{2,1,0:T(8,128)(2,1)}, u32[]{:S(2)}) copy-start(bf16[4,256,256]{2,1,0:T(8,128)(2,1)} %own_any.3) | copy-start | bytes 1572868
  21.7 6.6 %collective-permute-start.6 = (bf16[272,256]{1,0:T(8,128)(2,1)S(1)}, bf16[272,256]{1,0:T(8,128)(2,1)S(1)}, u32[]{:S(2)}, u32[]{:S(2)}) collective-permute-start(bf16[272,256]{1,0:T(8,128)(2,1)S(1)} %get-tuple-element.30.refs_4_), channel_id=1, source_target_pairs={{0,2},{2,0},{1,3},{3,1},{4,6},{6,4},{5,7},{7,5},{8,10},{10,8},{9,1... | collective-permute-start | bytes 417800 | tf_op jit(solution)/shard_map/ppermute | solution.py:610
  26.2 5.5 %collective-permute-start.5 = (bf16[272,256]{1,0:T(8,128)(2,1)S(1)}, bf16[272,256]{1,0:T(8,128)(2,1)S(1)}, u32[]{:S(2)}, u32[]{:S(2)}) collective-permute-start(bf16[272,256]{1,0:T(8,128)(2,1)S(1)} %get-tuple-element.25.state_any.refs_4_), channel_id=1, source_target_pairs={{0,2},{2,0},{1,3},{3,1},{4,6},{6,4},{5,7},{7,5},{8,10},{10,8},{9,1... | collective-permute-start | bytes 417800 | tf_op jit(solution)/shard_map/ppermute | solution.py:610
  35.5 1.6 %collective-permute-start.7 = (f32[520,128]{1,0:T(8,128)S(1)}, f32[520,128]{1,0:T(8,128)S(1)}, u32[]{:S(2)}, u32[]{:S(2)}) collective-permute-start(f32[520,128]{1,0:T(8,128)S(1)} %get-tuple-element.35), channel_id=1, source_target_pairs={{0,1},{1,0},{2,3},{3,2},{4,5},{5,4},{6,7},{7,6},{8,9},{9,8},{10,11... | collective-permute-start | bytes 798728 | tf_op jit(solution)/shard_map/ppermute | solution.py:648

commit v5 on v4

--- a/solution.py
+++ b/solution.py
@@ -93,11 +93,11 @@
     )
 
 
-def join_kernel(*refs):
-    out_ref = refs[-1]
-    here = lax.axis_index("hh")
-    for r, ref in enumerate(refs[:-2]):
-        out_ref[here ^ r] = ref[...]
+def join_kernel(bit, mine_ref, got_ref, after_any, out_ref):
+    count = mine_ref.shape[0]
+    upper = (lax.axis_index("hh") // bit) % 2
+    out_ref[pl.ds(upper * count, count)] = mine_ref[...]
+    out_ref[pl.ds((1 - upper) * count, count)] = got_ref[...]
 
 
 def put(ref, at, value):
@@ -107,29 +107,32 @@
     ref[at, states : 2 * states, :] = (value - high.astype(F32)).astype(BF16)
 
 
-def fill_periods(mat, row_probs, scratch, turned_pass, sources):
-    for source, ref in sources:
-
-        @pl.loop(0, ref.shape[0])
-        def _(i):
-            at = source * ref.shape[0] + i
-            lifted = jnp.exp(ref[i].astype(F32))
-            probs = lifted * (1.0 / jnp.sum(lifted, axis=1, keepdims=True))
-            if row_probs is not None:
-                rows = row_probs.shape[1]
-                scratch[...] = probs
-                row_probs[at] = scratch[own_rows(lax.axis_index("hh") * rows, rows), :]
-
-            @pl.when(turned_pass)
-            def _():
-                put(mat, at, probs.T)
-
-            @pl.when(jnp.logical_not(turned_pass))
-            def _():
-                put(mat, at, probs)
-
-
-def prep_own_kernel(own_any, vec_any, mat, consts, own_ref, vec_ref, sems):
+def fill_periods(mat, row_probs, scratch, turned_pass, source, ref, periods, part):
+    @pl.loop(periods[0], periods[1])
+    def _(i):
+        at = source * part + i
+        lifted = jnp.exp(ref[i].astype(F32))
+        probs = lifted * (1.0 / jnp.sum(lifted, axis=1, keepdims=True))
+        if row_probs is not None:
+            rows = row_probs.shape[1]
+            scratch[...] = probs
+            row_probs[at] = scratch[own_rows(lax.axis_index("hh") * rows, rows), :]
+
+        @pl.when(turned_pass)
+        def _():
+            put(mat, at, probs.T)
+
+        @pl.when(jnp.logical_not(turned_pass))
+        def _():
+            put(mat, at, probs)
+
+
+def prep_own_kernel(periods, own_any, packed_any, mat, packed, own_ref, sems):
+    fetch(((own_any, own_ref), (packed_any, packed)), sems)
+    fill_periods(mat, None, None, is_forward_first(), core_index(), own_ref, periods, own_ref.shape[0])
+
+
+def prep_rest_kernel(periods, own_any, vec_any, after_any, mat_in, mat, consts, own_ref, vec_ref, sems):
     fetch(((own_any, own_ref), (vec_any, vec_ref)), sems)
     states = own_ref.shape[1]
     for i in range(4):
@@ -140,20 +143,20 @@
     start_rows = jnp.where(row == 0, start_high, jnp.where(row == 1, start - start_high, 0.0)).astype(BF16)
     for k in range(mat.shape[0]):
         mat[k, 2 * states :, :] = start_rows
-    fill_periods(mat, None, None, is_forward_first(), ((core_index(), own_ref),))
-
-
-def prep_other_kernel(other_any, rows_any, mat_in, mat, other_ref, sems):
+    fill_periods(mat, None, None, is_forward_first(), core_index(), own_ref, periods, own_ref.shape[0])
+
+
+def prep_other_kernel(other_any, after_any, mat_in, mat, other_ref, sems):
     fetch(((other_any, other_ref),), sems)
-    fill_periods(mat, None, None, is_forward_first(), ((1 - core_index(), other_ref),))
-
-
-def prep_second_kernel(own_any, other_any, state_any, mat, row_probs, scratch, own_ref, other_ref, sems):
+    part = other_ref.shape[0]
+    fill_periods(mat, None, None, is_forward_first(), 1 - core_index(), other_ref, (0, part), part)
+
+
+def prep_second_kernel(own_any, other_any, after_any, mat, row_probs, scratch, own_ref, other_ref, sems):
     fetch(((own_any, own_ref), (other_any, other_ref)), sems)
-    core = core_index()
-    fill_periods(
-        mat, row_probs, scratch, jnp.logical_not(is_forward_first()), ((core, own_ref), (1 - core, other_ref))
-    )
+    turned_pass, part = jnp.logical_not(is_forward_first()), own_ref.shape[0]
+    for source, ref in ((core_index(), own_ref), (1 - core_index(), other_ref)):
+        fill_periods(mat, row_probs, scratch, turned_pass, source, ref, (0, part), part)
 
 
 def emission(sel_ref, consts, step_now, cols):
@@ -489,42 +492,66 @@
     )
     first_shape = shaped((steps, 2 * states + EXTRA, states), BF16)
     half_logits = pltpu.VMEM(trans_logits.shape, BF16)
-    first_mat, consts = pl.pallas_call(
-        prep_own_kernel,
-        out_shape=[first_shape, shaped((4, states, LANES), F32)],
+    early = (part + 1) // 2
+    first_mat, kept_rows = pl.pallas_call(
+        functools.partial(prep_own_kernel, (0, early)),
+        out_shape=[first_shape, shaped(packed.shape, F32)],
         in_specs=[hbm()] * 2,
         out_specs=[vmem()] * 2,
-        scratch_shapes=[half_logits, pltpu.VMEM((8, states), F32), dma((2,))],
+        scratch_shapes=[half_logits, dma((2,))],
         compiler_params=params(4),
         name="prep_own",
-    )(trans_logits, vectors)
+    )(trans_logits, packed)
+
+    def prep_rest(mat, after):
+        return pl.pallas_call(
+            functools.partial(prep_rest_kernel, (early, part)),
+            out_shape=[first_shape, shaped((4, states, LANES), F32)],
+            in_specs=[hbm(), hbm(), hbm(), vmem()],
+            out_specs=[vmem()] * 2,
+            scratch_shapes=[half_logits, pltpu.VMEM((8, states), F32), dma((2,))],
+            input_output_aliases={3: 0},
+            compiler_params=params(4),
+            name="prep_rest",
+        )(trans_logits, vectors, after, mat)
+
+    def prep_other(mat, after):
+        return pl.pallas_call(
+            prep_other_kernel,
+            out_shape=first_shape,
+            in_specs=[hbm(), hbm(), vmem()],
+            out_specs=vmem(),
+            scratch_shapes=[half_logits, dma((1,))],
+            input_output_aliases={2: 0},
+            compiler_params=params(4),
+            name="prep_other",
+        )(other_logits, after, mat)
+
     if near:
-        pieces = [packed] + [
-            lax.ppermute(packed, "hh", [(i, i ^ r) for i in range(along)]) for r in range(1, along)
-        ]
-        joined = pl.pallas_call(
-            join_kernel,
-            out_shape=shaped((along,) + row_shape, F32),
-            in_specs=[vmem()] * along + [hbm()],
-            out_specs=vmem(),
-            compiler_params=params(2),
-            name="join",
-        )(*pieces, consts)
-        gathered = [joined, lax.ppermute(joined, "per", swap)]
+        rows_here, sent, consts = kept_rows[None], packed[None], None
+        bit = along // 2
+        while bit:
+            got = lax.ppermute(sent, "hh", [(i, i ^ bit) for i in range(along)])
+            if bit < along // 2 and consts is None:
+                first_mat, consts = prep_rest(first_mat, rows_here)
+            after = rows_here if consts is None else consts
+            rows_here = pl.pallas_call(
+                functools.partial(join_kernel, bit),
+                out_shape=shaped((2 * rows_here.shape[0],) + row_shape, F32),
+                in_specs=[vmem(), vmem(), hbm()],
+                out_specs=vmem(),
+                compiler_params=params(2),
+                name="join",
+            )(rows_here, got, after)
+            sent = rows_here
+            bit //= 2
+        if consts is None:
+            first_mat, consts = prep_rest(first_mat, rows_here)
+        gathered = [rows_here, lax.ppermute(rows_here, "per", swap)]
     else:
         gathered = [lax.all_to_all(packed, ("hh", "per"), split_axis=0, concat_axis=0, tiled=True)]
-        joined = gathered[0]
-
-    first_mat = pl.pallas_call(
-        prep_other_kernel,
-        out_shape=first_shape,
-        in_specs=[hbm(), hbm(), vmem()],
-        out_specs=vmem(),
-        scratch_shapes=[half_logits, dma((1,))],
-        input_output_aliases={2: 0},
-        compiler_params=params(4),
-        name="prep_other",
-    )(other_logits, joined, first_mat)
+        first_mat, consts = prep_rest(first_mat, gathered[0])
+    first_mat = prep_other(first_mat, gathered[0])
 
     def prep_second(after):
         return pl.pallas_call(
@@ -620,7 +647,7 @@
     else:
         kept = [jnp.zeros(x.shape, x.dtype) for x in (hist_shape, state_shape, sel_shape)]
         done = [jnp.zeros(x.shape, x.dtype) for x in (swap_shape, swap_shape, state_shape)]
-        second_mat, row_probs = prep_second(joined)
+        second_mat, row_probs = prep_second(gathered[0])
         state = None
         for stage in range(sides):
             active = (side == stage) | (side == sides - 1 - stage)

time: 38.4 us -> 36.7 us (0.956)
  waiting for transfers between devices: 5.59 us -> 3.94 us
    ppermute x4 -> x3, waiting for transfers between devices: 4.05 us -> 2.4 us  [the longest x1 1.65 us: per_device(): gathered = [rows_here, lax.ppermute(rows_here, 'per', swap)]]
    ppermute x4 -> x3, starting transfers between devices: 6.73 us -> 6.59 us  [the longest x2 5.3 us: per_device(): got = lax.ppermute(sent, 'hh', [(i, i ^ bit) for i in range(along)])]
    pallas_call x3 -> x5, Pallas kernels: 2.47 us -> 2.56 us  [the longest x1 1.12 us: prep_other(): pl.pallas_call(prep_other_kernel, out_shape=first_shape, in_specs=[hbm(),...]
  transfers between devices with their start and end apart: 8 -> 7, of which waited for: 3 -> 3; matrix products, arithmetic and copies ran while one was open for 0% -> 0% of each run, Pallas kernels for 30% -> 32%
where the time goes in v5:
time: 36.7 us; the launch traced here: 36.3 us
  Pallas kernels  18.8 us (51%)
  starting transfers between devices  9.62 us (26%)
  waiting for transfers between devices  3.94 us (11%)
  local copies, waits for them, and re-layouts  2.45 us (7%)
  between operations  1.57 us (4%)
    pallas_call x2, Pallas kernels, second_pass(): pl.pallas_call(functools.partial(second_kernel, resume, last, extend, gri...  7.15 us
    ppermute x2, starting transfers between devices, per_device(): got = lax.ppermute(sent, 'hh', [(i, i ^ bit) for i in range(along)])  5.3 us
    pallas_call x2, Pallas kernels, first_pass(): pl.pallas_call(functools.partial(first_kernel, resume, grids, index, near...  5.26 us
    unnamed x8, local copies, waits for them, and re-layouts  2.45 us
    ppermute x2, starting transfers between devices, hand_over(): return lax.ppermute(state, 'per', moves)  2.44 us
    ppermute x1, waiting for transfers between devices, per_device(): gathered = [rows_here, lax.ppermute(rows_here, 'per', swap)]  1.65 us
    ppermute x1, waiting for transfers between devices, per_device(): received = lax.ppermute(other, 'st', swap)  1.53 us
    pallas_call x1, Pallas kernels, per_device(): pl.pallas_call(pack_kernel, out_shape=[shaped(row_shape if near else (gro...  1.52 us
  transfers between devices with their start and end apart: 7, of which 3 were waited for; matrix products, arithmetic and copies ran while one was open for 0% of the time, Pallas kernels for 32%

profile of v5, /device:TPU:0, one launch (start us, length us, event | category | flops | bytes accessed | tf_op | source)
XLA Modules:
  0.0 36.3 jit_solution(4324532465580209385)
XLA Ops:
  0.6 0.5 %collective-permute-start.3 = (bf16[4,256,256]{2,1,0:T(8,128)(2,1)}, bf16[4,256,256]{2,1,0:T(8,128)(2,1)S(1)}, u32[]{:S(2)}, u32[]{:S(2)}) collective-permute-start(bf16[4,256,256]{2,1,0:T(8,128)(2,1)} %own_any.5), channel_id=1, source_target_pairs={{0,1},{1,0},{2,3},{3,2},{4,5},{5,4},{6,7},{7,6},{8,9},{9,8},{10,11... | collective-permute-start | bytes 1572872 | tf_op jit(solution)/shard_map/ppermute | solution.py:470
  1.8 1.5 %pack.1 = (f32[8,384]{1,0:T(8,128)}, f32[8,256]{1,0:T(8,128)}) custom-call(s32[1]{0:T(128)S(6)} %copy.14.count_any, f32[16,384]{1,0:T(8,128)} %bitcast.12, s32[3,128]{1,0:T(4,128)} %bitcast.13, s32[3,128]{1,0:T(4,128)} %bitcast.14, f32[1,256]{1,0:T(1,128)} %bitcast.15, f32[1,256]{1,0:T(1,128)} %bitcast.16, f32[1,256]{1,0:T(1,128)} %bitcast.17), custom_call_target="tpu_custom_call" | custom-call | tf_op jit(solution)/shard_map/pack/pallas_call | solution.py:473
  3.3 3.7 %collective-permute-start = (f32[1,8,384]{2,1,0:T(8,128)}, f32[1,8,384]{2,1,0:T(8,128)S(1)}, u32[]{:S(2)}, u32[]{:S(2)}) collective-permute-start(f32[1,8,384]{2,1,0:T(8,128)} %bitcast.11), channel_id=1, source_target_pairs={{0,8},{4,12},{8,0},{12,4},{1,9},{5,13},{9,1},{13,5},{2,10},{6,14},... | collective-permute-start | bytes 36872 | tf_op jit(solution)/shard_map/ppermute | solution.py:534
  7.0 0.0 copy-start
  7.0 1.0 %copy-done = bf16[4,256,256]{2,1,0:T(8,128)(2,1)S(1)} copy-done((bf16[4,256,256]{2,1,0:T(8,128)(2,1)S(1)}, bf16[4,256,256]{2,1,0:T(8,128)(2,1)}, u32[]{:S(2)}) %copy-start) | copy-done | bytes 524312
  8.0 0.0 copy-start.2
  8.0 0.7 %copy-done.2 = f32[8,384]{1,0:T(8,128)S(1)} copy-done((f32[8,384]{1,0:T(8,128)S(1)}, f32[8,384]{1,0:T(8,128)}, u32[]{:S(2)}) %copy-start.2) | copy-done | bytes 12312
  8.7 0.6 %prep_own.1 = (bf16[8,528,256]{2,1,0:T(8,128)(2,1)S(1)}, f32[8,384]{1,0:T(8,128)S(1)}) custom-call(bf16[4,256,256]{2,1,0:T(8,128)(2,1)S(1)} %copy-done, f32[8,384]{1,0:T(8,128)S(1)} %copy-done.2), custom_call_target="tpu_custom_call" | custom-call | tf_op jit(solution)/shard_map/prep_own/pallas_call | solution.py:496
  9.4 0.0 collective-permute-done.got_ref
  9.4 1.6 %collective-permute-start.1 = (f32[2,8,384]{2,1,0:T(8,128)S(1)}, f32[2,8,384]{2,1,0:T(8,128)S(1)}, u32[]{:S(2)}, u32[]{:S(2)}) collective-permute-start(f32[2,8,384]{2,1,0:T(8,128)S(1)} %join.2.after_any.mine_ref), channel_id=1, source_target_pairs={{0,4},{4,0},{8,12},{12,8},{1,5},{5,1},{9,13},{13,9},{2,6},{6,2},{1... | collective-permute-start | bytes 73736 | tf_op jit(solution)/shard_map/ppermute | solution.py:534
  11.0 0.0 copy-start.3
  11.0 0.7 %copy-done.3 = f32[8,256]{1,0:T(8,128)S(1)} copy-done((f32[8,256]{1,0:T(8,128)S(1)}, f32[8,256]{1,0:T(8,128)}, u32[]{:S(2)}) %copy-start.3) | copy-done | bytes 8216
  11.7 0.8 %prep_rest.1 = (bf16[8,528,256]{2,1,0:T(8,128)(2,1)S(1)}, f32[4,256,128]{2,1,0:T(8,128)S(1)}) custom-call(bf16[4,256,256]{2,1,0:T(8,128)(2,1)S(1)} %copy-done, f32[8,256]{1,0:T(8,128)S(1)} %copy-done.3, f32[2,8,384]{2,1,0:T(8,128)S(1)} %join.2.after_any.mine_ref, bf16[8,528,256]{2,1,0:T(8,128)(2,1)S(1)} %get-tuple-element.25.mat_in), custom_call_target="tpu_custom_call", output_to_operand_aliasing={{0}: (3, {})} | custom-call | tf_op jit(solution)/shard_map/prep_rest/pallas_call | solution.py:507
  12.5 0.7 %collective-permute-done.1.got_ref = f32[2,8,384]{2,1,0:T(8,128)S(1)} collective-permute-done((f32[2,8,384]{2,1,0:T(8,128)S(1)}, f32[2,8,384]{2,1,0:T(8,128)S(1)}, u32[]{:S(2)}, u32[]{:S(2)}) %collective-permute-start.1) | collective-permute-done | bytes 24608 | tf_op jit(solution)/shard_map/ppermute | solution.py:534
  13.3 1.3 %collective-permute-start.2 = (f32[4,8,384]{2,1,0:T(8,128)S(1)}, f32[4,8,384]{2,1,0:T(8,128)S(1)}, u32[]{:S(2)}, u32[]{:S(2)}) collective-permute-start(f32[4,8,384]{2,1,0:T(8,128)S(1)} %join.3.after_any.refs_0_), channel_id=1, source_target_pairs={{0,2},{2,0},{1,3},{3,1},{4,6},{6,4},{5,7},{7,5},{8,10},{10,8},{9,1... | collective-permute-start | bytes 147464 | tf_op jit(solution)/shard_map/ppermute | solution.py:550
  14.6 0.0 collective-permute-done.3.other_any
  14.6 1.1 %prep_other.1.refs_2_ = bf16[8,528,256]{2,1,0:T(8,128)(2,1)S(1)} custom-call(bf16[4,256,256]{2,1,0:T(8,128)(2,1)S(1)} %collective-permute-done.3.other_any, f32[4,8,384]{2,1,0:T(8,128)S(1)} %join.3.after_any.refs_0_, bf16[8,528,256]{2,1,0:T(8,128)(2,1)S(1)} %get-tuple-element.27.mat_in), custom_call_target="tpu_custom_call", output_to_operand_aliasing={{}: (2, {})} | custom-call | tf_op jit(solution)/shard_map/prep_other/pallas_call | solution.py:519
  15.7 0.0 copy-start.1
  15.7 1.7 %collective-permute-done.2.refs_1_ = f32[4,8,384]{2,1,0:T(8,128)S(1)} collective-permute-done((f32[4,8,384]{2,1,0:T(8,128)S(1)}, f32[4,8,384]{2,1,0:T(8,128)S(1)}, u32[]{:S(2)}, u32[]{:S(2)}) %collective-permute-start.2) | collective-permute-done | bytes 49184 | tf_op jit(solution)/shard_map/ppermute | solution.py:550
  17.4 2.6 %first_pass.3 = (bf16[8,256,256]{2,1,0:T(8,128)(2,1)S(1)}, bf16[272,256]{1,0:T(8,128)(2,1)S(1)}, f32[3,16,8,256]{3,2,1,0:T(8,128)S(1)}) custom-call(f32[4,8,384]{2,1,0:T(8,128)S(1)} %join.3.after_any.refs_0_, f32[4,8,384]{2,1,0:T(8,128)S(1)} %collective-permute-done.2.refs_1_, bf16[8,528,256]{2,1,0:T(8,128)(2,1)S(1)} %prep_other.1.refs_2_, ...), custom_call_target="tpu_custom_call" | custom-call | tf_op jit(solution)/shard_map/first_pass/pallas_call | solution.py:589
  20.0 1.6 %collective-permute-start.5 = (bf16[272,256]{1,0:T(8,128)(2,1)S(1)}, bf16[272,256]{1,0:T(8,128)(2,1)S(1)}, u32[]{:S(2)}, u32[]{:S(2)}) collective-permute-start(bf16[272,256]{1,0:T(8,128)(2,1)S(1)} %get-tuple-element.34.refs_4_), channel_id=1, source_target_pairs={{0,2},{2,0},{1,3},{3,1},{4,6},{6,4},{5,7},{7,5},{8,10},{10,8},{9,1... | collective-permute-start | bytes 417800 | tf_op jit(solution)/shard_map/ppermute | solution.py:637
  21.7 2.6 %first_pass.2 = (bf16[8,256,256]{2,1,0:T(8,128)(2,1)S(1)}, bf16[272,256]{1,0:T(8,128)(2,1)S(1)}, f32[3,16,8,256]{3,2,1,0:T(8,128)S(1)}) custom-call(f32[4,8,384]{2,1,0:T(8,128)S(1)} %join.3.after_any.refs_0_, f32[4,8,384]{2,1,0:T(8,128)S(1)} %collective-permute-done.2.refs_1_, bf16[8,528,256]{2,1,0:T(8,128)(2,1)S(1)} %prep_other.1.refs_2_, ...), custom_call_target="tpu_custom_call" | custom-call | tf_op jit(solution)/shard_map/first_pass/pallas_call | solution.py:589
  24.3 0.8 %collective-permute-start.4 = (bf16[272,256]{1,0:T(8,128)(2,1)S(1)}, bf16[272,256]{1,0:T(8,128)(2,1)S(1)}, u32[]{:S(2)}, u32[]{:S(2)}) collective-permute-start(bf16[272,256]{1,0:T(8,128)(2,1)S(1)} %get-tuple-element.29.after_any.refs_4_), channel_id=1, source_target_pairs={{0,2},{2,0},{1,3},{3,1},{4,6},{6,4},{5,7},{7,5},{8,10},{10,8},{9,1... | collective-permute-start | bytes 417800 | tf_op jit(solution)/shard_map/ppermute | solution.py:637
  25.1 0.0 copy-done.1
  25.1 1.5 %prep_second.1 = (bf16[8,512,256]{2,1,0:T(8,128)(2,1)S(1)}, f32[8,64,256]{2,1,0:T(8,128)S(1)}) custom-call(bf16[4,256,256]{2,1,0:T(8,128)(2,1)S(1)} %copy-done.1, bf16[4,256,256]{2,1,0:T(8,128)(2,1)S(1)} %collective-permute-done.3.other_any, bf16[272,256]{1,0:T(8,128)(2,1)S(1)} %get-tuple-element.29.after_any.refs_4_), custom_call_target="tpu_custom_call" | custom-call | tf_op jit(solution)/shard_map/prep_second/pallas_call | solution.py:557
  26.6 0.0 collective-permute-done.5.refs_5_
  26.6 3.3 %second_pass.2 = (f32[8,64,256]{2,1,0:T(8,128)S(1)}, f32[8,128]{1,0:T(8,128)S(1)}) custom-call(f32[3,16,8,256]{3,2,1,0:T(8,128)S(1)} %get-tuple-element.32.refs_0_, bf16[8,512,256]{2,1,0:T(8,128)(2,1)S(1)} %get-tuple-element.30.refs_1_, f32[4,256,128]{2,1,0:T(8,128)S(1)} %get-tuple-element.26.after_any.refs_3_.refs_2_, ...), custom_call_target="tpu_custom_call" | custom-call | tf_op jit(solution)/shard_map/second_pass/pallas_call | solution.py:618
  29.9 0.0 collective-permute-done.4.refs_5_
  30.0 3.8 %second_pass.3 = (f32[520,128]{1,0:T(8,128)S(1)}, f32[520,128]{1,0:T(8,128)S(1)}) custom-call(f32[3,16,8,256]{3,2,1,0:T(8,128)S(1)} %get-tuple-element.28.refs_0_, bf16[8,512,256]{2,1,0:T(8,128)(2,1)S(1)} %get-tuple-element.30.refs_1_, f32[4,256,128]{2,1,0:T(8,128)S(1)} %get-tuple-element.26.after_any.refs_3_.refs_2_, ...), custom_call_target="tpu_custom_call" | custom-call | tf_op jit(solution)/shard_map/second_pass/pallas_call | solution.py:618
  33.8 0.1 collective-permute-start.6
  33.9 1.5 %collective-permute-done.6.other_ref = f32[520,128]{1,0:T(8,128)S(1)} collective-permute-done((f32[520,128]{1,0:T(8,128)S(1)}, f32[520,128]{1,0:T(8,128)S(1)}, u32[]{:S(2)}, u32[]{:S(2)}) %collective-permute-start.6) | collective-permute-done | bytes 266272 | tf_op jit(solution)/shard_map/ppermute | solution.py:675
  35.4 0.8 %finish.1 = (f32[512,128]{1,0:T(8,128)}, f32[1]{0:T(128)}) custom-call(f32[520,128]{1,0:T(8,128)S(1)} %get-tuple-element.38.mine_ref, f32[520,128]{1,0:T(8,128)S(1)} %collective-permute-done.6.other_ref), custom_call_target="tpu_custom_call" | custom-call | tf_op jit(solution)/shard_map/finish/pallas_call | solution.py:676
  (2 shorter events, 0.0 us)
Async XLA Ops:
  0.6 14.0 %collective-permute-start.3 = (bf16[4,256,256]{2,1,0:T(8,128)(2,1)}, bf16[4,256,256]{2,1,0:T(8,128)(2,1)S(1)}, u32[]{:S(2)}, u32[]{:S(2)}) collective-permute-start(bf16[4,256,256]{2,1,0:T(8,128)(2,1)} %own_any.5), channel_id=1, source_target_pairs={{0,1},{1,0},{2,3},{3,2},{4,5},{5,4},{6,7},{7,6},{8,9},{9,8},{10,11... | collective-permute-start | bytes 1572872 | tf_op jit(solution)/shard_map/ppermute | solution.py:470
  3.3 6.0 %collective-permute-start = (f32[1,8,384]{2,1,0:T(8,128)}, f32[1,8,384]{2,1,0:T(8,128)S(1)}, u32[]{:S(2)}, u32[]{:S(2)}) collective-permute-start(f32[1,8,384]{2,1,0:T(8,128)} %bitcast.11), channel_id=1, source_target_pairs={{0,8},{4,12},{8,0},{12,4},{1,9},{5,13},{9,1},{13,5},{2,10},{6,14},... | collective-permute-start | bytes 36872 | tf_op jit(solution)/shard_map/ppermute | solution.py:534
  7.0 1.0 %copy-start = (bf16[4,256,256]{2,1,0:T(8,128)(2,1)S(1)}, bf16[4,256,256]{2,1,0:T(8,128)(2,1)}, u32[]{:S(2)}) copy-start(bf16[4,256,256]{2,1,0:T(8,128)(2,1)} %own_any.5) | copy-start | bytes 1572868
  8.0 0.7 %copy-start.2 = (f32[8,384]{1,0:T(8,128)S(1)}, f32[8,384]{1,0:T(8,128)}, u32[]{:S(2)}) copy-start(f32[8,384]{1,0:T(8,128)} %get-tuple-element.22.packed_any) | copy-start | bytes 36868
  9.4 3.9 %collective-permute-start.1 = (f32[2,8,384]{2,1,0:T(8,128)S(1)}, f32[2,8,384]{2,1,0:T(8,128)S(1)}, u32[]{:S(2)}, u32[]{:S(2)}) collective-permute-start(f32[2,8,384]{2,1,0:T(8,128)S(1)} %join.2.after_any.mine_ref), channel_id=1, source_target_pairs={{0,4},{4,0},{8,12},{12,8},{1,5},{5,1},{9,13},{13,9},{2,6},{6,2},{1... | collective-permute-start | bytes 73736 | tf_op jit(solution)/shard_map/ppermute | solution.py:534
  11.0 0.7 %copy-start.3 = (f32[8,256]{1,0:T(8,128)S(1)}, f32[8,256]{1,0:T(8,128)}, u32[]{:S(2)}) copy-start(f32[8,256]{1,0:T(8,128)} %get-tuple-element.24.vec_any) | copy-start | bytes 24580
  13.3 4.1 %collective-permute-start.2 = (f32[4,8,384]{2,1,0:T(8,128)S(1)}, f32[4,8,384]{2,1,0:T(8,128)S(1)}, u32[]{:S(2)}, u32[]{:S(2)}) collective-permute-start(f32[4,8,384]{2,1,0:T(8,128)S(1)} %join.3.after_any.refs_0_), channel_id=1, source_target_pairs={{0,2},{2,0},{1,3},{3,1},{4,6},{6,4},{5,7},{7,5},{8,10},{10,8},{9,1... | collective-permute-start | bytes 147464 | tf_op jit(solution)/shard_map/ppermute | solution.py:550
  15.7 9.4 %copy-start.1 = (bf16[4,256,256]{2,1,0:T(8,128)(2,1)S(1)}, bf16[4,256,256]{2,1,0:T(8,128)(2,1)}, u32[]{:S(2)}) copy-start(bf16[4,256,256]{2,1,0:T(8,128)(2,1)} %own_any.5) | copy-start | bytes 1572868
  20.0 6.6 %collective-permute-start.5 = (bf16[272,256]{1,0:T(8,128)(2,1)S(1)}, bf16[272,256]{1,0:T(8,128)(2,1)S(1)}, u32[]{:S(2)}, u32[]{:S(2)}) collective-permute-start(bf16[272,256]{1,0:T(8,128)(2,1)S(1)} %get-tuple-element.34.refs_4_), channel_id=1, source_target_pairs={{0,2},{2,0},{1,3},{3,1},{4,6},{6,4},{5,7},{7,5},{8,10},{10,8},{9,1... | collective-permute-start | bytes 417800 | tf_op jit(solution)/shard_map/ppermute | solution.py:637
  24.3 5.6 %collective-permute-start.4 = (bf16[272,256]{1,0:T(8,128)(2,1)S(1)}, bf16[272,256]{1,0:T(8,128)(2,1)S(1)}, u32[]{:S(2)}, u32[]{:S(2)}) collective-permute-start(bf16[272,256]{1,0:T(8,128)(2,1)S(1)} %get-tuple-element.29.after_any.refs_4_), channel_id=1, source_target_pairs={{0,2},{2,0},{1,3},{3,1},{4,6},{6,4},{5,7},{7,5},{8,10},{10,8},{9,1... | collective-permute-start | bytes 417800 | tf_op jit(solution)/shard_map/ppermute | solution.py:637
  33.8 1.6 %collective-permute-start.6 = (f32[520,128]{1,0:T(8,128)S(1)}, f32[520,128]{1,0:T(8,128)S(1)}, u32[]{:S(2)}, u32[]{:S(2)}) collective-permute-start(f32[520,128]{1,0:T(8,128)S(1)} %get-tuple-element.39), channel_id=1, source_target_pairs={{0,1},{1,0},{2,3},{3,2},{4,5},{5,4},{6,7},{7,6},{8,9},{9,8},{10,11... | collective-permute-start | bytes 798728 | tf_op jit(solution)/shard_map/ppermute | solution.py:675

commit v6 on v5

--- a/solution.py
+++ b/solution.py
@@ -79,11 +79,8 @@
         early, late = value[: periods // 2], value[periods // 2 :]
         turned = pltpu.roll(jnp.where(core == 0, late, early), HALF, 1)
         packed = jnp.where(low_lane, jnp.where(core == 0, early, turned), jnp.where(core == 0, turned, late))
-        if len(out_ref.shape) == 2:
-            out_ref[:, cols] = packed
-        else:
-            for to in range(out_ref.shape[0]):
-                out_ref[to, :, cols] = packed
+        for to in range(out_ref.shape[0]):
+            out_ref[to, :, cols] = packed
     raised = jnp.exp(init_ref[...])
     start = raised / jnp.sum(raised, axis=1, keepdims=True)
     row = lax.broadcasted_iota(jnp.int32, vec_ref.shape, 0)
@@ -93,13 +90,6 @@
     )
 
 
-def join_kernel(bit, mine_ref, got_ref, after_any, out_ref):
-    count = mine_ref.shape[0]
-    upper = (lax.axis_index("hh") // bit) % 2
-    out_ref[pl.ds(upper * count, count)] = mine_ref[...]
-    out_ref[pl.ds((1 - upper) * count, count)] = got_ref[...]
-
-
 def put(ref, at, value):
     states = value.shape[0]
     high = value.astype(BF16)
@@ -107,10 +97,10 @@
     ref[at, states : 2 * states, :] = (value - high.astype(F32)).astype(BF16)
 
 
-def fill_periods(mat, row_probs, scratch, turned_pass, source, ref, periods, part):
-    @pl.loop(periods[0], periods[1])
+def fill_periods(mat, row_probs, scratch, turned_pass, source, ref):
+    @pl.loop(0, ref.shape[0])
     def _(i):
-        at = source * part + i
+        at = source * ref.shape[0] + i
         lifted = jnp.exp(ref[i].astype(F32))
         probs = lifted * (1.0 / jnp.sum(lifted, axis=1, keepdims=True))
         if row_probs is not None:
@@ -127,14 +117,9 @@
             put(mat, at, probs)
 
 
-def prep_own_kernel(periods, own_any, packed_any, mat, packed, own_ref, sems):
-    fetch(((own_any, own_ref), (packed_any, packed)), sems)
-    fill_periods(mat, None, None, is_forward_first(), core_index(), own_ref, periods, own_ref.shape[0])
-
-
-def prep_rest_kernel(periods, own_any, vec_any, after_any, mat_in, mat, consts, own_ref, vec_ref, sems):
-    fetch(((own_any, own_ref), (vec_any, vec_ref)), sems)
-    states = own_ref.shape[1]
+def prep_first_kernel(own_any, other_any, vec_any, after_any, mat, consts, own_ref, other_ref, vec_ref, sems):
+    fetch(((own_any, own_ref), (other_any, other_ref), (vec_any, vec_ref)), sems)
+    part, states, _ = own_ref.shape
     for i in range(4):
         consts[i] = jnp.broadcast_to(vec_ref[i : i + 1, :], (LANES, states)).T
     start = vec_ref[:1, :]
@@ -143,20 +128,14 @@
     start_rows = jnp.where(row == 0, start_high, jnp.where(row == 1, start - start_high, 0.0)).astype(BF16)
     for k in range(mat.shape[0]):
         mat[k, 2 * states :, :] = start_rows
-    fill_periods(mat, None, None, is_forward_first(), core_index(), own_ref, periods, own_ref.shape[0])
-
-
-def prep_other_kernel(other_any, after_any, mat_in, mat, other_ref, sems):
-    fetch(((other_any, other_ref),), sems)
-    part = other_ref.shape[0]
-    fill_periods(mat, None, None, is_forward_first(), 1 - core_index(), other_ref, (0, part), part)
+    for source, ref in ((core_index(), own_ref), (1 - core_index(), other_ref)):
+        fill_periods(mat, None, None, is_forward_first(), source, ref)
 
 
 def prep_second_kernel(own_any, other_any, after_any, mat, row_probs, scratch, own_ref, other_ref, sems):
     fetch(((own_any, own_ref), (other_any, other_ref)), sems)
-    turned_pass, part = jnp.logical_not(is_forward_first()), own_ref.shape[0]
     for source, ref in ((core_index(), own_ref), (1 - core_index(), other_ref)):
-        fill_periods(mat, row_probs, scratch, turned_pass, source, ref, (0, part), part)
+        fill_periods(mat, row_probs, scratch, jnp.logical_not(is_forward_first()), source, ref)
 
 
 def emission(sel_ref, consts, step_now, cols):
@@ -275,11 +254,7 @@
     return [column_sum(state_ref[states:, cols].astype(F32)) for cols in tiles(state_ref.shape[1])]
 
 
-def first_kernel(resume, grids, part, near, *refs):
-    refs = list(refs)
-    rows_ref = refs.pop(0)
-    rows_other = refs.pop(0) if near else None
-    mat, consts = refs.pop(0), refs.pop(0)
+def first_kernel(resume, grids, part, rows_ref, mat, consts, *refs):
     state_in = refs[0] if resume else None
     hist, state_out, sel_ref, ab_ref, back_ref = refs[-5:]
     chunk = part * grids + (pl.program_id(0) if grids > 1 else 0)
@@ -293,19 +268,15 @@
         rank, picked = carry
         for slot in range(slot_rows // HB):
             cols = slice(slot * HB, (slot + 1) * HB)
-            if near:
-                here = lax.axis_index("per") == d // group
-                block = jnp.where(here, rows_ref[d % group, :, cols], rows_other[d % group, :, cols])
-            else:
-                block = rows_ref[d, :, cols]
+            block = rows_ref[d, :, cols]
             live = block > -0.5 * SEEN
             picked = [jnp.where(live & (rank == chunk * tops + i), block, old) for i, old in enumerate(picked)]
             rank = rank + live.astype(jnp.int32)
         return rank, picked
 
     carry = (jnp.zeros((half_periods, HB), jnp.int32), [jnp.zeros((half_periods, HB), F32)] * tops)
-    if near:
-        for d in range(2 * group):
+    if group <= 8:
+        for d in range(group):
             carry = scan_source(d, carry)
     else:
         carry = lax.fori_loop(0, group, scan_source, carry)
@@ -463,16 +434,12 @@
     shaped = jax.ShapeDtypeStruct
     dma = pltpu.SemaphoreType.DMA
 
-    along = lax.axis_size("hh")
-    near = sides == 2 and along <= 8 and along & (along - 1) == 0
-
     swap = [(0, 1), (1, 0)]
     other_logits = lax.ppermute(trans_logits, "st", swap)
-    row_shape = (periods // 2, slot_rows)
     vec_row = pltpu.VMEM((1, states), F32)
     packed, vectors = pl.pallas_call(
         pack_kernel,
-        out_shape=[shaped(row_shape if near else (group,) + row_shape, F32), shaped((8, states), F32)],
+        out_shape=[shaped((group, periods // 2, slot_rows), F32), shaped((8, states), F32)],
         in_specs=[hbm()] * 7,
         out_specs=[vmem()] * 2,
         scratch_shapes=[
@@ -490,68 +457,17 @@
         block_count, earnings.T, starts.reshape(-1, HB), lengths.reshape(-1, HB),
         init_logits.reshape(1, states), state_mean.reshape(1, states), log_sd.reshape(1, states),
     )
-    first_shape = shaped((steps, 2 * states + EXTRA, states), BF16)
+    gathered = lax.all_to_all(packed, ("hh", "per"), split_axis=0, concat_axis=0, tiled=True)
     half_logits = pltpu.VMEM(trans_logits.shape, BF16)
-    early = (part + 1) // 2
-    first_mat, kept_rows = pl.pallas_call(
-        functools.partial(prep_own_kernel, (0, early)),
-        out_shape=[first_shape, shaped(packed.shape, F32)],
-        in_specs=[hbm()] * 2,
+    first_mat, consts = pl.pallas_call(
+        prep_first_kernel,
+        out_shape=[shaped((steps, 2 * states + EXTRA, states), BF16), shaped((4, states, LANES), F32)],
+        in_specs=[hbm()] * 4,
         out_specs=[vmem()] * 2,
-        scratch_shapes=[half_logits, dma((2,))],
+        scratch_shapes=[half_logits, half_logits, pltpu.VMEM((8, states), F32), dma((3,))],
         compiler_params=params(4),
-        name="prep_own",
-    )(trans_logits, packed)
-
-    def prep_rest(mat, after):
-        return pl.pallas_call(
-            functools.partial(prep_rest_kernel, (early, part)),
-            out_shape=[first_shape, shaped((4, states, LANES), F32)],
-            in_specs=[hbm(), hbm(), hbm(), vmem()],
-            out_specs=[vmem()] * 2,
-            scratch_shapes=[half_logits, pltpu.VMEM((8, states), F32), dma((2,))],
-            input_output_aliases={3: 0},
-            compiler_params=params(4),
-            name="prep_rest",
-        )(trans_logits, vectors, after, mat)
-
-    def prep_other(mat, after):
-        return pl.pallas_call(
-            prep_other_kernel,
-            out_shape=first_shape,
-            in_specs=[hbm(), hbm(), vmem()],
-            out_specs=vmem(),
-            scratch_shapes=[half_logits, dma((1,))],
-            input_output_aliases={2: 0},
-            compiler_params=params(4),
-            name="prep_other",
-        )(other_logits, after, mat)
-
-    if near:
-        rows_here, sent, consts = kept_rows[None], packed[None], None
-        bit = along // 2
-        while bit:
-            got = lax.ppermute(sent, "hh", [(i, i ^ bit) for i in range(along)])
-            if bit < along // 2 and consts is None:
-                first_mat, consts = prep_rest(first_mat, rows_here)
-            after = rows_here if consts is None else consts
-            rows_here = pl.pallas_call(
-                functools.partial(join_kernel, bit),
-                out_shape=shaped((2 * rows_here.shape[0],) + row_shape, F32),
-                in_specs=[vmem(), vmem(), hbm()],
-                out_specs=vmem(),
-                compiler_params=params(2),
-                name="join",
-            )(rows_here, got, after)
-            sent = rows_here
-            bit //= 2
-        if consts is None:
-            first_mat, consts = prep_rest(first_mat, rows_here)
-        gathered = [rows_here, lax.ppermute(rows_here, "per", swap)]
-    else:
-        gathered = [lax.all_to_all(packed, ("hh", "per"), split_axis=0, concat_axis=0, tiled=True)]
-        first_mat, consts = prep_rest(first_mat, gathered[0])
-    first_mat = prep_other(first_mat, gathered[0])
+        name="prep_first",
+    )(trans_logits, other_logits, vectors, packed)
 
     def prep_second(after):
         return pl.pallas_call(
@@ -587,16 +503,16 @@
     def first_pass(index, state_in):
         resume = state_in is not None
         return pl.pallas_call(
-            functools.partial(first_kernel, resume, grids, index, near),
+            functools.partial(first_kernel, resume, grids, index),
             grid=grid,
             out_shape=[hist_shape, state_shape, sel_shape],
-            in_specs=[whole(*x.shape) for x in gathered + [first_mat]] + [const_spec]
+            in_specs=[whole(*gathered.shape), whole(*first_mat.shape), const_spec]
             + [state_spec] * resume,
             out_specs=[hist_spec, state_spec, sel_spec],
             scratch_shapes=[pltpu.VMEM((states, width), BF16), pltpu.VMEM((states, width), F32)],
             compiler_params=params(8 if grids == 1 else 32),
             name="first_pass",
-        )(*gathered, first_mat, consts, *([state_in] if resume else []))
+        )(gathered, first_mat, consts, *([state_in] if resume else []))
 
     def second_pass(kept, state_in, sums_in, last, extend):
         hist, own_state, sel = kept
@@ -647,7 +563,7 @@
     else:
         kept = [jnp.zeros(x.shape, x.dtype) for x in (hist_shape, state_shape, sel_shape)]
         done = [jnp.zeros(x.shape, x.dtype) for x in (swap_shape, swap_shape, state_shape)]
-        second_mat, row_probs = prep_second(gathered[0])
+        second_mat, row_probs = prep_second(gathered)
         state = None
         for stage in range(sides):
             active = (side == stage) | (side == sides - 1 - stage)

time: 36.7 us -> 36.7 us (level)
    all_to_all x0 -> x1, starting transfers between devices: none -> 6.82 us  [per_device(): lax.all_to_all(packed, ('hh', 'per'), split_axis=0, concat_axis=0, tiled=...]
    ppermute x3 -> x0, starting transfers between devices: 6.59 us -> none  [the longest x2 5.3 us: per_device(): got = lax.ppermute(sent, 'hh', [(i, i ^ bit) for i in range(along)])]
    ppermute x3 -> x0, waiting for transfers between devices: 2.4 us -> none  [the longest x1 1.65 us: per_device(): gathered = [rows_here, lax.ppermute(rows_here, 'per', swap)]]
    all_to_all x0 -> x1, waiting for transfers between devices: none -> 2.06 us  [per_device(): lax.all_to_all(packed, ('hh', 'per'), split_axis=0, concat_axis=0, tiled=...]
    pallas_call x8 -> x4, Pallas kernels: 9.34 us -> 9.19 us  [the longest x2 5.18 us: first_pass(): pl.pallas_call(functools.partial(first_kernel, resume, grids, index), gri...]
  transfers between devices with their start and end apart: 7 -> 5, of which waited for: 3 -> 2; matrix products, arithmetic and copies ran while one was open for 0% -> 0% of each run, Pallas kernels for 32% -> 31%
where the time goes in v6:
time: 36.7 us; the launch traced here: 36.3 us
  Pallas kernels  18.6 us (51%)
  starting transfers between devices  9.88 us (27%)
  waiting for transfers between devices  3.6 us (10%)
  local copies, waits for them, and re-layouts  2.63 us (7%)
  between operations  1.54 us (4%)
    pallas_call x2, Pallas kernels, second_pass(): pl.pallas_call(functools.partial(second_kernel, resume, last, extend, gri...  7.16 us
    all_to_all x1, starting transfers between devices, per_device(): lax.all_to_all(packed, ('hh', 'per'), split_axis=0, concat_axis=0, tiled=...  6.82 us
    pallas_call x2, Pallas kernels, first_pass(): pl.pallas_call(functools.partial(first_kernel, resume, grids, index), gri...  5.18 us
    unnamed x8, local copies, waits for them, and re-layouts  2.63 us
    ppermute x2, starting transfers between devices, hand_over(): return lax.ppermute(state, 'per', moves)  2.47 us
    pallas_call x1, Pallas kernels, per_device(): pl.pallas_call(prep_first_kernel, out_shape=[shaped((steps, 2 * states +...  2.45 us
    all_to_all x1, waiting for transfers between devices, per_device(): lax.all_to_all(packed, ('hh', 'per'), split_axis=0, concat_axis=0, tiled=...  2.06 us
    pallas_call x1, Pallas kernels, per_device(): pl.pallas_call(pack_kernel, out_shape=[shaped((group, periods // 2, slot_...  1.56 us
  transfers between devices with their start and end apart: 5, of which 2 were waited for; matrix products, arithmetic and copies ran while one was open for 0% of the time, Pallas kernels for 31%

profile of v6, /device:TPU:0, one launch (start us, length us, event | category | flops | bytes accessed | tf_op | source)
XLA Modules:
  0.0 36.3 jit_solution(8309193019394195546)
XLA Ops:
  0.6 0.5 %collective-permute-start = (bf16[4,256,256]{2,1,0:T(8,128)(2,1)}, bf16[4,256,256]{2,1,0:T(8,128)(2,1)S(1)}, u32[]{:S(2)}, u32[]{:S(2)}) collective-permute-start(bf16[4,256,256]{2,1,0:T(8,128)(2,1)} %own_any.3), channel_id=1, source_target_pairs={{0,1},{1,0},{2,3},{3,2},{4,5},{5,4},{6,7},{7,6},{8,9},{9,8},{10,11... | collective-permute-start | bytes 1572872 | tf_op jit(solution)/shard_map/ppermute | solution.py:438
  1.8 1.6 %pack.1 = (f32[8,8,384]{2,1,0:T(8,128)}, f32[8,256]{1,0:T(8,128)}) custom-call(s32[1]{0:T(128)S(6)} %copy.10.count_any, f32[16,384]{1,0:T(8,128)} %bitcast.7, s32[3,128]{1,0:T(4,128)} %bitcast.8, s32[3,128]{1,0:T(4,128)} %bitcast.9, f32[1,256]{1,0:T(1,128)} %bitcast.10, f32[1,256]{1,0:T(1,128)} %bitcast.11, f32[1,256]{1,0:T(1,128)} %bitcast.12), custom_call_target="tpu_custom_call" | custom-call | tf_op jit(solution)/shard_map/pack/pallas_call | solution.py:440
  3.4 6.8 %all-to-all-start = ((f32[8,8,384]{2,1,0:T(8,128)}), f32[8,8,384]{2,1,0:T(8,128)S(1)}, u32[]{:S(2)}, u32[]{:S(2)}) async-start(f32[8,8,384]{2,1,0:T(8,128)} %get-tuple-element.20.after_any), calls=%async_computation | async-start | bytes 196608 | tf_op jit(solution)/shard_map/all_to_all | solution.py:460
  10.2 0.0 collective-permute-done.other_any
  10.2 0.0 copy-start
  10.2 1.0 %copy-done = bf16[4,256,256]{2,1,0:T(8,128)(2,1)S(1)} copy-done((bf16[4,256,256]{2,1,0:T(8,128)(2,1)S(1)}, bf16[4,256,256]{2,1,0:T(8,128)(2,1)}, u32[]{:S(2)}) %copy-start) | copy-done | bytes 524312
  11.2 0.0 copy-start.2
  11.2 0.9 %copy-done.2 = f32[8,8,384]{2,1,0:T(8,128)S(1)} copy-done((f32[8,8,384]{2,1,0:T(8,128)S(1)}, f32[8,8,384]{2,1,0:T(8,128)}, u32[]{:S(2)}) %copy-start.2) | copy-done | bytes 98328
  12.1 0.0 copy-start.3
  12.1 0.7 %copy-done.3 = f32[8,256]{1,0:T(8,128)S(1)} copy-done((f32[8,256]{1,0:T(8,128)S(1)}, f32[8,256]{1,0:T(8,128)}, u32[]{:S(2)}) %copy-start.3) | copy-done | bytes 8216
  12.8 2.5 %prep_first.1 = (bf16[8,528,256]{2,1,0:T(8,128)(2,1)S(1)}, f32[4,256,128]{2,1,0:T(8,128)S(1)}) custom-call(bf16[4,256,256]{2,1,0:T(8,128)(2,1)S(1)} %copy-done, bf16[4,256,256]{2,1,0:T(8,128)(2,1)S(1)} %collective-permute-done.other_any, f32[8,256]{1,0:T(8,128)S(1)} %copy-done.3, f32[8,8,384]{2,1,0:T(8,128)S(1)} %copy-done.2), custom_call_target="tpu_custom_call" | custom-call | tf_op jit(solution)/shard_map/prep_first/pallas_call | solution.py:462
  15.3 2.1 %all-to-all-done.rows_ref = f32[8,8,384]{2,1,0:T(8,128)S(1)} async-done(((f32[8,8,384]{2,1,0:T(8,128)}), f32[8,8,384]{2,1,0:T(8,128)S(1)}, u32[]{:S(2)}, u32[]{:S(2)}) %all-to-all-start) | async-done | bytes 98336 | tf_op jit(solution)/shard_map/all_to_all | solution.py:460
  17.4 0.0 copy-start.1
  17.4 2.6 %first_pass.3 = (bf16[8,256,256]{2,1,0:T(8,128)(2,1)S(1)}, bf16[272,256]{1,0:T(8,128)(2,1)S(1)}, f32[3,16,8,256]{3,2,1,0:T(8,128)S(1)}) custom-call(f32[8,8,384]{2,1,0:T(8,128)S(1)} %all-to-all-done.rows_ref, bf16[8,528,256]{2,1,0:T(8,128)(2,1)S(1)} %get-tuple-element.22.mat, f32[4,256,128]{2,1,0:T(8,128)S(1)} %get-tuple-element.23.consts.refs_2_), custom_call_target="tpu_custom_call" | custom-call | tf_op jit(solution)/shard_map/first_pass/pallas_call | solution.py:505
  20.0 0.7 %collective-permute-start.2 = (bf16[272,256]{1,0:T(8,128)(2,1)S(1)}, bf16[272,256]{1,0:T(8,128)(2,1)S(1)}, u32[]{:S(2)}, u32[]{:S(2)}) collective-permute-start(bf16[272,256]{1,0:T(8,128)(2,1)S(1)} %get-tuple-element.30.refs_4_), channel_id=1, source_target_pairs={{0,2},{2,0},{1,3},{3,1},{4,6},{6,4},{5,7},{7,5},{8,10},{10,8},{9,1... | collective-permute-start | bytes 417800 | tf_op jit(solution)/shard_map/ppermute | solution.py:553
  20.6 2.6 %first_pass.2 = (bf16[8,256,256]{2,1,0:T(8,128)(2,1)S(1)}, bf16[272,256]{1,0:T(8,128)(2,1)S(1)}, f32[3,16,8,256]{3,2,1,0:T(8,128)S(1)}) custom-call(f32[8,8,384]{2,1,0:T(8,128)S(1)} %all-to-all-done.rows_ref, bf16[8,528,256]{2,1,0:T(8,128)(2,1)S(1)} %get-tuple-element.22.mat, f32[4,256,128]{2,1,0:T(8,128)S(1)} %get-tuple-element.23.consts.refs_2_), custom_call_target="tpu_custom_call" | custom-call | tf_op jit(solution)/shard_map/first_pass/pallas_call | solution.py:505
  23.2 1.8 %collective-permute-start.1 = (bf16[272,256]{1,0:T(8,128)(2,1)S(1)}, bf16[272,256]{1,0:T(8,128)(2,1)S(1)}, u32[]{:S(2)}, u32[]{:S(2)}) collective-permute-start(bf16[272,256]{1,0:T(8,128)(2,1)S(1)} %get-tuple-element.25.after_any.refs_4_), channel_id=1, source_target_pairs={{0,2},{2,0},{1,3},{3,1},{4,6},{6,4},{5,7},{7,5},{8,10},{10,8},{9,1... | collective-permute-start | bytes 417800 | tf_op jit(solution)/shard_map/ppermute | solution.py:553
  25.0 0.0 copy-done.1
  25.0 1.5 %prep_second.1 = (bf16[8,512,256]{2,1,0:T(8,128)(2,1)S(1)}, f32[8,64,256]{2,1,0:T(8,128)S(1)}) custom-call(bf16[4,256,256]{2,1,0:T(8,128)(2,1)S(1)} %copy-done.1, bf16[4,256,256]{2,1,0:T(8,128)(2,1)S(1)} %collective-permute-done.other_any, bf16[272,256]{1,0:T(8,128)(2,1)S(1)} %get-tuple-element.25.after_any.refs_4_), custom_call_target="tpu_custom_call" | custom-call | tf_op jit(solution)/shard_map/prep_second/pallas_call | solution.py:473
  26.5 0.0 collective-permute-done.2.refs_5_
  26.6 3.3 %second_pass.2 = (f32[8,64,256]{2,1,0:T(8,128)S(1)}, f32[8,128]{1,0:T(8,128)S(1)}) custom-call(f32[3,16,8,256]{3,2,1,0:T(8,128)S(1)} %get-tuple-element.28.refs_0_, bf16[8,512,256]{2,1,0:T(8,128)(2,1)S(1)} %get-tuple-element.26.refs_1_, f32[4,256,128]{2,1,0:T(8,128)S(1)} %get-tuple-element.23.consts.refs_2_, ...), custom_call_target="tpu_custom_call" | custom-call | tf_op jit(solution)/shard_map/second_pass/pallas_call | solution.py:534
  29.9 0.0 collective-permute-done.1.refs_5_
  29.9 3.9 %second_pass.3 = (f32[520,128]{1,0:T(8,128)S(1)}, f32[520,128]{1,0:T(8,128)S(1)}) custom-call(f32[3,16,8,256]{3,2,1,0:T(8,128)S(1)} %get-tuple-element.24.refs_0_, bf16[8,512,256]{2,1,0:T(8,128)(2,1)S(1)} %get-tuple-element.26.refs_1_, f32[4,256,128]{2,1,0:T(8,128)S(1)} %get-tuple-element.23.consts.refs_2_, ...), custom_call_target="tpu_custom_call" | custom-call | tf_op jit(solution)/shard_map/second_pass/pallas_call | solution.py:534
  33.7 0.1 collective-permute-start.3
  33.8 1.5 %collective-permute-done.3.other_ref = f32[520,128]{1,0:T(8,128)S(1)} collective-permute-done((f32[520,128]{1,0:T(8,128)S(1)}, f32[520,128]{1,0:T(8,128)S(1)}, u32[]{:S(2)}, u32[]{:S(2)}) %collective-permute-start.3) | collective-permute-done | bytes 266272 | tf_op jit(solution)/shard_map/ppermute | solution.py:591
  35.3 0.8 %finish.1 = (f32[512,128]{1,0:T(8,128)}, f32[1]{0:T(128)}) custom-call(f32[520,128]{1,0:T(8,128)S(1)} %get-tuple-element.34.mine_ref, f32[520,128]{1,0:T(8,128)S(1)} %collective-permute-done.3.other_ref), custom_call_target="tpu_custom_call" | custom-call | tf_op jit(solution)/shard_map/finish/pallas_call | solution.py:592
Async XLA Ops:
  0.6 9.6 %collective-permute-start = (bf16[4,256,256]{2,1,0:T(8,128)(2,1)}, bf16[4,256,256]{2,1,0:T(8,128)(2,1)S(1)}, u32[]{:S(2)}, u32[]{:S(2)}) collective-permute-start(bf16[4,256,256]{2,1,0:T(8,128)(2,1)} %own_any.3), channel_id=1, source_target_pairs={{0,1},{1,0},{2,3},{3,2},{4,5},{5,4},{6,7},{7,6},{8,9},{9,8},{10,11... | collective-permute-start | bytes 1572872 | tf_op jit(solution)/shard_map/ppermute | solution.py:438
  3.4 14.0 %all-to-all-start = ((f32[8,8,384]{2,1,0:T(8,128)}), f32[8,8,384]{2,1,0:T(8,128)S(1)}, u32[]{:S(2)}, u32[]{:S(2)}) async-start(f32[8,8,384]{2,1,0:T(8,128)} %get-tuple-element.20.after_any), calls=%async_computation | async-start | bytes 196608 | tf_op jit(solution)/shard_map/all_to_all | solution.py:460
  10.2 1.0 %copy-start = (bf16[4,256,256]{2,1,0:T(8,128)(2,1)S(1)}, bf16[4,256,256]{2,1,0:T(8,128)(2,1)}, u32[]{:S(2)}) copy-start(bf16[4,256,256]{2,1,0:T(8,128)(2,1)} %own_any.3) | copy-start | bytes 1572868
  11.2 0.9 %copy-start.2 = (f32[8,8,384]{2,1,0:T(8,128)S(1)}, f32[8,8,384]{2,1,0:T(8,128)}, u32[]{:S(2)}) copy-start(f32[8,8,384]{2,1,0:T(8,128)} %get-tuple-element.20.after_any) | copy-start | bytes 294916
  12.1 0.7 %copy-start.3 = (f32[8,256]{1,0:T(8,128)S(1)}, f32[8,256]{1,0:T(8,128)}, u32[]{:S(2)}) copy-start(f32[8,256]{1,0:T(8,128)} %get-tuple-element.21.vec_any) | copy-start | bytes 24580
  17.4 7.7 %copy-start.1 = (bf16[4,256,256]{2,1,0:T(8,128)(2,1)S(1)}, bf16[4,256,256]{2,1,0:T(8,128)(2,1)}, u32[]{:S(2)}) copy-start(bf16[4,256,256]{2,1,0:T(8,128)(2,1)} %own_any.3) | copy-start | bytes 1572868
  20.0 6.6 %collective-permute-start.2 = (bf16[272,256]{1,0:T(8,128)(2,1)S(1)}, bf16[272,256]{1,0:T(8,128)(2,1)S(1)}, u32[]{:S(2)}, u32[]{:S(2)}) collective-permute-start(bf16[272,256]{1,0:T(8,128)(2,1)S(1)} %get-tuple-element.30.refs_4_), channel_id=1, source_target_pairs={{0,2},{2,0},{1,3},{3,1},{4,6},{6,4},{5,7},{7,5},{8,10},{10,8},{9,1... | collective-permute-start | bytes 417800 | tf_op jit(solution)/shard_map/ppermute | solution.py:553
  23.2 6.6 %collective-permute-start.1 = (bf16[272,256]{1,0:T(8,128)(2,1)S(1)}, bf16[272,256]{1,0:T(8,128)(2,1)S(1)}, u32[]{:S(2)}, u32[]{:S(2)}) collective-permute-start(bf16[272,256]{1,0:T(8,128)(2,1)S(1)} %get-tuple-element.25.after_any.refs_4_), channel_id=1, source_target_pairs={{0,2},{2,0},{1,3},{3,1},{4,6},{6,4},{5,7},{7,5},{8,10},{10,8},{9,1... | collective-permute-start | bytes 417800 | tf_op jit(solution)/shard_map/ppermute | solution.py:553
  33.7 1.6 %collective-permute-start.3 = (f32[520,128]{1,0:T(8,128)S(1)}, f32[520,128]{1,0:T(8,128)S(1)}, u32[]{:S(2)}, u32[]{:S(2)}) collective-permute-start(f32[520,128]{1,0:T(8,128)S(1)} %get-tuple-element.35), channel_id=1, source_target_pairs={{0,1},{1,0},{2,3},{3,2},{4,5},{5,4},{6,7},{7,6},{8,9},{9,8},{10,11... | collective-permute-start | bytes 798728 | tf_op jit(solution)/shard_map/ppermute | solution.py:591

commit v7 on v6

--- a/solution.py
+++ b/solution.py
@@ -16,6 +16,7 @@
 LOG2E = 1.4426950408889634
 LN2 = 0.6931471805599453
 EXTRA = 16
+PACK = 16
 
 
 def vmem():
@@ -93,8 +94,18 @@
 def put(ref, at, value):
     states = value.shape[0]
     high = value.astype(BF16)
-    ref[at, :states, :] = high
-    ref[at, states : 2 * states, :] = (value - high.astype(F32)).astype(BF16)
+    low = (value - high.astype(F32)).astype(BF16)
+    ref[at, : states // PACK, :PACK, :] = high.reshape(states // PACK, PACK, states)
+    ref[at, : states // PACK, PACK:, :] = low.reshape(states // PACK, PACK, states)
+
+
+def both_halves(mat, state):
+    blocks, rows, states = mat.shape
+    product = jnp.dot(mat.reshape(blocks * rows, states), state, preferred_element_type=F32)
+    product = product.reshape(blocks, rows, state.shape[1])
+    main = product[: states // PACK]
+    main = (main[:, :PACK] + main[:, PACK:]).reshape(states, state.shape[1])
+    return main, product[states // PACK :]
 
 
 def fill_periods(mat, row_probs, scratch, turned_pass, source, ref):
@@ -124,10 +135,10 @@
         consts[i] = jnp.broadcast_to(vec_ref[i : i + 1, :], (LANES, states)).T
     start = vec_ref[:1, :]
     start_high = start.astype(BF16).astype(F32)
-    row = lax.broadcasted_iota(jnp.int32, (EXTRA, states), 0)
+    row = lax.broadcasted_iota(jnp.int32, (2 * PACK, states), 0)
     start_rows = jnp.where(row == 0, start_high, jnp.where(row == 1, start - start_high, 0.0)).astype(BF16)
     for k in range(mat.shape[0]):
-        mat[k, 2 * states :, :] = start_rows
+        mat[k, states // PACK] = start_rows
     for source, ref in ((core_index(), own_ref), (1 - core_index(), other_ref)):
         fill_periods(mat, None, None, is_forward_first(), source, ref)
 
@@ -177,8 +188,8 @@
             weights_ref, counts_ref, row_begin = second
             own_alpha = ab_ref[own_rows(row_begin, weights_ref.shape[0]), :].astype(F32)
         for q, cols in enumerate(cuts):
-            product = jnp.dot(mat[k, : 2 * states, :], ab_ref[:, cols], preferred_element_type=F32)
-            moved = (product[:states] + product[states:]) * inverse[q]
+            moved, _ = both_halves(mat[k, : states // PACK], ab_ref[:, cols])
+            moved = moved * inverse[q]
             moving = is_moving(sel_ref, step_now, cols)
             if second is not None:
                 total = column_sum(moved * hist[k, :, cols].astype(F32))
@@ -218,12 +229,12 @@
             weights_ref, counts_ref, row_begin = second
             own_alpha = hist[k, own_rows(row_begin, weights_ref.shape[0]), :].astype(F32)
         for q, cols in enumerate(cuts):
-            product = jnp.dot(mat[k], ub_ref[:, cols], preferred_element_type=F32)
+            pulled, more = both_halves(mat[k], ub_ref[:, cols])
             moving = is_moving(sel_ref, step_now, cols)
-            pulled = (product[:states] + product[states : 2 * states]) * shrink[q]
+            pulled = pulled * shrink[q]
             if second is None:
                 seen = is_seen(sel_ref, step_now, cols)
-                begun = column_sum(product[2 * states :]) * shrink[q]
+                begun = column_sum(more[0]) * shrink[q]
                 rest = jnp.where(seen, begun, back_ref[:, cols])
             else:
                 total = column_sum(pulled * hist[k, :, cols].astype(F32))
@@ -249,15 +260,23 @@
         state_out[states:, cols] = piece.astype(BF16)
 
 
+def put_states(state_outs, values_ref, logs):
+    share = values_ref.shape[1] // len(state_outs)
+    for i, state_out in enumerate(state_outs):
+        tile = i * share // LANES
+        piece = values_ref[:, i * share : (i + 1) * share].astype(BF16)
+        put_state(state_out, piece, logs[tile : tile + share // LANES])
+
+
 def state_logs(state_ref):
     states = state_ref.shape[0] - EXTRA
     return [column_sum(state_ref[states:, cols].astype(F32)) for cols in tiles(state_ref.shape[1])]
 
 
-def first_kernel(resume, grids, part, rows_ref, mat, consts, *refs):
+def first_kernel(resume, grids, rows_ref, mat, consts, *refs):
     state_in = refs[0] if resume else None
-    hist, state_out, sel_ref, ab_ref, back_ref = refs[-5:]
-    chunk = part * grids + (pl.program_id(0) if grids > 1 else 0)
+    hist, sel_ref, *state_outs, ab_ref, back_ref = refs[1:] if resume else refs
+    chunk = pl.program_id(0) if grids > 1 else 0
     steps, states, width = hist.shape
     forward_first, lead = is_forward_first(), lax.axis_index("per") * steps
     cuts = tiles(width)
@@ -311,7 +330,7 @@
                 ab_ref[:, cols] = consts[0].astype(BF16)
         logs = state_logs(state_in) if resume else list(zeros)
         logs = run_forward(lead, mat, hist, sel_ref, consts, ab_ref, logs)
-        put_state(state_out, ab_ref[...], logs)
+        put_states(state_outs, ab_ref, logs)
 
     @pl.when(jnp.logical_not(forward_first))
     def _():
@@ -321,12 +340,14 @@
             back_ref[...] = jnp.ones_like(back_ref)
         logs = state_logs(state_in) if resume else list(zeros)
         logs = run_backward(lead, mat, hist, sel_ref, consts, back_ref, ab_ref, logs)
-        put_state(state_out, back_ref[...].astype(BF16), logs)
-
-
-def second_kernel(resume, last, extend, grids, *refs):
+        put_states(state_outs, back_ref, logs)
+
+
+def second_kernel(resume, last, extend, grids, begin, *refs):
     refs = list(refs)
     sel_ref, mat, consts, hist, own_state, state_in = (refs.pop(0) for _ in range(6))
+    width = own_state.shape[1]
+    sel_ref, hist = sel_ref.at[:, :, :, pl.ds(begin, width)], hist.at[:, :, pl.ds(begin, width)]
     counts_in, sums_in = (refs.pop(0), refs.pop(0)) if resume else (None, None)
     row_probs = refs.pop(0) if last else None
     mine_ref, other_ref = (refs.pop(0), refs.pop(0)) if last else (None, None)
@@ -426,10 +447,10 @@
     steps = part * cores
     rows = states // lax.axis_size("hh")
     households = group * HB // cores
-    parts = 2 if households <= 4 * HB else 1
+    width = min(4 * HB, households)
+    grids = households // width
+    parts = 2 if sides == 2 and grids == 1 else 1
     share = households // parts
-    width = min(2 * HB, share)
-    grids = share // width
     side = lax.axis_index("per")
     shaped = jax.ShapeDtypeStruct
     dma = pltpu.SemaphoreType.DMA
@@ -461,7 +482,7 @@
     half_logits = pltpu.VMEM(trans_logits.shape, BF16)
     first_mat, consts = pl.pallas_call(
         prep_first_kernel,
-        out_shape=[shaped((steps, 2 * states + EXTRA, states), BF16), shaped((4, states, LANES), F32)],
+        out_shape=[shaped((steps, states // PACK + 1, 2 * PACK, states), BF16), shaped((4, states, LANES), F32)],
         in_specs=[hbm()] * 4,
         out_specs=[vmem()] * 2,
         scratch_shapes=[half_logits, half_logits, pltpu.VMEM((8, states), F32), dma((3,))],
@@ -472,7 +493,7 @@
     def prep_second(after):
         return pl.pallas_call(
             prep_second_kernel,
-            out_shape=[shaped((steps, 2 * states, states), BF16), shaped((steps, rows, states), F32)],
+            out_shape=[shaped((steps, states // PACK, 2 * PACK, states), BF16), shaped((steps, rows, states), F32)],
             in_specs=[hbm()] * 3,
             out_specs=[vmem()] * 2,
             scratch_shapes=[pltpu.VMEM((states, states), F32), half_logits, half_logits, dma((2,))],
@@ -491,36 +512,37 @@
         return pl.BlockSpec(lead + (width,), lambda g: (0,) * len(lead) + (g,))
 
     grid = (grids,) if grids > 1 else ()
-    hist_shape = shaped((steps, states, share), BF16)
+    hist_shape = shaped((steps, states, households), BF16)
     state_shape = shaped((states + EXTRA, share), BF16)
-    sel_shape = shaped((3, periods, 8, share), F32)
+    sel_shape = shaped((3, periods, 8, households), F32)
     swap_shape = shaped((steps * rows + 8, LANES), F32)
     counts_shape = shaped((steps, rows, states), F32)
     sums_shape = shaped((8, LANES), F32)
     hist_spec, state_spec, sel_spec = lanes(steps, states), lanes(states + EXTRA), lanes(3, periods, 8)
     const_spec = whole(4, states, LANES)
 
-    def first_pass(index, state_in):
+    def first_pass(state_in):
         resume = state_in is not None
         return pl.pallas_call(
-            functools.partial(first_kernel, resume, grids, index),
+            functools.partial(first_kernel, resume, grids),
             grid=grid,
-            out_shape=[hist_shape, state_shape, sel_shape],
+            out_shape=[hist_shape, sel_shape] + [state_shape] * parts,
             in_specs=[whole(*gathered.shape), whole(*first_mat.shape), const_spec]
             + [state_spec] * resume,
-            out_specs=[hist_spec, state_spec, sel_spec],
+            out_specs=[hist_spec, sel_spec] + [state_spec] * parts,
             scratch_shapes=[pltpu.VMEM((states, width), BF16), pltpu.VMEM((states, width), F32)],
             compiler_params=params(8 if grids == 1 else 32),
             name="first_pass",
         )(gathered, first_mat, consts, *([state_in] if resume else []))
 
-    def second_pass(kept, state_in, sums_in, last, extend):
-        hist, own_state, sel = kept
+    def second_pass(kept, index, state_in, sums_in, last, extend):
+        hist, sel, own_state = kept[0], kept[1], kept[2 + index]
         resume = sums_in is not None
+        span = width // parts
         scratch = [
-            pltpu.VMEM((states, width), BF16),
-            pltpu.VMEM((states, width), F32),
-            pltpu.VMEM((rows, width), BF16),
+            pltpu.VMEM((states, span), BF16),
+            pltpu.VMEM((states, span), F32),
+            pltpu.VMEM((rows, span), BF16),
         ]
         counts_spec, sums_spec = whole(*counts_shape.shape), whole(*sums_shape.shape)
         if last:
@@ -532,7 +554,7 @@
         if extend:
             out_shape, out_specs = out_shape + [state_shape], out_specs + [state_spec]
         return pl.pallas_call(
-            functools.partial(second_kernel, resume, last, extend, grids),
+            functools.partial(second_kernel, resume, last, extend, grids, index * span),
             grid=grid,
             out_shape=out_shape,
             in_specs=[sel_spec, whole(*second_mat.shape), const_spec, hist_spec, state_spec, state_spec]
@@ -553,15 +575,15 @@
         return lax.ppermute(state, "per", moves)
 
     if sides == 2:
-        kept = [first_pass(index, None) for index in range(parts)]
-        arrived = [hand_over(each[1], 0) for each in kept]
-        second_mat, row_probs = prep_second(kept[-1][1])
+        kept = first_pass(None)
+        arrived = [hand_over(each, 0) for each in kept[2:]]
+        second_mat, row_probs = prep_second(kept[2])
         sums = None
         for index in range(parts):
-            sums = second_pass(kept[index], arrived[index], sums, index == parts - 1, False)
+            sums = second_pass(kept, index, arrived[index], sums, index == parts - 1, False)
         mine, other = sums
     else:
-        kept = [jnp.zeros(x.shape, x.dtype) for x in (hist_shape, state_shape, sel_shape)]
+        kept = [jnp.zeros(x.shape, x.dtype) for x in (hist_shape, sel_shape, state_shape)]
         done = [jnp.zeros(x.shape, x.dtype) for x in (swap_shape, swap_shape, state_shape)]
         second_mat, row_probs = prep_second(gathered)
         state = None
@@ -569,13 +591,13 @@
             active = (side == stage) | (side == sides - 1 - stage)
             if stage < sides // 2:
                 kept = lax.cond(
-                    active, lambda x, kept: list(first_pass(0, x)), lambda x, kept: kept, state, kept
+                    active, lambda x, kept: list(first_pass(x)), lambda x, kept: kept, state, kept
                 )
-                state = kept[1]
+                state = kept[2]
             else:
                 done = lax.cond(
                     active,
-                    lambda x, done: list(second_pass(kept, x, None, True, True)),
+                    lambda x, done: list(second_pass(kept, 0, x, None, True, True)),
                     lambda x, done: done,
                     state,
                     done,

time: 36.7 us -> 38.5 us (1.049)
  local copies, waits for them, and re-layouts: 2.63 us -> 4.47 us
  waiting for transfers between devices: 3.6 us -> 4.74 us
  Pallas kernels: 18.6 us -> 17.8 us
    ppermute x2, waiting for transfers between devices: 0.01 us -> 2.99 us  [hand_over(): return lax.ppermute(state, 'per', moves)]
    all_to_all x1, waiting for transfers between devices: 2.06 us -> 0.22 us  [per_device(): lax.all_to_all(packed, ('hh', 'per'), split_axis=0, concat_axis=0, tiled=...]
    unnamed x8 -> x14, local copies, waits for them, and re-layouts: 2.63 us -> 4.47 us
    pallas_call x4 -> x3, Pallas kernels: 9.14 us -> 7.91 us  [the longest x1 3.95 us: first_pass(): pl.pallas_call(functools.partial(first_kernel, resume, grids), grid=grid,...]
    pallas_call x2, Pallas kernels: 7.16 us -> 7.6 us  [second_pass(): pl.pallas_call(functools.partial(second_kernel, resume, last, extend, gri...]
  transfers between devices with their start and end apart: 5 -> 5, of which waited for: 2 -> 3; matrix products, arithmetic and copies ran while one was open for 0% -> 0% of each run, Pallas kernels for 31% -> 24%
where the time goes in v7:
time: 38.5 us; the launch traced here: 38.1 us
  Pallas kernels  17.8 us (46%)
  starting transfers between devices  9.5 us (25%)
  waiting for transfers between devices  4.74 us (12%)
  local copies, waits for them, and re-layouts  4.47 us (12%)
  between operations  1.53 us (4%)
    pallas_call x2, Pallas kernels, second_pass(): pl.pallas_call(functools.partial(second_kernel, resume, last, extend, gri...  7.6 us
    all_to_all x1, starting transfers between devices, per_device(): lax.all_to_all(packed, ('hh', 'per'), split_axis=0, concat_axis=0, tiled=...  6.82 us
    unnamed x14, local copies, waits for them, and re-layouts  4.47 us
    pallas_call x1, Pallas kernels, first_pass(): pl.pallas_call(functools.partial(first_kernel, resume, grids), grid=grid,...  3.95 us
    ppermute x2, waiting for transfers between devices, hand_over(): return lax.ppermute(state, 'per', moves)  2.99 us
    pallas_call x1, Pallas kernels, per_device(): pl.pallas_call(prep_first_kernel, out_shape=[shaped((steps, states // PAC...  2.45 us
    ppermute x2, starting transfers between devices, hand_over(): return lax.ppermute(state, 'per', moves)  2.09 us
    pallas_call x1, Pallas kernels, per_device(): pl.pallas_call(pack_kernel, out_shape=[shaped((group, periods // 2, slot_...  1.56 us
  transfers between devices with their start and end apart: 5, of which 3 were waited for; matrix products, arithmetic and copies ran while one was open for 0% of the time, Pallas kernels for 24%

profile of v7, /device:TPU:0, one launch (start us, length us, event | category | flops | bytes accessed | tf_op | source)
XLA Modules:
  0.0 38.1 jit_solution(13057857312204550915)
XLA Ops:
  0.6 0.5 %collective-permute-start = (bf16[4,256,256]{2,1,0:T(8,128)(2,1)}, bf16[4,256,256]{2,1,0:T(8,128)(2,1)S(1)}, u32[]{:S(2)}, u32[]{:S(2)}) collective-permute-start(bf16[4,256,256]{2,1,0:T(8,128)(2,1)} %own_any.3), channel_id=1, source_target_pairs={{0,1},{1,0},{2,3},{3,2},{4,5},{5,4},{6,7},{7,6},{8,9},{9,8},{10,11... | collective-permute-start | bytes 1572872 | tf_op jit(solution)/shard_map/ppermute | solution.py:459
  1.8 1.6 %pack.1 = (f32[8,8,384]{2,1,0:T(8,128)}, f32[8,256]{1,0:T(8,128)}) custom-call(s32[1]{0:T(128)S(6)} %copy.10.count_any, f32[16,384]{1,0:T(8,128)} %bitcast.7, s32[3,128]{1,0:T(4,128)} %bitcast.8, s32[3,128]{1,0:T(4,128)} %bitcast.9, f32[1,256]{1,0:T(1,128)} %bitcast.10, f32[1,256]{1,0:T(1,128)} %bitcast.11, f32[1,256]{1,0:T(1,128)} %bitcast.12), custom_call_target="tpu_custom_call" | custom-call | tf_op jit(solution)/shard_map/pack/pallas_call | solution.py:461
  3.4 6.8 %all-to-all-start = ((f32[8,8,384]{2,1,0:T(8,128)}), f32[8,8,384]{2,1,0:T(8,128)S(1)}, u32[]{:S(2)}, u32[]{:S(2)}) async-start(f32[8,8,384]{2,1,0:T(8,128)} %get-tuple-element.18.after_any), calls=%async_computation | async-start | bytes 196608 | tf_op jit(solution)/shard_map/all_to_all | solution.py:481
  10.2 0.0 collective-permute-done.other_any
  10.2 0.0 copy-start.2
  10.2 0.8 %copy-done.2 = bf16[4,256,256]{2,1,0:T(8,128)(2,1)} copy-done((bf16[4,256,256]{2,1,0:T(8,128)(2,1)}, bf16[4,256,256]{2,1,0:T(8,128)(2,1)S(1)}, u32[]{:S(2)}) %copy-start.2) | copy-done | bytes 524312
  11.0 0.0 copy-start
  11.0 1.0 %copy-done = bf16[4,256,256]{2,1,0:T(8,128)(2,1)S(1)} copy-done((bf16[4,256,256]{2,1,0:T(8,128)(2,1)S(1)}, bf16[4,256,256]{2,1,0:T(8,128)(2,1)}, u32[]{:S(2)}) %copy-start) | copy-done | bytes 524312
  12.0 0.0 copy-start.3
  12.0 1.0 %copy-done.3 = bf16[4,256,256]{2,1,0:T(8,128)(2,1)S(1)} copy-done((bf16[4,256,256]{2,1,0:T(8,128)(2,1)S(1)}, bf16[4,256,256]{2,1,0:T(8,128)(2,1)}, u32[]{:S(2)}) %copy-start.3) | copy-done | bytes 524312
  13.1 0.0 copy-start.5
  13.1 0.9 %copy-done.5 = f32[8,8,384]{2,1,0:T(8,128)S(1)} copy-done((f32[8,8,384]{2,1,0:T(8,128)S(1)}, f32[8,8,384]{2,1,0:T(8,128)}, u32[]{:S(2)}) %copy-start.5) | copy-done | bytes 98328
  14.0 0.0 copy-start.6
  14.0 0.7 %copy-done.6 = f32[8,256]{1,0:T(8,128)S(1)} copy-done((f32[8,256]{1,0:T(8,128)S(1)}, f32[8,256]{1,0:T(8,128)}, u32[]{:S(2)}) %copy-start.6) | copy-done | bytes 8216
  14.7 0.0 copy-start.1
  14.7 2.5 %prep_first.1 = (bf16[8,17,32,256]{3,2,1,0:T(8,128)(2,1)S(1)}, f32[4,256,128]{2,1,0:T(8,128)S(1)}) custom-call(bf16[4,256,256]{2,1,0:T(8,128)(2,1)S(1)} %copy-done, bf16[4,256,256]{2,1,0:T(8,128)(2,1)S(1)} %copy-done.3, f32[8,256]{1,0:T(8,128)S(1)} %copy-done.6, f32[8,8,384]{2,1,0:T(8,128)S(1)} %copy-done.5), custom_call_target="tpu_custom_call" | custom-call | tf_op jit(solution)/shard_map/prep_first/pallas_call | solution.py:483
  17.1 0.2 all-to-all-done.rows_ref
  17.4 0.0 copy-start.4
  17.4 3.9 %first_pass.1 = (bf16[8,256,512]{2,1,0:T(8,128)(2,1)S(1)}, f32[3,16,8,512]{3,2,1,0:T(8,128)S(1)}, bf16[272,256]{1,0:T(8,128)(2,1)S(1)}, bf16[272,256]{1,0:T(8,128)(2,1)S(1)}) custom-call(f32[8,8,384]{2,1,0:T(8,128)S(1)} %all-to-all-done.rows_ref, bf16[8,17,32,256]{3,2,1,0:T(8,128)(2,1)S(1)} %get-tuple-element.20.mat, ...), custom_call_target="tpu_custom_call" | custom-call | tf_op jit(solution)/shard_map/first_pass/pallas_call | solution.py:526
  21.3 1.4 %collective-permute-start.2 = (bf16[272,256]{1,0:T(8,128)(2,1)S(1)}, bf16[272,256]{1,0:T(8,128)(2,1)S(1)}, u32[]{:S(2)}, u32[]{:S(2)}) collective-permute-start(bf16[272,256]{1,0:T(8,128)(2,1)S(1)} %get-tuple-element.23.after_any.refs_4_), channel_id=1, source_target_pairs={{0,2},{2,0},{1,3},{3,1},{4,6},{6,4},{5,7},{7,5},{8,10},{10,8},{9,1... | collective-permute-start | bytes 417800 | tf_op jit(solution)/shard_map/ppermute | solution.py:575
  22.7 0.7 %collective-permute-start.1 = (bf16[272,256]{1,0:T(8,128)(2,1)S(1)}, bf16[272,256]{1,0:T(8,128)(2,1)S(1)}, u32[]{:S(2)}, u32[]{:S(2)}) collective-permute-start(bf16[272,256]{1,0:T(8,128)(2,1)S(1)} %get-tuple-element.26.refs_4_), channel_id=1, source_target_pairs={{0,2},{2,0},{1,3},{3,1},{4,6},{6,4},{5,7},{7,5},{8,10},{10,8},{9,1... | collective-permute-start | bytes 417800 | tf_op jit(solution)/shard_map/ppermute | solution.py:575
  23.4 0.0 copy-done.1
  23.4 0.0 copy-done.4
  23.4 1.5 %prep_second.1 = (bf16[8,16,32,256]{3,2,1,0:T(8,128)(2,1)S(1)}, f32[8,64,256]{2,1,0:T(8,128)S(1)}) custom-call(bf16[4,256,256]{2,1,0:T(8,128)(2,1)S(1)} %copy-done.1, bf16[4,256,256]{2,1,0:T(8,128)(2,1)S(1)} %copy-done.4, bf16[272,256]{1,0:T(8,128)(2,1)S(1)} %get-tuple-element.23.after_any.refs_4_), custom_call_target="tpu_custom_call" | custom-call | tf_op jit(solution)/shard_map/prep_second/pallas_call | solution.py:494
  24.9 3.0 %collective-permute-done.2.refs_5_ = bf16[272,256]{1,0:T(8,128)(2,1)S(1)} collective-permute-done((bf16[272,256]{1,0:T(8,128)(2,1)S(1)}, bf16[272,256]{1,0:T(8,128)(2,1)S(1)}, u32[]{:S(2)}, u32[]{:S(2)}) %collective-permute-start.2) | collective-permute-done | bytes 139296 | tf_op jit(solution)/shard_map/ppermute | solution.py:575
  27.9 3.5 %second_pass.2 = (f32[8,64,256]{2,1,0:T(8,128)S(1)}, f32[8,128]{1,0:T(8,128)S(1)}) custom-call(f32[3,16,8,512]{3,2,1,0:T(8,128)S(1)} %get-tuple-element.22.refs_0_, bf16[8,16,32,256]{3,2,1,0:T(8,128)(2,1)S(1)} %get-tuple-element.24.refs_1_, f32[4,256,128]{2,1,0:T(8,128)S(1)} %get-tuple-element.21.consts.refs_2_, ...), custom_call_target="tpu_custom_call" | custom-call | tf_op jit(solution)/shard_map/second_pass/pallas_call | solution.py:556
  31.5 0.0 collective-permute-done.1.refs_5_
  31.5 4.1 %second_pass.3 = (f32[520,128]{1,0:T(8,128)S(1)}, f32[520,128]{1,0:T(8,128)S(1)}) custom-call(f32[3,16,8,512]{3,2,1,0:T(8,128)S(1)} %get-tuple-element.22.refs_0_, bf16[8,16,32,256]{3,2,1,0:T(8,128)(2,1)S(1)} %get-tuple-element.24.refs_1_, f32[4,256,128]{2,1,0:T(8,128)S(1)} %get-tuple-element.21.consts.refs_2_, ...), custom_call_target="tpu_custom_call" | custom-call | tf_op jit(solution)/shard_map/second_pass/pallas_call | solution.py:556
  35.5 0.1 collective-permute-start.3
  35.6 1.5 %collective-permute-done.3.other_ref = f32[520,128]{1,0:T(8,128)S(1)} collective-permute-done((f32[520,128]{1,0:T(8,128)S(1)}, f32[520,128]{1,0:T(8,128)S(1)}, u32[]{:S(2)}, u32[]{:S(2)}) %collective-permute-start.3) | collective-permute-done | bytes 266272 | tf_op jit(solution)/shard_map/ppermute | solution.py:613
  37.1 0.8 %finish.1 = (f32[512,128]{1,0:T(8,128)}, f32[1]{0:T(128)}) custom-call(f32[520,128]{1,0:T(8,128)S(1)} %get-tuple-element.30.mine_ref, f32[520,128]{1,0:T(8,128)S(1)} %collective-permute-done.3.other_ref), custom_call_target="tpu_custom_call" | custom-call | tf_op jit(solution)/shard_map/finish/pallas_call | solution.py:614
Async XLA Ops:
  0.6 9.6 %collective-permute-start = (bf16[4,256,256]{2,1,0:T(8,128)(2,1)}, bf16[4,256,256]{2,1,0:T(8,128)(2,1)S(1)}, u32[]{:S(2)}, u32[]{:S(2)}) collective-permute-start(bf16[4,256,256]{2,1,0:T(8,128)(2,1)} %own_any.3), channel_id=1, source_target_pairs={{0,1},{1,0},{2,3},{3,2},{4,5},{5,4},{6,7},{7,6},{8,9},{9,8},{10,11... | collective-permute-start | bytes 1572872 | tf_op jit(solution)/shard_map/ppermute | solution.py:459
  3.4 14.0 %all-to-all-start = ((f32[8,8,384]{2,1,0:T(8,128)}), f32[8,8,384]{2,1,0:T(8,128)S(1)}, u32[]{:S(2)}, u32[]{:S(2)}) async-start(f32[8,8,384]{2,1,0:T(8,128)} %get-tuple-element.18.after_any), calls=%async_computation | async-start | bytes 196608 | tf_op jit(solution)/shard_map/all_to_all | solution.py:481
  10.2 0.8 %copy-start.2 = (bf16[4,256,256]{2,1,0:T(8,128)(2,1)}, bf16[4,256,256]{2,1,0:T(8,128)(2,1)S(1)}, u32[]{:S(2)}) copy-start(bf16[4,256,256]{2,1,0:T(8,128)(2,1)S(1)} %collective-permute-done.other_any) | copy-start | bytes 1572868
  11.0 1.0 %copy-start = (bf16[4,256,256]{2,1,0:T(8,128)(2,1)S(1)}, bf16[4,256,256]{2,1,0:T(8,128)(2,1)}, u32[]{:S(2)}) copy-start(bf16[4,256,256]{2,1,0:T(8,128)(2,1)} %own_any.3) | copy-start | bytes 1572868
  12.0 1.0 %copy-start.3 = (bf16[4,256,256]{2,1,0:T(8,128)(2,1)S(1)}, bf16[4,256,256]{2,1,0:T(8,128)(2,1)}, u32[]{:S(2)}) copy-start(bf16[4,256,256]{2,1,0:T(8,128)(2,1)} %copy-done.2) | copy-start | bytes 1572868
  13.1 0.9 %copy-start.5 = (f32[8,8,384]{2,1,0:T(8,128)S(1)}, f32[8,8,384]{2,1,0:T(8,128)}, u32[]{:S(2)}) copy-start(f32[8,8,384]{2,1,0:T(8,128)} %get-tuple-element.18.after_any) | copy-start | bytes 294916
  14.0 0.7 %copy-start.6 = (f32[8,256]{1,0:T(8,128)S(1)}, f32[8,256]{1,0:T(8,128)}, u32[]{:S(2)}) copy-start(f32[8,256]{1,0:T(8,128)} %get-tuple-element.19.vec_any) | copy-start | bytes 24580
  14.7 8.7 %copy-start.1 = (bf16[4,256,256]{2,1,0:T(8,128)(2,1)S(1)}, bf16[4,256,256]{2,1,0:T(8,128)(2,1)}, u32[]{:S(2)}) copy-start(bf16[4,256,256]{2,1,0:T(8,128)(2,1)} %own_any.3) | copy-start | bytes 1572868
  17.4 6.1 %copy-start.4 = (bf16[4,256,256]{2,1,0:T(8,128)(2,1)S(1)}, bf16[4,256,256]{2,1,0:T(8,128)(2,1)}, u32[]{:S(2)}) copy-start(bf16[4,256,256]{2,1,0:T(8,128)(2,1)} %copy-done.2) | copy-start | bytes 1572868
  21.3 6.6 %collective-permute-start.2 = (bf16[272,256]{1,0:T(8,128)(2,1)S(1)}, bf16[272,256]{1,0:T(8,128)(2,1)S(1)}, u32[]{:S(2)}, u32[]{:S(2)}) collective-permute-start(bf16[272,256]{1,0:T(8,128)(2,1)S(1)} %get-tuple-element.23.after_any.refs_4_), channel_id=1, source_target_pairs={{0,2},{2,0},{1,3},{3,1},{4,6},{6,4},{5,7},{7,5},{8,10},{10,8},{9,1... | collective-permute-start | bytes 417800 | tf_op jit(solution)/shard_map/ppermute | solution.py:575
  22.7 8.8 %collective-permute-start.1 = (bf16[272,256]{1,0:T(8,128)(2,1)S(1)}, bf16[272,256]{1,0:T(8,128)(2,1)S(1)}, u32[]{:S(2)}, u32[]{:S(2)}) collective-permute-start(bf16[272,256]{1,0:T(8,128)(2,1)S(1)} %get-tuple-element.26.refs_4_), channel_id=1, source_target_pairs={{0,2},{2,0},{1,3},{3,1},{4,6},{6,4},{5,7},{7,5},{8,10},{10,8},{9,1... | collective-permute-start | bytes 417800 | tf_op jit(solution)/shard_map/ppermute | solution.py:575
  35.5 1.6 %collective-permute-start.3 = (f32[520,128]{1,0:T(8,128)S(1)}, f32[520,128]{1,0:T(8,128)S(1)}, u32[]{:S(2)}, u32[]{:S(2)}) collective-permute-start(f32[520,128]{1,0:T(8,128)S(1)} %get-tuple-element.31), channel_id=1, source_target_pairs={{0,1},{1,0},{2,3},{3,2},{4,5},{5,4},{6,7},{7,6},{8,9},{9,8},{10,11... | collective-permute-start | bytes 798728 | tf_op jit(solution)/shard_map/ppermute | solution.py:613

commit v8 on v6

--- a/solution.py
+++ b/solution.py
@@ -30,6 +30,10 @@
     return pl.BlockSpec(memory_space=pltpu.HBM)
 
 
+def in_hbm(*arrays):
+    return [pltpu.with_memory_space_constraint(x, pltpu.HBM) for x in arrays]
+
+
 def params(mebibytes):
     return pltpu.CompilerParams(vmem_limit_bytes=mebibytes * 1024 * 1024)
 
@@ -55,12 +59,12 @@
 
 
 def pack_kernel(
-    count_any, earn_any, start_any, len_any, init_any, mean_any, sd_any, out_ref, vec_ref,
-    count_ref, earn_ref, start_ref, len_ref, init_ref, mean_ref, sd_ref, sems,
+    count_ref, earn_any, start_any, len_any, init_any, mean_any, sd_any, out_ref, vec_ref,
+    earn_ref, start_ref, len_ref, init_ref, mean_ref, sd_ref, sems,
 ):
     fetch(
         (
-            (count_any, count_ref), (earn_any, earn_ref), (start_any, start_ref), (len_any, len_ref),
+            (earn_any, earn_ref), (start_any, start_ref), (len_any, len_ref),
             (init_any, init_ref), (mean_any, mean_ref), (sd_any, sd_ref),
         ),
         sems,
@@ -97,45 +101,42 @@
     ref[at, states : 2 * states, :] = (value - high.astype(F32)).astype(BF16)
 
 
-def fill_periods(mat, row_probs, scratch, turned_pass, source, ref):
-    @pl.loop(0, ref.shape[0])
-    def _(i):
-        at = source * ref.shape[0] + i
-        lifted = jnp.exp(ref[i].astype(F32))
-        probs = lifted * (1.0 / jnp.sum(lifted, axis=1, keepdims=True))
-        if row_probs is not None:
-            rows = row_probs.shape[1]
-            scratch[...] = probs
-            row_probs[at] = scratch[own_rows(lax.axis_index("hh") * rows, rows), :]
-
-        @pl.when(turned_pass)
-        def _():
-            put(mat, at, probs.T)
-
-        @pl.when(jnp.logical_not(turned_pass))
-        def _():
-            put(mat, at, probs)
-
-
-def prep_first_kernel(own_any, other_any, vec_any, after_any, mat, consts, own_ref, other_ref, vec_ref, sems):
-    fetch(((own_any, own_ref), (other_any, other_ref), (vec_any, vec_ref)), sems)
+def prep_kernel(
+    own_any, other_ref, vec_ref, first_mat, second_mat, row_probs, consts, scratch, own_ref, sem
+):
+    copy = pltpu.make_async_copy(own_any, own_ref, sem)
+    copy.start()
     part, states, _ = own_ref.shape
+    rows = row_probs.shape[1]
     for i in range(4):
         consts[i] = jnp.broadcast_to(vec_ref[i : i + 1, :], (LANES, states)).T
     start = vec_ref[:1, :]
     start_high = start.astype(BF16).astype(F32)
     row = lax.broadcasted_iota(jnp.int32, (EXTRA, states), 0)
     start_rows = jnp.where(row == 0, start_high, jnp.where(row == 1, start - start_high, 0.0)).astype(BF16)
-    for k in range(mat.shape[0]):
-        mat[k, 2 * states :, :] = start_rows
-    for source, ref in ((core_index(), own_ref), (1 - core_index(), other_ref)):
-        fill_periods(mat, None, None, is_forward_first(), source, ref)
-
-
-def prep_second_kernel(own_any, other_any, after_any, mat, row_probs, scratch, own_ref, other_ref, sems):
-    fetch(((own_any, own_ref), (other_any, other_ref)), sems)
-    for source, ref in ((core_index(), own_ref), (1 - core_index(), other_ref)):
-        fill_periods(mat, row_probs, scratch, jnp.logical_not(is_forward_first()), source, ref)
+    for k in range(first_mat.shape[0]):
+        first_mat[k, 2 * states :, :] = start_rows
+    for source, ref in ((1 - core_index(), other_ref), (core_index(), own_ref)):
+        if ref is own_ref:
+            copy.wait()
+
+        @pl.loop(0, part)
+        def _(i):
+            at = source * part + i
+            lifted = jnp.exp(ref[i].astype(F32))
+            probs = lifted * (1.0 / jnp.sum(lifted, axis=1, keepdims=True))
+            scratch[...] = probs
+            row_probs[at] = scratch[own_rows(lax.axis_index("hh") * rows, rows), :]
+
+            @pl.when(is_forward_first())
+            def _():
+                put(first_mat, at, probs.T)
+                put(second_mat, at, probs)
+
+            @pl.when(jnp.logical_not(is_forward_first()))
+            def _():
+                put(first_mat, at, probs)
+                put(second_mat, at, probs.T)
 
 
 def emission(sel_ref, consts, step_now, cols):
@@ -440,45 +441,41 @@
     packed, vectors = pl.pallas_call(
         pack_kernel,
         out_shape=[shaped((group, periods // 2, slot_rows), F32), shaped((8, states), F32)],
-        in_specs=[hbm()] * 7,
+        in_specs=[smem()] + [hbm()] * 6,
         out_specs=[vmem()] * 2,
         scratch_shapes=[
-            pltpu.SMEM((1,), jnp.int32),
             pltpu.VMEM((periods, slot_rows), F32),
             pltpu.VMEM((slot_rows // HB, HB), jnp.int32),
             pltpu.VMEM((slot_rows // HB, HB), jnp.int32),
             vec_row,
             vec_row,
             vec_row,
-            dma((7,)),
+            dma((6,)),
         ],
+        compiler_params=params(2),
         name="pack",
     )(
-        block_count, earnings.T, starts.reshape(-1, HB), lengths.reshape(-1, HB),
-        init_logits.reshape(1, states), state_mean.reshape(1, states), log_sd.reshape(1, states),
+        block_count,
+        *in_hbm(
+            earnings.T, starts.reshape(-1, HB), lengths.reshape(-1, HB),
+            init_logits.reshape(1, states), state_mean.reshape(1, states), log_sd.reshape(1, states),
+        ),
     )
     gathered = lax.all_to_all(packed, ("hh", "per"), split_axis=0, concat_axis=0, tiled=True)
-    half_logits = pltpu.VMEM(trans_logits.shape, BF16)
-    first_mat, consts = pl.pallas_call(
-        prep_first_kernel,
-        out_shape=[shaped((steps, 2 * states + EXTRA, states), BF16), shaped((4, states, LANES), F32)],
-        in_specs=[hbm()] * 4,
-        out_specs=[vmem()] * 2,
-        scratch_shapes=[half_logits, half_logits, pltpu.VMEM((8, states), F32), dma((3,))],
+    first_mat, second_mat, row_probs, consts = pl.pallas_call(
+        prep_kernel,
+        out_shape=[
+            pltpu.VMEM((steps, 2 * states + EXTRA, states), BF16),
+            pltpu.VMEM((steps, 2 * states, states), BF16),
+            pltpu.VMEM((steps, rows, states), F32),
+            pltpu.VMEM((4, states, LANES), F32),
+        ],
+        in_specs=[hbm(), vmem(), vmem()],
+        out_specs=[vmem()] * 4,
+        scratch_shapes=[pltpu.VMEM((states, states), F32), pltpu.VMEM(trans_logits.shape, BF16), dma],
         compiler_params=params(4),
-        name="prep_first",
-    )(trans_logits, other_logits, vectors, packed)
-
-    def prep_second(after):
-        return pl.pallas_call(
-            prep_second_kernel,
-            out_shape=[shaped((steps, 2 * states, states), BF16), shaped((steps, rows, states), F32)],
-            in_specs=[hbm()] * 3,
-            out_specs=[vmem()] * 2,
-            scratch_shapes=[pltpu.VMEM((states, states), F32), half_logits, half_logits, dma((2,))],
-            compiler_params=params(4),
-            name="prep_second",
-        )(trans_logits, other_logits, after)
+        name="prep",
+    )(*in_hbm(trans_logits), pltpu.with_memory_space_constraint(other_logits, pltpu.VMEM), vectors)
 
     def whole(*shape):
         if grids == 1:
@@ -555,7 +552,6 @@
     if sides == 2:
         kept = [first_pass(index, None) for index in range(parts)]
         arrived = [hand_over(each[1], 0) for each in kept]
-        second_mat, row_probs = prep_second(kept[-1][1])
         sums = None
         for index in range(parts):
             sums = second_pass(kept[index], arrived[index], sums, index == parts - 1, False)
@@ -563,7 +559,6 @@
     else:
         kept = [jnp.zeros(x.shape, x.dtype) for x in (hist_shape, state_shape, sel_shape)]
         done = [jnp.zeros(x.shape, x.dtype) for x in (swap_shape, swap_shape, state_shape)]
-        second_mat, row_probs = prep_second(gathered)
         state = None
         for stage in range(sides):
             active = (side == stage) | (side == sides - 1 - stage)

time: 36.7 us -> 35.4 us (0.965)
  Pallas kernels: 18.6 us -> 17.1 us
  local copies, waits for them, and re-layouts: 2.63 us -> 3.15 us
    pallas_call x2 -> x1, Pallas kernels: 3.96 us -> 2.54 us  [per_device(): pl.pallas_call(prep_kernel, out_shape=[pltpu.VMEM((steps, 2 * states + EX...]
    all_to_all x1, waiting for transfers between devices: 2.06 us -> 1.45 us  [per_device(): lax.all_to_all(packed, ('hh', 'per'), split_axis=0, concat_axis=0, tiled=...]
    unnamed x8, local copies, waits for them, and re-layouts: 2.63 us -> 3.15 us
    ppermute x2, waiting for transfers between devices: 0.01 us -> 0.43 us  [hand_over(): return lax.ppermute(state, 'per', moves)]
  transfers between devices with their start and end apart: 5 -> 5, of which waited for: 2 -> 4; matrix products, arithmetic and copies ran while one was open for 0% -> 0% of each run, Pallas kernels for 31% -> 28%
where the time goes in v8:
time: 35.4 us; the launch traced here: 35.1 us
  Pallas kernels  17.1 us (48%)
  starting transfers between devices  9.88 us (28%)
  waiting for transfers between devices  3.41 us (10%)
  local copies, waits for them, and re-layouts  3.15 us (9%)
  between operations  1.53 us (4%)
    pallas_call x2, Pallas kernels, second_pass(): pl.pallas_call(functools.partial(second_kernel, resume, last, extend, gri...  7.1 us
    all_to_all x1, starting transfers between devices, per_device(): lax.all_to_all(packed, ('hh', 'per'), split_axis=0, concat_axis=0, tiled=...  6.82 us
    pallas_call x2, Pallas kernels, first_pass(): pl.pallas_call(functools.partial(first_kernel, resume, grids, index), gri...  5.17 us
    unnamed x8, local copies, waits for them, and re-layouts  3.15 us
    pallas_call x1, Pallas kernels, per_device(): pl.pallas_call(prep_kernel, out_shape=[pltpu.VMEM((steps, 2 * states + EX...  2.54 us
    ppermute x2, starting transfers between devices, hand_over(): return lax.ppermute(state, 'per', moves)  2.47 us
    pallas_call x1, Pallas kernels, per_device(): pl.pallas_call(pack_kernel, out_shape=[shaped((group, periods // 2, slot_...  1.54 us
    ppermute x1, waiting for transfers between devices, per_device(): received = lax.ppermute(other, 'st', swap)  1.53 us
  transfers between devices with their start and end apart: 5, of which 4 were waited for; matrix products, arithmetic and copies ran while one was open for 0% of the time, Pallas kernels for 28%

profile of v8, /device:TPU:0, one launch (start us, length us, event | category | flops | bytes accessed | tf_op | source)
XLA Modules:
  0.0 35.1 jit_solution(9981014346218727266)
XLA Ops:
  0.6 0.5 %collective-permute-start = (bf16[4,256,256]{2,1,0:T(8,128)(2,1)}, bf16[4,256,256]{2,1,0:T(8,128)(2,1)S(1)}, u32[]{:S(2)}, u32[]{:S(2)}) collective-permute-start(bf16[4,256,256]{2,1,0:T(8,128)(2,1)} %own_any.1), channel_id=1, source_target_pairs={{0,1},{1,0},{2,3},{3,2},{4,5},{5,4},{6,7},{7,6},{8,9},{9,8},{10,11... | collective-permute-start | bytes 1572872 | tf_op jit(solution)/shard_map/ppermute | solution.py:439
  1.8 1.5 %pack.1 = (f32[8,8,384]{2,1,0:T(8,128)}, f32[8,256]{1,0:T(8,128)S(1)}) custom-call(s32[1]{0:T(128)S(6)} %copy.10.count_ref, f32[16,384]{1,0:T(8,128)} %bitcast.7, s32[3,128]{1,0:T(4,128)} %bitcast.8, s32[3,128]{1,0:T(4,128)} %bitcast.9, f32[1,256]{1,0:T(1,128)} %bitcast.10, f32[1,256]{1,0:T(1,128)} %bitcast.11, f32[1,256]{1,0:T(1,128)} %bitcast.12), custom_call_target="tpu_custom_call" | custom-call | tf_op jit(solution)/shard_map/pack/pallas_call | solution.py:441
  3.4 6.8 %all-to-all-start = ((f32[8,8,384]{2,1,0:T(8,128)}), f32[8,8,384]{2,1,0:T(8,128)S(1)}, u32[]{:S(2)}, u32[]{:S(2)}) async-start(f32[8,8,384]{2,1,0:T(8,128)} %get-tuple-element.20), calls=%async_computation | async-start | bytes 196608 | tf_op jit(solution)/shard_map/all_to_all | solution.py:464
  10.2 0.0 collective-permute-done.other_ref
  10.2 0.0 copy-start.2
  10.2 0.8 %copy-done.2 = bf16[4,256,256]{2,1,0:T(8,128)(2,1)} copy-done((bf16[4,256,256]{2,1,0:T(8,128)(2,1)}, bf16[4,256,256]{2,1,0:T(8,128)(2,1)S(1)}, u32[]{:S(2)}) %copy-start.2) | copy-done | bytes 524312
  11.0 0.0 copy-start.3
  11.0 1.0 %copy-done.3 = bf16[4,256,256]{2,1,0:T(8,128)(2,1)S(1)} copy-done((bf16[4,256,256]{2,1,0:T(8,128)(2,1)S(1)}, bf16[4,256,256]{2,1,0:T(8,128)(2,1)}, u32[]{:S(2)}) %copy-start.3) | copy-done | bytes 524312
  12.0 2.5 %prep.1 = (bf16[8,528,256]{2,1,0:T(8,128)(2,1)S(1)}, bf16[8,512,256]{2,1,0:T(8,128)(2,1)S(1)}, f32[8,64,256]{2,1,0:T(8,128)S(1)}, f32[4,256,128]{2,1,0:T(8,128)S(1)}) custom-call(bf16[4,256,256]{2,1,0:T(8,128)(2,1)} %own_any.1, bf16[4,256,256]{2,1,0:T(8,128)(2,1)S(1)} %copy-done.3, f32[8,256]{1,0:T(8,128)S(1)} %get-tuple-element.21.vec_ref), custom_call_target="tpu_custom_call" | custom-call | tf_op jit(solution)/shard_map/prep/pallas_call | solution.py:465
  14.6 0.0 copy-start
  14.6 1.3 %copy-done = bf16[8,512,256]{2,1,0:T(8,128)(2,1)} copy-done((bf16[8,512,256]{2,1,0:T(8,128)(2,1)}, bf16[8,512,256]{2,1,0:T(8,128)(2,1)S(1)}, u32[]{:S(2)}) %copy-start) | copy-done | bytes 2097176
  15.9 1.4 %all-to-all-done.rows_ref = f32[8,8,384]{2,1,0:T(8,128)S(1)} async-done(((f32[8,8,384]{2,1,0:T(8,128)}), f32[8,8,384]{2,1,0:T(8,128)S(1)}, u32[]{:S(2)}, u32[]{:S(2)}) %all-to-all-start) | async-done | bytes 98336 | tf_op jit(solution)/shard_map/all_to_all | solution.py:464
  17.3 0.0 copy-start.1
  17.3 2.6 %first_pass.3 = (bf16[8,256,256]{2,1,0:T(8,128)(2,1)S(1)}, bf16[272,256]{1,0:T(8,128)(2,1)S(1)}, f32[3,16,8,256]{3,2,1,0:T(8,128)S(1)}) custom-call(f32[8,8,384]{2,1,0:T(8,128)S(1)} %all-to-all-done.rows_ref, bf16[8,528,256]{2,1,0:T(8,128)(2,1)S(1)} %get-tuple-element.22.mat, f32[4,256,128]{2,1,0:T(8,128)S(1)} %get-tuple-element.23.consts.refs_2_), custom_call_target="tpu_custom_call" | custom-call | tf_op jit(solution)/shard_map/first_pass/pallas_call | solution.py:502
  19.9 0.9 %collective-permute-start.2 = (bf16[272,256]{1,0:T(8,128)(2,1)S(1)}, bf16[272,256]{1,0:T(8,128)(2,1)S(1)}, u32[]{:S(2)}, u32[]{:S(2)}) collective-permute-start(bf16[272,256]{1,0:T(8,128)(2,1)S(1)} %get-tuple-element.30.refs_4_), channel_id=1, source_target_pairs={{0,2},{2,0},{1,3},{3,1},{4,6},{6,4},{5,7},{7,5},{8,10},{10,8},{9,1... | collective-permute-start | bytes 417800 | tf_op jit(solution)/shard_map/ppermute | solution.py:550
  20.8 2.6 %first_pass.2 = (bf16[8,256,256]{2,1,0:T(8,128)(2,1)S(1)}, bf16[272,256]{1,0:T(8,128)(2,1)S(1)}, f32[3,16,8,256]{3,2,1,0:T(8,128)S(1)}) custom-call(f32[8,8,384]{2,1,0:T(8,128)S(1)} %all-to-all-done.rows_ref, bf16[8,528,256]{2,1,0:T(8,128)(2,1)S(1)} %get-tuple-element.22.mat, f32[4,256,128]{2,1,0:T(8,128)S(1)} %get-tuple-element.23.consts.refs_2_), custom_call_target="tpu_custom_call" | custom-call | tf_op jit(solution)/shard_map/first_pass/pallas_call | solution.py:502
  23.4 1.6 %collective-permute-start.1 = (bf16[272,256]{1,0:T(8,128)(2,1)S(1)}, bf16[272,256]{1,0:T(8,128)(2,1)S(1)}, u32[]{:S(2)}, u32[]{:S(2)}) collective-permute-start(bf16[272,256]{1,0:T(8,128)(2,1)S(1)} %get-tuple-element.27.refs_4_), channel_id=1, source_target_pairs={{0,2},{2,0},{1,3},{3,1},{4,6},{6,4},{5,7},{7,5},{8,10},{10,8},{9,1... | collective-permute-start | bytes 417800 | tf_op jit(solution)/shard_map/ppermute | solution.py:550
  25.0 0.1 collective-permute-done.2.refs_5_
  25.1 0.0 copy-done.1
  25.1 3.3 %second_pass.2 = (f32[8,64,256]{2,1,0:T(8,128)S(1)}, f32[8,128]{1,0:T(8,128)S(1)}) custom-call(f32[3,16,8,256]{3,2,1,0:T(8,128)S(1)} %get-tuple-element.28.refs_0_, bf16[8,512,256]{2,1,0:T(8,128)(2,1)S(1)} %copy-done.1, f32[4,256,128]{2,1,0:T(8,128)S(1)} %get-tuple-element.23.consts.refs_2_, bf16[8,256,256]{2,1,0:T(8,128)(2,1)S(1)} %get-tuple-element.29.refs_3_, ...), custom_call_target="tpu_custom_call" | custom-call | tf_op jit(solution)/shard_map/second_pass/pallas_call | solution.py:531
  28.4 0.4 %collective-permute-done.1.refs_5_ = bf16[272,256]{1,0:T(8,128)(2,1)S(1)} collective-permute-done((bf16[272,256]{1,0:T(8,128)(2,1)S(1)}, bf16[272,256]{1,0:T(8,128)(2,1)S(1)}, u32[]{:S(2)}, u32[]{:S(2)}) %collective-permute-start.1) | collective-permute-done | bytes 139296 | tf_op jit(solution)/shard_map/ppermute | solution.py:550
  28.7 3.8 %second_pass.3 = (f32[520,128]{1,0:T(8,128)S(1)}, f32[520,128]{1,0:T(8,128)S(1)}) custom-call(f32[3,16,8,256]{3,2,1,0:T(8,128)S(1)} %get-tuple-element.24.refs_0_, bf16[8,512,256]{2,1,0:T(8,128)(2,1)S(1)} %copy-done.1, f32[4,256,128]{2,1,0:T(8,128)S(1)} %get-tuple-element.23.consts.refs_2_, bf16[8,256,256]{2,1,0:T(8,128)(2,1)S(1)} %get-tuple-element.26.refs_3_, ...), custom_call_target="tpu_custom_call" | custom-call | tf_op jit(solution)/shard_map/second_pass/pallas_call | solution.py:531
  32.6 0.1 collective-permute-start.3
  32.6 1.5 %collective-permute-done.3.other_ref = f32[520,128]{1,0:T(8,128)S(1)} collective-permute-done((f32[520,128]{1,0:T(8,128)S(1)}, f32[520,128]{1,0:T(8,128)S(1)}, u32[]{:S(2)}, u32[]{:S(2)}) %collective-permute-start.3) | collective-permute-done | bytes 266272 | tf_op jit(solution)/shard_map/ppermute | solution.py:586
  34.2 0.8 %finish.1 = (f32[512,128]{1,0:T(8,128)}, f32[1]{0:T(128)}) custom-call(f32[520,128]{1,0:T(8,128)S(1)} %get-tuple-element.34.mine_ref, f32[520,128]{1,0:T(8,128)S(1)} %collective-permute-done.3.other_ref), custom_call_target="tpu_custom_call" | custom-call | tf_op jit(solution)/shard_map/finish/pallas_call | solution.py:587
Async XLA Ops:
  0.6 9.5 %collective-permute-start = (bf16[4,256,256]{2,1,0:T(8,128)(2,1)}, bf16[4,256,256]{2,1,0:T(8,128)(2,1)S(1)}, u32[]{:S(2)}, u32[]{:S(2)}) collective-permute-start(bf16[4,256,256]{2,1,0:T(8,128)(2,1)} %own_any.1), channel_id=1, source_target_pairs={{0,1},{1,0},{2,3},{3,2},{4,5},{5,4},{6,7},{7,6},{8,9},{9,8},{10,11... | collective-permute-start | bytes 1572872 | tf_op jit(solution)/shard_map/ppermute | solution.py:439
  3.4 14.0 %all-to-all-start = ((f32[8,8,384]{2,1,0:T(8,128)}), f32[8,8,384]{2,1,0:T(8,128)S(1)}, u32[]{:S(2)}, u32[]{:S(2)}) async-start(f32[8,8,384]{2,1,0:T(8,128)} %get-tuple-element.20), calls=%async_computation | async-start | bytes 196608 | tf_op jit(solution)/shard_map/all_to_all | solution.py:464
  10.2 0.8 %copy-start.2 = (bf16[4,256,256]{2,1,0:T(8,128)(2,1)}, bf16[4,256,256]{2,1,0:T(8,128)(2,1)S(1)}, u32[]{:S(2)}) copy-start(bf16[4,256,256]{2,1,0:T(8,128)(2,1)S(1)} %collective-permute-done.other_ref) | copy-start | bytes 1572868
  11.0 1.0 %copy-start.3 = (bf16[4,256,256]{2,1,0:T(8,128)(2,1)S(1)}, bf16[4,256,256]{2,1,0:T(8,128)(2,1)}, u32[]{:S(2)}) copy-start(bf16[4,256,256]{2,1,0:T(8,128)(2,1)} %copy-done.2) | copy-start | bytes 1572868
  14.6 1.3 %copy-start = (bf16[8,512,256]{2,1,0:T(8,128)(2,1)}, bf16[8,512,256]{2,1,0:T(8,128)(2,1)S(1)}, u32[]{:S(2)}) copy-start(bf16[8,512,256]{2,1,0:T(8,128)(2,1)S(1)} %get-tuple-element.25.refs_1_) | copy-start | bytes 6291460
  17.3 7.7 %copy-start.1 = (bf16[8,512,256]{2,1,0:T(8,128)(2,1)S(1)}, bf16[8,512,256]{2,1,0:T(8,128)(2,1)}, u32[]{:S(2)}) copy-start(bf16[8,512,256]{2,1,0:T(8,128)(2,1)} %copy-done) | copy-start | bytes 6291460
  19.9 5.1 %collective-permute-start.2 = (bf16[272,256]{1,0:T(8,128)(2,1)S(1)}, bf16[272,256]{1,0:T(8,128)(2,1)S(1)}, u32[]{:S(2)}, u32[]{:S(2)}) collective-permute-start(bf16[272,256]{1,0:T(8,128)(2,1)S(1)} %get-tuple-element.30.refs_4_), channel_id=1, source_target_pairs={{0,2},{2,0},{1,3},{3,1},{4,6},{6,4},{5,7},{7,5},{8,10},{10,8},{9,1... | collective-permute-start | bytes 417800 | tf_op jit(solution)/shard_map/ppermute | solution.py:550
  23.4 5.3 %collective-permute-start.1 = (bf16[272,256]{1,0:T(8,128)(2,1)S(1)}, bf16[272,256]{1,0:T(8,128)(2,1)S(1)}, u32[]{:S(2)}, u32[]{:S(2)}) collective-permute-start(bf16[272,256]{1,0:T(8,128)(2,1)S(1)} %get-tuple-element.27.refs_4_), channel_id=1, source_target_pairs={{0,2},{2,0},{1,3},{3,1},{4,6},{6,4},{5,7},{7,5},{8,10},{10,8},{9,1... | collective-permute-start | bytes 417800 | tf_op jit(solution)/shard_map/ppermute | solution.py:550
  32.6 1.6 %collective-permute-start.3 = (f32[520,128]{1,0:T(8,128)S(1)}, f32[520,128]{1,0:T(8,128)S(1)}, u32[]{:S(2)}, u32[]{:S(2)}) collective-permute-start(f32[520,128]{1,0:T(8,128)S(1)} %get-tuple-element.35), channel_id=1, source_target_pairs={{0,1},{1,0},{2,3},{3,2},{4,5},{5,4},{6,7},{7,6},{8,9},{9,8},{10,11... | collective-permute-start | bytes 798728 | tf_op jit(solution)/shard_map/ppermute | solution.py:586

commit v9 on v8

--- a/solution.py
+++ b/solution.py
@@ -97,28 +97,43 @@
 def put(ref, at, value):
     states = value.shape[0]
     high = value.astype(BF16)
-    ref[at, :states, :] = high
-    ref[at, states : 2 * states, :] = (value - high.astype(F32)).astype(BF16)
+    ref[at, :states, :states] = high
+    ref[at, :states, states:] = (value - high.astype(F32)).astype(BF16)
+
+
+def put_twice(ref, cols, value):
+    states = value.shape[0]
+    value = value.astype(BF16)
+    ref[:states, cols] = value
+    ref[states:, cols] = value
 
 
 def prep_kernel(
-    own_any, other_ref, vec_ref, first_mat, second_mat, row_probs, consts, scratch, own_ref, sem
+    own_any, other_any, vec_ref, first_mat, second_any, row_probs, consts,
+    second_mat, scratch, own_ref, other_ref, sems, out_sems,
 ):
-    copy = pltpu.make_async_copy(own_any, own_ref, sem)
-    copy.start()
+    copies = [
+        pltpu.make_async_copy(src, dst, sems.at[i])
+        for i, (src, dst) in enumerate(((own_any, own_ref), (other_any, other_ref)))
+    ]
+    for copy in copies:
+        copy.start()
     part, states, _ = own_ref.shape
+
+    def leave(at):
+        return pltpu.make_async_copy(second_mat.at[at], second_any.at[at], out_sems.at[at])
+
     rows = row_probs.shape[1]
     for i in range(4):
         consts[i] = jnp.broadcast_to(vec_ref[i : i + 1, :], (LANES, states)).T
     start = vec_ref[:1, :]
     start_high = start.astype(BF16).astype(F32)
     row = lax.broadcasted_iota(jnp.int32, (EXTRA, states), 0)
-    start_rows = jnp.where(row == 0, start_high, jnp.where(row == 1, start - start_high, 0.0)).astype(BF16)
     for k in range(first_mat.shape[0]):
-        first_mat[k, 2 * states :, :] = start_rows
-    for source, ref in ((1 - core_index(), other_ref), (core_index(), own_ref)):
-        if ref is own_ref:
-            copy.wait()
+        first_mat[k, states:, :states] = jnp.where(row == 0, start_high, 0.0).astype(BF16)
+        first_mat[k, states:, states:] = jnp.where(row == 0, start - start_high, 0.0).astype(BF16)
+    for copy, source, ref in zip(copies, (core_index(), 1 - core_index()), (own_ref, other_ref)):
+        copy.wait()
 
         @pl.loop(0, part)
         def _(i):
@@ -138,6 +153,11 @@
                 put(first_mat, at, probs)
                 put(second_mat, at, probs.T)
 
+            leave(at).start()
+
+    for at in range(2 * part):
+        leave(at).wait()
+
 
 def emission(sel_ref, consts, step_now, cols):
     gap = sel_ref[0, step_now, :1, cols] - consts[1]
@@ -169,17 +189,16 @@
 def run_forward(lead, mat, hist, sel_ref, consts, ab_ref, logs, second=None):
     steps, states, width = hist.shape
     cuts = tiles(width)
-    inverse = [1.0 / column_sum(ab_ref[:, cols].astype(F32)) for cols in cuts]
+    inverse = [1.0 / column_sum(ab_ref[:states, cols].astype(F32)) for cols in cuts]
     for k in range(steps):
         step_now = lead + k
         if second is None:
-            hist[k] = ab_ref[...]
+            hist[k] = ab_ref[:states, :]
         else:
-            weights_ref, counts_ref, row_begin = second
+            weights_ref, row_begin, add_counts = second
             own_alpha = ab_ref[own_rows(row_begin, weights_ref.shape[0]), :].astype(F32)
         for q, cols in enumerate(cuts):
-            product = jnp.dot(mat[k, : 2 * states, :], ab_ref[:, cols], preferred_element_type=F32)
-            moved = (product[:states] + product[states:]) * inverse[q]
+            moved = jnp.dot(mat[k, :states, :], ab_ref[:, cols], preferred_element_type=F32) * inverse[q]
             moving = is_moving(sel_ref, step_now, cols)
             if second is not None:
                 total = column_sum(moved * hist[k, :, cols].astype(F32))
@@ -192,16 +211,17 @@
                 seen = is_seen(sel_ref, step_now, cols)
                 logs[q] = logs[q] + jnp.where(seen, jnp.log(scale) + top * LN2, 0.0)
             inverse[q] = 1.0 / scale
-            ab_ref[:, cols] = joint.astype(BF16)
+            put_twice(ab_ref, cols, joint)
         if second is not None:
-            counts_ref[k] += outer_sum(weights_ref, hist[k])
+            add_counts(k, outer_sum(weights_ref, hist[k]))
     return logs
 
 
 def run_backward(lead, mat, hist, sel_ref, consts, back_ref, ub_ref, logs, second=None):
     steps, states, width = hist.shape
     cuts = tiles(width)
-    for k in reversed(range(steps)):
+
+    def step(k):
         step_now = lead + k
         shrink = []
         for q, cols in enumerate(cuts):
@@ -212,19 +232,19 @@
                 seen = is_seen(sel_ref, step_now, cols)
                 logs[q] = logs[q] + jnp.where(seen, jnp.log(size) + top * LN2, 0.0)
             shrink.append(1.0 / size)
-            ub_ref[:, cols] = carried.astype(BF16)
+            put_twice(ub_ref, cols, carried)
         if second is None:
-            hist[k] = ub_ref[...]
+            hist[k] = ub_ref[:states, :]
         else:
-            weights_ref, counts_ref, row_begin = second
+            weights_ref, row_begin, add_counts = second
             own_alpha = hist[k, own_rows(row_begin, weights_ref.shape[0]), :].astype(F32)
         for q, cols in enumerate(cuts):
             product = jnp.dot(mat[k], ub_ref[:, cols], preferred_element_type=F32)
             moving = is_moving(sel_ref, step_now, cols)
-            pulled = (product[:states] + product[states : 2 * states]) * shrink[q]
+            pulled = product[:states] * shrink[q]
             if second is None:
                 seen = is_seen(sel_ref, step_now, cols)
-                begun = column_sum(product[2 * states :]) * shrink[q]
+                begun = product[states : states + 1] * shrink[q]
                 rest = jnp.where(seen, begun, back_ref[:, cols])
             else:
                 total = column_sum(pulled * hist[k, :, cols].astype(F32))
@@ -233,7 +253,15 @@
                 rest = 1.0
             back_ref[:, cols] = jnp.where(moving, pulled, rest)
         if second is not None:
-            counts_ref[k] += outer_sum(weights_ref, ub_ref[...])
+            add_counts(k, outer_sum(weights_ref, ub_ref[:states, :]))
+
+    for k in reversed(range(1, steps)):
+        step(k)
+    if second is None:
+        step(0)
+    else:
+        pl.when(lead > 0)(lambda: step(0))
+        pl.when(lead == 0)(lambda: second[2](0, jnp.zeros((second[0].shape[0], states), F32)))
     return logs
 
 
@@ -306,13 +334,13 @@
     @pl.when(forward_first)
     def _():
         if resume:
-            ab_ref[...] = state_in[:states, :]
+            put_twice(ab_ref, slice(None), state_in[:states, :])
         else:
             for cols in cuts:
-                ab_ref[:, cols] = consts[0].astype(BF16)
+                put_twice(ab_ref, cols, consts[0])
         logs = state_logs(state_in) if resume else list(zeros)
         logs = run_forward(lead, mat, hist, sel_ref, consts, ab_ref, logs)
-        put_state(state_out, ab_ref[...], logs)
+        put_state(state_out, ab_ref[:states, :], logs)
 
     @pl.when(jnp.logical_not(forward_first))
     def _():
@@ -338,18 +366,37 @@
     chunk = pl.program_id(0) if grids > 1 else 0
     steps, states, width = hist.shape
     core, forward_first = core_index(), is_forward_first()
-    row_begin = lax.axis_index("hh") * counts_ref.shape[1]
+    row_begin = lax.axis_index("hh") * weights_ref.shape[0]
     lead = lax.axis_index("per") * steps
-    second = (weights_ref, counts_ref, row_begin)
+    rows = weights_ref.shape[0]
+
+    def centre(k, counts):
+        probs = row_probs[k]
+        weighted = probs * counts
+        grad = weighted - probs * jnp.sum(weighted, axis=1, keepdims=True)
+        at = slice(k * rows, (k + 1) * rows)
+        left, right = grad[:, :LANES], grad[:, LANES:]
+        mine_ref[at, :] = jnp.where(core == 0, left, right)
+        other_ref[at, :] = jnp.where(core == 0, right, left)
+
+    def add_counts(k, counts):
+        if grids > 1:
+            counts_ref[k] += counts
+            return
+        if resume:
+            counts = counts + counts_in[k]
+        if last:
+            centre(k, counts)
+        else:
+            counts_ref[k] = counts
+
+    second = (weights_ref, row_begin, add_counts)
 
     @pl.when(chunk == 0)
     def _():
-        if resume:
-            counts_ref[...] = counts_in[...]
-            sums_ref[...] = sums_in[...]
-        else:
+        if grids > 1:
             counts_ref[...] = jnp.zeros_like(counts_ref)
-            sums_ref[...] = jnp.zeros_like(sums_ref)
+        sums_ref[...] = sums_in[...] if resume else jnp.zeros_like(sums_ref)
 
     def add_sums(alpha_ref, other_state):
         total = jnp.zeros((1, LANES), F32)
@@ -369,10 +416,10 @@
     @pl.when(jnp.logical_not(forward_first))
     def _():
         add_sums(state_in, own_state)
-        ab_ref[...] = state_in[:states, :]
+        put_twice(ab_ref, slice(None), state_in[:states, :])
         run_forward(lead, mat, hist, sel_ref, consts, ab_ref, list(zeros), second)
         if extend:
-            put_state(state_out, ab_ref[...], zeros)
+            put_state(state_out, ab_ref[:states, :], zeros)
 
     @pl.when(forward_first)
     def _():
@@ -386,23 +433,9 @@
 
         @pl.when(chunk == grids - 1)
         def _():
-            rows = counts_ref.shape[1]
-            for k in range(steps):
-                probs = row_probs[k]
-                weighted = probs * counts_ref[k]
-                grad = weighted - probs * jnp.sum(weighted, axis=1, keepdims=True)
-                for side in range(2):
-                    piece = grad[:, side * LANES : (side + 1) * LANES]
-                    at = slice(k * rows, (k + 1) * rows)
-
-                    @pl.when(core == side)
-                    def _():
-                        mine_ref[at, :] = piece
-
-                    @pl.when(core != side)
-                    def _():
-                        other_ref[at, :] = piece
-
+            if grids > 1:
+                for k in range(steps):
+                    centre(k, counts_ref[k])
             mine_ref[steps * rows :, :] = sums_ref[...]
             other_ref[steps * rows :, :] = sums_ref[...]
 
@@ -465,17 +498,24 @@
     first_mat, second_mat, row_probs, consts = pl.pallas_call(
         prep_kernel,
         out_shape=[
-            pltpu.VMEM((steps, 2 * states + EXTRA, states), BF16),
-            pltpu.VMEM((steps, 2 * states, states), BF16),
+            pltpu.VMEM((steps, states + EXTRA, 2 * states), BF16),
+            pltpu.HBM((steps, states, 2 * states), BF16),
             pltpu.VMEM((steps, rows, states), F32),
             pltpu.VMEM((4, states, LANES), F32),
         ],
-        in_specs=[hbm(), vmem(), vmem()],
-        out_specs=[vmem()] * 4,
-        scratch_shapes=[pltpu.VMEM((states, states), F32), pltpu.VMEM(trans_logits.shape, BF16), dma],
-        compiler_params=params(4),
+        in_specs=[hbm(), hbm(), vmem()],
+        out_specs=[vmem(), hbm(), vmem(), vmem()],
+        scratch_shapes=[
+            pltpu.VMEM((steps, states, 2 * states), BF16),
+            pltpu.VMEM((states, states), F32),
+            pltpu.VMEM(trans_logits.shape, BF16),
+            pltpu.VMEM(trans_logits.shape, BF16),
+            dma((2,)),
+            dma((steps,)),
+        ],
+        compiler_params=params(6),
         name="prep",
-    )(*in_hbm(trans_logits), pltpu.with_memory_space_constraint(other_logits, pltpu.VMEM), vectors)
+    )(*in_hbm(trans_logits, other_logits), vectors)
 
     def whole(*shape):
         if grids == 1:
@@ -506,7 +546,7 @@
             in_specs=[whole(*gathered.shape), whole(*first_mat.shape), const_spec]
             + [state_spec] * resume,
             out_specs=[hist_spec, state_spec, sel_spec],
-            scratch_shapes=[pltpu.VMEM((states, width), BF16), pltpu.VMEM((states, width), F32)],
+            scratch_shapes=[pltpu.VMEM((2 * states, width), BF16), pltpu.VMEM((states, width), F32)],
             compiler_params=params(8 if grids == 1 else 32),
             name="first_pass",
         )(gathered, first_mat, consts, *([state_in] if resume else []))
@@ -515,7 +555,7 @@
         hist, own_state, sel = kept
         resume = sums_in is not None
         scratch = [
-            pltpu.VMEM((states, width), BF16),
+            pltpu.VMEM((2 * states, width), BF16),
             pltpu.VMEM((states, width), F32),
             pltpu.VMEM((rows, width), BF16),
         ]

time: 35.4 us -> 33.6 us (0.949)
  local copies, waits for them, and re-layouts: 3.15 us -> 0.79 us
  waiting for transfers between devices: 3.41 us -> 4.32 us
  Pallas kernels: 17.1 us -> 16.3 us
  starting transfers between devices: 9.88 us -> 10.3 us
    unnamed x8 -> x4, local copies, waits for them, and re-layouts: 3.15 us -> 0.79 us
    pallas_call x2, Pallas kernels: 7.1 us -> 5.39 us  [second_pass(): pl.pallas_call(functools.partial(second_kernel, resume, last, extend, gri...]
    pallas_call x1, Pallas kernels: 2.54 us -> 4.18 us  [per_device(): pl.pallas_call(prep_kernel, out_shape=[pltpu.VMEM((steps, states + EXTRA,...]
    all_to_all x1, waiting for transfers between devices: 1.45 us -> 2.17 us  [per_device(): lax.all_to_all(packed, ('hh', 'per'), split_axis=0, concat_axis=0, tiled=...]
    pallas_call x2, Pallas kernels: 5.17 us -> 4.47 us  [first_pass(): pl.pallas_call(functools.partial(first_kernel, resume, grids, index), gri...]
    ppermute x2, starting transfers between devices: 2.47 us -> 2.93 us  [hand_over(): return lax.ppermute(state, 'per', moves)]
  transfers between devices with their start and end apart: 5 -> 5, of which waited for: 4 -> 3; matrix products, arithmetic and copies ran while one was open for 0% -> 0% of each run, Pallas kernels for 28% -> 32%
where the time goes in v9:
time: 33.6 us; the launch traced here: 33.3 us
  Pallas kernels  16.3 us (49%)
  starting transfers between devices  10.3 us (31%)
  waiting for transfers between devices  4.32 us (13%)
  between operations  1.51 us (4%)
  local copies, waits for them, and re-layouts  0.79 us (2%)
    all_to_all x1, starting transfers between devices, per_device(): lax.all_to_all(packed, ('hh', 'per'), split_axis=0, concat_axis=0, tiled=...  6.82 us
    pallas_call x2, Pallas kernels, second_pass(): pl.pallas_call(functools.partial(second_kernel, resume, last, extend, gri...  5.39 us
    pallas_call x2, Pallas kernels, first_pass(): pl.pallas_call(functools.partial(first_kernel, resume, grids, index), gri...  4.47 us
    pallas_call x1, Pallas kernels, per_device(): pl.pallas_call(prep_kernel, out_shape=[pltpu.VMEM((steps, states + EXTRA,...  4.18 us
    ppermute x2, starting transfers between devices, hand_over(): return lax.ppermute(state, 'per', moves)  2.93 us
    all_to_all x1, waiting for transfers between devices, per_device(): lax.all_to_all(packed, ('hh', 'per'), split_axis=0, concat_axis=0, tiled=...  2.17 us
    pallas_call x1, Pallas kernels, per_device(): pl.pallas_call(pack_kernel, out_shape=[shaped((group, periods // 2, slot_...  1.54 us
    ppermute x1, waiting for transfers between devices, per_device(): received = lax.ppermute(other, 'st', swap)  1.53 us
  transfers between devices with their start and end apart: 5, of which 3 were waited for; matrix products, arithmetic and copies ran while one was open for 0% of the time, Pallas kernels for 32%

profile of v9, /device:TPU:0, one launch (start us, length us, event | category | flops | bytes accessed | tf_op | source)
XLA Modules:
  0.0 33.3 jit_solution(6113638576994626688)
XLA Ops:
  0.6 0.5 %collective-permute-start = (bf16[4,256,256]{2,1,0:T(8,128)(2,1)}, bf16[4,256,256]{2,1,0:T(8,128)(2,1)S(1)}, u32[]{:S(2)}, u32[]{:S(2)}) collective-permute-start(bf16[4,256,256]{2,1,0:T(8,128)(2,1)} %own_any.1), channel_id=1, source_target_pairs={{0,1},{1,0},{2,3},{3,2},{4,5},{5,4},{6,7},{7,6},{8,9},{9,8},{10,11... | collective-permute-start | bytes 1572872 | tf_op jit(solution)/shard_map/ppermute | solution.py:472
  1.8 1.5 %pack.1 = (f32[8,8,384]{2,1,0:T(8,128)}, f32[8,256]{1,0:T(8,128)S(1)}) custom-call(s32[1]{0:T(128)S(6)} %copy.10.count_ref, f32[16,384]{1,0:T(8,128)} %bitcast.7, s32[3,128]{1,0:T(4,128)} %bitcast.8, s32[3,128]{1,0:T(4,128)} %bitcast.9, f32[1,256]{1,0:T(1,128)} %bitcast.10, f32[1,256]{1,0:T(1,128)} %bitcast.11, f32[1,256]{1,0:T(1,128)} %bitcast.12), custom_call_target="tpu_custom_call" | custom-call | tf_op jit(solution)/shard_map/pack/pallas_call | solution.py:474
  3.4 6.8 %all-to-all-start = ((f32[8,8,384]{2,1,0:T(8,128)}), f32[8,8,384]{2,1,0:T(8,128)S(1)}, u32[]{:S(2)}, u32[]{:S(2)}) async-start(f32[8,8,384]{2,1,0:T(8,128)} %get-tuple-element.20), calls=%async_computation | async-start | bytes 196608 | tf_op jit(solution)/shard_map/all_to_all | solution.py:497
  10.2 0.0 collective-permute-done.other_any
  10.2 0.0 copy-start.1
  10.2 0.8 %copy-done.1 = bf16[4,256,256]{2,1,0:T(8,128)(2,1)} copy-done((bf16[4,256,256]{2,1,0:T(8,128)(2,1)}, bf16[4,256,256]{2,1,0:T(8,128)(2,1)S(1)}, u32[]{:S(2)}) %copy-start.1) | copy-done | bytes 524312
  11.0 4.2 %prep.1 = (bf16[8,272,512]{2,1,0:T(8,128)(2,1)S(1)}, bf16[8,256,512]{2,1,0:T(8,128)(2,1)}, f32[8,64,256]{2,1,0:T(8,128)S(1)}, f32[4,256,128]{2,1,0:T(8,128)S(1)}) custom-call(bf16[4,256,256]{2,1,0:T(8,128)(2,1)} %own_any.1, bf16[4,256,256]{2,1,0:T(8,128)(2,1)} %copy-done.1, f32[8,256]{1,0:T(8,128)S(1)} %get-tuple-element.21.vec_ref), custom_call_target="tpu_custom_call" | custom-call | tf_op jit(solution)/shard_map/prep/pallas_call | solution.py:498
  15.2 2.2 %all-to-all-done.rows_ref = f32[8,8,384]{2,1,0:T(8,128)S(1)} async-done(((f32[8,8,384]{2,1,0:T(8,128)}), f32[8,8,384]{2,1,0:T(8,128)S(1)}, u32[]{:S(2)}, u32[]{:S(2)}) %all-to-all-start) | async-done | bytes 98336 | tf_op jit(solution)/shard_map/all_to_all | solution.py:497
  17.3 0.0 copy-start
  17.3 2.2 %first_pass.3 = (bf16[8,256,256]{2,1,0:T(8,128)(2,1)S(1)}, bf16[272,256]{1,0:T(8,128)(2,1)S(1)}, f32[3,16,8,256]{3,2,1,0:T(8,128)S(1)}) custom-call(f32[8,8,384]{2,1,0:T(8,128)S(1)} %all-to-all-done.rows_ref, bf16[8,272,512]{2,1,0:T(8,128)(2,1)S(1)} %get-tuple-element.22.mat, f32[4,256,128]{2,1,0:T(8,128)S(1)} %get-tuple-element.23.consts.refs_2_), custom_call_target="tpu_custom_call" | custom-call | tf_op jit(solution)/shard_map/first_pass/pallas_call | solution.py:542
  19.6 1.1 %collective-permute-start.2 = (bf16[272,256]{1,0:T(8,128)(2,1)S(1)}, bf16[272,256]{1,0:T(8,128)(2,1)S(1)}, u32[]{:S(2)}, u32[]{:S(2)}) collective-permute-start(bf16[272,256]{1,0:T(8,128)(2,1)S(1)} %get-tuple-element.30.refs_4_), channel_id=1, source_target_pairs={{0,2},{2,0},{1,3},{3,1},{4,6},{6,4},{5,7},{7,5},{8,10},{10,8},{9,1... | collective-permute-start | bytes 417800 | tf_op jit(solution)/shard_map/ppermute | solution.py:590
  20.7 2.2 %first_pass.2 = (bf16[8,256,256]{2,1,0:T(8,128)(2,1)S(1)}, bf16[272,256]{1,0:T(8,128)(2,1)S(1)}, f32[3,16,8,256]{3,2,1,0:T(8,128)S(1)}) custom-call(f32[8,8,384]{2,1,0:T(8,128)S(1)} %all-to-all-done.rows_ref, bf16[8,272,512]{2,1,0:T(8,128)(2,1)S(1)} %get-tuple-element.22.mat, f32[4,256,128]{2,1,0:T(8,128)S(1)} %get-tuple-element.23.consts.refs_2_), custom_call_target="tpu_custom_call" | custom-call | tf_op jit(solution)/shard_map/first_pass/pallas_call | solution.py:542
  23.0 1.8 %collective-permute-start.1 = (bf16[272,256]{1,0:T(8,128)(2,1)S(1)}, bf16[272,256]{1,0:T(8,128)(2,1)S(1)}, u32[]{:S(2)}, u32[]{:S(2)}) collective-permute-start(bf16[272,256]{1,0:T(8,128)(2,1)S(1)} %get-tuple-element.27.refs_4_), channel_id=1, source_target_pairs={{0,2},{2,0},{1,3},{3,1},{4,6},{6,4},{5,7},{7,5},{8,10},{10,8},{9,1... | collective-permute-start | bytes 417800 | tf_op jit(solution)/shard_map/ppermute | solution.py:590
  24.8 0.0 collective-permute-done.2.refs_5_
  24.8 0.0 copy-done
  24.8 2.7 %second_pass.2 = (f32[8,64,256]{2,1,0:T(8,128)S(1)}, f32[8,128]{1,0:T(8,128)S(1)}) custom-call(f32[3,16,8,256]{3,2,1,0:T(8,128)S(1)} %get-tuple-element.28.refs_0_, bf16[8,256,512]{2,1,0:T(8,128)(2,1)S(1)} %copy-done, f32[4,256,128]{2,1,0:T(8,128)S(1)} %get-tuple-element.23.consts.refs_2_, bf16[8,256,256]{2,1,0:T(8,128)(2,1)S(1)} %get-tuple-element.29.refs_3_, ...), custom_call_target="tpu_custom_call" | custom-call | tf_op jit(solution)/shard_map/second_pass/pallas_call | solution.py:571
  27.5 0.6 %collective-permute-done.1.refs_5_ = bf16[272,256]{1,0:T(8,128)(2,1)S(1)} collective-permute-done((bf16[272,256]{1,0:T(8,128)(2,1)S(1)}, bf16[272,256]{1,0:T(8,128)(2,1)S(1)}, u32[]{:S(2)}, u32[]{:S(2)}) %collective-permute-start.1) | collective-permute-done | bytes 139296 | tf_op jit(solution)/shard_map/ppermute | solution.py:590
  28.1 2.7 %second_pass.3 = (f32[520,128]{1,0:T(8,128)S(1)}, f32[520,128]{1,0:T(8,128)S(1)}) custom-call(f32[3,16,8,256]{3,2,1,0:T(8,128)S(1)} %get-tuple-element.24.refs_0_, bf16[8,256,512]{2,1,0:T(8,128)(2,1)S(1)} %copy-done, f32[4,256,128]{2,1,0:T(8,128)S(1)} %get-tuple-element.23.consts.refs_2_, bf16[8,256,256]{2,1,0:T(8,128)(2,1)S(1)} %get-tuple-element.26.refs_3_, ...), custom_call_target="tpu_custom_call" | custom-call | tf_op jit(solution)/shard_map/second_pass/pallas_call | solution.py:571
  30.8 0.1 collective-permute-start.3
  30.9 1.5 %collective-permute-done.3.other_ref = f32[520,128]{1,0:T(8,128)S(1)} collective-permute-done((f32[520,128]{1,0:T(8,128)S(1)}, f32[520,128]{1,0:T(8,128)S(1)}, u32[]{:S(2)}, u32[]{:S(2)}) %collective-permute-start.3) | collective-permute-done | bytes 266272 | tf_op jit(solution)/shard_map/ppermute | solution.py:626
  32.4 0.8 %finish.1 = (f32[512,128]{1,0:T(8,128)}, f32[1]{0:T(128)}) custom-call(f32[520,128]{1,0:T(8,128)S(1)} %get-tuple-element.34.mine_ref, f32[520,128]{1,0:T(8,128)S(1)} %collective-permute-done.3.other_ref), custom_call_target="tpu_custom_call" | custom-call | tf_op jit(solution)/shard_map/finish/pallas_call | solution.py:627
Async XLA Ops:
  0.6 9.5 %collective-permute-start = (bf16[4,256,256]{2,1,0:T(8,128)(2,1)}, bf16[4,256,256]{2,1,0:T(8,128)(2,1)S(1)}, u32[]{:S(2)}, u32[]{:S(2)}) collective-permute-start(bf16[4,256,256]{2,1,0:T(8,128)(2,1)} %own_any.1), channel_id=1, source_target_pairs={{0,1},{1,0},{2,3},{3,2},{4,5},{5,4},{6,7},{7,6},{8,9},{9,8},{10,11... | collective-permute-start | bytes 1572872 | tf_op jit(solution)/shard_map/ppermute | solution.py:472
  3.4 14.0 %all-to-all-start = ((f32[8,8,384]{2,1,0:T(8,128)}), f32[8,8,384]{2,1,0:T(8,128)S(1)}, u32[]{:S(2)}, u32[]{:S(2)}) async-start(f32[8,8,384]{2,1,0:T(8,128)} %get-tuple-element.20), calls=%async_computation | async-start | bytes 196608 | tf_op jit(solution)/shard_map/all_to_all | solution.py:497
  10.2 0.8 %copy-start.1 = (bf16[4,256,256]{2,1,0:T(8,128)(2,1)}, bf16[4,256,256]{2,1,0:T(8,128)(2,1)S(1)}, u32[]{:S(2)}) copy-start(bf16[4,256,256]{2,1,0:T(8,128)(2,1)S(1)} %collective-permute-done.other_any) | copy-start | bytes 1572868
  17.3 7.4 %copy-start = (bf16[8,256,512]{2,1,0:T(8,128)(2,1)S(1)}, bf16[8,256,512]{2,1,0:T(8,128)(2,1)}, u32[]{:S(2)}) copy-start(bf16[8,256,512]{2,1,0:T(8,128)(2,1)} %get-tuple-element.25.refs_1_) | copy-start | bytes 6291460
  19.6 5.2 %collective-permute-start.2 = (bf16[272,256]{1,0:T(8,128)(2,1)S(1)}, bf16[272,256]{1,0:T(8,128)(2,1)S(1)}, u32[]{:S(2)}, u32[]{:S(2)}) collective-permute-start(bf16[272,256]{1,0:T(8,128)(2,1)S(1)} %get-tuple-element.30.refs_4_), channel_id=1, source_target_pairs={{0,2},{2,0},{1,3},{3,1},{4,6},{6,4},{5,7},{7,5},{8,10},{10,8},{9,1... | collective-permute-start | bytes 417800 | tf_op jit(solution)/shard_map/ppermute | solution.py:590
  23.0 5.1 %collective-permute-start.1 = (bf16[272,256]{1,0:T(8,128)(2,1)S(1)}, bf16[272,256]{1,0:T(8,128)(2,1)S(1)}, u32[]{:S(2)}, u32[]{:S(2)}) collective-permute-start(bf16[272,256]{1,0:T(8,128)(2,1)S(1)} %get-tuple-element.27.refs_4_), channel_id=1, source_target_pairs={{0,2},{2,0},{1,3},{3,1},{4,6},{6,4},{5,7},{7,5},{8,10},{10,8},{9,1... | collective-permute-start | bytes 417800 | tf_op jit(solution)/shard_map/ppermute | solution.py:590
  30.8 1.6 %collective-permute-start.3 = (f32[520,128]{1,0:T(8,128)S(1)}, f32[520,128]{1,0:T(8,128)S(1)}, u32[]{:S(2)}, u32[]{:S(2)}) collective-permute-start(f32[520,128]{1,0:T(8,128)S(1)} %get-tuple-element.35), channel_id=1, source_target_pairs={{0,1},{1,0},{2,3},{3,2},{4,5},{5,4},{6,7},{7,6},{8,9},{9,8},{10,11... | collective-permute-start | bytes 798728 | tf_op jit(solution)/shard_map/ppermute | solution.py:626

commit v10 on v9

--- a/solution.py
+++ b/solution.py
@@ -59,13 +59,13 @@
 
 
 def pack_kernel(
-    count_ref, earn_any, start_any, len_any, init_any, mean_any, sd_any, out_ref, vec_ref,
+    count_ref, earn_any, start_any, len_any, init_any, mean_any, sd_any, own_any, out_ref, vec_ref, own_ref,
     earn_ref, start_ref, len_ref, init_ref, mean_ref, sd_ref, sems,
 ):
     fetch(
         (
             (earn_any, earn_ref), (start_any, start_ref), (len_any, len_ref),
-            (init_any, init_ref), (mean_any, mean_ref), (sd_any, sd_ref),
+            (init_any, init_ref), (mean_any, mean_ref), (sd_any, sd_ref), (own_any, own_ref),
         ),
         sems,
     )
@@ -109,15 +109,11 @@
 
 
 def prep_kernel(
-    own_any, other_any, vec_ref, first_mat, second_any, row_probs, consts,
-    second_mat, scratch, own_ref, other_ref, sems, out_sems,
+    own_ref, other_any, vec_ref, first_mat, second_any, row_probs, consts,
+    second_mat, scratch, other_ref, sem, out_sems,
 ):
-    copies = [
-        pltpu.make_async_copy(src, dst, sems.at[i])
-        for i, (src, dst) in enumerate(((own_any, own_ref), (other_any, other_ref)))
-    ]
-    for copy in copies:
-        copy.start()
+    copy = pltpu.make_async_copy(other_any, other_ref, sem)
+    copy.start()
     part, states, _ = own_ref.shape
 
     def leave(at):
@@ -126,14 +122,9 @@
     rows = row_probs.shape[1]
     for i in range(4):
         consts[i] = jnp.broadcast_to(vec_ref[i : i + 1, :], (LANES, states)).T
-    start = vec_ref[:1, :]
-    start_high = start.astype(BF16).astype(F32)
-    row = lax.broadcasted_iota(jnp.int32, (EXTRA, states), 0)
-    for k in range(first_mat.shape[0]):
-        first_mat[k, states:, :states] = jnp.where(row == 0, start_high, 0.0).astype(BF16)
-        first_mat[k, states:, states:] = jnp.where(row == 0, start - start_high, 0.0).astype(BF16)
-    for copy, source, ref in zip(copies, (core_index(), 1 - core_index()), (own_ref, other_ref)):
-        copy.wait()
+    for source, ref in ((core_index(), own_ref), (1 - core_index(), other_ref)):
+        if ref is other_ref:
+            copy.wait()
 
         @pl.loop(0, part)
         def _(i):
@@ -159,11 +150,11 @@
         leave(at).wait()
 
 
-def emission(sel_ref, consts, step_now, cols):
+def emission(sel_ref, consts, step_now, cols, less):
     gap = sel_ref[0, step_now, :1, cols] - consts[1]
     power = gap * gap * consts[2] + consts[3]
     top = jnp.max(power, axis=0, keepdims=True)
-    return jnp.exp2(power - top), top
+    return jnp.exp2(power - (top + less)), top
 
 
 def is_moving(sel_ref, step_now, cols):
@@ -189,7 +180,7 @@
 def run_forward(lead, mat, hist, sel_ref, consts, ab_ref, logs, second=None):
     steps, states, width = hist.shape
     cuts = tiles(width)
-    inverse = [1.0 / column_sum(ab_ref[:states, cols].astype(F32)) for cols in cuts]
+    size = [jnp.log2(column_sum(ab_ref[:states, cols].astype(F32))) for cols in cuts]
     for k in range(steps):
         step_now = lead + k
         if second is None:
@@ -198,41 +189,45 @@
             weights_ref, row_begin, add_counts = second
             own_alpha = ab_ref[own_rows(row_begin, weights_ref.shape[0]), :].astype(F32)
         for q, cols in enumerate(cuts):
-            moved = jnp.dot(mat[k, :states, :], ab_ref[:, cols], preferred_element_type=F32) * inverse[q]
+            product = jnp.dot(mat[k], ab_ref[:, cols], preferred_element_type=F32)
             moving = is_moving(sel_ref, step_now, cols)
             if second is not None:
-                total = column_sum(moved * hist[k, :, cols].astype(F32))
-                weight = jnp.where(moving, inverse[q] / total, 0.0)
+                total = column_sum(product * hist[k, :, cols].astype(F32))
+                weight = jnp.where(moving, 1.0 / total, 0.0)
                 weights_ref[:, cols] = (own_alpha[:, cols] * weight).astype(BF16)
-            emit, top = emission(sel_ref, consts, step_now, cols)
-            joint = jnp.where(moving, moved, consts[0]) * emit
-            scale = column_sum(joint)
+            emit, top = emission(sel_ref, consts, step_now, cols, jnp.where(moving, size[q], 0.0))
+            joint = jnp.where(moving, product, consts[0]) * emit
+            put_twice(ab_ref, cols, joint)
+            size[q] = jnp.log2(column_sum(joint))
             if second is None:
                 seen = is_seen(sel_ref, step_now, cols)
-                logs[q] = logs[q] + jnp.where(seen, jnp.log(scale) + top * LN2, 0.0)
-            inverse[q] = 1.0 / scale
-            put_twice(ab_ref, cols, joint)
+                logs[q] = logs[q] + jnp.where(seen, size[q] + top, 0.0)
         if second is not None:
             add_counts(k, outer_sum(weights_ref, hist[k]))
     return logs
 
 
-def run_backward(lead, mat, hist, sel_ref, consts, back_ref, ub_ref, logs, second=None):
+def run_backward(lead, mat, hist, sel_ref, consts, state, ub_ref, logs, leave, second=None):
     steps, states, width = hist.shape
     cuts = tiles(width)
+    rest = [x[:1] for x in state]
+    size = [jnp.zeros((1, LANES), F32) for _ in cuts]
 
     def step(k):
         step_now = lead + k
-        shrink = []
+        grown = []
         for q, cols in enumerate(cuts):
-            emit, top = emission(sel_ref, consts, step_now, cols)
-            carried = emit * back_ref[:, cols]
-            size = column_sum(carried)
+            emit, top = emission(sel_ref, consts, step_now, cols, size[q])
+            carried = emit * state[q]
+            put_twice(ub_ref, cols, carried)
+            whole = column_sum(carried)
+            grown.append(whole)
+            size[q] = jnp.log2(whole)
             if second is None:
                 seen = is_seen(sel_ref, step_now, cols)
-                logs[q] = logs[q] + jnp.where(seen, jnp.log(size) + top * LN2, 0.0)
-            shrink.append(1.0 / size)
-            put_twice(ub_ref, cols, carried)
+                logs[q] = logs[q] + jnp.where(seen, size[q] + top, 0.0)
+                begun = column_sum(carried * consts[0]) / whole
+                rest[q] = jnp.where(seen, begun, rest[q])
         if second is None:
             hist[k] = ub_ref[:states, :]
         else:
@@ -241,37 +236,41 @@
         for q, cols in enumerate(cuts):
             product = jnp.dot(mat[k], ub_ref[:, cols], preferred_element_type=F32)
             moving = is_moving(sel_ref, step_now, cols)
-            pulled = product[:states] * shrink[q]
-            if second is None:
-                seen = is_seen(sel_ref, step_now, cols)
-                begun = product[states : states + 1] * shrink[q]
-                rest = jnp.where(seen, begun, back_ref[:, cols])
-            else:
-                total = column_sum(pulled * hist[k, :, cols].astype(F32))
-                weight = jnp.where(moving, shrink[q] / total, 0.0)
+            if second is not None:
+                total = column_sum(product * hist[k, :, cols].astype(F32))
+                weight = jnp.where(moving, 1.0 / total, 0.0)
                 weights_ref[:, cols] = (own_alpha[:, cols] * weight).astype(BF16)
-                rest = 1.0
-            back_ref[:, cols] = jnp.where(moving, pulled, rest)
+            state[q] = jnp.where(moving, product, rest[q] * grown[q])
         if second is not None:
             add_counts(k, outer_sum(weights_ref, ub_ref[:states, :]))
+
+    def left():
+        return [x * jnp.exp2(-y) for x, y in zip(state, size)]
 
     for k in reversed(range(1, steps)):
         step(k)
     if second is None:
         step(0)
-    else:
-        pl.when(lead > 0)(lambda: step(0))
-        pl.when(lead == 0)(lambda: second[2](0, jnp.zeros((second[0].shape[0], states), F32)))
-    return logs
+        leave(left())
+        return
+
+    @pl.when(lead > 0)
+    def _():
+        step(0)
+        leave(left())
+
+    @pl.when(lead == 0)
+    def _():
+        second[2](0, jnp.zeros((second[0].shape[0], states), F32))
 
 
 def put_state(state_out, values, logs):
     states = state_out.shape[0] - EXTRA
-    state_out[:states, :] = values
+    row = lax.broadcasted_iota(jnp.int32, (EXTRA, LANES), 0)
     for q, cols in enumerate(tiles(state_out.shape[1])):
+        state_out[:states, cols] = values[q].astype(BF16)
         high = logs[q].astype(BF16).astype(F32)
         middle = (logs[q] - high).astype(BF16).astype(F32)
-        row = lax.broadcasted_iota(jnp.int32, (EXTRA, LANES), 0)
         piece = jnp.where(
             row == 0, high, jnp.where(row == 1, middle, jnp.where(row == 2, logs[q] - high - middle, 0.0))
         )
@@ -285,7 +284,7 @@
 
 def first_kernel(resume, grids, part, rows_ref, mat, consts, *refs):
     state_in = refs[0] if resume else None
-    hist, state_out, sel_ref, ab_ref, back_ref = refs[-5:]
+    hist, state_out, sel_ref, ab_ref = refs[-4:]
     chunk = part * grids + (pl.program_id(0) if grids > 1 else 0)
     steps, states, width = hist.shape
     forward_first, lead = is_forward_first(), lax.axis_index("per") * steps
@@ -339,18 +338,17 @@
             for cols in cuts:
                 put_twice(ab_ref, cols, consts[0])
         logs = state_logs(state_in) if resume else list(zeros)
-        logs = run_forward(lead, mat, hist, sel_ref, consts, ab_ref, logs)
-        put_state(state_out, ab_ref[:states, :], logs)
+        run_forward(lead, mat, hist, sel_ref, consts, ab_ref, logs)
+        put_state(state_out, [ab_ref[:states, cols] for cols in cuts], logs)
 
     @pl.when(jnp.logical_not(forward_first))
     def _():
-        if resume:
-            back_ref[...] = state_in[:states, :].astype(F32)
-        else:
-            back_ref[...] = jnp.ones_like(back_ref)
+        state = [
+            state_in[:states, cols].astype(F32) if resume else jnp.ones((states, LANES), F32) for cols in cuts
+        ]
         logs = state_logs(state_in) if resume else list(zeros)
-        logs = run_backward(lead, mat, hist, sel_ref, consts, back_ref, ab_ref, logs)
-        put_state(state_out, back_ref[...].astype(BF16), logs)
+        leave = lambda values: put_state(state_out, values, logs)
+        run_backward(lead, mat, hist, sel_ref, consts, state, ab_ref, logs, leave)
 
 
 def second_kernel(resume, last, extend, grids, *refs):
@@ -361,8 +359,8 @@
     mine_ref, other_ref = (refs.pop(0), refs.pop(0)) if last else (None, None)
     counts_out, sums_out = (None, None) if last else (refs.pop(0), refs.pop(0))
     state_out = refs.pop(0) if extend else None
-    ab_ref, back_ref, weights_ref = refs[:3]
-    counts_ref, sums_ref = refs[3:] if last else (counts_out, sums_out)
+    ab_ref, weights_ref = refs[:2]
+    counts_ref, sums_ref = refs[2:] if last else (counts_out, sums_out)
     chunk = pl.program_id(0) if grids > 1 else 0
     steps, states, width = hist.shape
     core, forward_first = core_index(), is_forward_first()
@@ -404,7 +402,7 @@
         for cols, here, there in zip(tiles(width), state_logs(alpha_ref), state_logs(other_state)):
             alpha = alpha_ref[:states, cols].astype(F32)
             meet = column_sum(alpha * other_state[:states, cols].astype(F32))
-            total += here + there + jnp.log(meet / column_sum(alpha))
+            total += (here + there + jnp.log2(meet / column_sum(alpha))) * LN2
             years += jnp.sum(sel_ref[2, :, :, cols], axis=0)
         total = jnp.broadcast_to(jnp.sum(total, axis=1, keepdims=True), (1, LANES))
         years = jnp.broadcast_to(jnp.sum(years[:1], axis=1, keepdims=True), (1, LANES))
@@ -419,15 +417,14 @@
         put_twice(ab_ref, slice(None), state_in[:states, :])
         run_forward(lead, mat, hist, sel_ref, consts, ab_ref, list(zeros), second)
         if extend:
-            put_state(state_out, ab_ref[:states, :], zeros)
+            put_state(state_out, [ab_ref[:states, cols] for cols in tiles(width)], zeros)
 
     @pl.when(forward_first)
     def _():
         add_sums(own_state, state_in)
-        back_ref[...] = state_in[:states, :].astype(F32)
-        run_backward(lead, mat, hist, sel_ref, consts, back_ref, ab_ref, list(zeros), second)
-        if extend:
-            put_state(state_out, back_ref[...].astype(BF16), zeros)
+        state = [state_in[:states, cols].astype(F32) for cols in tiles(width)]
+        leave = lambda values: put_state(state_out, values, zeros) if extend else None
+        run_backward(lead, mat, hist, sel_ref, consts, state, ab_ref, list(zeros), leave, second)
 
     if last:
 
@@ -471,11 +468,15 @@
     swap = [(0, 1), (1, 0)]
     other_logits = lax.ppermute(trans_logits, "st", swap)
     vec_row = pltpu.VMEM((1, states), F32)
-    packed, vectors = pl.pallas_call(
+    packed, vectors, own_logits = pl.pallas_call(
         pack_kernel,
-        out_shape=[shaped((group, periods // 2, slot_rows), F32), shaped((8, states), F32)],
-        in_specs=[smem()] + [hbm()] * 6,
-        out_specs=[vmem()] * 2,
+        out_shape=[
+            shaped((group, periods // 2, slot_rows), F32),
+            shaped((8, states), F32),
+            pltpu.VMEM(trans_logits.shape, BF16),
+        ],
+        in_specs=[smem()] + [hbm()] * 7,
+        out_specs=[vmem()] * 3,
         scratch_shapes=[
             pltpu.VMEM((periods, slot_rows), F32),
             pltpu.VMEM((slot_rows // HB, HB), jnp.int32),
@@ -483,7 +484,7 @@
             vec_row,
             vec_row,
             vec_row,
-            dma((6,)),
+            dma((7,)),
         ],
         compiler_params=params(2),
         name="pack",
@@ -491,31 +492,30 @@
         block_count,
         *in_hbm(
             earnings.T, starts.reshape(-1, HB), lengths.reshape(-1, HB),
-            init_logits.reshape(1, states), state_mean.reshape(1, states), log_sd.reshape(1, states),
+            init_logits.reshape(1, states), state_mean.reshape(1, states), log_sd.reshape(1, states), trans_logits,
         ),
     )
     gathered = lax.all_to_all(packed, ("hh", "per"), split_axis=0, concat_axis=0, tiled=True)
     first_mat, second_mat, row_probs, consts = pl.pallas_call(
         prep_kernel,
         out_shape=[
-            pltpu.VMEM((steps, states + EXTRA, 2 * states), BF16),
+            pltpu.VMEM((steps, states, 2 * states), BF16),
             pltpu.HBM((steps, states, 2 * states), BF16),
             pltpu.VMEM((steps, rows, states), F32),
             pltpu.VMEM((4, states, LANES), F32),
         ],
-        in_specs=[hbm(), hbm(), vmem()],
+        in_specs=[vmem(), hbm(), vmem()],
         out_specs=[vmem(), hbm(), vmem(), vmem()],
         scratch_shapes=[
             pltpu.VMEM((steps, states, 2 * states), BF16),
             pltpu.VMEM((states, states), F32),
             pltpu.VMEM(trans_logits.shape, BF16),
-            pltpu.VMEM(trans_logits.shape, BF16),
-            dma((2,)),
+            dma,
             dma((steps,)),
         ],
         compiler_params=params(6),
         name="prep",
-    )(*in_hbm(trans_logits, other_logits), vectors)
+    )(own_logits, *in_hbm(other_logits), vectors)
 
     def whole(*shape):
         if grids == 1:
@@ -546,7 +546,7 @@
             in_specs=[whole(*gathered.shape), whole(*first_mat.shape), const_spec]
             + [state_spec] * resume,
             out_specs=[hist_spec, state_spec, sel_spec],
-            scratch_shapes=[pltpu.VMEM((2 * states, width), BF16), pltpu.VMEM((states, width), F32)],
+            scratch_shapes=[pltpu.VMEM((2 * states, width), BF16)],
             compiler_params=params(8 if grids == 1 else 32),
             name="first_pass",
         )(gathered, first_mat, consts, *([state_in] if resume else []))
@@ -556,7 +556,6 @@
         resume = sums_in is not None
         scratch = [
             pltpu.VMEM((2 * states, width), BF16),
-            pltpu.VMEM((states, width), F32),
             pltpu.VMEM((rows, width), BF16),
         ]
         counts_spec, sums_spec = whole(*counts_shape.shape), whole(*sums_shape.shape)

time: 33.6 us -> 34.7 us (1.033)
  local copies, waits for them, and re-layouts: 0.79 us -> 2.64 us
  starting transfers between devices: 10.3 us -> 9.55 us
    unnamed x4 -> x8, local copies, waits for them, and re-layouts: 0.79 us -> 2.64 us
    pallas_call x1, Pallas kernels: 4.18 us -> 3.31 us  [per_device(): pl.pallas_call(prep_kernel, out_shape=[pltpu.VMEM((steps, states, 2 * sta...]
    ppermute x2, starting transfers between devices: 2.93 us -> 2.16 us  [hand_over(): return lax.ppermute(state, 'per', moves)]
    ppermute x2, waiting for transfers between devices: 0.62 us -> 1.01 us  [hand_over(): return lax.ppermute(state, 'per', moves)]
    pallas_call x1, Pallas kernels: 1.54 us -> 1.93 us  [per_device(): pl.pallas_call(pack_kernel, out_shape=[shaped((group, periods // 2, slot_...]
  transfers between devices with their start and end apart: 5 -> 5, of which waited for: 3 -> 3; matrix products, arithmetic and copies ran while one was open for 0% -> 0% of each run, Pallas kernels for 32% -> 30%
where the time goes in v10:
time: 34.7 us; the launch traced here: 34.4 us
  Pallas kernels  16.1 us (46%)
  starting transfers between devices  9.55 us (28%)
  waiting for transfers between devices  4.52 us (13%)
  local copies, waits for them, and re-layouts  2.64 us (8%)
  between operations  1.53 us (4%)
    all_to_all x1, starting transfers between devices, per_device(): lax.all_to_all(packed, ('hh', 'per'), split_axis=0, concat_axis=0, tiled=...  6.81 us
    pallas_call x2, Pallas kernels, second_pass(): pl.pallas_call(functools.partial(second_kernel, resume, last, extend, gri...  5.51 us
    pallas_call x2, Pallas kernels, first_pass(): pl.pallas_call(functools.partial(first_kernel, resume, grids, index), gri...  4.63 us
    pallas_call x1, Pallas kernels, per_device(): pl.pallas_call(prep_kernel, out_shape=[pltpu.VMEM((steps, states, 2 * sta...  3.31 us
    unnamed x8, local copies, waits for them, and re-layouts  2.64 us
    ppermute x2, starting transfers between devices, hand_over(): return lax.ppermute(state, 'per', moves)  2.16 us
    all_to_all x1, waiting for transfers between devices, per_device(): lax.all_to_all(packed, ('hh', 'per'), split_axis=0, concat_axis=0, tiled=...  1.98 us
    pallas_call x1, Pallas kernels, per_device(): pl.pallas_call(pack_kernel, out_shape=[shaped((group, periods // 2, slot_...  1.93 us
  transfers between devices with their start and end apart: 5, of which 3 were waited for; matrix products, arithmetic and copies ran while one was open for 0% of the time, Pallas kernels for 30%

profile of v10, /device:TPU:0, one launch (start us, length us, event | category | flops | bytes accessed | tf_op | source)
XLA Modules:
  0.0 34.4 jit_solution(6512081520591757778)
XLA Ops:
  0.6 0.5 %collective-permute-start = (bf16[4,256,256]{2,1,0:T(8,128)(2,1)}, bf16[4,256,256]{2,1,0:T(8,128)(2,1)S(1)}, u32[]{:S(2)}, u32[]{:S(2)}) collective-permute-start(bf16[4,256,256]{2,1,0:T(8,128)(2,1)} %own_any.1), channel_id=1, source_target_pairs={{0,1},{1,0},{2,3},{3,2},{4,5},{5,4},{6,7},{7,6},{8,9},{9,8},{10,11... | collective-permute-start | bytes 1572872 | tf_op jit(solution)/shard_map/ppermute | solution.py:469
  1.8 1.9 %pack.1 = (f32[8,8,384]{2,1,0:T(8,128)}, f32[8,256]{1,0:T(8,128)S(1)}, bf16[4,256,256]{2,1,0:T(8,128)(2,1)S(1)}) custom-call(s32[1]{0:T(128)S(6)} %copy.10.count_ref, f32[16,384]{1,0:T(8,128)} %bitcast.7, s32[3,128]{1,0:T(4,128)} %bitcast.8, s32[3,128]{1,0:T(4,128)} %bitcast.9, f32[1,256]{1,0:T(1,128)} %bitcast.10, f32[1,256]{1,0:T(1,128)} %bitcast.11, ...), custom_call_target="tpu_custom_call" | custom-call | tf_op jit(solution)/shard_map/pack/pallas_call | solution.py:471
  3.7 0.0 copy-start.1
  3.8 0.8 %copy-done.1 = bf16[4,256,256]{2,1,0:T(8,128)(2,1)} copy-done((bf16[4,256,256]{2,1,0:T(8,128)(2,1)}, bf16[4,256,256]{2,1,0:T(8,128)(2,1)S(1)}, u32[]{:S(2)}) %copy-start.1) | copy-done | bytes 524312
  4.5 6.8 %all-to-all-start = ((f32[8,8,384]{2,1,0:T(8,128)}), f32[8,8,384]{2,1,0:T(8,128)S(1)}, u32[]{:S(2)}, u32[]{:S(2)}) async-start(f32[8,8,384]{2,1,0:T(8,128)} %get-tuple-element.21), calls=%async_computation | async-start | bytes 196608 | tf_op jit(solution)/shard_map/all_to_all | solution.py:498
  11.3 0.0 collective-permute-done.other_any
  11.3 0.0 copy-start.3
  11.4 0.8 %copy-done.3 = bf16[4,256,256]{2,1,0:T(8,128)(2,1)} copy-done((bf16[4,256,256]{2,1,0:T(8,128)(2,1)}, bf16[4,256,256]{2,1,0:T(8,128)(2,1)S(1)}, u32[]{:S(2)}) %copy-start.3) | copy-done | bytes 524312
  12.2 0.0 copy-start.2
  12.2 1.0 %copy-done.2 = bf16[4,256,256]{2,1,0:T(8,128)(2,1)S(1)} copy-done((bf16[4,256,256]{2,1,0:T(8,128)(2,1)S(1)}, bf16[4,256,256]{2,1,0:T(8,128)(2,1)}, u32[]{:S(2)}) %copy-start.2) | copy-done | bytes 524312
  13.2 3.3 %prep.1 = (bf16[8,256,512]{2,1,0:T(8,128)(2,1)S(1)}, bf16[8,256,512]{2,1,0:T(8,128)(2,1)}, f32[8,64,256]{2,1,0:T(8,128)S(1)}, f32[4,256,128]{2,1,0:T(8,128)S(1)}) custom-call(bf16[4,256,256]{2,1,0:T(8,128)(2,1)S(1)} %copy-done.2, bf16[4,256,256]{2,1,0:T(8,128)(2,1)} %copy-done.3, f32[8,256]{1,0:T(8,128)S(1)} %get-tuple-element.23.vec_ref), custom_call_target="tpu_custom_call" | custom-call | tf_op jit(solution)/shard_map/prep/pallas_call | solution.py:499
  16.5 2.0 %all-to-all-done.rows_ref = f32[8,8,384]{2,1,0:T(8,128)S(1)} async-done(((f32[8,8,384]{2,1,0:T(8,128)}), f32[8,8,384]{2,1,0:T(8,128)S(1)}, u32[]{:S(2)}, u32[]{:S(2)}) %all-to-all-start) | async-done | bytes 98336 | tf_op jit(solution)/shard_map/all_to_all | solution.py:498
  18.5 0.0 copy-start
  18.5 2.3 %first_pass.3 = (bf16[8,256,256]{2,1,0:T(8,128)(2,1)S(1)}, bf16[272,256]{1,0:T(8,128)(2,1)S(1)}, f32[3,16,8,256]{3,2,1,0:T(8,128)S(1)}) custom-call(f32[8,8,384]{2,1,0:T(8,128)S(1)} %all-to-all-done.rows_ref, bf16[8,256,512]{2,1,0:T(8,128)(2,1)S(1)} %get-tuple-element.24.mat, f32[4,256,128]{2,1,0:T(8,128)S(1)} %get-tuple-element.25.consts.refs_2_), custom_call_target="tpu_custom_call" | custom-call | tf_op jit(solution)/shard_map/first_pass/pallas_call | solution.py:542
  20.8 0.4 %collective-permute-start.2 = (bf16[272,256]{1,0:T(8,128)(2,1)S(1)}, bf16[272,256]{1,0:T(8,128)(2,1)S(1)}, u32[]{:S(2)}, u32[]{:S(2)}) collective-permute-start(bf16[272,256]{1,0:T(8,128)(2,1)S(1)} %get-tuple-element.32.refs_4_), channel_id=1, source_target_pairs={{0,2},{2,0},{1,3},{3,1},{4,6},{6,4},{5,7},{7,5},{8,10},{10,8},{9,1... | collective-permute-start | bytes 417800 | tf_op jit(solution)/shard_map/ppermute | solution.py:589
  21.2 2.3 %first_pass.2 = (bf16[8,256,256]{2,1,0:T(8,128)(2,1)S(1)}, bf16[272,256]{1,0:T(8,128)(2,1)S(1)}, f32[3,16,8,256]{3,2,1,0:T(8,128)S(1)}) custom-call(f32[8,8,384]{2,1,0:T(8,128)S(1)} %all-to-all-done.rows_ref, bf16[8,256,512]{2,1,0:T(8,128)(2,1)S(1)} %get-tuple-element.24.mat, f32[4,256,128]{2,1,0:T(8,128)S(1)} %get-tuple-element.25.consts.refs_2_), custom_call_target="tpu_custom_call" | custom-call | tf_op jit(solution)/shard_map/first_pass/pallas_call | solution.py:542
  23.6 1.8 %collective-permute-start.1 = (bf16[272,256]{1,0:T(8,128)(2,1)S(1)}, bf16[272,256]{1,0:T(8,128)(2,1)S(1)}, u32[]{:S(2)}, u32[]{:S(2)}) collective-permute-start(bf16[272,256]{1,0:T(8,128)(2,1)S(1)} %get-tuple-element.29.refs_4_), channel_id=1, source_target_pairs={{0,2},{2,0},{1,3},{3,1},{4,6},{6,4},{5,7},{7,5},{8,10},{10,8},{9,1... | collective-permute-start | bytes 417800 | tf_op jit(solution)/shard_map/ppermute | solution.py:589
  25.3 1.0 %collective-permute-done.2.refs_5_ = bf16[272,256]{1,0:T(8,128)(2,1)S(1)} collective-permute-done((bf16[272,256]{1,0:T(8,128)(2,1)S(1)}, bf16[272,256]{1,0:T(8,128)(2,1)S(1)}, u32[]{:S(2)}, u32[]{:S(2)}) %collective-permute-start.2) | collective-permute-done | bytes 139296 | tf_op jit(solution)/shard_map/ppermute | solution.py:589
  26.3 0.0 copy-done
  26.3 2.8 %second_pass.2 = (f32[8,64,256]{2,1,0:T(8,128)S(1)}, f32[8,128]{1,0:T(8,128)S(1)}) custom-call(f32[3,16,8,256]{3,2,1,0:T(8,128)S(1)} %get-tuple-element.30.refs_0_, bf16[8,256,512]{2,1,0:T(8,128)(2,1)S(1)} %copy-done, f32[4,256,128]{2,1,0:T(8,128)S(1)} %get-tuple-element.25.consts.refs_2_, bf16[8,256,256]{2,1,0:T(8,128)(2,1)S(1)} %get-tuple-element.31.refs_3_, ...), custom_call_target="tpu_custom_call" | custom-call | tf_op jit(solution)/shard_map/second_pass/pallas_call | solution.py:570
  29.1 0.0 collective-permute-done.1.refs_5_
  29.1 2.7 %second_pass.3 = (f32[520,128]{1,0:T(8,128)S(1)}, f32[520,128]{1,0:T(8,128)S(1)}) custom-call(f32[3,16,8,256]{3,2,1,0:T(8,128)S(1)} %get-tuple-element.26.refs_0_, bf16[8,256,512]{2,1,0:T(8,128)(2,1)S(1)} %copy-done, f32[4,256,128]{2,1,0:T(8,128)S(1)} %get-tuple-element.25.consts.refs_2_, bf16[8,256,256]{2,1,0:T(8,128)(2,1)S(1)} %get-tuple-element.28.refs_3_, ...), custom_call_target="tpu_custom_call" | custom-call | tf_op jit(solution)/shard_map/second_pass/pallas_call | solution.py:570
  31.9 0.1 collective-permute-start.3
  32.0 1.5 %collective-permute-done.3.other_ref = f32[520,128]{1,0:T(8,128)S(1)} collective-permute-done((f32[520,128]{1,0:T(8,128)S(1)}, f32[520,128]{1,0:T(8,128)S(1)}, u32[]{:S(2)}, u32[]{:S(2)}) %collective-permute-start.3) | collective-permute-done | bytes 266272 | tf_op jit(solution)/shard_map/ppermute | solution.py:625
  33.5 0.8 %finish.1 = (f32[512,128]{1,0:T(8,128)}, f32[1]{0:T(128)}) custom-call(f32[520,128]{1,0:T(8,128)S(1)} %get-tuple-element.36.mine_ref, f32[520,128]{1,0:T(8,128)S(1)} %collective-permute-done.3.other_ref), custom_call_target="tpu_custom_call" | custom-call | tf_op jit(solution)/shard_map/finish/pallas_call | solution.py:626
Async XLA Ops:
  0.6 10.7 %collective-permute-start = (bf16[4,256,256]{2,1,0:T(8,128)(2,1)}, bf16[4,256,256]{2,1,0:T(8,128)(2,1)S(1)}, u32[]{:S(2)}, u32[]{:S(2)}) collective-permute-start(bf16[4,256,256]{2,1,0:T(8,128)(2,1)} %own_any.1), channel_id=1, source_target_pairs={{0,1},{1,0},{2,3},{3,2},{4,5},{5,4},{6,7},{7,6},{8,9},{9,8},{10,11... | collective-permute-start | bytes 1572872 | tf_op jit(solution)/shard_map/ppermute | solution.py:469
  3.7 0.8 %copy-start.1 = (bf16[4,256,256]{2,1,0:T(8,128)(2,1)}, bf16[4,256,256]{2,1,0:T(8,128)(2,1)S(1)}, u32[]{:S(2)}) copy-start(bf16[4,256,256]{2,1,0:T(8,128)(2,1)S(1)} %get-tuple-element.22.own_ref) | copy-start | bytes 1572868
  4.5 14.0 %all-to-all-start = ((f32[8,8,384]{2,1,0:T(8,128)}), f32[8,8,384]{2,1,0:T(8,128)S(1)}, u32[]{:S(2)}, u32[]{:S(2)}) async-start(f32[8,8,384]{2,1,0:T(8,128)} %get-tuple-element.21), calls=%async_computation | async-start | bytes 196608 | tf_op jit(solution)/shard_map/all_to_all | solution.py:498
  11.3 0.8 %copy-start.3 = (bf16[4,256,256]{2,1,0:T(8,128)(2,1)}, bf16[4,256,256]{2,1,0:T(8,128)(2,1)S(1)}, u32[]{:S(2)}) copy-start(bf16[4,256,256]{2,1,0:T(8,128)(2,1)S(1)} %collective-permute-done.other_any) | copy-start | bytes 1572868
  12.2 1.0 %copy-start.2 = (bf16[4,256,256]{2,1,0:T(8,128)(2,1)S(1)}, bf16[4,256,256]{2,1,0:T(8,128)(2,1)}, u32[]{:S(2)}) copy-start(bf16[4,256,256]{2,1,0:T(8,128)(2,1)} %copy-done.1) | copy-start | bytes 1572868
  18.5 7.8 %copy-start = (bf16[8,256,512]{2,1,0:T(8,128)(2,1)S(1)}, bf16[8,256,512]{2,1,0:T(8,128)(2,1)}, u32[]{:S(2)}) copy-start(bf16[8,256,512]{2,1,0:T(8,128)(2,1)} %get-tuple-element.27.refs_1_) | copy-start | bytes 6291460
  20.8 5.5 %collective-permute-start.2 = (bf16[272,256]{1,0:T(8,128)(2,1)S(1)}, bf16[272,256]{1,0:T(8,128)(2,1)S(1)}, u32[]{:S(2)}, u32[]{:S(2)}) collective-permute-start(bf16[272,256]{1,0:T(8,128)(2,1)S(1)} %get-tuple-element.32.refs_4_), channel_id=1, source_target_pairs={{0,2},{2,0},{1,3},{3,1},{4,6},{6,4},{5,7},{7,5},{8,10},{10,8},{9,1... | collective-permute-start | bytes 417800 | tf_op jit(solution)/shard_map/ppermute | solution.py:589
  23.6 5.6 %collective-permute-start.1 = (bf16[272,256]{1,0:T(8,128)(2,1)S(1)}, bf16[272,256]{1,0:T(8,128)(2,1)S(1)}, u32[]{:S(2)}, u32[]{:S(2)}) collective-permute-start(bf16[272,256]{1,0:T(8,128)(2,1)S(1)} %get-tuple-element.29.refs_4_), channel_id=1, source_target_pairs={{0,2},{2,0},{1,3},{3,1},{4,6},{6,4},{5,7},{7,5},{8,10},{10,8},{9,1... | collective-permute-start | bytes 417800 | tf_op jit(solution)/shard_map/ppermute | solution.py:589
  31.9 1.6 %collective-permute-start.3 = (f32[520,128]{1,0:T(8,128)S(1)}, f32[520,128]{1,0:T(8,128)S(1)}, u32[]{:S(2)}, u32[]{:S(2)}) collective-permute-start(f32[520,128]{1,0:T(8,128)S(1)} %get-tuple-element.37), channel_id=1, source_target_pairs={{0,1},{1,0},{2,3},{3,2},{4,5},{5,4},{6,7},{7,6},{8,9},{9,8},{10,11... | collective-permute-start | bytes 798728 | tf_op jit(solution)/shard_map/ppermute | solution.py:625

commit v11 on v10

--- a/solution.py
+++ b/solution.py
@@ -59,13 +59,13 @@
 
 
 def pack_kernel(
-    count_ref, earn_any, start_any, len_any, init_any, mean_any, sd_any, own_any, out_ref, vec_ref, own_ref,
+    count_ref, earn_any, start_any, len_any, init_any, mean_any, sd_any, out_ref, vec_ref,
     earn_ref, start_ref, len_ref, init_ref, mean_ref, sd_ref, sems,
 ):
     fetch(
         (
             (earn_any, earn_ref), (start_any, start_ref), (len_any, len_ref),
-            (init_any, init_ref), (mean_any, mean_ref), (sd_any, sd_ref), (own_any, own_ref),
+            (init_any, init_ref), (mean_any, mean_ref), (sd_any, sd_ref),
         ),
         sems,
     )
@@ -109,11 +109,15 @@
 
 
 def prep_kernel(
-    own_ref, other_any, vec_ref, first_mat, second_any, row_probs, consts,
-    second_mat, scratch, other_ref, sem, out_sems,
+    own_any, other_any, vec_ref, first_mat, second_any, row_probs, consts,
+    second_mat, scratch, own_ref, other_ref, sems, out_sems,
 ):
-    copy = pltpu.make_async_copy(other_any, other_ref, sem)
-    copy.start()
+    copies = [
+        pltpu.make_async_copy(src, dst, sems.at[i])
+        for i, (src, dst) in enumerate(((own_any, own_ref), (other_any, other_ref)))
+    ]
+    for copy in copies:
+        copy.start()
     part, states, _ = own_ref.shape
 
     def leave(at):
@@ -122,9 +126,8 @@
     rows = row_probs.shape[1]
     for i in range(4):
         consts[i] = jnp.broadcast_to(vec_ref[i : i + 1, :], (LANES, states)).T
-    for source, ref in ((core_index(), own_ref), (1 - core_index(), other_ref)):
-        if ref is other_ref:
-            copy.wait()
+    for copy, source, ref in zip(copies, (core_index(), 1 - core_index()), (own_ref, other_ref)):
+        copy.wait()
 
         @pl.loop(0, part)
         def _(i):
@@ -154,7 +157,7 @@
     gap = sel_ref[0, step_now, :1, cols] - consts[1]
     power = gap * gap * consts[2] + consts[3]
     top = jnp.max(power, axis=0, keepdims=True)
-    return jnp.exp2(power - (top + less)), top
+    return jnp.exp2(power - (top if less is None else top + less)), top
 
 
 def is_moving(sel_ref, step_now, cols):
@@ -180,7 +183,7 @@
 def run_forward(lead, mat, hist, sel_ref, consts, ab_ref, logs, second=None):
     steps, states, width = hist.shape
     cuts = tiles(width)
-    size = [jnp.log2(column_sum(ab_ref[:states, cols].astype(F32))) for cols in cuts]
+    inverse = [1.0 / column_sum(ab_ref[:states, cols].astype(F32)) for cols in cuts]
     for k in range(steps):
         step_now = lead + k
         if second is None:
@@ -189,19 +192,20 @@
             weights_ref, row_begin, add_counts = second
             own_alpha = ab_ref[own_rows(row_begin, weights_ref.shape[0]), :].astype(F32)
         for q, cols in enumerate(cuts):
-            product = jnp.dot(mat[k], ab_ref[:, cols], preferred_element_type=F32)
+            moved = jnp.dot(mat[k], ab_ref[:, cols], preferred_element_type=F32) * inverse[q]
             moving = is_moving(sel_ref, step_now, cols)
             if second is not None:
-                total = column_sum(product * hist[k, :, cols].astype(F32))
-                weight = jnp.where(moving, 1.0 / total, 0.0)
+                total = column_sum(moved * hist[k, :, cols].astype(F32))
+                weight = jnp.where(moving, inverse[q] / total, 0.0)
                 weights_ref[:, cols] = (own_alpha[:, cols] * weight).astype(BF16)
-            emit, top = emission(sel_ref, consts, step_now, cols, jnp.where(moving, size[q], 0.0))
-            joint = jnp.where(moving, product, consts[0]) * emit
-            put_twice(ab_ref, cols, joint)
-            size[q] = jnp.log2(column_sum(joint))
+            emit, top = emission(sel_ref, consts, step_now, cols, None)
+            joint = jnp.where(moving, moved, consts[0]) * emit
+            scale = column_sum(joint)
             if second is None:
                 seen = is_seen(sel_ref, step_now, cols)
-                logs[q] = logs[q] + jnp.where(seen, size[q] + top, 0.0)
+                logs[q] = logs[q] + jnp.where(seen, jnp.log2(scale) + top, 0.0)
+            inverse[q] = 1.0 / scale
+            put_twice(ab_ref, cols, joint)
         if second is not None:
             add_counts(k, outer_sum(weights_ref, hist[k]))
     return logs
@@ -466,17 +470,15 @@
     dma = pltpu.SemaphoreType.DMA
 
     swap = [(0, 1), (1, 0)]
-    other_logits = lax.ppermute(trans_logits, "st", swap)
     vec_row = pltpu.VMEM((1, states), F32)
-    packed, vectors, own_logits = pl.pallas_call(
+    packed, vectors = pl.pallas_call(
         pack_kernel,
         out_shape=[
             shaped((group, periods // 2, slot_rows), F32),
             shaped((8, states), F32),
-            pltpu.VMEM(trans_logits.shape, BF16),
         ],
-        in_specs=[smem()] + [hbm()] * 7,
-        out_specs=[vmem()] * 3,
+        in_specs=[smem()] + [hbm()] * 6,
+        out_specs=[vmem()] * 2,
         scratch_shapes=[
             pltpu.VMEM((periods, slot_rows), F32),
             pltpu.VMEM((slot_rows // HB, HB), jnp.int32),
@@ -484,7 +486,7 @@
             vec_row,
             vec_row,
             vec_row,
-            dma((7,)),
+            dma((6,)),
         ],
         compiler_params=params(2),
         name="pack",
@@ -492,9 +494,11 @@
         block_count,
         *in_hbm(
             earnings.T, starts.reshape(-1, HB), lengths.reshape(-1, HB),
-            init_logits.reshape(1, states), state_mean.reshape(1, states), log_sd.reshape(1, states), trans_logits,
+            init_logits.reshape(1, states), state_mean.reshape(1, states), log_sd.reshape(1, states),
         ),
     )
+    packed, later_logits = lax.optimization_barrier((packed, trans_logits))
+    other_logits = lax.ppermute(later_logits, "st", swap)
     gathered = lax.all_to_all(packed, ("hh", "per"), split_axis=0, concat_axis=0, tiled=True)
     first_mat, second_mat, row_probs, consts = pl.pallas_call(
         prep_kernel,
@@ -504,18 +508,19 @@
             pltpu.VMEM((steps, rows, states), F32),
             pltpu.VMEM((4, states, LANES), F32),
         ],
-        in_specs=[vmem(), hbm(), vmem()],
+        in_specs=[hbm(), hbm(), vmem()],
         out_specs=[vmem(), hbm(), vmem(), vmem()],
         scratch_shapes=[
             pltpu.VMEM((steps, states, 2 * states), BF16),
             pltpu.VMEM((states, states), F32),
             pltpu.VMEM(trans_logits.shape, BF16),
-            dma,
+            pltpu.VMEM(trans_logits.shape, BF16),
+            dma((2,)),
             dma((steps,)),
         ],
         compiler_params=params(6),
         name="prep",
-    )(own_logits, *in_hbm(other_logits), vectors)
+    )(*in_hbm(trans_logits, other_logits), vectors)
 
     def whole(*shape):
         if grids == 1:

time: 34.7 us -> 33.6 us (0.968)
  local copies, waits for them, and re-layouts: 2.64 us -> 0.79 us
  waiting for transfers between devices: 4.52 us -> 4.92 us
  Pallas kernels: 16.1 us -> 16.5 us
    unnamed x8 -> x4, local copies, waits for them, and re-layouts: 2.64 us -> 0.79 us
    pallas_call x1, Pallas kernels: 3.31 us -> 4.14 us  [per_device(): pl.pallas_call(prep_kernel, out_shape=[pltpu.VMEM((steps, states, 2 * sta...]
    pallas_call x1, Pallas kernels: 1.93 us -> 1.54 us  [per_device(): pl.pallas_call(pack_kernel, out_shape=[shaped((group, periods // 2, slot_...]
  transfers between devices with their start and end apart: 5 -> 5, of which waited for: 3 -> 3; matrix products, arithmetic and copies ran while one was open for 0% -> 0% of each run, Pallas kernels for 30% -> 28%
where the time goes in v11:
time: 33.6 us; the launch traced here: 33.3 us
  Pallas kernels  16.5 us (49%)
  starting transfers between devices  9.64 us (29%)
  waiting for transfers between devices  4.92 us (15%)
  between operations  1.52 us (5%)
  local copies, waits for them, and re-layouts  0.79 us (2%)
    all_to_all x1, starting transfers between devices, per_device(): lax.all_to_all(packed, ('hh', 'per'), split_axis=0, concat_axis=0, tiled=...  6.83 us
    pallas_call x2, Pallas kernels, second_pass(): pl.pallas_call(functools.partial(second_kernel, resume, last, extend, gri...  5.52 us
    pallas_call x2, Pallas kernels, first_pass(): pl.pallas_call(functools.partial(first_kernel, resume, grids, index), gri...  4.51 us
    pallas_call x1, Pallas kernels, per_device(): pl.pallas_call(prep_kernel, out_shape=[pltpu.VMEM((steps, states, 2 * sta...  4.14 us
    ppermute x2, starting transfers between devices, hand_over(): return lax.ppermute(state, 'per', moves)  2.23 us
    all_to_all x1, waiting for transfers between devices, per_device(): lax.all_to_all(packed, ('hh', 'per'), split_axis=0, concat_axis=0, tiled=...  2.19 us
    pallas_call x1, Pallas kernels, per_device(): pl.pallas_call(pack_kernel, out_shape=[shaped((group, periods // 2, slot_...  1.54 us
    ppermute x1, waiting for transfers between devices, per_device(): received = lax.ppermute(other, 'st', swap)  1.53 us
  transfers between devices with their start and end apart: 5, of which 3 were waited for; matrix products, arithmetic and copies ran while one was open for 0% of the time, Pallas kernels for 28%

profile of v11, /device:TPU:0, one launch (start us, length us, event | category | flops | bytes accessed | tf_op | source)
XLA Modules:
  0.0 33.3 jit_solution(14550020871490008561)
XLA Ops:
  1.3 1.5 %pack.1 = (f32[8,8,384]{2,1,0:T(8,128)}, f32[8,256]{1,0:T(8,128)S(1)}) custom-call(s32[1]{0:T(128)S(6)} %copy.10.count_ref, f32[16,384]{1,0:T(8,128)} %bitcast.7, s32[3,128]{1,0:T(4,128)} %bitcast.8, s32[3,128]{1,0:T(4,128)} %bitcast.9, f32[1,256]{1,0:T(1,128)} %bitcast.10, f32[1,256]{1,0:T(1,128)} %bitcast.11, f32[1,256]{1,0:T(1,128)} %bitcast.12), custom_call_target="tpu_custom_call" | custom-call | tf_op jit(solution)/shard_map/pack/pallas_call | solution.py:474
  2.8 0.5 %collective-permute-start = (bf16[4,256,256]{2,1,0:T(8,128)(2,1)}, bf16[4,256,256]{2,1,0:T(8,128)(2,1)S(1)}, u32[]{:S(2)}, u32[]{:S(2)}) collective-permute-start(bf16[4,256,256]{2,1,0:T(8,128)(2,1)} %own_any.1), channel_id=1, source_target_pairs={{0,1},{1,0},{2,3},{3,2},{4,5},{5,4},{6,7},{7,6},{8,9},{9,8},{10,11... | collective-permute-start | bytes 1572872 | tf_op jit(solution)/shard_map/ppermute | solution.py:501
  3.3 6.8 %all-to-all-start = ((f32[8,8,384]{2,1,0:T(8,128)}), f32[8,8,384]{2,1,0:T(8,128)S(1)}, u32[]{:S(2)}, u32[]{:S(2)}) async-start(f32[8,8,384]{2,1,0:T(8,128)} %get-tuple-element.23), calls=%async_computation | async-start | bytes 196608 | tf_op jit(solution)/shard_map/all_to_all | solution.py:502
  10.2 0.0 collective-permute-done.other_any
  10.2 0.0 copy-start.1
  10.2 0.8 %copy-done.1 = bf16[4,256,256]{2,1,0:T(8,128)(2,1)} copy-done((bf16[4,256,256]{2,1,0:T(8,128)(2,1)}, bf16[4,256,256]{2,1,0:T(8,128)(2,1)S(1)}, u32[]{:S(2)}) %copy-start.1) | copy-done | bytes 524312
  11.0 4.1 %prep.1 = (bf16[8,256,512]{2,1,0:T(8,128)(2,1)S(1)}, bf16[8,256,512]{2,1,0:T(8,128)(2,1)}, f32[8,64,256]{2,1,0:T(8,128)S(1)}, f32[4,256,128]{2,1,0:T(8,128)S(1)}) custom-call(bf16[4,256,256]{2,1,0:T(8,128)(2,1)} %own_any.1, bf16[4,256,256]{2,1,0:T(8,128)(2,1)} %copy-done.1, f32[8,256]{1,0:T(8,128)S(1)} %get-tuple-element.25.vec_ref), custom_call_target="tpu_custom_call" | custom-call | tf_op jit(solution)/shard_map/prep/pallas_call | solution.py:503
  15.1 2.2 %all-to-all-done.rows_ref = f32[8,8,384]{2,1,0:T(8,128)S(1)} async-done(((f32[8,8,384]{2,1,0:T(8,128)}), f32[8,8,384]{2,1,0:T(8,128)S(1)}, u32[]{:S(2)}, u32[]{:S(2)}) %all-to-all-start) | async-done | bytes 98336 | tf_op jit(solution)/shard_map/all_to_all | solution.py:502
  17.3 0.0 copy-start
  17.3 2.2 %first_pass.3 = (bf16[8,256,256]{2,1,0:T(8,128)(2,1)S(1)}, bf16[272,256]{1,0:T(8,128)(2,1)S(1)}, f32[3,16,8,256]{3,2,1,0:T(8,128)S(1)}) custom-call(f32[8,8,384]{2,1,0:T(8,128)S(1)} %all-to-all-done.rows_ref, bf16[8,256,512]{2,1,0:T(8,128)(2,1)S(1)} %get-tuple-element.26.mat, f32[4,256,128]{2,1,0:T(8,128)S(1)} %get-tuple-element.27.consts.refs_2_), custom_call_target="tpu_custom_call" | custom-call | tf_op jit(solution)/shard_map/first_pass/pallas_call | solution.py:547
  19.6 0.5 %collective-permute-start.2 = (bf16[272,256]{1,0:T(8,128)(2,1)S(1)}, bf16[272,256]{1,0:T(8,128)(2,1)S(1)}, u32[]{:S(2)}, u32[]{:S(2)}) collective-permute-start(bf16[272,256]{1,0:T(8,128)(2,1)S(1)} %get-tuple-element.34.refs_4_), channel_id=1, source_target_pairs={{0,2},{2,0},{1,3},{3,1},{4,6},{6,4},{5,7},{7,5},{8,10},{10,8},{9,1... | collective-permute-start | bytes 417800 | tf_op jit(solution)/shard_map/ppermute | solution.py:594
  20.0 2.3 %first_pass.2 = (bf16[8,256,256]{2,1,0:T(8,128)(2,1)S(1)}, bf16[272,256]{1,0:T(8,128)(2,1)S(1)}, f32[3,16,8,256]{3,2,1,0:T(8,128)S(1)}) custom-call(f32[8,8,384]{2,1,0:T(8,128)S(1)} %all-to-all-done.rows_ref, bf16[8,256,512]{2,1,0:T(8,128)(2,1)S(1)} %get-tuple-element.26.mat, f32[4,256,128]{2,1,0:T(8,128)S(1)} %get-tuple-element.27.consts.refs_2_), custom_call_target="tpu_custom_call" | custom-call | tf_op jit(solution)/shard_map/first_pass/pallas_call | solution.py:547
  22.3 1.8 %collective-permute-start.1 = (bf16[272,256]{1,0:T(8,128)(2,1)S(1)}, bf16[272,256]{1,0:T(8,128)(2,1)S(1)}, u32[]{:S(2)}, u32[]{:S(2)}) collective-permute-start(bf16[272,256]{1,0:T(8,128)(2,1)S(1)} %get-tuple-element.31.refs_4_), channel_id=1, source_target_pairs={{0,2},{2,0},{1,3},{3,1},{4,6},{6,4},{5,7},{7,5},{8,10},{10,8},{9,1... | collective-permute-start | bytes 417800 | tf_op jit(solution)/shard_map/ppermute | solution.py:594
  24.1 1.2 %collective-permute-done.2.refs_5_ = bf16[272,256]{1,0:T(8,128)(2,1)S(1)} collective-permute-done((bf16[272,256]{1,0:T(8,128)(2,1)S(1)}, bf16[272,256]{1,0:T(8,128)(2,1)S(1)}, u32[]{:S(2)}, u32[]{:S(2)}) %collective-permute-start.2) | collective-permute-done | bytes 139296 | tf_op jit(solution)/shard_map/ppermute | solution.py:594
  25.3 0.0 copy-done
  25.3 2.8 %second_pass.2 = (f32[8,64,256]{2,1,0:T(8,128)S(1)}, f32[8,128]{1,0:T(8,128)S(1)}) custom-call(f32[3,16,8,256]{3,2,1,0:T(8,128)S(1)} %get-tuple-element.32.refs_0_, bf16[8,256,512]{2,1,0:T(8,128)(2,1)S(1)} %copy-done, f32[4,256,128]{2,1,0:T(8,128)S(1)} %get-tuple-element.27.consts.refs_2_, bf16[8,256,256]{2,1,0:T(8,128)(2,1)S(1)} %get-tuple-element.33.refs_3_, ...), custom_call_target="tpu_custom_call" | custom-call | tf_op jit(solution)/shard_map/second_pass/pallas_call | solution.py:575
  28.1 0.0 collective-permute-done.1.refs_5_
  28.1 2.7 %second_pass.3 = (f32[520,128]{1,0:T(8,128)S(1)}, f32[520,128]{1,0:T(8,128)S(1)}) custom-call(f32[3,16,8,256]{3,2,1,0:T(8,128)S(1)} %get-tuple-element.28.refs_0_, bf16[8,256,512]{2,1,0:T(8,128)(2,1)S(1)} %copy-done, f32[4,256,128]{2,1,0:T(8,128)S(1)} %get-tuple-element.27.consts.refs_2_, bf16[8,256,256]{2,1,0:T(8,128)(2,1)S(1)} %get-tuple-element.30.refs_3_, ...), custom_call_target="tpu_custom_call" | custom-call | tf_op jit(solution)/shard_map/second_pass/pallas_call | solution.py:575
  30.8 0.1 collective-permute-start.3
  30.9 1.5 %collective-permute-done.3.other_ref = f32[520,128]{1,0:T(8,128)S(1)} collective-permute-done((f32[520,128]{1,0:T(8,128)S(1)}, f32[520,128]{1,0:T(8,128)S(1)}, u32[]{:S(2)}, u32[]{:S(2)}) %collective-permute-start.3) | collective-permute-done | bytes 266272 | tf_op jit(solution)/shard_map/ppermute | solution.py:630
  32.4 0.8 %finish.1 = (f32[512,128]{1,0:T(8,128)}, f32[1]{0:T(128)}) custom-call(f32[520,128]{1,0:T(8,128)S(1)} %get-tuple-element.38.mine_ref, f32[520,128]{1,0:T(8,128)S(1)} %collective-permute-done.3.other_ref), custom_call_target="tpu_custom_call" | custom-call | tf_op jit(solution)/shard_map/finish/pallas_call | solution.py:631
Async XLA Ops:
  2.8 7.3 %collective-permute-start = (bf16[4,256,256]{2,1,0:T(8,128)(2,1)}, bf16[4,256,256]{2,1,0:T(8,128)(2,1)S(1)}, u32[]{:S(2)}, u32[]{:S(2)}) collective-permute-start(bf16[4,256,256]{2,1,0:T(8,128)(2,1)} %own_any.1), channel_id=1, source_target_pairs={{0,1},{1,0},{2,3},{3,2},{4,5},{5,4},{6,7},{7,6},{8,9},{9,8},{10,11... | collective-permute-start | bytes 1572872 | tf_op jit(solution)/shard_map/ppermute | solution.py:501
  3.3 14.0 %all-to-all-start = ((f32[8,8,384]{2,1,0:T(8,128)}), f32[8,8,384]{2,1,0:T(8,128)S(1)}, u32[]{:S(2)}, u32[]{:S(2)}) async-start(f32[8,8,384]{2,1,0:T(8,128)} %get-tuple-element.23), calls=%async_computation | async-start | bytes 196608 | tf_op jit(solution)/shard_map/all_to_all | solution.py:502
  10.2 0.8 %copy-start.1 = (bf16[4,256,256]{2,1,0:T(8,128)(2,1)}, bf16[4,256,256]{2,1,0:T(8,128)(2,1)S(1)}, u32[]{:S(2)}) copy-start(bf16[4,256,256]{2,1,0:T(8,128)(2,1)S(1)} %collective-permute-done.other_any) | copy-start | bytes 1572868
  17.3 8.0 %copy-start = (bf16[8,256,512]{2,1,0:T(8,128)(2,1)S(1)}, bf16[8,256,512]{2,1,0:T(8,128)(2,1)}, u32[]{:S(2)}) copy-start(bf16[8,256,512]{2,1,0:T(8,128)(2,1)} %get-tuple-element.29.refs_1_) | copy-start | bytes 6291460
  19.6 5.7 %collective-permute-start.2 = (bf16[272,256]{1,0:T(8,128)(2,1)S(1)}, bf16[272,256]{1,0:T(8,128)(2,1)S(1)}, u32[]{:S(2)}, u32[]{:S(2)}) collective-permute-start(bf16[272,256]{1,0:T(8,128)(2,1)S(1)} %get-tuple-element.34.refs_4_), channel_id=1, source_target_pairs={{0,2},{2,0},{1,3},{3,1},{4,6},{6,4},{5,7},{7,5},{8,10},{10,8},{9,1... | collective-permute-start | bytes 417800 | tf_op jit(solution)/shard_map/ppermute | solution.py:594
  22.3 5.8 %collective-permute-start.1 = (bf16[272,256]{1,0:T(8,128)(2,1)S(1)}, bf16[272,256]{1,0:T(8,128)(2,1)S(1)}, u32[]{:S(2)}, u32[]{:S(2)}) collective-permute-start(bf16[272,256]{1,0:T(8,128)(2,1)S(1)} %get-tuple-element.31.refs_4_), channel_id=1, source_target_pairs={{0,2},{2,0},{1,3},{3,1},{4,6},{6,4},{5,7},{7,5},{8,10},{10,8},{9,1... | collective-permute-start | bytes 417800 | tf_op jit(solution)/shard_map/ppermute | solution.py:594
  30.8 1.6 %collective-permute-start.3 = (f32[520,128]{1,0:T(8,128)S(1)}, f32[520,128]{1,0:T(8,128)S(1)}, u32[]{:S(2)}, u32[]{:S(2)}) collective-permute-start(f32[520,128]{1,0:T(8,128)S(1)} %get-tuple-element.39), channel_id=1, source_target_pairs={{0,1},{1,0},{2,3},{3,2},{4,5},{5,4},{6,7},{7,6},{8,9},{9,8},{10,11... | collective-permute-start | bytes 798728 | tf_op jit(solution)/shard_map/ppermute | solution.py:630

commit v12 on v11

--- a/solution.py
+++ b/solution.py
@@ -153,11 +153,10 @@
         leave(at).wait()
 
 
-def emission(sel_ref, consts, step_now, cols, less):
+def emission(sel_ref, consts, step_now, cols, less=None):
     gap = sel_ref[0, step_now, :1, cols] - consts[1]
     power = gap * gap * consts[2] + consts[3]
-    top = jnp.max(power, axis=0, keepdims=True)
-    return jnp.exp2(power - (top if less is None else top + less)), top
+    return jnp.exp2(power if less is None else power - less)
 
 
 def is_moving(sel_ref, step_now, cols):
@@ -196,14 +195,14 @@
             moving = is_moving(sel_ref, step_now, cols)
             if second is not None:
                 total = column_sum(moved * hist[k, :, cols].astype(F32))
-                weight = jnp.where(moving, inverse[q] / total, 0.0)
-                weights_ref[:, cols] = (own_alpha[:, cols] * weight).astype(BF16)
-            emit, top = emission(sel_ref, consts, step_now, cols, None)
+                weight = jnp.where(moving, 1.0 / total, 0.0)
+                weights_ref[:, cols] = (own_alpha[:, cols] * inverse[q] * weight).astype(BF16)
+            emit = emission(sel_ref, consts, step_now, cols)
             joint = jnp.where(moving, moved, consts[0]) * emit
             scale = column_sum(joint)
             if second is None:
                 seen = is_seen(sel_ref, step_now, cols)
-                logs[q] = logs[q] + jnp.where(seen, jnp.log2(scale) + top, 0.0)
+                logs[q] = logs[q] + jnp.where(seen, jnp.log2(scale), 0.0)
             inverse[q] = 1.0 / scale
             put_twice(ab_ref, cols, joint)
         if second is not None:
@@ -221,15 +220,15 @@
         step_now = lead + k
         grown = []
         for q, cols in enumerate(cuts):
-            emit, top = emission(sel_ref, consts, step_now, cols, size[q])
+            emit = emission(sel_ref, consts, step_now, cols, size[q] if second is None else None)
             carried = emit * state[q]
             put_twice(ub_ref, cols, carried)
             whole = column_sum(carried)
             grown.append(whole)
-            size[q] = jnp.log2(whole)
             if second is None:
+                size[q] = jnp.log2(whole)
                 seen = is_seen(sel_ref, step_now, cols)
-                logs[q] = logs[q] + jnp.where(seen, size[q] + top, 0.0)
+                logs[q] = logs[q] + jnp.where(seen, size[q], 0.0)
                 begun = column_sum(carried * consts[0]) / whole
                 rest[q] = jnp.where(seen, begun, rest[q])
         if second is None:
@@ -240,11 +239,15 @@
         for q, cols in enumerate(cuts):
             product = jnp.dot(mat[k], ub_ref[:, cols], preferred_element_type=F32)
             moving = is_moving(sel_ref, step_now, cols)
-            if second is not None:
+            if second is None:
+                state[q] = jnp.where(moving, product, rest[q] * grown[q])
+            else:
+                shrink = 1.0 / grown[q]
+                product = product * shrink
                 total = column_sum(product * hist[k, :, cols].astype(F32))
                 weight = jnp.where(moving, 1.0 / total, 0.0)
-                weights_ref[:, cols] = (own_alpha[:, cols] * weight).astype(BF16)
-            state[q] = jnp.where(moving, product, rest[q] * grown[q])
+                weights_ref[:, cols] = (own_alpha[:, cols] * weight * shrink).astype(BF16)
+                state[q] = jnp.where(moving, product, rest[q])
         if second is not None:
             add_counts(k, outer_sum(weights_ref, ub_ref[:states, :]))
 

time: 33.6 us -> 33.6 us (level)
  transfers between devices with their start and end apart: 5 -> 5, of which waited for: 3 -> 3; matrix products, arithmetic and copies ran while one was open for 0% -> 0% of each run, Pallas kernels for 28% -> 27%
where the time goes in v12:
time: 33.6 us; the launch traced here: 33.4 us
  Pallas kernels  16.4 us (49%)
  starting transfers between devices  9.51 us (28%)
  waiting for transfers between devices  5.18 us (15%)
  between operations  1.52 us (5%)
  local copies, waits for them, and re-layouts  0.79 us (2%)
    all_to_all x1, starting transfers between devices, per_device(): lax.all_to_all(packed, ('hh', 'per'), split_axis=0, concat_axis=0, tiled=...  6.83 us
    pallas_call x2, Pallas kernels, second_pass(): pl.pallas_call(functools.partial(second_kernel, resume, last, extend, gri...  5.39 us
    pallas_call x2, Pallas kernels, first_pass(): pl.pallas_call(functools.partial(first_kernel, resume, grids, index), gri...  4.52 us
    pallas_call x1, Pallas kernels, per_device(): pl.pallas_call(prep_kernel, out_shape=[pltpu.VMEM((steps, states, 2 * sta...  4.14 us
    all_to_all x1, waiting for transfers between devices, per_device(): lax.all_to_all(packed, ('hh', 'per'), split_axis=0, concat_axis=0, tiled=...  2.19 us
    ppermute x2, starting transfers between devices, hand_over(): return lax.ppermute(state, 'per', moves)  2.09 us
    pallas_call x1, Pallas kernels, per_device(): pl.pallas_call(pack_kernel, out_shape=[shaped((group, periods // 2, slot_...  1.54 us
    ppermute x1, waiting for transfers between devices, per_device(): received = lax.ppermute(other, 'st', swap)  1.53 us
  transfers between devices with their start and end apart: 5, of which 3 were waited for; matrix products, arithmetic and copies ran while one was open for 0% of the time, Pallas kernels for 27%

profile of v12, /device:TPU:0, one launch (start us, length us, event | category | flops | bytes accessed | tf_op | source)
XLA Modules:
  0.0 33.4 jit_solution(1383568736390493659)
XLA Ops:
  1.3 1.5 %pack.1 = (f32[8,8,384]{2,1,0:T(8,128)}, f32[8,256]{1,0:T(8,128)S(1)}) custom-call(s32[1]{0:T(128)S(6)} %copy.10.count_ref, f32[16,384]{1,0:T(8,128)} %bitcast.7, s32[3,128]{1,0:T(4,128)} %bitcast.8, s32[3,128]{1,0:T(4,128)} %bitcast.9, f32[1,256]{1,0:T(1,128)} %bitcast.10, f32[1,256]{1,0:T(1,128)} %bitcast.11, f32[1,256]{1,0:T(1,128)} %bitcast.12), custom_call_target="tpu_custom_call" | custom-call | tf_op jit(solution)/shard_map/pack/pallas_call | solution.py:477
  2.8 0.5 %collective-permute-start = (bf16[4,256,256]{2,1,0:T(8,128)(2,1)}, bf16[4,256,256]{2,1,0:T(8,128)(2,1)S(1)}, u32[]{:S(2)}, u32[]{:S(2)}) collective-permute-start(bf16[4,256,256]{2,1,0:T(8,128)(2,1)} %own_any.1), channel_id=1, source_target_pairs={{0,1},{1,0},{2,3},{3,2},{4,5},{5,4},{6,7},{7,6},{8,9},{9,8},{10,11... | collective-permute-start | bytes 1572872 | tf_op jit(solution)/shard_map/ppermute | solution.py:504
  3.3 6.8 %all-to-all-start = ((f32[8,8,384]{2,1,0:T(8,128)}), f32[8,8,384]{2,1,0:T(8,128)S(1)}, u32[]{:S(2)}, u32[]{:S(2)}) async-start(f32[8,8,384]{2,1,0:T(8,128)} %get-tuple-element.23), calls=%async_computation | async-start | bytes 196608 | tf_op jit(solution)/shard_map/all_to_all | solution.py:505
  10.2 0.0 collective-permute-done.other_any
  10.2 0.0 copy-start.1
  10.2 0.8 %copy-done.1 = bf16[4,256,256]{2,1,0:T(8,128)(2,1)} copy-done((bf16[4,256,256]{2,1,0:T(8,128)(2,1)}, bf16[4,256,256]{2,1,0:T(8,128)(2,1)S(1)}, u32[]{:S(2)}) %copy-start.1) | copy-done | bytes 524312
  11.0 4.1 %prep.1 = (bf16[8,256,512]{2,1,0:T(8,128)(2,1)S(1)}, bf16[8,256,512]{2,1,0:T(8,128)(2,1)}, f32[8,64,256]{2,1,0:T(8,128)S(1)}, f32[4,256,128]{2,1,0:T(8,128)S(1)}) custom-call(bf16[4,256,256]{2,1,0:T(8,128)(2,1)} %own_any.1, bf16[4,256,256]{2,1,0:T(8,128)(2,1)} %copy-done.1, f32[8,256]{1,0:T(8,128)S(1)} %get-tuple-element.25.vec_ref), custom_call_target="tpu_custom_call" | custom-call | tf_op jit(solution)/shard_map/prep/pallas_call | solution.py:506
  15.1 2.2 %all-to-all-done.rows_ref = f32[8,8,384]{2,1,0:T(8,128)S(1)} async-done(((f32[8,8,384]{2,1,0:T(8,128)}), f32[8,8,384]{2,1,0:T(8,128)S(1)}, u32[]{:S(2)}, u32[]{:S(2)}) %all-to-all-start) | async-done | bytes 98336 | tf_op jit(solution)/shard_map/all_to_all | solution.py:505
  17.3 0.0 copy-start
  17.3 2.2 %first_pass.3 = (bf16[8,256,256]{2,1,0:T(8,128)(2,1)S(1)}, bf16[272,256]{1,0:T(8,128)(2,1)S(1)}, f32[3,16,8,256]{3,2,1,0:T(8,128)S(1)}) custom-call(f32[8,8,384]{2,1,0:T(8,128)S(1)} %all-to-all-done.rows_ref, bf16[8,256,512]{2,1,0:T(8,128)(2,1)S(1)} %get-tuple-element.26.mat, f32[4,256,128]{2,1,0:T(8,128)S(1)} %get-tuple-element.27.consts.refs_2_), custom_call_target="tpu_custom_call" | custom-call | tf_op jit(solution)/shard_map/first_pass/pallas_call | solution.py:550
  19.6 0.3 collective-permute-start.2
  19.9 2.3 %first_pass.2 = (bf16[8,256,256]{2,1,0:T(8,128)(2,1)S(1)}, bf16[272,256]{1,0:T(8,128)(2,1)S(1)}, f32[3,16,8,256]{3,2,1,0:T(8,128)S(1)}) custom-call(f32[8,8,384]{2,1,0:T(8,128)S(1)} %all-to-all-done.rows_ref, bf16[8,256,512]{2,1,0:T(8,128)(2,1)S(1)} %get-tuple-element.26.mat, f32[4,256,128]{2,1,0:T(8,128)S(1)} %get-tuple-element.27.consts.refs_2_), custom_call_target="tpu_custom_call" | custom-call | tf_op jit(solution)/shard_map/first_pass/pallas_call | solution.py:550
  22.2 1.8 %collective-permute-start.1 = (bf16[272,256]{1,0:T(8,128)(2,1)S(1)}, bf16[272,256]{1,0:T(8,128)(2,1)S(1)}, u32[]{:S(2)}, u32[]{:S(2)}) collective-permute-start(bf16[272,256]{1,0:T(8,128)(2,1)S(1)} %get-tuple-element.31.refs_4_), channel_id=1, source_target_pairs={{0,2},{2,0},{1,3},{3,1},{4,6},{6,4},{5,7},{7,5},{8,10},{10,8},{9,1... | collective-permute-start | bytes 417800 | tf_op jit(solution)/shard_map/ppermute | solution.py:597
  24.0 1.5 %collective-permute-done.2.refs_5_ = bf16[272,256]{1,0:T(8,128)(2,1)S(1)} collective-permute-done((bf16[272,256]{1,0:T(8,128)(2,1)S(1)}, bf16[272,256]{1,0:T(8,128)(2,1)S(1)}, u32[]{:S(2)}, u32[]{:S(2)}) %collective-permute-start.2) | collective-permute-done | bytes 139296 | tf_op jit(solution)/shard_map/ppermute | solution.py:597
  25.4 0.0 copy-done
  25.4 2.7 %second_pass.2 = (f32[8,64,256]{2,1,0:T(8,128)S(1)}, f32[8,128]{1,0:T(8,128)S(1)}) custom-call(f32[3,16,8,256]{3,2,1,0:T(8,128)S(1)} %get-tuple-element.32.refs_0_, bf16[8,256,512]{2,1,0:T(8,128)(2,1)S(1)} %copy-done, f32[4,256,128]{2,1,0:T(8,128)S(1)} %get-tuple-element.27.consts.refs_2_, bf16[8,256,256]{2,1,0:T(8,128)(2,1)S(1)} %get-tuple-element.33.refs_3_, ...), custom_call_target="tpu_custom_call" | custom-call | tf_op jit(solution)/shard_map/second_pass/pallas_call | solution.py:578
  28.1 0.0 collective-permute-done.1.refs_5_
  28.1 2.7 %second_pass.3 = (f32[520,128]{1,0:T(8,128)S(1)}, f32[520,128]{1,0:T(8,128)S(1)}) custom-call(f32[3,16,8,256]{3,2,1,0:T(8,128)S(1)} %get-tuple-element.28.refs_0_, bf16[8,256,512]{2,1,0:T(8,128)(2,1)S(1)} %copy-done, f32[4,256,128]{2,1,0:T(8,128)S(1)} %get-tuple-element.27.consts.refs_2_, bf16[8,256,256]{2,1,0:T(8,128)(2,1)S(1)} %get-tuple-element.30.refs_3_, ...), custom_call_target="tpu_custom_call" | custom-call | tf_op jit(solution)/shard_map/second_pass/pallas_call | solution.py:578
  30.8 0.1 collective-permute-start.3
  30.9 1.5 %collective-permute-done.3.other_ref = f32[520,128]{1,0:T(8,128)S(1)} collective-permute-done((f32[520,128]{1,0:T(8,128)S(1)}, f32[520,128]{1,0:T(8,128)S(1)}, u32[]{:S(2)}, u32[]{:S(2)}) %collective-permute-start.3) | collective-permute-done | bytes 266272 | tf_op jit(solution)/shard_map/ppermute | solution.py:633
  32.4 0.8 %finish.1 = (f32[512,128]{1,0:T(8,128)}, f32[1]{0:T(128)}) custom-call(f32[520,128]{1,0:T(8,128)S(1)} %get-tuple-element.38.mine_ref, f32[520,128]{1,0:T(8,128)S(1)} %collective-permute-done.3.other_ref), custom_call_target="tpu_custom_call" | custom-call | tf_op jit(solution)/shard_map/finish/pallas_call | solution.py:634
Async XLA Ops:
  2.8 7.3 %collective-permute-start = (bf16[4,256,256]{2,1,0:T(8,128)(2,1)}, bf16[4,256,256]{2,1,0:T(8,128)(2,1)S(1)}, u32[]{:S(2)}, u32[]{:S(2)}) collective-permute-start(bf16[4,256,256]{2,1,0:T(8,128)(2,1)} %own_any.1), channel_id=1, source_target_pairs={{0,1},{1,0},{2,3},{3,2},{4,5},{5,4},{6,7},{7,6},{8,9},{9,8},{10,11... | collective-permute-start | bytes 1572872 | tf_op jit(solution)/shard_map/ppermute | solution.py:504
  3.3 14.0 %all-to-all-start = ((f32[8,8,384]{2,1,0:T(8,128)}), f32[8,8,384]{2,1,0:T(8,128)S(1)}, u32[]{:S(2)}, u32[]{:S(2)}) async-start(f32[8,8,384]{2,1,0:T(8,128)} %get-tuple-element.23), calls=%async_computation | async-start | bytes 196608 | tf_op jit(solution)/shard_map/all_to_all | solution.py:505
  10.2 0.8 %copy-start.1 = (bf16[4,256,256]{2,1,0:T(8,128)(2,1)}, bf16[4,256,256]{2,1,0:T(8,128)(2,1)S(1)}, u32[]{:S(2)}) copy-start(bf16[4,256,256]{2,1,0:T(8,128)(2,1)S(1)} %collective-permute-done.other_any) | copy-start | bytes 1572868
  17.3 8.1 %copy-start = (bf16[8,256,512]{2,1,0:T(8,128)(2,1)S(1)}, bf16[8,256,512]{2,1,0:T(8,128)(2,1)}, u32[]{:S(2)}) copy-start(bf16[8,256,512]{2,1,0:T(8,128)(2,1)} %get-tuple-element.29.refs_1_) | copy-start | bytes 6291460
  19.6 5.8 %collective-permute-start.2 = (bf16[272,256]{1,0:T(8,128)(2,1)S(1)}, bf16[272,256]{1,0:T(8,128)(2,1)S(1)}, u32[]{:S(2)}, u32[]{:S(2)}) collective-permute-start(bf16[272,256]{1,0:T(8,128)(2,1)S(1)} %get-tuple-element.34.refs_4_), channel_id=1, source_target_pairs={{0,2},{2,0},{1,3},{3,1},{4,6},{6,4},{5,7},{7,5},{8,10},{10,8},{9,1... | collective-permute-start | bytes 417800 | tf_op jit(solution)/shard_map/ppermute | solution.py:597
  22.2 5.9 %collective-permute-start.1 = (bf16[272,256]{1,0:T(8,128)(2,1)S(1)}, bf16[272,256]{1,0:T(8,128)(2,1)S(1)}, u32[]{:S(2)}, u32[]{:S(2)}) collective-permute-start(bf16[272,256]{1,0:T(8,128)(2,1)S(1)} %get-tuple-element.31.refs_4_), channel_id=1, source_target_pairs={{0,2},{2,0},{1,3},{3,1},{4,6},{6,4},{5,7},{7,5},{8,10},{10,8},{9,1... | collective-permute-start | bytes 417800 | tf_op jit(solution)/shard_map/ppermute | solution.py:597
  30.8 1.6 %collective-permute-start.3 = (f32[520,128]{1,0:T(8,128)S(1)}, f32[520,128]{1,0:T(8,128)S(1)}, u32[]{:S(2)}, u32[]{:S(2)}) collective-permute-start(f32[520,128]{1,0:T(8,128)S(1)} %get-tuple-element.39), channel_id=1, source_target_pairs={{0,1},{1,0},{2,3},{3,2},{4,5},{5,4},{6,7},{7,6},{8,9},{9,8},{10,11... | collective-permute-start | bytes 798728 | tf_op jit(solution)/shard_map/ppermute | solution.py:633

commit v13 on v12

--- a/solution.py
+++ b/solution.py
@@ -101,11 +101,10 @@
     ref[at, :states, states:] = (value - high.astype(F32)).astype(BF16)
 
 
-def put_twice(ref, cols, value):
-    states = value.shape[0]
-    value = value.astype(BF16)
-    ref[:states, cols] = value
-    ref[states:, cols] = value
+def both_halves(mat, state):
+    states = mat.shape[0]
+    high = jnp.dot(mat[:, :states], state, preferred_element_type=F32)
+    return high + jnp.dot(mat[:, states:], state, preferred_element_type=F32)
 
 
 def prep_kernel(
@@ -182,16 +181,16 @@
 def run_forward(lead, mat, hist, sel_ref, consts, ab_ref, logs, second=None):
     steps, states, width = hist.shape
     cuts = tiles(width)
-    inverse = [1.0 / column_sum(ab_ref[:states, cols].astype(F32)) for cols in cuts]
+    inverse = [1.0 / column_sum(ab_ref[:, cols].astype(F32)) for cols in cuts]
     for k in range(steps):
         step_now = lead + k
         if second is None:
-            hist[k] = ab_ref[:states, :]
+            hist[k] = ab_ref[...]
         else:
             weights_ref, row_begin, add_counts = second
             own_alpha = ab_ref[own_rows(row_begin, weights_ref.shape[0]), :].astype(F32)
         for q, cols in enumerate(cuts):
-            moved = jnp.dot(mat[k], ab_ref[:, cols], preferred_element_type=F32) * inverse[q]
+            moved = both_halves(mat[k], ab_ref[:, cols]) * inverse[q]
             moving = is_moving(sel_ref, step_now, cols)
             if second is not None:
                 total = column_sum(moved * hist[k, :, cols].astype(F32))
@@ -204,13 +203,13 @@
                 seen = is_seen(sel_ref, step_now, cols)
                 logs[q] = logs[q] + jnp.where(seen, jnp.log2(scale), 0.0)
             inverse[q] = 1.0 / scale
-            put_twice(ab_ref, cols, joint)
+            ab_ref[:, cols] = joint.astype(BF16)
         if second is not None:
             add_counts(k, outer_sum(weights_ref, hist[k]))
     return logs
 
 
-def run_backward(lead, mat, hist, sel_ref, consts, state, ub_ref, logs, leave, second=None):
+def run_backward(lead, mat, hist, sel_ref, consts, state, ub_ref, logs, leave, second=None, between=None):
     steps, states, width = hist.shape
     cuts = tiles(width)
     rest = [x[:1] for x in state]
@@ -222,7 +221,7 @@
         for q, cols in enumerate(cuts):
             emit = emission(sel_ref, consts, step_now, cols, size[q] if second is None else None)
             carried = emit * state[q]
-            put_twice(ub_ref, cols, carried)
+            ub_ref[:, cols] = carried.astype(BF16)
             whole = column_sum(carried)
             grown.append(whole)
             if second is None:
@@ -232,12 +231,12 @@
                 begun = column_sum(carried * consts[0]) / whole
                 rest[q] = jnp.where(seen, begun, rest[q])
         if second is None:
-            hist[k] = ub_ref[:states, :]
+            hist[k] = ub_ref[...]
         else:
             weights_ref, row_begin, add_counts = second
             own_alpha = hist[k, own_rows(row_begin, weights_ref.shape[0]), :].astype(F32)
         for q, cols in enumerate(cuts):
-            product = jnp.dot(mat[k], ub_ref[:, cols], preferred_element_type=F32)
+            product = both_halves(mat[k], ub_ref[:, cols])
             moving = is_moving(sel_ref, step_now, cols)
             if second is None:
                 state[q] = jnp.where(moving, product, rest[q] * grown[q])
@@ -249,7 +248,7 @@
                 weights_ref[:, cols] = (own_alpha[:, cols] * weight * shrink).astype(BF16)
                 state[q] = jnp.where(moving, product, rest[q])
         if second is not None:
-            add_counts(k, outer_sum(weights_ref, ub_ref[:states, :]))
+            add_counts(k, outer_sum(weights_ref, ub_ref[...]))
 
     def left():
         return [x * jnp.exp2(-y) for x, y in zip(state, size)]
@@ -260,6 +259,7 @@
         step(0)
         leave(left())
         return
+    between()
 
     @pl.when(lead > 0)
     def _():
@@ -340,13 +340,13 @@
     @pl.when(forward_first)
     def _():
         if resume:
-            put_twice(ab_ref, slice(None), state_in[:states, :])
+            ab_ref[...] = state_in[:states, :]
         else:
             for cols in cuts:
-                put_twice(ab_ref, cols, consts[0])
+                ab_ref[:, cols] = consts[0].astype(BF16)
         logs = state_logs(state_in) if resume else list(zeros)
         run_forward(lead, mat, hist, sel_ref, consts, ab_ref, logs)
-        put_state(state_out, [ab_ref[:states, cols] for cols in cuts], logs)
+        put_state(state_out, [ab_ref[:, cols] for cols in cuts], logs)
 
     @pl.when(jnp.logical_not(forward_first))
     def _():
@@ -420,18 +420,17 @@
 
     @pl.when(jnp.logical_not(forward_first))
     def _():
+        ab_ref[...] = state_in[:states, :]
+        run_forward(lead, mat, hist, sel_ref, consts, ab_ref, list(zeros), second)
         add_sums(state_in, own_state)
-        put_twice(ab_ref, slice(None), state_in[:states, :])
-        run_forward(lead, mat, hist, sel_ref, consts, ab_ref, list(zeros), second)
         if extend:
-            put_state(state_out, [ab_ref[:states, cols] for cols in tiles(width)], zeros)
+            put_state(state_out, [ab_ref[:, cols] for cols in tiles(width)], zeros)
 
     @pl.when(forward_first)
     def _():
-        add_sums(own_state, state_in)
         state = [state_in[:states, cols].astype(F32) for cols in tiles(width)]
         leave = lambda values: put_state(state_out, values, zeros) if extend else None
-        run_backward(lead, mat, hist, sel_ref, consts, state, ab_ref, list(zeros), leave, second)
+        run_backward(lead, mat, hist, sel_ref, consts, state, ab_ref, list(zeros), leave, second, lambda: add_sums(own_state, state_in))
 
     if last:
 
@@ -477,8 +476,8 @@
     packed, vectors = pl.pallas_call(
         pack_kernel,
         out_shape=[
-            shaped((group, periods // 2, slot_rows), F32),
-            shaped((8, states), F32),
+            pltpu.VMEM((group, periods // 2, slot_rows), F32),
+            pltpu.VMEM((8, states), F32),
         ],
         in_specs=[smem()] + [hbm()] * 6,
         out_specs=[vmem()] * 2,
@@ -554,7 +553,7 @@
             in_specs=[whole(*gathered.shape), whole(*first_mat.shape), const_spec]
             + [state_spec] * resume,
             out_specs=[hist_spec, state_spec, sel_spec],
-            scratch_shapes=[pltpu.VMEM((2 * states, width), BF16)],
+            scratch_shapes=[pltpu.VMEM((states, width), BF16)],
             compiler_params=params(8 if grids == 1 else 32),
             name="first_pass",
         )(gathered, first_mat, consts, *([state_in] if resume else []))
@@ -563,7 +562,7 @@
         hist, own_state, sel = kept
         resume = sums_in is not None
         scratch = [
-            pltpu.VMEM((2 * states, width), BF16),
+            pltpu.VMEM((states, width), BF16),
             pltpu.VMEM((rows, width), BF16),
         ]
         counts_spec, sums_spec = whole(*counts_shape.shape), whole(*sums_shape.shape)

time: 33.6 us -> 33.5 us (level)
  no operation moved by 1% of the time
where the time goes in v13:
time: 33.5 us; the launch traced here: 33.2 us
  Pallas kernels  16.1 us (48%)
  starting transfers between devices  9.54 us (28%)
  waiting for transfers between devices  5.29 us (16%)
  between operations  1.52 us (5%)
  local copies, waits for them, and re-layouts  0.79 us (2%)
    all_to_all x1, starting transfers between devices, per_device(): lax.all_to_all(packed, ('hh', 'per'), split_axis=0, concat_axis=0, tiled=...  6.83 us
    pallas_call x2, Pallas kernels, second_pass(): pl.pallas_call(functools.partial(second_kernel, resume, last, extend, gri...  5.28 us
    pallas_call x2, Pallas kernels, first_pass(): pl.pallas_call(functools.partial(first_kernel, resume, grids, index), gri...  4.38 us
    pallas_call x1, Pallas kernels, per_device(): pl.pallas_call(prep_kernel, out_shape=[pltpu.VMEM((steps, states, 2 * sta...  4.14 us
    all_to_all x1, waiting for transfers between devices, per_device(): lax.all_to_all(packed, ('hh', 'per'), split_axis=0, concat_axis=0, tiled=...  2.19 us
    ppermute x2, starting transfers between devices, hand_over(): return lax.ppermute(state, 'per', moves)  2.12 us
    ppermute x2, waiting for transfers between devices, hand_over(): return lax.ppermute(state, 'per', moves)  1.57 us
    pallas_call x1, Pallas kernels, per_device(): pl.pallas_call(pack_kernel, out_shape=[pltpu.VMEM((group, periods // 2, s...  1.54 us
  transfers between devices with their start and end apart: 5, of which 3 were waited for; matrix products, arithmetic and copies ran while one was open for 0% of the time, Pallas kernels for 27%

profile of v13, /device:TPU:0, one launch (start us, length us, event | category | flops | bytes accessed | tf_op | source)
XLA Modules:
  0.0 33.2 jit_solution(15268136647632230235)
XLA Ops:
  1.3 1.5 %pack.1 = (f32[8,8,384]{2,1,0:T(8,128)}, f32[8,256]{1,0:T(8,128)S(1)}) custom-call(s32[1]{0:T(128)S(6)} %copy.10.count_ref, f32[16,384]{1,0:T(8,128)} %bitcast.7, s32[3,128]{1,0:T(4,128)} %bitcast.8, s32[3,128]{1,0:T(4,128)} %bitcast.9, f32[1,256]{1,0:T(1,128)} %bitcast.10, f32[1,256]{1,0:T(1,128)} %bitcast.11, f32[1,256]{1,0:T(1,128)} %bitcast.12), custom_call_target="tpu_custom_call" | custom-call | tf_op jit(solution)/shard_map/pack/pallas_call | solution.py:476
  2.8 0.5 %collective-permute-start = (bf16[4,256,256]{2,1,0:T(8,128)(2,1)}, bf16[4,256,256]{2,1,0:T(8,128)(2,1)S(1)}, u32[]{:S(2)}, u32[]{:S(2)}) collective-permute-start(bf16[4,256,256]{2,1,0:T(8,128)(2,1)} %own_any.1), channel_id=1, source_target_pairs={{0,1},{1,0},{2,3},{3,2},{4,5},{5,4},{6,7},{7,6},{8,9},{9,8},{10,11... | collective-permute-start | bytes 1572872 | tf_op jit(solution)/shard_map/ppermute | solution.py:503
  3.3 6.8 %all-to-all-start = ((f32[8,8,384]{2,1,0:T(8,128)}), f32[8,8,384]{2,1,0:T(8,128)S(1)}, u32[]{:S(2)}, u32[]{:S(2)}) async-start(f32[8,8,384]{2,1,0:T(8,128)} %get-tuple-element.23), calls=%async_computation | async-start | bytes 196608 | tf_op jit(solution)/shard_map/all_to_all | solution.py:504
  10.2 0.0 collective-permute-done.other_any
  10.2 0.0 copy-start.1
  10.2 0.8 %copy-done.1 = bf16[4,256,256]{2,1,0:T(8,128)(2,1)} copy-done((bf16[4,256,256]{2,1,0:T(8,128)(2,1)}, bf16[4,256,256]{2,1,0:T(8,128)(2,1)S(1)}, u32[]{:S(2)}) %copy-start.1) | copy-done | bytes 524312
  11.0 4.1 %prep.1 = (bf16[8,256,512]{2,1,0:T(8,128)(2,1)S(1)}, bf16[8,256,512]{2,1,0:T(8,128)(2,1)}, f32[8,64,256]{2,1,0:T(8,128)S(1)}, f32[4,256,128]{2,1,0:T(8,128)S(1)}) custom-call(bf16[4,256,256]{2,1,0:T(8,128)(2,1)} %own_any.1, bf16[4,256,256]{2,1,0:T(8,128)(2,1)} %copy-done.1, f32[8,256]{1,0:T(8,128)S(1)} %get-tuple-element.25.vec_ref), custom_call_target="tpu_custom_call" | custom-call | tf_op jit(solution)/shard_map/prep/pallas_call | solution.py:505
  15.1 2.2 %all-to-all-done.rows_ref = f32[8,8,384]{2,1,0:T(8,128)S(1)} async-done(((f32[8,8,384]{2,1,0:T(8,128)}), f32[8,8,384]{2,1,0:T(8,128)S(1)}, u32[]{:S(2)}, u32[]{:S(2)}) %all-to-all-start) | async-done | bytes 98336 | tf_op jit(solution)/shard_map/all_to_all | solution.py:504
  17.3 0.0 copy-start
  17.3 2.2 %first_pass.3 = (bf16[8,256,256]{2,1,0:T(8,128)(2,1)S(1)}, bf16[272,256]{1,0:T(8,128)(2,1)S(1)}, f32[3,16,8,256]{3,2,1,0:T(8,128)S(1)}) custom-call(f32[8,8,384]{2,1,0:T(8,128)S(1)} %all-to-all-done.rows_ref, bf16[8,256,512]{2,1,0:T(8,128)(2,1)S(1)} %get-tuple-element.26.mat, f32[4,256,128]{2,1,0:T(8,128)S(1)} %get-tuple-element.27.consts.refs_2_), custom_call_target="tpu_custom_call" | custom-call | tf_op jit(solution)/shard_map/first_pass/pallas_call | solution.py:549
  19.5 0.4 %collective-permute-start.2 = (bf16[272,256]{1,0:T(8,128)(2,1)S(1)}, bf16[272,256]{1,0:T(8,128)(2,1)S(1)}, u32[]{:S(2)}, u32[]{:S(2)}) collective-permute-start(bf16[272,256]{1,0:T(8,128)(2,1)S(1)} %get-tuple-element.34.refs_4_), channel_id=1, source_target_pairs={{0,2},{2,0},{1,3},{3,1},{4,6},{6,4},{5,7},{7,5},{8,10},{10,8},{9,1... | collective-permute-start | bytes 417800 | tf_op jit(solution)/shard_map/ppermute | solution.py:596
  19.9 2.2 %first_pass.2 = (bf16[8,256,256]{2,1,0:T(8,128)(2,1)S(1)}, bf16[272,256]{1,0:T(8,128)(2,1)S(1)}, f32[3,16,8,256]{3,2,1,0:T(8,128)S(1)}) custom-call(f32[8,8,384]{2,1,0:T(8,128)S(1)} %all-to-all-done.rows_ref, bf16[8,256,512]{2,1,0:T(8,128)(2,1)S(1)} %get-tuple-element.26.mat, f32[4,256,128]{2,1,0:T(8,128)S(1)} %get-tuple-element.27.consts.refs_2_), custom_call_target="tpu_custom_call" | custom-call | tf_op jit(solution)/shard_map/first_pass/pallas_call | solution.py:549
  22.1 1.8 %collective-permute-start.1 = (bf16[272,256]{1,0:T(8,128)(2,1)S(1)}, bf16[272,256]{1,0:T(8,128)(2,1)S(1)}, u32[]{:S(2)}, u32[]{:S(2)}) collective-permute-start(bf16[272,256]{1,0:T(8,128)(2,1)S(1)} %get-tuple-element.31.refs_4_), channel_id=1, source_target_pairs={{0,2},{2,0},{1,3},{3,1},{4,6},{6,4},{5,7},{7,5},{8,10},{10,8},{9,1... | collective-permute-start | bytes 417800 | tf_op jit(solution)/shard_map/ppermute | solution.py:596
  23.8 1.6 %collective-permute-done.2.refs_5_ = bf16[272,256]{1,0:T(8,128)(2,1)S(1)} collective-permute-done((bf16[272,256]{1,0:T(8,128)(2,1)S(1)}, bf16[272,256]{1,0:T(8,128)(2,1)S(1)}, u32[]{:S(2)}, u32[]{:S(2)}) %collective-permute-start.2) | collective-permute-done | bytes 139296 | tf_op jit(solution)/shard_map/ppermute | solution.py:596
  25.4 0.0 copy-done
  25.4 2.7 %second_pass.2 = (f32[8,64,256]{2,1,0:T(8,128)S(1)}, f32[8,128]{1,0:T(8,128)S(1)}) custom-call(f32[3,16,8,256]{3,2,1,0:T(8,128)S(1)} %get-tuple-element.32.refs_0_, bf16[8,256,512]{2,1,0:T(8,128)(2,1)S(1)} %copy-done, f32[4,256,128]{2,1,0:T(8,128)S(1)} %get-tuple-element.27.consts.refs_2_, bf16[8,256,256]{2,1,0:T(8,128)(2,1)S(1)} %get-tuple-element.33.refs_3_, ...), custom_call_target="tpu_custom_call" | custom-call | tf_op jit(solution)/shard_map/second_pass/pallas_call | solution.py:577
  28.1 0.0 collective-permute-done.1.refs_5_
  28.1 2.6 %second_pass.3 = (f32[520,128]{1,0:T(8,128)S(1)}, f32[520,128]{1,0:T(8,128)S(1)}) custom-call(f32[3,16,8,256]{3,2,1,0:T(8,128)S(1)} %get-tuple-element.28.refs_0_, bf16[8,256,512]{2,1,0:T(8,128)(2,1)S(1)} %copy-done, f32[4,256,128]{2,1,0:T(8,128)S(1)} %get-tuple-element.27.consts.refs_2_, bf16[8,256,256]{2,1,0:T(8,128)(2,1)S(1)} %get-tuple-element.30.refs_3_, ...), custom_call_target="tpu_custom_call" | custom-call | tf_op jit(solution)/shard_map/second_pass/pallas_call | solution.py:577
  30.7 0.1 collective-permute-start.3
  30.8 1.5 %collective-permute-done.3.other_ref = f32[520,128]{1,0:T(8,128)S(1)} collective-permute-done((f32[520,128]{1,0:T(8,128)S(1)}, f32[520,128]{1,0:T(8,128)S(1)}, u32[]{:S(2)}, u32[]{:S(2)}) %collective-permute-start.3) | collective-permute-done | bytes 266272 | tf_op jit(solution)/shard_map/ppermute | solution.py:632
  32.3 0.8 %finish.1 = (f32[512,128]{1,0:T(8,128)}, f32[1]{0:T(128)}) custom-call(f32[520,128]{1,0:T(8,128)S(1)} %get-tuple-element.38.mine_ref, f32[520,128]{1,0:T(8,128)S(1)} %collective-permute-done.3.other_ref), custom_call_target="tpu_custom_call" | custom-call | tf_op jit(solution)/shard_map/finish/pallas_call | solution.py:633
Async XLA Ops:
  2.8 7.3 %collective-permute-start = (bf16[4,256,256]{2,1,0:T(8,128)(2,1)}, bf16[4,256,256]{2,1,0:T(8,128)(2,1)S(1)}, u32[]{:S(2)}, u32[]{:S(2)}) collective-permute-start(bf16[4,256,256]{2,1,0:T(8,128)(2,1)} %own_any.1), channel_id=1, source_target_pairs={{0,1},{1,0},{2,3},{3,2},{4,5},{5,4},{6,7},{7,6},{8,9},{9,8},{10,11... | collective-permute-start | bytes 1572872 | tf_op jit(solution)/shard_map/ppermute | solution.py:503
  3.3 14.0 %all-to-all-start = ((f32[8,8,384]{2,1,0:T(8,128)}), f32[8,8,384]{2,1,0:T(8,128)S(1)}, u32[]{:S(2)}, u32[]{:S(2)}) async-start(f32[8,8,384]{2,1,0:T(8,128)} %get-tuple-element.23), calls=%async_computation | async-start | bytes 196608 | tf_op jit(solution)/shard_map/all_to_all | solution.py:504
  10.2 0.8 %copy-start.1 = (bf16[4,256,256]{2,1,0:T(8,128)(2,1)}, bf16[4,256,256]{2,1,0:T(8,128)(2,1)S(1)}, u32[]{:S(2)}) copy-start(bf16[4,256,256]{2,1,0:T(8,128)(2,1)S(1)} %collective-permute-done.other_any) | copy-start | bytes 1572868
  17.3 8.1 %copy-start = (bf16[8,256,512]{2,1,0:T(8,128)(2,1)S(1)}, bf16[8,256,512]{2,1,0:T(8,128)(2,1)}, u32[]{:S(2)}) copy-start(bf16[8,256,512]{2,1,0:T(8,128)(2,1)} %get-tuple-element.29.refs_1_) | copy-start | bytes 6291460
  19.5 5.9 %collective-permute-start.2 = (bf16[272,256]{1,0:T(8,128)(2,1)S(1)}, bf16[272,256]{1,0:T(8,128)(2,1)S(1)}, u32[]{:S(2)}, u32[]{:S(2)}) collective-permute-start(bf16[272,256]{1,0:T(8,128)(2,1)S(1)} %get-tuple-element.34.refs_4_), channel_id=1, source_target_pairs={{0,2},{2,0},{1,3},{3,1},{4,6},{6,4},{5,7},{7,5},{8,10},{10,8},{9,1... | collective-permute-start | bytes 417800 | tf_op jit(solution)/shard_map/ppermute | solution.py:596
  22.1 6.0 %collective-permute-start.1 = (bf16[272,256]{1,0:T(8,128)(2,1)S(1)}, bf16[272,256]{1,0:T(8,128)(2,1)S(1)}, u32[]{:S(2)}, u32[]{:S(2)}) collective-permute-start(bf16[272,256]{1,0:T(8,128)(2,1)S(1)} %get-tuple-element.31.refs_4_), channel_id=1, source_target_pairs={{0,2},{2,0},{1,3},{3,1},{4,6},{6,4},{5,7},{7,5},{8,10},{10,8},{9,1... | collective-permute-start | bytes 417800 | tf_op jit(solution)/shard_map/ppermute | solution.py:596
  30.7 1.6 %collective-permute-start.3 = (f32[520,128]{1,0:T(8,128)S(1)}, f32[520,128]{1,0:T(8,128)S(1)}, u32[]{:S(2)}, u32[]{:S(2)}) collective-permute-start(f32[520,128]{1,0:T(8,128)S(1)} %get-tuple-element.39), channel_id=1, source_target_pairs={{0,1},{1,0},{2,3},{3,2},{4,5},{5,4},{6,7},{7,6},{8,9},{9,8},{10,11... | collective-permute-start | bytes 798728 | tf_op jit(solution)/shard_map/ppermute | solution.py:632

commit v14 on v13

--- a/solution.py
+++ b/solution.py
@@ -40,6 +40,10 @@
 
 def core_index():
     return lax.axis_index("st")
+
+
+def half_index():
+    return (lax.axis_index("st") + lax.axis_index("per")) % 2
 
 
 def is_forward_first():
@@ -70,7 +74,7 @@
         sems,
     )
     periods, slot_rows = earn_ref.shape
-    core = core_index()
+    core = half_index()
     low_lane = lax.broadcasted_iota(jnp.int32, (periods // 2, HB), 1) < HALF
     time = lax.broadcasted_iota(jnp.int32, (periods, HB), 0)
     for slot in range(slot_rows // HB):
@@ -501,7 +505,15 @@
     )
     packed, later_logits = lax.optimization_barrier((packed, trans_logits))
     other_logits = lax.ppermute(later_logits, "st", swap)
-    gathered = lax.all_to_all(packed, ("hh", "per"), split_axis=0, concat_axis=0, tiled=True)
+    places = [(z, x) for z in range(group // sides) for x in range(sides)]
+    gathered = lax.all_to_all(
+        packed,
+        ("hh", "per", "st"),
+        split_axis=0,
+        concat_axis=0,
+        axis_index_groups=[[(z * sides + x) * 2 + (half + x) % 2 for z, x in places] for half in range(2)],
+        tiled=True,
+    )
     first_mat, second_mat, row_probs, consts = pl.pallas_call(
         prep_kernel,
         out_shape=[
@@ -593,7 +605,7 @@
 
     def hand_over(state, stage):
         moves = [(stage, stage + 1), (sides - 1 - stage, sides - 2 - stage)]
-        return lax.ppermute(state, "per", moves)
+        return lax.ppermute(state, ("per", "st"), [(2 * a + c, 2 * b + 1 - c) for a, b in moves for c in range(2)])
 
     if sides == 2:
         kept = [first_pass(index, None) for index in range(parts)]

time: 33.5 us -> 33.7 us (level)
    ppermute x1, starting transfers between devices: 0.07 us -> 0.58 us  [per_device(): received = lax.ppermute(other, 'st', swap)]
    ppermute x2, waiting for transfers between devices: 1.57 us -> 1.95 us  [hand_over(): lax.ppermute(state, ('per', 'st'), [(2 * a + c, 2 * b + 1 - c) for a, b i...]
    ppermute x1, waiting for transfers between devices: 1.53 us -> 1.17 us  [per_device(): received = lax.ppermute(other, 'st', swap)]
  transfers between devices with their start and end apart: 5 -> 5, of which waited for: 3 -> 4; matrix products, arithmetic and copies ran while one was open for 0% -> 0% of each run, Pallas kernels for 27% -> 27%
where the time goes in v14:
time: 33.7 us; the launch traced here: 33.4 us
  Pallas kernels  16.1 us (48%)
  starting transfers between devices  9.85 us (29%)
  waiting for transfers between devices  5.16 us (15%)
  between operations  1.51 us (4%)
  local copies, waits for them, and re-layouts  0.79 us (2%)
    all_to_all x1, starting transfers between devices, per_device(): lax.all_to_all(packed, ('hh', 'per', 'st'), split_axis=0, concat_axis=0,...  6.91 us
    pallas_call x2, Pallas kernels, second_pass(): pl.pallas_call(functools.partial(second_kernel, resume, last, extend, gri...  5.27 us
    pallas_call x2, Pallas kernels, first_pass(): pl.pallas_call(functools.partial(first_kernel, resume, grids, index), gri...  4.39 us
    pallas_call x1, Pallas kernels, per_device(): pl.pallas_call(prep_kernel, out_shape=[pltpu.VMEM((steps, states, 2 * sta...  4.14 us
    all_to_all x1, waiting for transfers between devices, per_device(): lax.all_to_all(packed, ('hh', 'per', 'st'), split_axis=0, concat_axis=0,...  2.04 us
    ppermute x2, waiting for transfers between devices, hand_over(): lax.ppermute(state, ('per', 'st'), [(2 * a + c, 2 * b + 1 - c) for a, b i...  1.95 us
    ppermute x2, starting transfers between devices, hand_over(): lax.ppermute(state, ('per', 'st'), [(2 * a + c, 2 * b + 1 - c) for a, b i...  1.83 us
    pallas_call x1, Pallas kernels, per_device(): pl.pallas_call(pack_kernel, out_shape=[pltpu.VMEM((group, periods // 2, s...  1.55 us
  transfers between devices with their start and end apart: 5, of which 4 were waited for; matrix products, arithmetic and copies ran while one was open for 0% of the time, Pallas kernels for 27%

profile of v14, /device:TPU:0, one launch (start us, length us, event | category | flops | bytes accessed | tf_op | source)
XLA Modules:
  0.0 33.4 jit_solution(7569362233814705199)
XLA Ops:
  1.3 1.5 %pack.1 = (f32[8,8,384]{2,1,0:T(8,128)}, f32[8,256]{1,0:T(8,128)S(1)}) custom-call(s32[1]{0:T(128)S(6)} %copy.10.count_ref, f32[16,384]{1,0:T(8,128)} %bitcast.7, s32[3,128]{1,0:T(4,128)} %bitcast.8, s32[3,128]{1,0:T(4,128)} %bitcast.9, f32[1,256]{1,0:T(1,128)} %bitcast.10, f32[1,256]{1,0:T(1,128)} %bitcast.11, f32[1,256]{1,0:T(1,128)} %bitcast.12), custom_call_target="tpu_custom_call" | custom-call | tf_op jit(solution)/shard_map/pack/pallas_call | solution.py:480
  2.8 0.5 %collective-permute-start = (bf16[4,256,256]{2,1,0:T(8,128)(2,1)}, bf16[4,256,256]{2,1,0:T(8,128)(2,1)S(1)}, u32[]{:S(2)}, u32[]{:S(2)}) collective-permute-start(bf16[4,256,256]{2,1,0:T(8,128)(2,1)} %own_any.1), channel_id=1, source_target_pairs={{0,1},{1,0},{2,3},{3,2},{4,5},{5,4},{6,7},{7,6},{8,9},{9,8},{10,11... | collective-permute-start | bytes 1572872 | tf_op jit(solution)/shard_map/ppermute | solution.py:507
  3.3 6.9 %all-to-all-start = ((f32[8,8,384]{2,1,0:T(8,128)}), f32[8,8,384]{2,1,0:T(8,128)S(1)}, u32[]{:S(2)}, u32[]{:S(2)}) async-start(f32[8,8,384]{2,1,0:T(8,128)} %get-tuple-element.23), calls=%async_computation | async-start | bytes 196608 | tf_op jit(solution)/shard_map/all_to_all | solution.py:509
  10.3 0.0 collective-permute-done.other_any
  10.3 0.0 copy-start.1
  10.3 0.8 %copy-done.1 = bf16[4,256,256]{2,1,0:T(8,128)(2,1)} copy-done((bf16[4,256,256]{2,1,0:T(8,128)(2,1)}, bf16[4,256,256]{2,1,0:T(8,128)(2,1)S(1)}, u32[]{:S(2)}) %copy-start.1) | copy-done | bytes 524312
  11.1 4.1 %prep.1 = (bf16[8,256,512]{2,1,0:T(8,128)(2,1)S(1)}, bf16[8,256,512]{2,1,0:T(8,128)(2,1)}, f32[8,64,256]{2,1,0:T(8,128)S(1)}, f32[4,256,128]{2,1,0:T(8,128)S(1)}) custom-call(bf16[4,256,256]{2,1,0:T(8,128)(2,1)} %own_any.1, bf16[4,256,256]{2,1,0:T(8,128)(2,1)} %copy-done.1, f32[8,256]{1,0:T(8,128)S(1)} %get-tuple-element.25.vec_ref), custom_call_target="tpu_custom_call" | custom-call | tf_op jit(solution)/shard_map/prep/pallas_call | solution.py:517
  15.2 2.0 %all-to-all-done.rows_ref = f32[8,8,384]{2,1,0:T(8,128)S(1)} async-done(((f32[8,8,384]{2,1,0:T(8,128)}), f32[8,8,384]{2,1,0:T(8,128)S(1)}, u32[]{:S(2)}, u32[]{:S(2)}) %all-to-all-start) | async-done | bytes 98336 | tf_op jit(solution)/shard_map/all_to_all | solution.py:509
  17.3 0.0 copy-start
  17.3 2.2 %first_pass.3 = (bf16[8,256,256]{2,1,0:T(8,128)(2,1)S(1)}, bf16[272,256]{1,0:T(8,128)(2,1)S(1)}, f32[3,16,8,256]{3,2,1,0:T(8,128)S(1)}) custom-call(f32[8,8,384]{2,1,0:T(8,128)S(1)} %all-to-all-done.rows_ref, bf16[8,256,512]{2,1,0:T(8,128)(2,1)S(1)} %get-tuple-element.26.mat, f32[4,256,128]{2,1,0:T(8,128)S(1)} %get-tuple-element.27.consts.refs_2_), custom_call_target="tpu_custom_call" | custom-call | tf_op jit(solution)/shard_map/first_pass/pallas_call | solution.py:561
  19.5 0.1 collective-permute-start.2
  19.5 2.2 %first_pass.2 = (bf16[8,256,256]{2,1,0:T(8,128)(2,1)S(1)}, bf16[272,256]{1,0:T(8,128)(2,1)S(1)}, f32[3,16,8,256]{3,2,1,0:T(8,128)S(1)}) custom-call(f32[8,8,384]{2,1,0:T(8,128)S(1)} %all-to-all-done.rows_ref, bf16[8,256,512]{2,1,0:T(8,128)(2,1)S(1)} %get-tuple-element.26.mat, f32[4,256,128]{2,1,0:T(8,128)S(1)} %get-tuple-element.27.consts.refs_2_), custom_call_target="tpu_custom_call" | custom-call | tf_op jit(solution)/shard_map/first_pass/pallas_call | solution.py:561
  21.7 1.8 %collective-permute-start.1 = (bf16[272,256]{1,0:T(8,128)(2,1)S(1)}, bf16[272,256]{1,0:T(8,128)(2,1)S(1)}, u32[]{:S(2)}, u32[]{:S(2)}) collective-permute-start(bf16[272,256]{1,0:T(8,128)(2,1)S(1)} %get-tuple-element.31.refs_4_), channel_id=1, source_target_pairs={{0,3},{1,2},{2,1},{3,0},{4,7},{5,6},{6,5},{7,4},{8,11},{9,10},{10,... | collective-permute-start | bytes 417800 | tf_op jit(solution)/shard_map/ppermute | solution.py:608
  23.5 1.6 %collective-permute-done.2.refs_5_ = bf16[272,256]{1,0:T(8,128)(2,1)S(1)} collective-permute-done((bf16[272,256]{1,0:T(8,128)(2,1)S(1)}, bf16[272,256]{1,0:T(8,128)(2,1)S(1)}, u32[]{:S(2)}, u32[]{:S(2)}) %collective-permute-start.2) | collective-permute-done | bytes 139296 | tf_op jit(solution)/shard_map/ppermute | solution.py:608
  25.1 0.0 copy-done
  25.2 2.7 %second_pass.2 = (f32[8,64,256]{2,1,0:T(8,128)S(1)}, f32[8,128]{1,0:T(8,128)S(1)}) custom-call(f32[3,16,8,256]{3,2,1,0:T(8,128)S(1)} %get-tuple-element.32.refs_0_, bf16[8,256,512]{2,1,0:T(8,128)(2,1)S(1)} %copy-done, f32[4,256,128]{2,1,0:T(8,128)S(1)} %get-tuple-element.27.consts.refs_2_, bf16[8,256,256]{2,1,0:T(8,128)(2,1)S(1)} %get-tuple-element.33.refs_3_, ...), custom_call_target="tpu_custom_call" | custom-call | tf_op jit(solution)/shard_map/second_pass/pallas_call | solution.py:589
  27.8 0.3 collective-permute-done.1.refs_5_
  28.1 2.6 %second_pass.3 = (f32[520,128]{1,0:T(8,128)S(1)}, f32[520,128]{1,0:T(8,128)S(1)}) custom-call(f32[3,16,8,256]{3,2,1,0:T(8,128)S(1)} %get-tuple-element.28.refs_0_, bf16[8,256,512]{2,1,0:T(8,128)(2,1)S(1)} %copy-done, f32[4,256,128]{2,1,0:T(8,128)S(1)} %get-tuple-element.27.consts.refs_2_, bf16[8,256,256]{2,1,0:T(8,128)(2,1)S(1)} %get-tuple-element.30.refs_3_, ...), custom_call_target="tpu_custom_call" | custom-call | tf_op jit(solution)/shard_map/second_pass/pallas_call | solution.py:589
  30.7 0.6 %collective-permute-start.3 = (f32[520,128]{1,0:T(8,128)S(1)}, f32[520,128]{1,0:T(8,128)S(1)}, u32[]{:S(2)}, u32[]{:S(2)}) collective-permute-start(f32[520,128]{1,0:T(8,128)S(1)} %get-tuple-element.39), channel_id=1, source_target_pairs={{0,1},{1,0},{2,3},{3,2},{4,5},{5,4},{6,7},{7,6},{8,9},{9,8},{10,11... | collective-permute-start | bytes 798728 | tf_op jit(solution)/shard_map/ppermute | solution.py:644
  31.3 1.2 %collective-permute-done.3.other_ref = f32[520,128]{1,0:T(8,128)S(1)} collective-permute-done((f32[520,128]{1,0:T(8,128)S(1)}, f32[520,128]{1,0:T(8,128)S(1)}, u32[]{:S(2)}, u32[]{:S(2)}) %collective-permute-start.3) | collective-permute-done | bytes 266272 | tf_op jit(solution)/shard_map/ppermute | solution.py:644
  32.5 0.8 %finish.1 = (f32[512,128]{1,0:T(8,128)}, f32[1]{0:T(128)}) custom-call(f32[520,128]{1,0:T(8,128)S(1)} %get-tuple-element.38.mine_ref, f32[520,128]{1,0:T(8,128)S(1)} %collective-permute-done.3.other_ref), custom_call_target="tpu_custom_call" | custom-call | tf_op jit(solution)/shard_map/finish/pallas_call | solution.py:645
Async XLA Ops:
  2.8 7.4 %collective-permute-start = (bf16[4,256,256]{2,1,0:T(8,128)(2,1)}, bf16[4,256,256]{2,1,0:T(8,128)(2,1)S(1)}, u32[]{:S(2)}, u32[]{:S(2)}) collective-permute-start(bf16[4,256,256]{2,1,0:T(8,128)(2,1)} %own_any.1), channel_id=1, source_target_pairs={{0,1},{1,0},{2,3},{3,2},{4,5},{5,4},{6,7},{7,6},{8,9},{9,8},{10,11... | collective-permute-start | bytes 1572872 | tf_op jit(solution)/shard_map/ppermute | solution.py:507
  3.3 13.9 %all-to-all-start = ((f32[8,8,384]{2,1,0:T(8,128)}), f32[8,8,384]{2,1,0:T(8,128)S(1)}, u32[]{:S(2)}, u32[]{:S(2)}) async-start(f32[8,8,384]{2,1,0:T(8,128)} %get-tuple-element.23), calls=%async_computation | async-start | bytes 196608 | tf_op jit(solution)/shard_map/all_to_all | solution.py:509
  10.3 0.8 %copy-start.1 = (bf16[4,256,256]{2,1,0:T(8,128)(2,1)}, bf16[4,256,256]{2,1,0:T(8,128)(2,1)S(1)}, u32[]{:S(2)}) copy-start(bf16[4,256,256]{2,1,0:T(8,128)(2,1)S(1)} %collective-permute-done.other_any) | copy-start | bytes 1572868
  17.3 7.9 %copy-start = (bf16[8,256,512]{2,1,0:T(8,128)(2,1)S(1)}, bf16[8,256,512]{2,1,0:T(8,128)(2,1)}, u32[]{:S(2)}) copy-start(bf16[8,256,512]{2,1,0:T(8,128)(2,1)} %get-tuple-element.29.refs_1_) | copy-start | bytes 6291460
  19.5 5.7 %collective-permute-start.2 = (bf16[272,256]{1,0:T(8,128)(2,1)S(1)}, bf16[272,256]{1,0:T(8,128)(2,1)S(1)}, u32[]{:S(2)}, u32[]{:S(2)}) collective-permute-start(bf16[272,256]{1,0:T(8,128)(2,1)S(1)} %get-tuple-element.34.refs_4_), channel_id=1, source_target_pairs={{0,3},{1,2},{2,1},{3,0},{4,7},{5,6},{6,5},{7,4},{8,11},{9,10},{10,... | collective-permute-start | bytes 417800 | tf_op jit(solution)/shard_map/ppermute | solution.py:608
  21.7 6.4 %collective-permute-start.1 = (bf16[272,256]{1,0:T(8,128)(2,1)S(1)}, bf16[272,256]{1,0:T(8,128)(2,1)S(1)}, u32[]{:S(2)}, u32[]{:S(2)}) collective-permute-start(bf16[272,256]{1,0:T(8,128)(2,1)S(1)} %get-tuple-element.31.refs_4_), channel_id=1, source_target_pairs={{0,3},{1,2},{2,1},{3,0},{4,7},{5,6},{6,5},{7,4},{8,11},{9,10},{10,... | collective-permute-start | bytes 417800 | tf_op jit(solution)/shard_map/ppermute | solution.py:608
  30.7 1.8 %collective-permute-start.3 = (f32[520,128]{1,0:T(8,128)S(1)}, f32[520,128]{1,0:T(8,128)S(1)}, u32[]{:S(2)}, u32[]{:S(2)}) collective-permute-start(f32[520,128]{1,0:T(8,128)S(1)} %get-tuple-element.39), channel_id=1, source_target_pairs={{0,1},{1,0},{2,3},{3,2},{4,5},{5,4},{6,7},{7,6},{8,9},{9,8},{10,11... | collective-permute-start | bytes 798728 | tf_op jit(solution)/shard_map/ppermute | solution.py:644

commit v15 on v13

--- a/solution.py
+++ b/solution.py
@@ -501,7 +501,10 @@
     )
     packed, later_logits = lax.optimization_barrier((packed, trans_logits))
     other_logits = lax.ppermute(later_logits, "st", swap)
-    gathered = lax.all_to_all(packed, ("hh", "per"), split_axis=0, concat_axis=0, tiled=True)
+    downward = [[n * cores + c for n in reversed(range(group))] for c in range(cores)]
+    gathered = lax.all_to_all(
+        packed, ("hh", "per", "st"), split_axis=0, concat_axis=0, axis_index_groups=downward, tiled=True
+    )
     first_mat, second_mat, row_probs, consts = pl.pallas_call(
         prep_kernel,
         out_shape=[

time: 33.5 us -> 33.8 us (level)
  starting transfers between devices: 9.54 us -> 11.6 us
  waiting for transfers between devices: 5.29 us -> 3.47 us
    all_to_all x1, waiting for transfers between devices: 2.19 us -> 0.01 us  [per_device(): lax.all_to_all(packed, ('hh', 'per', 'st'), split_axis=0, concat_axis=0,...]
    all_to_all x1, starting transfers between devices: 6.83 us -> 8.86 us  [per_device(): lax.all_to_all(packed, ('hh', 'per', 'st'), split_axis=0, concat_axis=0,...]
    ppermute x2, waiting for transfers between devices: 1.57 us -> 1.94 us  [hand_over(): return lax.ppermute(state, 'per', moves)]
  transfers between devices with their start and end apart: 5 -> 5, of which waited for: 3 -> 2; matrix products, arithmetic and copies ran while one was open for 0% -> 0% of each run, Pallas kernels for 27% -> 27%
where the time goes in v15:
time: 33.8 us; the launch traced here: 33.5 us
  Pallas kernels  16.1 us (48%)
  starting transfers between devices  11.6 us (34%)
  waiting for transfers between devices  3.47 us (10%)
  between operations  1.52 us (4%)
  local copies, waits for them, and re-layouts  0.8 us (2%)
    all_to_all x1, starting transfers between devices, per_device(): lax.all_to_all(packed, ('hh', 'per', 'st'), split_axis=0, concat_axis=0,...  8.86 us
    pallas_call x2, Pallas kernels, second_pass(): pl.pallas_call(functools.partial(second_kernel, resume, last, extend, gri...  5.28 us
    pallas_call x2, Pallas kernels, first_pass(): pl.pallas_call(functools.partial(first_kernel, resume, grids, index), gri...  4.39 us
    pallas_call x1, Pallas kernels, per_device(): pl.pallas_call(prep_kernel, out_shape=[pltpu.VMEM((steps, states, 2 * sta...  4.14 us
    ppermute x2, starting transfers between devices, hand_over(): return lax.ppermute(state, 'per', moves)  2.13 us
    ppermute x2, waiting for transfers between devices, hand_over(): return lax.ppermute(state, 'per', moves)  1.94 us
    pallas_call x1, Pallas kernels, per_device(): pl.pallas_call(pack_kernel, out_shape=[pltpu.VMEM((group, periods // 2, s...  1.54 us
    ppermute x1, waiting for transfers between devices, per_device(): received = lax.ppermute(other, 'st', swap)  1.53 us
  transfers between devices with their start and end apart: 5, of which 2 were waited for; matrix products, arithmetic and copies ran while one was open for 0% of the time, Pallas kernels for 27%

profile of v15, /device:TPU:0, one launch (start us, length us, event | category | flops | bytes accessed | tf_op | source)
XLA Modules:
  0.0 33.5 jit_solution(8415714883979782828)
XLA Ops:
  1.3 1.5 %pack.1 = (f32[8,8,384]{2,1,0:T(8,128)}, f32[8,256]{1,0:T(8,128)S(1)}) custom-call(s32[1]{0:T(128)S(6)} %copy.10.count_ref, f32[16,384]{1,0:T(8,128)} %bitcast.7, s32[3,128]{1,0:T(4,128)} %bitcast.8, s32[3,128]{1,0:T(4,128)} %bitcast.9, f32[1,256]{1,0:T(1,128)} %bitcast.10, f32[1,256]{1,0:T(1,128)} %bitcast.11, f32[1,256]{1,0:T(1,128)} %bitcast.12), custom_call_target="tpu_custom_call" | custom-call | tf_op jit(solution)/shard_map/pack/pallas_call | solution.py:476
  2.8 0.5 %collective-permute-start = (bf16[4,256,256]{2,1,0:T(8,128)(2,1)}, bf16[4,256,256]{2,1,0:T(8,128)(2,1)S(1)}, u32[]{:S(2)}, u32[]{:S(2)}) collective-permute-start(bf16[4,256,256]{2,1,0:T(8,128)(2,1)} %own_any.1), channel_id=1, source_target_pairs={{0,1},{1,0},{2,3},{3,2},{4,5},{5,4},{6,7},{7,6},{8,9},{9,8},{10,11... | collective-permute-start | bytes 1572872 | tf_op jit(solution)/shard_map/ppermute | solution.py:503
  3.3 8.9 %all-to-all-start = ((f32[8,8,384]{2,1,0:T(8,128)}), f32[8,8,384]{2,1,0:T(8,128)S(1)}, u32[]{:S(2)}, u32[]{:S(2)}) async-start(f32[8,8,384]{2,1,0:T(8,128)} %get-tuple-element.23), calls=%async_computation | async-start | bytes 196608 | tf_op jit(solution)/shard_map/all_to_all | solution.py:505
  12.2 0.0 collective-permute-done.other_any
  12.2 0.0 copy-start.1
  12.2 0.8 %copy-done.1 = bf16[4,256,256]{2,1,0:T(8,128)(2,1)} copy-done((bf16[4,256,256]{2,1,0:T(8,128)(2,1)}, bf16[4,256,256]{2,1,0:T(8,128)(2,1)S(1)}, u32[]{:S(2)}) %copy-start.1) | copy-done | bytes 524312
  13.0 4.1 %prep.1 = (bf16[8,256,512]{2,1,0:T(8,128)(2,1)S(1)}, bf16[8,256,512]{2,1,0:T(8,128)(2,1)}, f32[8,64,256]{2,1,0:T(8,128)S(1)}, f32[4,256,128]{2,1,0:T(8,128)S(1)}) custom-call(bf16[4,256,256]{2,1,0:T(8,128)(2,1)} %own_any.1, bf16[4,256,256]{2,1,0:T(8,128)(2,1)} %copy-done.1, f32[8,256]{1,0:T(8,128)S(1)} %get-tuple-element.25.vec_ref), custom_call_target="tpu_custom_call" | custom-call | tf_op jit(solution)/shard_map/prep/pallas_call | solution.py:508
  17.2 0.0 all-to-all-done.rows_ref
  17.2 0.0 copy-start
  17.2 2.2 %first_pass.3 = (bf16[8,256,256]{2,1,0:T(8,128)(2,1)S(1)}, bf16[272,256]{1,0:T(8,128)(2,1)S(1)}, f32[3,16,8,256]{3,2,1,0:T(8,128)S(1)}) custom-call(f32[8,8,384]{2,1,0:T(8,128)S(1)} %all-to-all-done.rows_ref, bf16[8,256,512]{2,1,0:T(8,128)(2,1)S(1)} %get-tuple-element.26.mat, f32[4,256,128]{2,1,0:T(8,128)S(1)} %get-tuple-element.27.consts.refs_2_), custom_call_target="tpu_custom_call" | custom-call | tf_op jit(solution)/shard_map/first_pass/pallas_call | solution.py:552
  19.4 0.6 %collective-permute-start.2 = (bf16[272,256]{1,0:T(8,128)(2,1)S(1)}, bf16[272,256]{1,0:T(8,128)(2,1)S(1)}, u32[]{:S(2)}, u32[]{:S(2)}) collective-permute-start(bf16[272,256]{1,0:T(8,128)(2,1)S(1)} %get-tuple-element.34.refs_4_), channel_id=1, source_target_pairs={{0,2},{2,0},{1,3},{3,1},{4,6},{6,4},{5,7},{7,5},{8,10},{10,8},{9,1... | collective-permute-start | bytes 417800 | tf_op jit(solution)/shard_map/ppermute | solution.py:599
  19.9 2.2 %first_pass.2 = (bf16[8,256,256]{2,1,0:T(8,128)(2,1)S(1)}, bf16[272,256]{1,0:T(8,128)(2,1)S(1)}, f32[3,16,8,256]{3,2,1,0:T(8,128)S(1)}) custom-call(f32[8,8,384]{2,1,0:T(8,128)S(1)} %all-to-all-done.rows_ref, bf16[8,256,512]{2,1,0:T(8,128)(2,1)S(1)} %get-tuple-element.26.mat, f32[4,256,128]{2,1,0:T(8,128)S(1)} %get-tuple-element.27.consts.refs_2_), custom_call_target="tpu_custom_call" | custom-call | tf_op jit(solution)/shard_map/first_pass/pallas_call | solution.py:552
  22.2 1.6 %collective-permute-start.1 = (bf16[272,256]{1,0:T(8,128)(2,1)S(1)}, bf16[272,256]{1,0:T(8,128)(2,1)S(1)}, u32[]{:S(2)}, u32[]{:S(2)}) collective-permute-start(bf16[272,256]{1,0:T(8,128)(2,1)S(1)} %get-tuple-element.31.refs_4_), channel_id=1, source_target_pairs={{0,2},{2,0},{1,3},{3,1},{4,6},{6,4},{5,7},{7,5},{8,10},{10,8},{9,1... | collective-permute-start | bytes 417800 | tf_op jit(solution)/shard_map/ppermute | solution.py:599
  23.7 1.9 %collective-permute-done.2.refs_5_ = bf16[272,256]{1,0:T(8,128)(2,1)S(1)} collective-permute-done((bf16[272,256]{1,0:T(8,128)(2,1)S(1)}, bf16[272,256]{1,0:T(8,128)(2,1)S(1)}, u32[]{:S(2)}, u32[]{:S(2)}) %collective-permute-start.2) | collective-permute-done | bytes 139296 | tf_op jit(solution)/shard_map/ppermute | solution.py:599
  25.6 0.0 copy-done
  25.6 2.7 %second_pass.2 = (f32[8,64,256]{2,1,0:T(8,128)S(1)}, f32[8,128]{1,0:T(8,128)S(1)}) custom-call(f32[3,16,8,256]{3,2,1,0:T(8,128)S(1)} %get-tuple-element.32.refs_0_, bf16[8,256,512]{2,1,0:T(8,128)(2,1)S(1)} %copy-done, f32[4,256,128]{2,1,0:T(8,128)S(1)} %get-tuple-element.27.consts.refs_2_, bf16[8,256,256]{2,1,0:T(8,128)(2,1)S(1)} %get-tuple-element.33.refs_3_, ...), custom_call_target="tpu_custom_call" | custom-call | tf_op jit(solution)/shard_map/second_pass/pallas_call | solution.py:580
  28.3 0.0 collective-permute-done.1.refs_5_
  28.3 2.6 %second_pass.3 = (f32[520,128]{1,0:T(8,128)S(1)}, f32[520,128]{1,0:T(8,128)S(1)}) custom-call(f32[3,16,8,256]{3,2,1,0:T(8,128)S(1)} %get-tuple-element.28.refs_0_, bf16[8,256,512]{2,1,0:T(8,128)(2,1)S(1)} %copy-done, f32[4,256,128]{2,1,0:T(8,128)S(1)} %get-tuple-element.27.consts.refs_2_, bf16[8,256,256]{2,1,0:T(8,128)(2,1)S(1)} %get-tuple-element.30.refs_3_, ...), custom_call_target="tpu_custom_call" | custom-call | tf_op jit(solution)/shard_map/second_pass/pallas_call | solution.py:580
  31.0 0.1 collective-permute-start.3
  31.0 1.5 %collective-permute-done.3.other_ref = f32[520,128]{1,0:T(8,128)S(1)} collective-permute-done((f32[520,128]{1,0:T(8,128)S(1)}, f32[520,128]{1,0:T(8,128)S(1)}, u32[]{:S(2)}, u32[]{:S(2)}) %collective-permute-start.3) | collective-permute-done | bytes 266272 | tf_op jit(solution)/shard_map/ppermute | solution.py:635
  32.6 0.8 %finish.1 = (f32[512,128]{1,0:T(8,128)}, f32[1]{0:T(128)}) custom-call(f32[520,128]{1,0:T(8,128)S(1)} %get-tuple-element.38.mine_ref, f32[520,128]{1,0:T(8,128)S(1)} %collective-permute-done.3.other_ref), custom_call_target="tpu_custom_call" | custom-call | tf_op jit(solution)/shard_map/finish/pallas_call | solution.py:636
Async XLA Ops:
  2.8 9.4 %collective-permute-start = (bf16[4,256,256]{2,1,0:T(8,128)(2,1)}, bf16[4,256,256]{2,1,0:T(8,128)(2,1)S(1)}, u32[]{:S(2)}, u32[]{:S(2)}) collective-permute-start(bf16[4,256,256]{2,1,0:T(8,128)(2,1)} %own_any.1), channel_id=1, source_target_pairs={{0,1},{1,0},{2,3},{3,2},{4,5},{5,4},{6,7},{7,6},{8,9},{9,8},{10,11... | collective-permute-start | bytes 1572872 | tf_op jit(solution)/shard_map/ppermute | solution.py:503
  3.3 13.8 %all-to-all-start = ((f32[8,8,384]{2,1,0:T(8,128)}), f32[8,8,384]{2,1,0:T(8,128)S(1)}, u32[]{:S(2)}, u32[]{:S(2)}) async-start(f32[8,8,384]{2,1,0:T(8,128)} %get-tuple-element.23), calls=%async_computation | async-start | bytes 196608 | tf_op jit(solution)/shard_map/all_to_all | solution.py:505
  12.2 0.8 %copy-start.1 = (bf16[4,256,256]{2,1,0:T(8,128)(2,1)}, bf16[4,256,256]{2,1,0:T(8,128)(2,1)S(1)}, u32[]{:S(2)}) copy-start(bf16[4,256,256]{2,1,0:T(8,128)(2,1)S(1)} %collective-permute-done.other_any) | copy-start | bytes 1572868
  17.2 8.5 %copy-start = (bf16[8,256,512]{2,1,0:T(8,128)(2,1)S(1)}, bf16[8,256,512]{2,1,0:T(8,128)(2,1)}, u32[]{:S(2)}) copy-start(bf16[8,256,512]{2,1,0:T(8,128)(2,1)} %get-tuple-element.29.refs_1_) | copy-start | bytes 6291460
  19.4 6.3 %collective-permute-start.2 = (bf16[272,256]{1,0:T(8,128)(2,1)S(1)}, bf16[272,256]{1,0:T(8,128)(2,1)S(1)}, u32[]{:S(2)}, u32[]{:S(2)}) collective-permute-start(bf16[272,256]{1,0:T(8,128)(2,1)S(1)} %get-tuple-element.34.refs_4_), channel_id=1, source_target_pairs={{0,2},{2,0},{1,3},{3,1},{4,6},{6,4},{5,7},{7,5},{8,10},{10,8},{9,1... | collective-permute-start | bytes 417800 | tf_op jit(solution)/shard_map/ppermute | solution.py:599
  22.2 6.2 %collective-permute-start.1 = (bf16[272,256]{1,0:T(8,128)(2,1)S(1)}, bf16[272,256]{1,0:T(8,128)(2,1)S(1)}, u32[]{:S(2)}, u32[]{:S(2)}) collective-permute-start(bf16[272,256]{1,0:T(8,128)(2,1)S(1)} %get-tuple-element.31.refs_4_), channel_id=1, source_target_pairs={{0,2},{2,0},{1,3},{3,1},{4,6},{6,4},{5,7},{7,5},{8,10},{10,8},{9,1... | collective-permute-start | bytes 417800 | tf_op jit(solution)/shard_map/ppermute | solution.py:599
  31.0 1.6 %collective-permute-start.3 = (f32[520,128]{1,0:T(8,128)S(1)}, f32[520,128]{1,0:T(8,128)S(1)}, u32[]{:S(2)}, u32[]{:S(2)}) collective-permute-start(f32[520,128]{1,0:T(8,128)S(1)} %get-tuple-element.39), channel_id=1, source_target_pairs={{0,1},{1,0},{2,3},{3,2},{4,5},{5,4},{6,7},{7,6},{8,9},{9,8},{10,11... | collective-permute-start | bytes 798728 | tf_op jit(solution)/shard_map/ppermute | solution.py:635

commit v16 on v15

--- a/solution.py
+++ b/solution.py
@@ -107,49 +107,43 @@
     return high + jnp.dot(mat[:, states:], state, preferred_element_type=F32)
 
 
-def prep_kernel(
-    own_any, other_any, vec_ref, first_mat, second_any, row_probs, consts,
-    second_mat, scratch, own_ref, other_ref, sems, out_sems,
-):
+def fill_periods(mat, row_probs, scratch, turned_pass, source, ref):
+    @pl.loop(0, ref.shape[0])
+    def _(i):
+        at = source * ref.shape[0] + i
+        lifted = jnp.exp(ref[i].astype(F32))
+        probs = lifted * (1.0 / jnp.sum(lifted, axis=1, keepdims=True))
+        if row_probs is not None:
+            rows = row_probs.shape[1]
+            scratch[...] = probs
+            row_probs[at] = scratch[own_rows(lax.axis_index("hh") * rows, rows), :]
+
+        @pl.when(turned_pass)
+        def _():
+            put(mat, at, probs.T)
+
+        @pl.when(jnp.logical_not(turned_pass))
+        def _():
+            put(mat, at, probs)
+
+
+def prep_first_kernel(own_any, other_any, vec_ref, mat, consts, own_ref, other_ref, sems):
     copies = [
         pltpu.make_async_copy(src, dst, sems.at[i])
         for i, (src, dst) in enumerate(((own_any, own_ref), (other_any, other_ref)))
     ]
     for copy in copies:
         copy.start()
-    part, states, _ = own_ref.shape
-
-    def leave(at):
-        return pltpu.make_async_copy(second_mat.at[at], second_any.at[at], out_sems.at[at])
-
-    rows = row_probs.shape[1]
     for i in range(4):
-        consts[i] = jnp.broadcast_to(vec_ref[i : i + 1, :], (LANES, states)).T
+        consts[i] = jnp.broadcast_to(vec_ref[i : i + 1, :], (LANES, own_ref.shape[1])).T
     for copy, source, ref in zip(copies, (core_index(), 1 - core_index()), (own_ref, other_ref)):
         copy.wait()
-
-        @pl.loop(0, part)
-        def _(i):
-            at = source * part + i
-            lifted = jnp.exp(ref[i].astype(F32))
-            probs = lifted * (1.0 / jnp.sum(lifted, axis=1, keepdims=True))
-            scratch[...] = probs
-            row_probs[at] = scratch[own_rows(lax.axis_index("hh") * rows, rows), :]
-
-            @pl.when(is_forward_first())
-            def _():
-                put(first_mat, at, probs.T)
-                put(second_mat, at, probs)
-
-            @pl.when(jnp.logical_not(is_forward_first()))
-            def _():
-                put(first_mat, at, probs)
-                put(second_mat, at, probs.T)
-
-            leave(at).start()
-
-    for at in range(2 * part):
-        leave(at).wait()
+        fill_periods(mat, None, None, is_forward_first(), source, ref)
+
+
+def prep_second_kernel(own_ref, other_ref, after_any, mat, row_probs, scratch):
+    for source, ref in ((core_index(), own_ref), (1 - core_index(), other_ref)):
+        fill_periods(mat, row_probs, scratch, jnp.logical_not(is_forward_first()), source, ref)
 
 
 def emission(sel_ref, consts, step_now, cols, less=None):
@@ -505,27 +499,27 @@
     gathered = lax.all_to_all(
         packed, ("hh", "per", "st"), split_axis=0, concat_axis=0, axis_index_groups=downward, tiled=True
     )
-    first_mat, second_mat, row_probs, consts = pl.pallas_call(
-        prep_kernel,
-        out_shape=[
-            pltpu.VMEM((steps, states, 2 * states), BF16),
-            pltpu.HBM((steps, states, 2 * states), BF16),
-            pltpu.VMEM((steps, rows, states), F32),
-            pltpu.VMEM((4, states, LANES), F32),
-        ],
+    mat_shape = shaped((steps, states, 2 * states), BF16)
+    first_mat, consts = pl.pallas_call(
+        prep_first_kernel,
+        out_shape=[pltpu.VMEM(mat_shape.shape, BF16), pltpu.VMEM((4, states, LANES), F32)],
         in_specs=[hbm(), hbm(), vmem()],
-        out_specs=[vmem(), hbm(), vmem(), vmem()],
-        scratch_shapes=[
-            pltpu.VMEM((steps, states, 2 * states), BF16),
-            pltpu.VMEM((states, states), F32),
-            pltpu.VMEM(trans_logits.shape, BF16),
-            pltpu.VMEM(trans_logits.shape, BF16),
-            dma((2,)),
-            dma((steps,)),
-        ],
-        compiler_params=params(6),
-        name="prep",
+        out_specs=[vmem(), vmem()],
+        scratch_shapes=[pltpu.VMEM(trans_logits.shape, BF16), pltpu.VMEM(trans_logits.shape, BF16), dma((2,))],
+        compiler_params=params(4),
+        name="prep_first",
     )(*in_hbm(trans_logits, other_logits), vectors)
+
+    def prep_second(after):
+        return pl.pallas_call(
+            prep_second_kernel,
+            out_shape=[mat_shape, shaped((steps, rows, states), F32)],
+            in_specs=[vmem(), vmem(), hbm()],
+            out_specs=[vmem(), vmem()],
+            scratch_shapes=[pltpu.VMEM((states, states), F32)],
+            compiler_params=params(4),
+            name="prep_second",
+        )(trans_logits, other_logits, after)
 
     def whole(*shape):
         if grids == 1:
@@ -601,6 +595,7 @@
     if sides == 2:
         kept = [first_pass(index, None) for index in range(parts)]
         arrived = [hand_over(each[1], 0) for each in kept]
+        second_mat, row_probs = prep_second(kept[-1][1])
         sums = None
         for index in range(parts):
             sums = second_pass(kept[index], arrived[index], sums, index == parts - 1, False)
@@ -609,6 +604,7 @@
         kept = [jnp.zeros(x.shape, x.dtype) for x in (hist_shape, state_shape, sel_shape)]
         done = [jnp.zeros(x.shape, x.dtype) for x in (swap_shape, swap_shape, state_shape)]
         state = None
+        second_mat, row_probs = prep_second(gathered)
         for stage in range(sides):
             active = (side == stage) | (side == sides - 1 - stage)
             if stage < sides // 2:

time: 33.8 us -> 33.1 us (0.979)
  waiting for transfers between devices: 3.47 us -> 2.24 us
  Pallas kernels: 16.1 us -> 16.6 us
    ppermute x2, waiting for transfers between devices: 1.94 us -> 0.71 us  [hand_over(): return lax.ppermute(state, 'per', moves)]
    pallas_call x1 -> x2, Pallas kernels: 4.14 us -> 4.61 us  [the longest x1 3.2 us: per_device(): pl.pallas_call(prep_first_kernel, out_shape=[pltpu.VMEM(mat_shape.shape,...]
    unnamed x4 -> x6, local copies, waits for them, and re-layouts: 0.8 us -> 0.8 us
  transfers between devices with their start and end apart: 5 -> 5, of which waited for: 2 -> 2; matrix products, arithmetic and copies ran while one was open for 0% -> 0% of each run, Pallas kernels for 27% -> 29%
where the time goes in v16:
time: 33.1 us; the launch traced here: 32.8 us
  Pallas kernels  16.6 us (50%)
  starting transfers between devices  11.6 us (35%)
  waiting for transfers between devices  2.24 us (7%)
  between operations  1.54 us (5%)
  local copies, waits for them, and re-layouts  0.8 us (2%)
    all_to_all x1, starting transfers between devices, per_device(): lax.all_to_all(packed, ('hh', 'per', 'st'), split_axis=0, concat_axis=0,...  8.86 us
    pallas_call x2, Pallas kernels, second_pass(): pl.pallas_call(functools.partial(second_kernel, resume, last, extend, gri...  5.31 us
    pallas_call x2, Pallas kernels, first_pass(): pl.pallas_call(functools.partial(first_kernel, resume, grids, index), gri...  4.4 us
    pallas_call x1, Pallas kernels, per_device(): pl.pallas_call(prep_first_kernel, out_shape=[pltpu.VMEM(mat_shape.shape,...  3.2 us
    ppermute x2, starting transfers between devices, hand_over(): return lax.ppermute(state, 'per', moves)  2.14 us
    pallas_call x1, Pallas kernels, per_device(): pl.pallas_call(pack_kernel, out_shape=[pltpu.VMEM((group, periods // 2, s...  1.54 us
    ppermute x1, waiting for transfers between devices, per_device(): received = lax.ppermute(other, 'st', swap)  1.53 us
    pallas_call x1, Pallas kernels, prep_second(): pl.pallas_call(prep_second_kernel, out_shape=[mat_shape, shaped((steps, r...  1.41 us
  transfers between devices with their start and end apart: 5, of which 2 were waited for; matrix products, arithmetic and copies ran while one was open for 0% of the time, Pallas kernels for 29%

profile of v16, /device:TPU:0, one launch (start us, length us, event | category | flops | bytes accessed | tf_op | source)
XLA Modules:
  0.0 32.8 jit_solution(12557835232731754552)
XLA Ops:
  1.3 1.5 %pack.1 = (f32[8,8,384]{2,1,0:T(8,128)}, f32[8,256]{1,0:T(8,128)S(1)}) custom-call(s32[1]{0:T(128)S(6)} %copy.10.count_ref, f32[16,384]{1,0:T(8,128)} %bitcast.7, s32[3,128]{1,0:T(4,128)} %bitcast.8, s32[3,128]{1,0:T(4,128)} %bitcast.9, f32[1,256]{1,0:T(1,128)} %bitcast.10, f32[1,256]{1,0:T(1,128)} %bitcast.11, f32[1,256]{1,0:T(1,128)} %bitcast.12), custom_call_target="tpu_custom_call" | custom-call | tf_op jit(solution)/shard_map/pack/pallas_call | solution.py:470
  2.8 0.5 %collective-permute-start = (bf16[4,256,256]{2,1,0:T(8,128)(2,1)}, bf16[4,256,256]{2,1,0:T(8,128)(2,1)S(1)}, u32[]{:S(2)}, u32[]{:S(2)}) collective-permute-start(bf16[4,256,256]{2,1,0:T(8,128)(2,1)} %own_ref.1), channel_id=1, source_target_pairs={{0,1},{1,0},{2,3},{3,2},{4,5},{5,4},{6,7},{7,6},{8,9},{9,8},{10,11... | collective-permute-start | bytes 1572872 | tf_op jit(solution)/shard_map/ppermute | solution.py:497
  3.3 8.9 %all-to-all-start = ((f32[8,8,384]{2,1,0:T(8,128)}), f32[8,8,384]{2,1,0:T(8,128)S(1)}, u32[]{:S(2)}, u32[]{:S(2)}) async-start(f32[8,8,384]{2,1,0:T(8,128)} %get-tuple-element.23), calls=%async_computation | async-start | bytes 196608 | tf_op jit(solution)/shard_map/all_to_all | solution.py:499
  12.2 0.0 collective-permute-done.other_any.other_ref
  12.2 0.0 copy-start.1
  12.2 0.8 %copy-done.1 = bf16[4,256,256]{2,1,0:T(8,128)(2,1)} copy-done((bf16[4,256,256]{2,1,0:T(8,128)(2,1)}, bf16[4,256,256]{2,1,0:T(8,128)(2,1)S(1)}, u32[]{:S(2)}) %copy-start.1) | copy-done | bytes 524312
  13.0 3.2 %prep_first.1 = (bf16[8,256,512]{2,1,0:T(8,128)(2,1)S(1)}, f32[4,256,128]{2,1,0:T(8,128)S(1)}) custom-call(bf16[4,256,256]{2,1,0:T(8,128)(2,1)} %own_ref.1, bf16[4,256,256]{2,1,0:T(8,128)(2,1)} %copy-done.1, f32[8,256]{1,0:T(8,128)S(1)} %get-tuple-element.25.vec_ref), custom_call_target="tpu_custom_call" | custom-call | tf_op jit(solution)/shard_map/prep_first/pallas_call | solution.py:503
  16.2 0.0 all-to-all-done.rows_ref
  16.2 0.0 copy-start
  16.2 0.0 copy-start.2
  16.2 2.2 %first_pass.3 = (bf16[8,256,256]{2,1,0:T(8,128)(2,1)S(1)}, bf16[272,256]{1,0:T(8,128)(2,1)S(1)}, f32[3,16,8,256]{3,2,1,0:T(8,128)S(1)}) custom-call(f32[8,8,384]{2,1,0:T(8,128)S(1)} %all-to-all-done.rows_ref, bf16[8,256,512]{2,1,0:T(8,128)(2,1)S(1)} %get-tuple-element.26.mat, f32[4,256,128]{2,1,0:T(8,128)S(1)} %get-tuple-element.27.consts.refs_2_), custom_call_target="tpu_custom_call" | custom-call | tf_op jit(solution)/shard_map/first_pass/pallas_call | solution.py:546
  18.5 0.6 %collective-permute-start.2 = (bf16[272,256]{1,0:T(8,128)(2,1)S(1)}, bf16[272,256]{1,0:T(8,128)(2,1)S(1)}, u32[]{:S(2)}, u32[]{:S(2)}) collective-permute-start(bf16[272,256]{1,0:T(8,128)(2,1)S(1)} %get-tuple-element.34.refs_4_), channel_id=1, source_target_pairs={{0,2},{2,0},{1,3},{3,1},{4,6},{6,4},{5,7},{7,5},{8,10},{10,8},{9,1... | collective-permute-start | bytes 417800 | tf_op jit(solution)/shard_map/ppermute | solution.py:593
  19.0 2.2 %first_pass.2 = (bf16[8,256,256]{2,1,0:T(8,128)(2,1)S(1)}, bf16[272,256]{1,0:T(8,128)(2,1)S(1)}, f32[3,16,8,256]{3,2,1,0:T(8,128)S(1)}) custom-call(f32[8,8,384]{2,1,0:T(8,128)S(1)} %all-to-all-done.rows_ref, bf16[8,256,512]{2,1,0:T(8,128)(2,1)S(1)} %get-tuple-element.26.mat, f32[4,256,128]{2,1,0:T(8,128)S(1)} %get-tuple-element.27.consts.refs_2_), custom_call_target="tpu_custom_call" | custom-call | tf_op jit(solution)/shard_map/first_pass/pallas_call | solution.py:546
  21.2 1.6 %collective-permute-start.1 = (bf16[272,256]{1,0:T(8,128)(2,1)S(1)}, bf16[272,256]{1,0:T(8,128)(2,1)S(1)}, u32[]{:S(2)}, u32[]{:S(2)}) collective-permute-start(bf16[272,256]{1,0:T(8,128)(2,1)S(1)} %get-tuple-element.29.after_any.refs_4_), channel_id=1, source_target_pairs={{0,2},{2,0},{1,3},{3,1},{4,6},{6,4},{5,7},{7,5},{8,10},{10,8},{9,1... | collective-permute-start | bytes 417800 | tf_op jit(solution)/shard_map/ppermute | solution.py:593
  22.8 0.0 copy-done
  22.8 0.0 copy-done.2
  22.8 1.4 %prep_second.1 = (bf16[8,256,512]{2,1,0:T(8,128)(2,1)S(1)}, f32[8,64,256]{2,1,0:T(8,128)S(1)}) custom-call(bf16[4,256,256]{2,1,0:T(8,128)(2,1)S(1)} %copy-done, bf16[4,256,256]{2,1,0:T(8,128)(2,1)S(1)} %copy-done.2, bf16[272,256]{1,0:T(8,128)(2,1)S(1)} %get-tuple-element.29.after_any.refs_4_), custom_call_target="tpu_custom_call" | custom-call | tf_op jit(solution)/shard_map/prep_second/pallas_call | solution.py:514
  24.2 0.7 %collective-permute-done.2.refs_5_ = bf16[272,256]{1,0:T(8,128)(2,1)S(1)} collective-permute-done((bf16[272,256]{1,0:T(8,128)(2,1)S(1)}, bf16[272,256]{1,0:T(8,128)(2,1)S(1)}, u32[]{:S(2)}, u32[]{:S(2)}) %collective-permute-start.2) | collective-permute-done | bytes 139296 | tf_op jit(solution)/shard_map/ppermute | solution.py:593
  24.9 2.6 %second_pass.2 = (f32[8,64,256]{2,1,0:T(8,128)S(1)}, f32[8,128]{1,0:T(8,128)S(1)}) custom-call(f32[3,16,8,256]{3,2,1,0:T(8,128)S(1)} %get-tuple-element.32.refs_0_, bf16[8,256,512]{2,1,0:T(8,128)(2,1)S(1)} %get-tuple-element.30.refs_1_, f32[4,256,128]{2,1,0:T(8,128)S(1)} %get-tuple-element.27.consts.refs_2_, ...), custom_call_target="tpu_custom_call" | custom-call | tf_op jit(solution)/shard_map/second_pass/pallas_call | solution.py:574
  27.6 0.0 collective-permute-done.1.refs_5_
  27.6 2.7 %second_pass.3 = (f32[520,128]{1,0:T(8,128)S(1)}, f32[520,128]{1,0:T(8,128)S(1)}) custom-call(f32[3,16,8,256]{3,2,1,0:T(8,128)S(1)} %get-tuple-element.28.refs_0_, bf16[8,256,512]{2,1,0:T(8,128)(2,1)S(1)} %get-tuple-element.30.refs_1_, f32[4,256,128]{2,1,0:T(8,128)S(1)} %get-tuple-element.27.consts.refs_2_, ...), custom_call_target="tpu_custom_call" | custom-call | tf_op jit(solution)/shard_map/second_pass/pallas_call | solution.py:574
  30.3 0.1 collective-permute-start.3
  30.3 1.5 %collective-permute-done.3.other_ref = f32[520,128]{1,0:T(8,128)S(1)} collective-permute-done((f32[520,128]{1,0:T(8,128)S(1)}, f32[520,128]{1,0:T(8,128)S(1)}, u32[]{:S(2)}, u32[]{:S(2)}) %collective-permute-start.3) | collective-permute-done | bytes 266272 | tf_op jit(solution)/shard_map/ppermute | solution.py:631
  31.9 0.8 %finish.1 = (f32[512,128]{1,0:T(8,128)}, f32[1]{0:T(128)}) custom-call(f32[520,128]{1,0:T(8,128)S(1)} %get-tuple-element.38.mine_ref, f32[520,128]{1,0:T(8,128)S(1)} %collective-permute-done.3.other_ref), custom_call_target="tpu_custom_call" | custom-call | tf_op jit(solution)/shard_map/finish/pallas_call | solution.py:632
Async XLA Ops:
  2.8 9.4 %collective-permute-start = (bf16[4,256,256]{2,1,0:T(8,128)(2,1)}, bf16[4,256,256]{2,1,0:T(8,128)(2,1)S(1)}, u32[]{:S(2)}, u32[]{:S(2)}) collective-permute-start(bf16[4,256,256]{2,1,0:T(8,128)(2,1)} %own_ref.1), channel_id=1, source_target_pairs={{0,1},{1,0},{2,3},{3,2},{4,5},{5,4},{6,7},{7,6},{8,9},{9,8},{10,11... | collective-permute-start | bytes 1572872 | tf_op jit(solution)/shard_map/ppermute | solution.py:497
  3.3 12.9 %all-to-all-start = ((f32[8,8,384]{2,1,0:T(8,128)}), f32[8,8,384]{2,1,0:T(8,128)S(1)}, u32[]{:S(2)}, u32[]{:S(2)}) async-start(f32[8,8,384]{2,1,0:T(8,128)} %get-tuple-element.23), calls=%async_computation | async-start | bytes 196608 | tf_op jit(solution)/shard_map/all_to_all | solution.py:499
  12.2 0.8 %copy-start.1 = (bf16[4,256,256]{2,1,0:T(8,128)(2,1)}, bf16[4,256,256]{2,1,0:T(8,128)(2,1)S(1)}, u32[]{:S(2)}) copy-start(bf16[4,256,256]{2,1,0:T(8,128)(2,1)S(1)} %collective-permute-done.other_any.other_ref) | copy-start | bytes 1572868
  16.2 6.6 %copy-start = (bf16[4,256,256]{2,1,0:T(8,128)(2,1)S(1)}, bf16[4,256,256]{2,1,0:T(8,128)(2,1)}, u32[]{:S(2)}) copy-start(bf16[4,256,256]{2,1,0:T(8,128)(2,1)} %own_ref.1) | copy-start | bytes 1572868
  16.2 6.6 %copy-start.2 = (bf16[4,256,256]{2,1,0:T(8,128)(2,1)S(1)}, bf16[4,256,256]{2,1,0:T(8,128)(2,1)}, u32[]{:S(2)}) copy-start(bf16[4,256,256]{2,1,0:T(8,128)(2,1)} %copy-done.1) | copy-start | bytes 1572868
  18.5 6.5 %collective-permute-start.2 = (bf16[272,256]{1,0:T(8,128)(2,1)S(1)}, bf16[272,256]{1,0:T(8,128)(2,1)S(1)}, u32[]{:S(2)}, u32[]{:S(2)}) collective-permute-start(bf16[272,256]{1,0:T(8,128)(2,1)S(1)} %get-tuple-element.34.refs_4_), channel_id=1, source_target_pairs={{0,2},{2,0},{1,3},{3,1},{4,6},{6,4},{5,7},{7,5},{8,10},{10,8},{9,1... | collective-permute-start | bytes 417800 | tf_op jit(solution)/shard_map/ppermute | solution.py:593
  21.2 6.4 %collective-permute-start.1 = (bf16[272,256]{1,0:T(8,128)(2,1)S(1)}, bf16[272,256]{1,0:T(8,128)(2,1)S(1)}, u32[]{:S(2)}, u32[]{:S(2)}) collective-permute-start(bf16[272,256]{1,0:T(8,128)(2,1)S(1)} %get-tuple-element.29.after_any.refs_4_), channel_id=1, source_target_pairs={{0,2},{2,0},{1,3},{3,1},{4,6},{6,4},{5,7},{7,5},{8,10},{10,8},{9,1... | collective-permute-start | bytes 417800 | tf_op jit(solution)/shard_map/ppermute | solution.py:593
  30.3 1.6 %collective-permute-start.3 = (f32[520,128]{1,0:T(8,128)S(1)}, f32[520,128]{1,0:T(8,128)S(1)}, u32[]{:S(2)}, u32[]{:S(2)}) collective-permute-start(f32[520,128]{1,0:T(8,128)S(1)} %get-tuple-element.39), channel_id=1, source_target_pairs={{0,1},{1,0},{2,3},{3,2},{4,5},{5,4},{6,7},{7,6},{8,9},{9,8},{10,11... | collective-permute-start | bytes 798728 | tf_op jit(solution)/shard_map/ppermute | solution.py:631

commit v17 on v16

--- a/solution.py
+++ b/solution.py
@@ -107,43 +107,43 @@
     return high + jnp.dot(mat[:, states:], state, preferred_element_type=F32)
 
 
-def fill_periods(mat, row_probs, scratch, turned_pass, source, ref):
+def fill_periods(mat, turned_pass, source, ref):
     @pl.loop(0, ref.shape[0])
     def _(i):
         at = source * ref.shape[0] + i
-        lifted = jnp.exp(ref[i].astype(F32))
-        probs = lifted * (1.0 / jnp.sum(lifted, axis=1, keepdims=True))
-        if row_probs is not None:
-            rows = row_probs.shape[1]
-            scratch[...] = probs
-            row_probs[at] = scratch[own_rows(lax.axis_index("hh") * rows, rows), :]
 
         @pl.when(turned_pass)
         def _():
-            put(mat, at, probs.T)
+            lifted = jnp.exp(ref[i].T.astype(F32))
+            put(mat, at, lifted * (1.0 / jnp.sum(lifted, axis=0, keepdims=True)))
 
         @pl.when(jnp.logical_not(turned_pass))
         def _():
-            put(mat, at, probs)
-
-
-def prep_first_kernel(own_any, other_any, vec_ref, mat, consts, own_ref, other_ref, sems):
-    copies = [
-        pltpu.make_async_copy(src, dst, sems.at[i])
-        for i, (src, dst) in enumerate(((own_any, own_ref), (other_any, other_ref)))
-    ]
-    for copy in copies:
-        copy.start()
+            lifted = jnp.exp(ref[i].astype(F32))
+            put(mat, at, lifted * (1.0 / jnp.sum(lifted, axis=1, keepdims=True)))
+
+
+def prep_own_kernel(own_any, vec_ref, mat, consts, own_ref, sem):
+    copy = pltpu.make_async_copy(own_any, own_ref, sem)
+    copy.start()
     for i in range(4):
         consts[i] = jnp.broadcast_to(vec_ref[i : i + 1, :], (LANES, own_ref.shape[1])).T
-    for copy, source, ref in zip(copies, (core_index(), 1 - core_index()), (own_ref, other_ref)):
-        copy.wait()
-        fill_periods(mat, None, None, is_forward_first(), source, ref)
-
-
-def prep_second_kernel(own_ref, other_ref, after_any, mat, row_probs, scratch):
+    copy.wait()
+    fill_periods(mat, is_forward_first(), core_index(), own_ref)
+
+
+def prep_other_kernel(other_ref, mat_in, mat):
+    fill_periods(mat, is_forward_first(), 1 - core_index(), other_ref)
+
+
+def prep_second_kernel(own_ref, other_ref, after_any, mat, row_probs):
+    rows = row_probs.shape[1]
+    here = own_rows(lax.axis_index("hh") * rows, rows)
     for source, ref in ((core_index(), own_ref), (1 - core_index(), other_ref)):
-        fill_periods(mat, row_probs, scratch, jnp.logical_not(is_forward_first()), source, ref)
+        for i in range(ref.shape[0]):
+            lifted = jnp.exp(ref[i, here, :].astype(F32))
+            row_probs[source * ref.shape[0] + i] = lifted * (1.0 / jnp.sum(lifted, axis=1, keepdims=True))
+        fill_periods(mat, jnp.logical_not(is_forward_first()), source, ref)
 
 
 def emission(sel_ref, consts, step_now, cols, less=None):
@@ -495,20 +495,33 @@
     )
     packed, later_logits = lax.optimization_barrier((packed, trans_logits))
     other_logits = lax.ppermute(later_logits, "st", swap)
-    downward = [[n * cores + c for n in reversed(range(group))] for c in range(cores)]
+    along = group // sides
+    centre = along // 2
+    outward = sorted(range(along), key=lambda z: (abs(z - centre), -z))
+    listed = [z * sides + x for z in outward for x in reversed(range(sides))]
     gathered = lax.all_to_all(
-        packed, ("hh", "per", "st"), split_axis=0, concat_axis=0, axis_index_groups=downward, tiled=True
+        packed, ("hh", "per", "st"), split_axis=0, concat_axis=0,
+        axis_index_groups=[[n * cores + c for n in listed] for c in range(cores)], tiled=True,
     )
     mat_shape = shaped((steps, states, 2 * states), BF16)
     first_mat, consts = pl.pallas_call(
-        prep_first_kernel,
+        prep_own_kernel,
         out_shape=[pltpu.VMEM(mat_shape.shape, BF16), pltpu.VMEM((4, states, LANES), F32)],
-        in_specs=[hbm(), hbm(), vmem()],
+        in_specs=[hbm(), vmem()],
         out_specs=[vmem(), vmem()],
-        scratch_shapes=[pltpu.VMEM(trans_logits.shape, BF16), pltpu.VMEM(trans_logits.shape, BF16), dma((2,))],
+        scratch_shapes=[pltpu.VMEM(trans_logits.shape, BF16), dma],
         compiler_params=params(4),
-        name="prep_first",
-    )(*in_hbm(trans_logits, other_logits), vectors)
+        name="prep_own",
+    )(*in_hbm(trans_logits), vectors)
+    first_mat = pl.pallas_call(
+        prep_other_kernel,
+        out_shape=pltpu.VMEM(mat_shape.shape, BF16),
+        in_specs=[vmem(), vmem()],
+        out_specs=vmem(),
+        input_output_aliases={1: 0},
+        compiler_params=params(4),
+        name="prep_other",
+    )(other_logits, first_mat)
 
     def prep_second(after):
         return pl.pallas_call(
@@ -516,7 +529,6 @@
             out_shape=[mat_shape, shaped((steps, rows, states), F32)],
             in_specs=[vmem(), vmem(), hbm()],
             out_specs=[vmem(), vmem()],
-            scratch_shapes=[pltpu.VMEM((states, states), F32)],
             compiler_params=params(4),
             name="prep_second",
         )(trans_logits, other_logits, after)

time: 33.1 us -> 31.7 us (0.958)
  waiting for transfers between devices: 2.24 us -> 3.37 us
  starting transfers between devices: 11.6 us -> 10.6 us
  local copies, waits for them, and re-layouts: 0.8 us -> 0.01 us
  Pallas kernels: 16.6 us -> 15.9 us
    all_to_all x1, waiting for transfers between devices: 0.01 us -> 1.83 us  [per_device(): lax.all_to_all(packed, ('hh', 'per', 'st'), split_axis=0, concat_axis=0,...]
    all_to_all x1, starting transfers between devices: 8.86 us -> 7.84 us  [per_device(): lax.all_to_all(packed, ('hh', 'per', 'st'), split_axis=0, concat_axis=0,...]
    unnamed x6 -> x2, local copies, waits for them, and re-layouts: 0.8 us -> 0.01 us
    pallas_call x1 -> x2, Pallas kernels: 3.2 us -> 2.41 us  [the longest x1 1.72 us: per_device(): pl.pallas_call(prep_own_kernel, out_shape=[pltpu.VMEM(mat_shape.shape, BF...]
    ppermute x2, waiting for transfers between devices: 0.71 us -> 0.01 us  [hand_over(): return lax.ppermute(state, 'per', moves)]
  transfers between devices with their start and end apart: 5 -> 5, of which waited for: 2 -> 2; matrix products, arithmetic and copies ran while one was open for 0% -> 0% of each run, Pallas kernels for 29% -> 28%
where the time goes in v17:
time: 31.7 us; the launch traced here: 31.3 us
  Pallas kernels  15.9 us (50%)
  starting transfers between devices  10.6 us (33%)
  waiting for transfers between devices  3.37 us (11%)
  between operations  1.54 us (5%)
    all_to_all x1, starting transfers between devices, per_device(): lax.all_to_all(packed, ('hh', 'per', 'st'), split_axis=0, concat_axis=0,...  7.84 us
    pallas_call x2, Pallas kernels, second_pass(): pl.pallas_call(functools.partial(second_kernel, resume, last, extend, gri...  5.34 us
    pallas_call x2, Pallas kernels, first_pass(): pl.pallas_call(functools.partial(first_kernel, resume, grids, index), gri...  4.39 us
    ppermute x2, starting transfers between devices, hand_over(): return lax.ppermute(state, 'per', moves)  2.13 us
    all_to_all x1, waiting for transfers between devices, per_device(): lax.all_to_all(packed, ('hh', 'per', 'st'), split_axis=0, concat_axis=0,...  1.83 us
    pallas_call x1, Pallas kernels, per_device(): pl.pallas_call(prep_own_kernel, out_shape=[pltpu.VMEM(mat_shape.shape, BF...  1.72 us
    pallas_call x1, Pallas kernels, per_device(): pl.pallas_call(pack_kernel, out_shape=[pltpu.VMEM((group, periods // 2, s...  1.54 us
    ppermute x1, waiting for transfers between devices, per_device(): received = lax.ppermute(other, 'st', swap)  1.53 us
  transfers between devices with their start and end apart: 5, of which 2 were waited for; matrix products, arithmetic and copies ran while one was open for 0% of the time, Pallas kernels for 28%

profile of v17, /device:TPU:0, one launch (start us, length us, event | category | flops | bytes accessed | tf_op | source)
XLA Modules:
  0.0 31.3 jit_solution(1391962579606753540)
XLA Ops:
  1.3 1.5 %pack.1 = (f32[8,8,384]{2,1,0:T(8,128)}, f32[8,256]{1,0:T(8,128)S(1)}) custom-call(s32[1]{0:T(128)S(6)} %copy.12.count_ref, f32[16,384]{1,0:T(8,128)} %bitcast.7, s32[3,128]{1,0:T(4,128)} %bitcast.8, s32[3,128]{1,0:T(4,128)} %bitcast.9, f32[1,256]{1,0:T(1,128)} %bitcast.10, f32[1,256]{1,0:T(1,128)} %bitcast.11, f32[1,256]{1,0:T(1,128)} %bitcast.12), custom_call_target="tpu_custom_call" | custom-call | tf_op jit(solution)/shard_map/pack/pallas_call | solution.py:470
  2.8 0.5 %collective-permute-start = (bf16[4,256,256]{2,1,0:T(8,128)(2,1)}, bf16[4,256,256]{2,1,0:T(8,128)(2,1)S(1)}, u32[]{:S(2)}, u32[]{:S(2)}) collective-permute-start(bf16[4,256,256]{2,1,0:T(8,128)(2,1)} %own_ref.1), channel_id=1, source_target_pairs={{0,1},{1,0},{2,3},{3,2},{4,5},{5,4},{6,7},{7,6},{8,9},{9,8},{10,11... | collective-permute-start | bytes 1572872 | tf_op jit(solution)/shard_map/ppermute | solution.py:497
  3.3 7.8 %all-to-all-start = ((f32[8,8,384]{2,1,0:T(8,128)}), f32[8,8,384]{2,1,0:T(8,128)S(1)}, u32[]{:S(2)}, u32[]{:S(2)}) async-start(f32[8,8,384]{2,1,0:T(8,128)} %get-tuple-element.23), calls=%async_computation | async-start | bytes 196608 | tf_op jit(solution)/shard_map/all_to_all | solution.py:502
  11.2 1.7 %prep_own.1 = (bf16[8,256,512]{2,1,0:T(8,128)(2,1)S(1)}, f32[4,256,128]{2,1,0:T(8,128)S(1)}) custom-call(bf16[4,256,256]{2,1,0:T(8,128)(2,1)} %own_ref.1, f32[8,256]{1,0:T(8,128)S(1)} %get-tuple-element.25.vec_ref), custom_call_target="tpu_custom_call" | custom-call | tf_op jit(solution)/shard_map/prep_own/pallas_call | solution.py:507
  12.9 0.0 collective-permute-done.other_ref
  12.9 0.7 %prep_other.1.mat = bf16[8,256,512]{2,1,0:T(8,128)(2,1)S(1)} custom-call(bf16[4,256,256]{2,1,0:T(8,128)(2,1)S(1)} %collective-permute-done.other_ref, bf16[8,256,512]{2,1,0:T(8,128)(2,1)S(1)} %get-tuple-element.26.mat_in), custom_call_target="tpu_custom_call", output_to_operand_aliasing={{}: (1, {})} | custom-call | tf_op jit(solution)/shard_map/prep_other/pallas_call | solution.py:516
  13.6 1.8 %all-to-all-done.rows_ref = f32[8,8,384]{2,1,0:T(8,128)S(1)} async-done(((f32[8,8,384]{2,1,0:T(8,128)}), f32[8,8,384]{2,1,0:T(8,128)S(1)}, u32[]{:S(2)}, u32[]{:S(2)}) %all-to-all-start) | async-done | bytes 98336 | tf_op jit(solution)/shard_map/all_to_all | solution.py:502
  15.5 0.0 copy-start
  15.5 2.2 %first_pass.3 = (bf16[8,256,256]{2,1,0:T(8,128)(2,1)S(1)}, bf16[272,256]{1,0:T(8,128)(2,1)S(1)}, f32[3,16,8,256]{3,2,1,0:T(8,128)S(1)}) custom-call(f32[8,8,384]{2,1,0:T(8,128)S(1)} %all-to-all-done.rows_ref, bf16[8,256,512]{2,1,0:T(8,128)(2,1)S(1)} %prep_other.1.mat, f32[4,256,128]{2,1,0:T(8,128)S(1)} %get-tuple-element.27.consts.refs_2_), custom_call_target="tpu_custom_call" | custom-call | tf_op jit(solution)/shard_map/first_pass/pallas_call | solution.py:558
  17.7 0.6 %collective-permute-start.2 = (bf16[272,256]{1,0:T(8,128)(2,1)S(1)}, bf16[272,256]{1,0:T(8,128)(2,1)S(1)}, u32[]{:S(2)}, u32[]{:S(2)}) collective-permute-start(bf16[272,256]{1,0:T(8,128)(2,1)S(1)} %get-tuple-element.34.refs_4_), channel_id=1, source_target_pairs={{0,2},{2,0},{1,3},{3,1},{4,6},{6,4},{5,7},{7,5},{8,10},{10,8},{9,1... | collective-permute-start | bytes 417800 | tf_op jit(solution)/shard_map/ppermute | solution.py:605
  18.3 2.2 %first_pass.2 = (bf16[8,256,256]{2,1,0:T(8,128)(2,1)S(1)}, bf16[272,256]{1,0:T(8,128)(2,1)S(1)}, f32[3,16,8,256]{3,2,1,0:T(8,128)S(1)}) custom-call(f32[8,8,384]{2,1,0:T(8,128)S(1)} %all-to-all-done.rows_ref, bf16[8,256,512]{2,1,0:T(8,128)(2,1)S(1)} %prep_other.1.mat, f32[4,256,128]{2,1,0:T(8,128)S(1)} %get-tuple-element.27.consts.refs_2_), custom_call_target="tpu_custom_call" | custom-call | tf_op jit(solution)/shard_map/first_pass/pallas_call | solution.py:558
  20.5 1.5 %collective-permute-start.1 = (bf16[272,256]{1,0:T(8,128)(2,1)S(1)}, bf16[272,256]{1,0:T(8,128)(2,1)S(1)}, u32[]{:S(2)}, u32[]{:S(2)}) collective-permute-start(bf16[272,256]{1,0:T(8,128)(2,1)S(1)} %get-tuple-element.29.after_any.refs_4_), channel_id=1, source_target_pairs={{0,2},{2,0},{1,3},{3,1},{4,6},{6,4},{5,7},{7,5},{8,10},{10,8},{9,1... | collective-permute-start | bytes 417800 | tf_op jit(solution)/shard_map/ppermute | solution.py:605
  22.0 0.0 copy-done
  22.0 1.4 %prep_second.1 = (bf16[8,256,512]{2,1,0:T(8,128)(2,1)S(1)}, f32[8,64,256]{2,1,0:T(8,128)S(1)}) custom-call(bf16[4,256,256]{2,1,0:T(8,128)(2,1)S(1)} %copy-done, bf16[4,256,256]{2,1,0:T(8,128)(2,1)S(1)} %collective-permute-done.other_ref, bf16[272,256]{1,0:T(8,128)(2,1)S(1)} %get-tuple-element.29.after_any.refs_4_), custom_call_target="tpu_custom_call" | custom-call | tf_op jit(solution)/shard_map/prep_second/pallas_call | solution.py:527
  23.4 0.0 collective-permute-done.2.refs_5_
  23.4 2.7 %second_pass.2 = (f32[8,64,256]{2,1,0:T(8,128)S(1)}, f32[8,128]{1,0:T(8,128)S(1)}) custom-call(f32[3,16,8,256]{3,2,1,0:T(8,128)S(1)} %get-tuple-element.32.refs_0_, bf16[8,256,512]{2,1,0:T(8,128)(2,1)S(1)} %get-tuple-element.30.refs_1_, f32[4,256,128]{2,1,0:T(8,128)S(1)} %get-tuple-element.27.consts.refs_2_, ...), custom_call_target="tpu_custom_call" | custom-call | tf_op jit(solution)/shard_map/second_pass/pallas_call | solution.py:586
  26.1 0.0 collective-permute-done.1.refs_5_
  26.1 2.7 %second_pass.3 = (f32[520,128]{1,0:T(8,128)S(1)}, f32[520,128]{1,0:T(8,128)S(1)}) custom-call(f32[3,16,8,256]{3,2,1,0:T(8,128)S(1)} %get-tuple-element.28.refs_0_, bf16[8,256,512]{2,1,0:T(8,128)(2,1)S(1)} %get-tuple-element.30.refs_1_, f32[4,256,128]{2,1,0:T(8,128)S(1)} %get-tuple-element.27.consts.refs_2_, ...), custom_call_target="tpu_custom_call" | custom-call | tf_op jit(solution)/shard_map/second_pass/pallas_call | solution.py:586
  28.8 0.1 collective-permute-start.3
  28.9 1.5 %collective-permute-done.3.other_ref = f32[520,128]{1,0:T(8,128)S(1)} collective-permute-done((f32[520,128]{1,0:T(8,128)S(1)}, f32[520,128]{1,0:T(8,128)S(1)}, u32[]{:S(2)}, u32[]{:S(2)}) %collective-permute-start.3) | collective-permute-done | bytes 266272 | tf_op jit(solution)/shard_map/ppermute | solution.py:643
  30.4 0.8 %finish.1 = (f32[512,128]{1,0:T(8,128)}, f32[1]{0:T(128)}) custom-call(f32[520,128]{1,0:T(8,128)S(1)} %get-tuple-element.38.mine_ref, f32[520,128]{1,0:T(8,128)S(1)} %collective-permute-done.3.other_ref), custom_call_target="tpu_custom_call" | custom-call | tf_op jit(solution)/shard_map/finish/pallas_call | solution.py:644
Async XLA Ops:
  2.8 10.1 %collective-permute-start = (bf16[4,256,256]{2,1,0:T(8,128)(2,1)}, bf16[4,256,256]{2,1,0:T(8,128)(2,1)S(1)}, u32[]{:S(2)}, u32[]{:S(2)}) collective-permute-start(bf16[4,256,256]{2,1,0:T(8,128)(2,1)} %own_ref.1), channel_id=1, source_target_pairs={{0,1},{1,0},{2,3},{3,2},{4,5},{5,4},{6,7},{7,6},{8,9},{9,8},{10,11... | collective-permute-start | bytes 1572872 | tf_op jit(solution)/shard_map/ppermute | solution.py:497
  3.3 12.1 %all-to-all-start = ((f32[8,8,384]{2,1,0:T(8,128)}), f32[8,8,384]{2,1,0:T(8,128)S(1)}, u32[]{:S(2)}, u32[]{:S(2)}) async-start(f32[8,8,384]{2,1,0:T(8,128)} %get-tuple-element.23), calls=%async_computation | async-start | bytes 196608 | tf_op jit(solution)/shard_map/all_to_all | solution.py:502
  15.5 6.5 %copy-start = (bf16[4,256,256]{2,1,0:T(8,128)(2,1)S(1)}, bf16[4,256,256]{2,1,0:T(8,128)(2,1)}, u32[]{:S(2)}) copy-start(bf16[4,256,256]{2,1,0:T(8,128)(2,1)} %own_ref.1) | copy-start | bytes 1572868
  17.7 5.8 %collective-permute-start.2 = (bf16[272,256]{1,0:T(8,128)(2,1)S(1)}, bf16[272,256]{1,0:T(8,128)(2,1)S(1)}, u32[]{:S(2)}, u32[]{:S(2)}) collective-permute-start(bf16[272,256]{1,0:T(8,128)(2,1)S(1)} %get-tuple-element.34.refs_4_), channel_id=1, source_target_pairs={{0,2},{2,0},{1,3},{3,1},{4,6},{6,4},{5,7},{7,5},{8,10},{10,8},{9,1... | collective-permute-start | bytes 417800 | tf_op jit(solution)/shard_map/ppermute | solution.py:605
  20.5 5.7 %collective-permute-start.1 = (bf16[272,256]{1,0:T(8,128)(2,1)S(1)}, bf16[272,256]{1,0:T(8,128)(2,1)S(1)}, u32[]{:S(2)}, u32[]{:S(2)}) collective-permute-start(bf16[272,256]{1,0:T(8,128)(2,1)S(1)} %get-tuple-element.29.after_any.refs_4_), channel_id=1, source_target_pairs={{0,2},{2,0},{1,3},{3,1},{4,6},{6,4},{5,7},{7,5},{8,10},{10,8},{9,1... | collective-permute-start | bytes 417800 | tf_op jit(solution)/shard_map/ppermute | solution.py:605
  28.8 1.6 %collective-permute-start.3 = (f32[520,128]{1,0:T(8,128)S(1)}, f32[520,128]{1,0:T(8,128)S(1)}, u32[]{:S(2)}, u32[]{:S(2)}) collective-permute-start(f32[520,128]{1,0:T(8,128)S(1)} %get-tuple-element.39), channel_id=1, source_target_pairs={{0,1},{1,0},{2,3},{3,2},{4,5},{5,4},{6,7},{7,6},{8,9},{9,8},{10,11... | collective-permute-start | bytes 798728 | tf_op jit(solution)/shard_map/ppermute | solution.py:643

commit v18 on v17

--- a/solution.py
+++ b/solution.py
@@ -58,17 +58,8 @@
         copy.wait()
 
 
-def pack_kernel(
-    count_ref, earn_any, start_any, len_any, init_any, mean_any, sd_any, out_ref, vec_ref,
-    earn_ref, start_ref, len_ref, init_ref, mean_ref, sd_ref, sems,
-):
-    fetch(
-        (
-            (earn_any, earn_ref), (start_any, start_ref), (len_any, len_ref),
-            (init_any, init_ref), (mean_any, mean_ref), (sd_any, sd_ref),
-        ),
-        sems,
-    )
+def pack_kernel(count_ref, earn_any, start_any, len_any, out_ref, earn_ref, start_ref, len_ref, sems):
+    fetch(((earn_any, earn_ref), (start_any, start_ref), (len_any, len_ref)), sems)
     periods, slot_rows = earn_ref.shape
     core = core_index()
     low_lane = lax.broadcasted_iota(jnp.int32, (periods // 2, HB), 1) < HALF
@@ -85,13 +76,6 @@
         packed = jnp.where(low_lane, jnp.where(core == 0, early, turned), jnp.where(core == 0, turned, late))
         for to in range(out_ref.shape[0]):
             out_ref[to, :, cols] = packed
-    raised = jnp.exp(init_ref[...])
-    start = raised / jnp.sum(raised, axis=1, keepdims=True)
-    row = lax.broadcasted_iota(jnp.int32, vec_ref.shape, 0)
-    power = (-0.5 * LOG2E) * jnp.exp(-2.0 * sd_ref[...])
-    vec_ref[...] = jnp.where(
-        row == 0, start, jnp.where(row == 1, mean_ref[...], jnp.where(row == 2, power, -LOG2E * sd_ref[...]))
-    )
 
 
 def put(ref, at, value):
@@ -123,11 +107,21 @@
             put(mat, at, lifted * (1.0 / jnp.sum(lifted, axis=1, keepdims=True)))
 
 
-def prep_own_kernel(own_any, vec_ref, mat, consts, own_ref, sem):
+def prep_own_kernel(
+    own_any, init_any, mean_any, sd_any, mat, consts, own_ref, init_ref, mean_ref, sd_ref, sem, sems
+):
     copy = pltpu.make_async_copy(own_any, own_ref, sem)
     copy.start()
-    for i in range(4):
-        consts[i] = jnp.broadcast_to(vec_ref[i : i + 1, :], (LANES, own_ref.shape[1])).T
+    fetch(((init_any, init_ref), (mean_any, mean_ref), (sd_any, sd_ref)), sems)
+    raised = jnp.exp(init_ref[...])
+    rows = (
+        raised / jnp.sum(raised, axis=1, keepdims=True),
+        mean_ref[...],
+        (-0.5 * LOG2E) * jnp.exp(-2.0 * sd_ref[...]),
+        -LOG2E * sd_ref[...],
+    )
+    for i, row in enumerate(rows):
+        consts[i] = jnp.broadcast_to(row, (LANES, own_ref.shape[1])).T
     copy.wait()
     fill_periods(mat, is_forward_first(), core_index(), own_ref)
 
@@ -172,7 +166,7 @@
     return lax.dot_general(weights_ref[...], carried, (((1,), (1,)), ((), ())), preferred_element_type=F32)
 
 
-def run_forward(lead, mat, hist, sel_ref, consts, ab_ref, logs, second=None):
+def run_forward(lead, mat, hist, sel_ref, consts, ab_ref, logs, second=None, fresh=False):
     steps, states, width = hist.shape
     cuts = tiles(width)
     inverse = [1.0 / column_sum(ab_ref[:, cols].astype(F32)) for cols in cuts]
@@ -184,14 +178,16 @@
             weights_ref, row_begin, add_counts = second
             own_alpha = ab_ref[own_rows(row_begin, weights_ref.shape[0]), :].astype(F32)
         for q, cols in enumerate(cuts):
-            moved = both_halves(mat[k], ab_ref[:, cols]) * inverse[q]
-            moving = is_moving(sel_ref, step_now, cols)
+            begins = fresh and k == 0
+            if not begins:
+                moved = both_halves(mat[k], ab_ref[:, cols]) * inverse[q]
+                moving = is_moving(sel_ref, step_now, cols)
             if second is not None:
                 total = column_sum(moved * hist[k, :, cols].astype(F32))
                 weight = jnp.where(moving, 1.0 / total, 0.0)
                 weights_ref[:, cols] = (own_alpha[:, cols] * inverse[q] * weight).astype(BF16)
             emit = emission(sel_ref, consts, step_now, cols)
-            joint = jnp.where(moving, moved, consts[0]) * emit
+            joint = (consts[0] if begins else jnp.where(moving, moved, consts[0])) * emit
             scale = column_sum(joint)
             if second is None:
                 seen = is_seen(sel_ref, step_now, cols)
@@ -339,7 +335,8 @@
             for cols in cuts:
                 ab_ref[:, cols] = consts[0].astype(BF16)
         logs = state_logs(state_in) if resume else list(zeros)
-        run_forward(lead, mat, hist, sel_ref, consts, ab_ref, logs)
+        fresh = lax.axis_size("per") == 2
+        run_forward(lead, mat, hist, sel_ref, consts, ab_ref, logs, fresh=fresh)
         put_state(state_out, [ab_ref[:, cols] for cols in cuts], logs)
 
     @pl.when(jnp.logical_not(forward_first))
@@ -467,32 +464,16 @@
 
     swap = [(0, 1), (1, 0)]
     vec_row = pltpu.VMEM((1, states), F32)
-    packed, vectors = pl.pallas_call(
+    slots = pltpu.VMEM((slot_rows // HB, HB), jnp.int32)
+    packed = pl.pallas_call(
         pack_kernel,
-        out_shape=[
-            pltpu.VMEM((group, periods // 2, slot_rows), F32),
-            pltpu.VMEM((8, states), F32),
-        ],
-        in_specs=[smem()] + [hbm()] * 6,
-        out_specs=[vmem()] * 2,
-        scratch_shapes=[
-            pltpu.VMEM((periods, slot_rows), F32),
-            pltpu.VMEM((slot_rows // HB, HB), jnp.int32),
-            pltpu.VMEM((slot_rows // HB, HB), jnp.int32),
-            vec_row,
-            vec_row,
-            vec_row,
-            dma((6,)),
-        ],
+        out_shape=pltpu.VMEM((group, periods // 2, slot_rows), F32),
+        in_specs=[smem()] + [hbm()] * 3,
+        out_specs=vmem(),
+        scratch_shapes=[pltpu.VMEM((periods, slot_rows), F32), slots, slots, dma((3,))],
         compiler_params=params(2),
         name="pack",
-    )(
-        block_count,
-        *in_hbm(
-            earnings.T, starts.reshape(-1, HB), lengths.reshape(-1, HB),
-            init_logits.reshape(1, states), state_mean.reshape(1, states), log_sd.reshape(1, states),
-        ),
-    )
+    )(block_count, *in_hbm(earnings.T, starts.reshape(-1, HB), lengths.reshape(-1, HB)))
     packed, later_logits = lax.optimization_barrier((packed, trans_logits))
     other_logits = lax.ppermute(later_logits, "st", swap)
     along = group // sides
@@ -507,12 +488,17 @@
     first_mat, consts = pl.pallas_call(
         prep_own_kernel,
         out_shape=[pltpu.VMEM(mat_shape.shape, BF16), pltpu.VMEM((4, states, LANES), F32)],
-        in_specs=[hbm(), vmem()],
+        in_specs=[hbm()] * 4,
         out_specs=[vmem(), vmem()],
-        scratch_shapes=[pltpu.VMEM(trans_logits.shape, BF16), dma],
+        scratch_shapes=[pltpu.VMEM(trans_logits.shape, BF16), vec_row, vec_row, vec_row, dma, dma((3,))],
         compiler_params=params(4),
         name="prep_own",
-    )(*in_hbm(trans_logits), vectors)
+    )(
+        *in_hbm(
+            trans_logits,
+            init_logits.reshape(1, states), state_mean.reshape(1, states), log_sd.reshape(1, states),
+        )
+    )
     first_mat = pl.pallas_call(
         prep_other_kernel,
         out_shape=pltpu.VMEM(mat_shape.shape, BF16),

time: 31.7 us -> 31.4 us (level)
  Pallas kernels: 15.9 us -> 15.5 us
    pallas_call x2, Pallas kernels: 4.39 us -> 4.03 us  [first_pass(): pl.pallas_call(functools.partial(first_kernel, resume, grids, index), gri...]
where the time goes in v18:
time: 31.4 us; the launch traced here: 31.1 us
  Pallas kernels  15.5 us (49%)
  starting transfers between devices  10.7 us (34%)
  waiting for transfers between devices  3.28 us (10%)
  between operations  1.54 us (5%)
    all_to_all x1, starting transfers between devices, per_device(): lax.all_to_all(packed, ('hh', 'per', 'st'), split_axis=0, concat_axis=0,...  7.84 us
    pallas_call x2, Pallas kernels, second_pass(): pl.pallas_call(functools.partial(second_kernel, resume, last, extend, gri...  5.34 us
    pallas_call x2, Pallas kernels, first_pass(): pl.pallas_call(functools.partial(first_kernel, resume, grids, index), gri...  4.03 us
    ppermute x2, starting transfers between devices, hand_over(): return lax.ppermute(state, 'per', moves)  2.32 us
    pallas_call x1, Pallas kernels, per_device(): pl.pallas_call(prep_own_kernel, out_shape=[pltpu.VMEM(mat_shape.shape, BF...  1.81 us
    all_to_all x1, waiting for transfers between devices, per_device(): lax.all_to_all(packed, ('hh', 'per', 'st'), split_axis=0, concat_axis=0,...  1.74 us
    ppermute x1, waiting for transfers between devices, per_device(): received = lax.ppermute(other, 'st', swap)  1.53 us
    pallas_call x1, Pallas kernels, per_device(): pl.pallas_call(pack_kernel, out_shape=pltpu.VMEM((group, periods // 2, sl...  1.49 us
  transfers between devices with their start and end apart: 5, of which 2 were waited for; matrix products, arithmetic and copies ran while one was open for 0% of the time, Pallas kernels for 28%

profile of v18, /device:TPU:0, one launch (start us, length us, event | category | flops | bytes accessed | tf_op | source)
XLA Modules:
  0.0 31.1 jit_solution(574786155624331494)
XLA Ops:
  1.3 1.5 %pack.1 = f32[8,8,384]{2,1,0:T(8,128)} custom-call(s32[1]{0:T(128)S(6)} %copy.12.count_ref, f32[16,384]{1,0:T(8,128)} %bitcast.7, s32[3,128]{1,0:T(4,128)} %bitcast.8, s32[3,128]{1,0:T(4,128)} %bitcast.9), custom_call_target="tpu_custom_call" | custom-call | tf_op jit(solution)/shard_map/pack/pallas_call | solution.py:468
  2.8 0.5 %collective-permute-start = (bf16[4,256,256]{2,1,0:T(8,128)(2,1)}, bf16[4,256,256]{2,1,0:T(8,128)(2,1)S(1)}, u32[]{:S(2)}, u32[]{:S(2)}) collective-permute-start(bf16[4,256,256]{2,1,0:T(8,128)(2,1)} %own_ref.1), channel_id=1, source_target_pairs={{0,1},{1,0},{2,3},{3,2},{4,5},{5,4},{6,7},{7,6},{8,9},{9,8},{10,11... | collective-permute-start | bytes 1572872 | tf_op jit(solution)/shard_map/ppermute | solution.py:478
  3.3 7.8 %all-to-all-start = ((f32[8,8,384]{2,1,0:T(8,128)}), f32[8,8,384]{2,1,0:T(8,128)S(1)}, u32[]{:S(2)}, u32[]{:S(2)}) async-start(f32[8,8,384]{2,1,0:T(8,128)} %pack.1), calls=%async_computation | async-start | bytes 196608 | tf_op jit(solution)/shard_map/all_to_all | solution.py:483
  11.1 1.8 %prep_own.1 = (bf16[8,256,512]{2,1,0:T(8,128)(2,1)S(1)}, f32[4,256,128]{2,1,0:T(8,128)S(1)}) custom-call(bf16[4,256,256]{2,1,0:T(8,128)(2,1)} %own_ref.1, f32[1,256]{1,0:T(1,128)} %bitcast.10, f32[1,256]{1,0:T(1,128)} %bitcast.11, f32[1,256]{1,0:T(1,128)} %bitcast.12), custom_call_target="tpu_custom_call" | custom-call | tf_op jit(solution)/shard_map/prep_own/pallas_call | solution.py:488
  13.0 0.0 collective-permute-done.other_ref
  13.0 0.7 %prep_other.1.mat = bf16[8,256,512]{2,1,0:T(8,128)(2,1)S(1)} custom-call(bf16[4,256,256]{2,1,0:T(8,128)(2,1)S(1)} %collective-permute-done.other_ref, bf16[8,256,512]{2,1,0:T(8,128)(2,1)S(1)} %get-tuple-element.22.mat_in), custom_call_target="tpu_custom_call", output_to_operand_aliasing={{}: (1, {})} | custom-call | tf_op jit(solution)/shard_map/prep_other/pallas_call | solution.py:502
  13.7 1.7 %all-to-all-done.rows_ref = f32[8,8,384]{2,1,0:T(8,128)S(1)} async-done(((f32[8,8,384]{2,1,0:T(8,128)}), f32[8,8,384]{2,1,0:T(8,128)S(1)}, u32[]{:S(2)}, u32[]{:S(2)}) %all-to-all-start) | async-done | bytes 98336 | tf_op jit(solution)/shard_map/all_to_all | solution.py:483
  15.4 0.0 copy-start
  15.4 2.0 %first_pass.3 = (bf16[8,256,256]{2,1,0:T(8,128)(2,1)S(1)}, bf16[272,256]{1,0:T(8,128)(2,1)S(1)}, f32[3,16,8,256]{3,2,1,0:T(8,128)S(1)}) custom-call(f32[8,8,384]{2,1,0:T(8,128)S(1)} %all-to-all-done.rows_ref, bf16[8,256,512]{2,1,0:T(8,128)(2,1)S(1)} %prep_other.1.mat, f32[4,256,128]{2,1,0:T(8,128)S(1)} %get-tuple-element.23.consts.refs_2_), custom_call_target="tpu_custom_call" | custom-call | tf_op jit(solution)/shard_map/first_pass/pallas_call | solution.py:544
  17.4 0.8 %collective-permute-start.2 = (bf16[272,256]{1,0:T(8,128)(2,1)S(1)}, bf16[272,256]{1,0:T(8,128)(2,1)S(1)}, u32[]{:S(2)}, u32[]{:S(2)}) collective-permute-start(bf16[272,256]{1,0:T(8,128)(2,1)S(1)} %get-tuple-element.30.refs_4_), channel_id=1, source_target_pairs={{0,2},{2,0},{1,3},{3,1},{4,6},{6,4},{5,7},{7,5},{8,10},{10,8},{9,1... | collective-permute-start | bytes 417800 | tf_op jit(solution)/shard_map/ppermute | solution.py:591
  18.2 2.0 %first_pass.2 = (bf16[8,256,256]{2,1,0:T(8,128)(2,1)S(1)}, bf16[272,256]{1,0:T(8,128)(2,1)S(1)}, f32[3,16,8,256]{3,2,1,0:T(8,128)S(1)}) custom-call(f32[8,8,384]{2,1,0:T(8,128)S(1)} %all-to-all-done.rows_ref, bf16[8,256,512]{2,1,0:T(8,128)(2,1)S(1)} %prep_other.1.mat, f32[4,256,128]{2,1,0:T(8,128)S(1)} %get-tuple-element.23.consts.refs_2_), custom_call_target="tpu_custom_call" | custom-call | tf_op jit(solution)/shard_map/first_pass/pallas_call | solution.py:544
  20.2 1.5 %collective-permute-start.1 = (bf16[272,256]{1,0:T(8,128)(2,1)S(1)}, bf16[272,256]{1,0:T(8,128)(2,1)S(1)}, u32[]{:S(2)}, u32[]{:S(2)}) collective-permute-start(bf16[272,256]{1,0:T(8,128)(2,1)S(1)} %get-tuple-element.25.after_any.refs_4_), channel_id=1, source_target_pairs={{0,2},{2,0},{1,3},{3,1},{4,6},{6,4},{5,7},{7,5},{8,10},{10,8},{9,1... | collective-permute-start | bytes 417800 | tf_op jit(solution)/shard_map/ppermute | solution.py:591
  21.8 0.0 copy-done
  21.8 1.4 %prep_second.1 = (bf16[8,256,512]{2,1,0:T(8,128)(2,1)S(1)}, f32[8,64,256]{2,1,0:T(8,128)S(1)}) custom-call(bf16[4,256,256]{2,1,0:T(8,128)(2,1)S(1)} %copy-done, bf16[4,256,256]{2,1,0:T(8,128)(2,1)S(1)} %collective-permute-done.other_ref, bf16[272,256]{1,0:T(8,128)(2,1)S(1)} %get-tuple-element.25.after_any.refs_4_), custom_call_target="tpu_custom_call" | custom-call | tf_op jit(solution)/shard_map/prep_second/pallas_call | solution.py:513
  23.2 0.0 collective-permute-done.2.refs_5_
  23.2 2.7 %second_pass.2 = (f32[8,64,256]{2,1,0:T(8,128)S(1)}, f32[8,128]{1,0:T(8,128)S(1)}) custom-call(f32[3,16,8,256]{3,2,1,0:T(8,128)S(1)} %get-tuple-element.28.refs_0_, bf16[8,256,512]{2,1,0:T(8,128)(2,1)S(1)} %get-tuple-element.26.refs_1_, f32[4,256,128]{2,1,0:T(8,128)S(1)} %get-tuple-element.23.consts.refs_2_, ...), custom_call_target="tpu_custom_call" | custom-call | tf_op jit(solution)/shard_map/second_pass/pallas_call | solution.py:572
  25.9 0.0 collective-permute-done.1.refs_5_
  25.9 2.7 %second_pass.3 = (f32[520,128]{1,0:T(8,128)S(1)}, f32[520,128]{1,0:T(8,128)S(1)}) custom-call(f32[3,16,8,256]{3,2,1,0:T(8,128)S(1)} %get-tuple-element.24.refs_0_, bf16[8,256,512]{2,1,0:T(8,128)(2,1)S(1)} %get-tuple-element.26.refs_1_, f32[4,256,128]{2,1,0:T(8,128)S(1)} %get-tuple-element.23.consts.refs_2_, ...), custom_call_target="tpu_custom_call" | custom-call | tf_op jit(solution)/shard_map/second_pass/pallas_call | solution.py:572
  28.6 0.1 collective-permute-start.3
  28.7 1.5 %collective-permute-done.3.other_ref = f32[520,128]{1,0:T(8,128)S(1)} collective-permute-done((f32[520,128]{1,0:T(8,128)S(1)}, f32[520,128]{1,0:T(8,128)S(1)}, u32[]{:S(2)}, u32[]{:S(2)}) %collective-permute-start.3) | collective-permute-done | bytes 266272 | tf_op jit(solution)/shard_map/ppermute | solution.py:629
  30.2 0.8 %finish.1 = (f32[512,128]{1,0:T(8,128)}, f32[1]{0:T(128)}) custom-call(f32[520,128]{1,0:T(8,128)S(1)} %get-tuple-element.34.mine_ref, f32[520,128]{1,0:T(8,128)S(1)} %collective-permute-done.3.other_ref), custom_call_target="tpu_custom_call" | custom-call | tf_op jit(solution)/shard_map/finish/pallas_call | solution.py:630
Async XLA Ops:
  2.8 10.2 %collective-permute-start = (bf16[4,256,256]{2,1,0:T(8,128)(2,1)}, bf16[4,256,256]{2,1,0:T(8,128)(2,1)S(1)}, u32[]{:S(2)}, u32[]{:S(2)}) collective-permute-start(bf16[4,256,256]{2,1,0:T(8,128)(2,1)} %own_ref.1), channel_id=1, source_target_pairs={{0,1},{1,0},{2,3},{3,2},{4,5},{5,4},{6,7},{7,6},{8,9},{9,8},{10,11... | collective-permute-start | bytes 1572872 | tf_op jit(solution)/shard_map/ppermute | solution.py:478
  3.3 12.1 %all-to-all-start = ((f32[8,8,384]{2,1,0:T(8,128)}), f32[8,8,384]{2,1,0:T(8,128)S(1)}, u32[]{:S(2)}, u32[]{:S(2)}) async-start(f32[8,8,384]{2,1,0:T(8,128)} %pack.1), calls=%async_computation | async-start | bytes 196608 | tf_op jit(solution)/shard_map/all_to_all | solution.py:483
  15.4 6.4 %copy-start = (bf16[4,256,256]{2,1,0:T(8,128)(2,1)S(1)}, bf16[4,256,256]{2,1,0:T(8,128)(2,1)}, u32[]{:S(2)}) copy-start(bf16[4,256,256]{2,1,0:T(8,128)(2,1)} %own_ref.1) | copy-start | bytes 1572868
  17.4 5.8 %collective-permute-start.2 = (bf16[272,256]{1,0:T(8,128)(2,1)S(1)}, bf16[272,256]{1,0:T(8,128)(2,1)S(1)}, u32[]{:S(2)}, u32[]{:S(2)}) collective-permute-start(bf16[272,256]{1,0:T(8,128)(2,1)S(1)} %get-tuple-element.30.refs_4_), channel_id=1, source_target_pairs={{0,2},{2,0},{1,3},{3,1},{4,6},{6,4},{5,7},{7,5},{8,10},{10,8},{9,1... | collective-permute-start | bytes 417800 | tf_op jit(solution)/shard_map/ppermute | solution.py:591
  20.2 5.7 %collective-permute-start.1 = (bf16[272,256]{1,0:T(8,128)(2,1)S(1)}, bf16[272,256]{1,0:T(8,128)(2,1)S(1)}, u32[]{:S(2)}, u32[]{:S(2)}) collective-permute-start(bf16[272,256]{1,0:T(8,128)(2,1)S(1)} %get-tuple-element.25.after_any.refs_4_), channel_id=1, source_target_pairs={{0,2},{2,0},{1,3},{3,1},{4,6},{6,4},{5,7},{7,5},{8,10},{10,8},{9,1... | collective-permute-start | bytes 417800 | tf_op jit(solution)/shard_map/ppermute | solution.py:591
  28.6 1.6 %collective-permute-start.3 = (f32[520,128]{1,0:T(8,128)S(1)}, f32[520,128]{1,0:T(8,128)S(1)}, u32[]{:S(2)}, u32[]{:S(2)}) collective-permute-start(f32[520,128]{1,0:T(8,128)S(1)} %get-tuple-element.35), channel_id=1, source_target_pairs={{0,1},{1,0},{2,3},{3,2},{4,5},{5,4},{6,7},{7,6},{8,9},{9,8},{10,11... | collective-permute-start | bytes 798728 | tf_op jit(solution)/shard_map/ppermute | solution.py:629

commit v19 on v18

--- a/solution.py
+++ b/solution.py
@@ -131,12 +131,12 @@
 
 
 def prep_second_kernel(own_ref, other_ref, after_any, mat, row_probs):
-    rows = row_probs.shape[1]
+    rows = row_probs.shape[2]
     here = own_rows(lax.axis_index("hh") * rows, rows)
     for source, ref in ((core_index(), own_ref), (1 - core_index(), other_ref)):
         for i in range(ref.shape[0]):
             lifted = jnp.exp(ref[i, here, :].astype(F32))
-            row_probs[source * ref.shape[0] + i] = lifted * (1.0 / jnp.sum(lifted, axis=1, keepdims=True))
+            row_probs[source * ref.shape[0] + i] = (lifted * (1.0 / jnp.sum(lifted, axis=1, keepdims=True))).T
         fill_periods(mat, jnp.logical_not(is_forward_first()), source, ref)
 
 
@@ -162,8 +162,8 @@
     return pl.ds(pl.multiple_of(row_begin, rows), rows)
 
 
-def outer_sum(weights_ref, carried):
-    return lax.dot_general(weights_ref[...], carried, (((1,), (1,)), ((), ())), preferred_element_type=F32)
+def outer_sum(carried, weights_ref):
+    return lax.dot_general(carried, weights_ref[...], (((1,), (1,)), ((), ())), preferred_element_type=F32)
 
 
 def run_forward(lead, mat, hist, sel_ref, consts, ab_ref, logs, second=None, fresh=False):
@@ -195,7 +195,7 @@
             inverse[q] = 1.0 / scale
             ab_ref[:, cols] = joint.astype(BF16)
         if second is not None:
-            add_counts(k, outer_sum(weights_ref, hist[k]))
+            add_counts(k, outer_sum(hist[k], weights_ref))
     return logs
 
 
@@ -238,7 +238,7 @@
                 weights_ref[:, cols] = (own_alpha[:, cols] * weight * shrink).astype(BF16)
                 state[q] = jnp.where(moving, product, rest[q])
         if second is not None:
-            add_counts(k, outer_sum(weights_ref, ub_ref[...]))
+            add_counts(k, outer_sum(ub_ref[...], weights_ref))
 
     def left():
         return [x * jnp.exp2(-y) for x, y in zip(state, size)]
@@ -258,7 +258,7 @@
 
     @pl.when(lead == 0)
     def _():
-        second[2](0, jnp.zeros((second[0].shape[0], states), F32))
+        second[2](0, jnp.zeros((states, second[0].shape[0]), F32))
 
 
 def put_state(state_out, values, logs):
@@ -369,11 +369,13 @@
     def centre(k, counts):
         probs = row_probs[k]
         weighted = probs * counts
-        grad = weighted - probs * jnp.sum(weighted, axis=1, keepdims=True)
-        at = slice(k * rows, (k + 1) * rows)
-        left, right = grad[:, :LANES], grad[:, LANES:]
-        mine_ref[at, :] = jnp.where(core == 0, left, right)
-        other_ref[at, :] = jnp.where(core == 0, right, left)
+        grad = weighted - probs * column_sum(weighted)
+        half = states // 2
+        beside = mine_ref.shape[1] // rows
+        at = slice(k // beside * half, (k // beside + 1) * half)
+        cols = slice(k % beside * rows, (k % beside + 1) * rows)
+        mine_ref[at, cols] = jnp.where(core == 0, grad[:half], grad[half:])
+        other_ref[at, cols] = jnp.where(core == 0, grad[half:], grad[:half])
 
     def add_counts(k, counts):
         if grids > 1:
@@ -430,15 +432,21 @@
             if grids > 1:
                 for k in range(steps):
                     centre(k, counts_ref[k])
-            mine_ref[steps * rows :, :] = sums_ref[...]
-            other_ref[steps * rows :, :] = sums_ref[...]
+            tail = mine_ref.shape[0] - 8
+            mine_ref[tail:, :] = sums_ref[:, : mine_ref.shape[1]]
+            other_ref[tail:, :] = sums_ref[:, : mine_ref.shape[1]]
 
 
 def finish_kernel(scale, mine_ref, other_ref, grad_ref, mean_ref):
-    count = grad_ref.shape[0]
+    count, beside = mine_ref.shape
+    count -= 8
     total = mine_ref[count : count + 1, :] + other_ref[count : count + 1, :]
     years = mine_ref[count + 1 : count + 2, :] + other_ref[count + 1 : count + 2, :]
-    grad_ref[...] = (mine_ref[:count, :] + other_ref[:count, :]) * (scale / years)
+    half = grad_ref.shape[1]
+    for at in range(count // half):
+        here = slice(at * half, (at + 1) * half)
+        grad = (mine_ref[here, :] + other_ref[here, :]) * (scale / years)
+        grad_ref[at * beside : (at + 1) * beside, :] = grad.T
     mean_ref[0] = (total / years)[0, 0]
 
 
@@ -512,7 +520,7 @@
     def prep_second(after):
         return pl.pallas_call(
             prep_second_kernel,
-            out_shape=[mat_shape, shaped((steps, rows, states), F32)],
+            out_shape=[mat_shape, shaped((steps, states, rows), F32)],
             in_specs=[vmem(), vmem(), hbm()],
             out_specs=[vmem(), vmem()],
             compiler_params=params(4),
@@ -533,8 +541,9 @@
     hist_shape = shaped((steps, states, share), BF16)
     state_shape = shaped((states + EXTRA, share), BF16)
     sel_shape = shaped((3, periods, 8, share), F32)
-    swap_shape = shaped((steps * rows + 8, LANES), F32)
-    counts_shape = shaped((steps, rows, states), F32)
+    beside = min(LANES, steps * rows)
+    swap_shape = shaped((steps * rows // beside * (states // cores) + 8, beside), F32)
+    counts_shape = shaped((steps, states, rows), F32)
     sums_shape = shaped((8, LANES), F32)
     hist_spec, state_spec, sel_spec = lanes(steps, states), lanes(states + EXTRA), lanes(3, periods, 8)
     const_spec = whole(4, states, LANES)
@@ -622,10 +631,10 @@
             if stage < sides - 1:
                 state = hand_over(state, stage)
         mine, other, _ = done
-        total = jnp.where(side == sides // 2, mine[steps * rows], 0.0)
+        total = jnp.where(side == sides // 2, mine[-8], 0.0)
         total = lax.psum(total, "per")
-        mine = mine.at[steps * rows].set(total)
-        other = other.at[steps * rows].set(total)
+        mine = mine.at[-8].set(total)
+        other = other.at[-8].set(total)
     received = lax.ppermute(other, "st", swap)
     trans_grad, mean_loglik = pl.pallas_call(
         functools.partial(finish_kernel, float(states * states * periods)),

time: 31.4 us -> 33.2 us (1.057)
  Pallas kernels: 15.5 us -> 17.3 us
    pallas_call x2, Pallas kernels: 5.34 us -> 6.65 us  [second_pass(): pl.pallas_call(functools.partial(second_kernel, resume, last, extend, gri...]
    pallas_call x1, Pallas kernels: 1.42 us -> 1.77 us  [prep_second(): pl.pallas_call(prep_second_kernel, out_shape=[mat_shape, shaped((steps, s...]
  transfers between devices with their start and end apart: 5 -> 5, of which waited for: 2 -> 2; matrix products, arithmetic and copies ran while one was open for 0% -> 0% of each run, Pallas kernels for 28% -> 29%
where the time goes in v19:
time: 33.2 us; the launch traced here: 32.9 us
  Pallas kernels  17.3 us (52%)
  starting transfers between devices  10.7 us (32%)
  waiting for transfers between devices  3.28 us (10%)
  between operations  1.56 us (5%)
    all_to_all x1, starting transfers between devices, per_device(): lax.all_to_all(packed, ('hh', 'per', 'st'), split_axis=0, concat_axis=0,...  7.84 us
    pallas_call x2, Pallas kernels, second_pass(): pl.pallas_call(functools.partial(second_kernel, resume, last, extend, gri...  6.65 us
    pallas_call x2, Pallas kernels, first_pass(): pl.pallas_call(functools.partial(first_kernel, resume, grids, index), gri...  4.03 us
    ppermute x2, starting transfers between devices, hand_over(): return lax.ppermute(state, 'per', moves)  2.32 us
    pallas_call x1, Pallas kernels, per_device(): pl.pallas_call(prep_own_kernel, out_shape=[pltpu.VMEM(mat_shape.shape, BF...  1.81 us
    pallas_call x1, Pallas kernels, prep_second(): pl.pallas_call(prep_second_kernel, out_shape=[mat_shape, shaped((steps, s...  1.77 us
    all_to_all x1, waiting for transfers between devices, per_device(): lax.all_to_all(packed, ('hh', 'per', 'st'), split_axis=0, concat_axis=0,...  1.74 us
    ppermute x1, waiting for transfers between devices, per_device(): received = lax.ppermute(other, 'st', swap)  1.53 us
  transfers between devices with their start and end apart: 5, of which 2 were waited for; matrix products, arithmetic and copies ran while one was open for 0% of the time, Pallas kernels for 29%

profile of v19, /device:TPU:0, one launch (start us, length us, event | category | flops | bytes accessed | tf_op | source)
XLA Modules:
  0.0 32.9 jit_solution(6518915073439679633)
XLA Ops:
  1.3 1.5 %pack.1 = f32[8,8,384]{2,1,0:T(8,128)} custom-call(s32[1]{0:T(128)S(6)} %copy.12.count_ref, f32[16,384]{1,0:T(8,128)} %bitcast.7, s32[3,128]{1,0:T(4,128)} %bitcast.8, s32[3,128]{1,0:T(4,128)} %bitcast.9), custom_call_target="tpu_custom_call" | custom-call | tf_op jit(solution)/shard_map/pack/pallas_call | solution.py:476
  2.8 0.5 %collective-permute-start = (bf16[4,256,256]{2,1,0:T(8,128)(2,1)}, bf16[4,256,256]{2,1,0:T(8,128)(2,1)S(1)}, u32[]{:S(2)}, u32[]{:S(2)}) collective-permute-start(bf16[4,256,256]{2,1,0:T(8,128)(2,1)} %own_ref.1), channel_id=1, source_target_pairs={{0,1},{1,0},{2,3},{3,2},{4,5},{5,4},{6,7},{7,6},{8,9},{9,8},{10,11... | collective-permute-start | bytes 1572872 | tf_op jit(solution)/shard_map/ppermute | solution.py:486
  3.3 7.8 %all-to-all-start = ((f32[8,8,384]{2,1,0:T(8,128)}), f32[8,8,384]{2,1,0:T(8,128)S(1)}, u32[]{:S(2)}, u32[]{:S(2)}) async-start(f32[8,8,384]{2,1,0:T(8,128)} %pack.1), calls=%async_computation | async-start | bytes 196608 | tf_op jit(solution)/shard_map/all_to_all | solution.py:491
  11.1 1.8 %prep_own.1 = (bf16[8,256,512]{2,1,0:T(8,128)(2,1)S(1)}, f32[4,256,128]{2,1,0:T(8,128)S(1)}) custom-call(bf16[4,256,256]{2,1,0:T(8,128)(2,1)} %own_ref.1, f32[1,256]{1,0:T(1,128)} %bitcast.10, f32[1,256]{1,0:T(1,128)} %bitcast.11, f32[1,256]{1,0:T(1,128)} %bitcast.12), custom_call_target="tpu_custom_call" | custom-call | tf_op jit(solution)/shard_map/prep_own/pallas_call | solution.py:496
  13.0 0.0 collective-permute-done.other_ref
  13.0 0.7 %prep_other.1.mat = bf16[8,256,512]{2,1,0:T(8,128)(2,1)S(1)} custom-call(bf16[4,256,256]{2,1,0:T(8,128)(2,1)S(1)} %collective-permute-done.other_ref, bf16[8,256,512]{2,1,0:T(8,128)(2,1)S(1)} %get-tuple-element.22.mat_in), custom_call_target="tpu_custom_call", output_to_operand_aliasing={{}: (1, {})} | custom-call | tf_op jit(solution)/shard_map/prep_other/pallas_call | solution.py:510
  13.7 1.7 %all-to-all-done.rows_ref = f32[8,8,384]{2,1,0:T(8,128)S(1)} async-done(((f32[8,8,384]{2,1,0:T(8,128)}), f32[8,8,384]{2,1,0:T(8,128)S(1)}, u32[]{:S(2)}, u32[]{:S(2)}) %all-to-all-start) | async-done | bytes 98336 | tf_op jit(solution)/shard_map/all_to_all | solution.py:491
  15.4 0.0 copy-start
  15.4 2.0 %first_pass.3 = (bf16[8,256,256]{2,1,0:T(8,128)(2,1)S(1)}, bf16[272,256]{1,0:T(8,128)(2,1)S(1)}, f32[3,16,8,256]{3,2,1,0:T(8,128)S(1)}) custom-call(f32[8,8,384]{2,1,0:T(8,128)S(1)} %all-to-all-done.rows_ref, bf16[8,256,512]{2,1,0:T(8,128)(2,1)S(1)} %prep_other.1.mat, f32[4,256,128]{2,1,0:T(8,128)S(1)} %get-tuple-element.23.consts.refs_2_), custom_call_target="tpu_custom_call" | custom-call | tf_op jit(solution)/shard_map/first_pass/pallas_call | solution.py:553
  17.4 0.8 %collective-permute-start.2 = (bf16[272,256]{1,0:T(8,128)(2,1)S(1)}, bf16[272,256]{1,0:T(8,128)(2,1)S(1)}, u32[]{:S(2)}, u32[]{:S(2)}) collective-permute-start(bf16[272,256]{1,0:T(8,128)(2,1)S(1)} %get-tuple-element.30.refs_4_), channel_id=1, source_target_pairs={{0,2},{2,0},{1,3},{3,1},{4,6},{6,4},{5,7},{7,5},{8,10},{10,8},{9,1... | collective-permute-start | bytes 417800 | tf_op jit(solution)/shard_map/ppermute | solution.py:600
  18.2 2.0 %first_pass.2 = (bf16[8,256,256]{2,1,0:T(8,128)(2,1)S(1)}, bf16[272,256]{1,0:T(8,128)(2,1)S(1)}, f32[3,16,8,256]{3,2,1,0:T(8,128)S(1)}) custom-call(f32[8,8,384]{2,1,0:T(8,128)S(1)} %all-to-all-done.rows_ref, bf16[8,256,512]{2,1,0:T(8,128)(2,1)S(1)} %prep_other.1.mat, f32[4,256,128]{2,1,0:T(8,128)S(1)} %get-tuple-element.23.consts.refs_2_), custom_call_target="tpu_custom_call" | custom-call | tf_op jit(solution)/shard_map/first_pass/pallas_call | solution.py:553
  20.2 1.5 %collective-permute-start.1 = (bf16[272,256]{1,0:T(8,128)(2,1)S(1)}, bf16[272,256]{1,0:T(8,128)(2,1)S(1)}, u32[]{:S(2)}, u32[]{:S(2)}) collective-permute-start(bf16[272,256]{1,0:T(8,128)(2,1)S(1)} %get-tuple-element.25.after_any.refs_4_), channel_id=1, source_target_pairs={{0,2},{2,0},{1,3},{3,1},{4,6},{6,4},{5,7},{7,5},{8,10},{10,8},{9,1... | collective-permute-start | bytes 417800 | tf_op jit(solution)/shard_map/ppermute | solution.py:600
  21.8 0.0 copy-done
  21.8 1.8 %prep_second.1 = (bf16[8,256,512]{2,1,0:T(8,128)(2,1)S(1)}, f32[8,256,64]{2,1,0:T(8,128)S(1)}) custom-call(bf16[4,256,256]{2,1,0:T(8,128)(2,1)S(1)} %copy-done, bf16[4,256,256]{2,1,0:T(8,128)(2,1)S(1)} %collective-permute-done.other_ref, bf16[272,256]{1,0:T(8,128)(2,1)S(1)} %get-tuple-element.25.after_any.refs_4_), custom_call_target="tpu_custom_call" | custom-call | tf_op jit(solution)/shard_map/prep_second/pallas_call | solution.py:521
  23.6 0.0 collective-permute-done.2.refs_5_
  23.6 3.4 %second_pass.2 = (f32[8,256,64]{2,1,0:T(8,128)S(1)}, f32[8,128]{1,0:T(8,128)S(1)}) custom-call(f32[3,16,8,256]{3,2,1,0:T(8,128)S(1)} %get-tuple-element.28.refs_0_, bf16[8,256,512]{2,1,0:T(8,128)(2,1)S(1)} %get-tuple-element.26.refs_1_, f32[4,256,128]{2,1,0:T(8,128)S(1)} %get-tuple-element.23.consts.refs_2_, ...), custom_call_target="tpu_custom_call" | custom-call | tf_op jit(solution)/shard_map/second_pass/pallas_call | solution.py:581
  27.0 0.0 collective-permute-done.1.refs_5_
  27.0 3.2 %second_pass.3 = (f32[520,128]{1,0:T(8,128)S(1)}, f32[520,128]{1,0:T(8,128)S(1)}) custom-call(f32[3,16,8,256]{3,2,1,0:T(8,128)S(1)} %get-tuple-element.24.refs_0_, bf16[8,256,512]{2,1,0:T(8,128)(2,1)S(1)} %get-tuple-element.26.refs_1_, f32[4,256,128]{2,1,0:T(8,128)S(1)} %get-tuple-element.23.consts.refs_2_, ...), custom_call_target="tpu_custom_call" | custom-call | tf_op jit(solution)/shard_map/second_pass/pallas_call | solution.py:581
  30.2 0.1 collective-permute-start.3
  30.3 1.5 %collective-permute-done.3.other_ref = f32[520,128]{1,0:T(8,128)S(1)} collective-permute-done((f32[520,128]{1,0:T(8,128)S(1)}, f32[520,128]{1,0:T(8,128)S(1)}, u32[]{:S(2)}, u32[]{:S(2)}) %collective-permute-start.3) | collective-permute-done | bytes 266272 | tf_op jit(solution)/shard_map/ppermute | solution.py:638
  31.9 0.9 %finish.1 = (f32[512,128]{1,0:T(8,128)}, f32[1]{0:T(128)}) custom-call(f32[520,128]{1,0:T(8,128)S(1)} %get-tuple-element.34.mine_ref, f32[520,128]{1,0:T(8,128)S(1)} %collective-permute-done.3.other_ref), custom_call_target="tpu_custom_call" | custom-call | tf_op jit(solution)/shard_map/finish/pallas_call | solution.py:639
Async XLA Ops:
  2.8 10.2 %collective-permute-start = (bf16[4,256,256]{2,1,0:T(8,128)(2,1)}, bf16[4,256,256]{2,1,0:T(8,128)(2,1)S(1)}, u32[]{:S(2)}, u32[]{:S(2)}) collective-permute-start(bf16[4,256,256]{2,1,0:T(8,128)(2,1)} %own_ref.1), channel_id=1, source_target_pairs={{0,1},{1,0},{2,3},{3,2},{4,5},{5,4},{6,7},{7,6},{8,9},{9,8},{10,11... | collective-permute-start | bytes 1572872 | tf_op jit(solution)/shard_map/ppermute | solution.py:486
  3.3 12.1 %all-to-all-start = ((f32[8,8,384]{2,1,0:T(8,128)}), f32[8,8,384]{2,1,0:T(8,128)S(1)}, u32[]{:S(2)}, u32[]{:S(2)}) async-start(f32[8,8,384]{2,1,0:T(8,128)} %pack.1), calls=%async_computation | async-start | bytes 196608 | tf_op jit(solution)/shard_map/all_to_all | solution.py:491
  15.4 6.4 %copy-start = (bf16[4,256,256]{2,1,0:T(8,128)(2,1)S(1)}, bf16[4,256,256]{2,1,0:T(8,128)(2,1)}, u32[]{:S(2)}) copy-start(bf16[4,256,256]{2,1,0:T(8,128)(2,1)} %own_ref.1) | copy-start | bytes 1572868
  17.4 6.1 %collective-permute-start.2 = (bf16[272,256]{1,0:T(8,128)(2,1)S(1)}, bf16[272,256]{1,0:T(8,128)(2,1)S(1)}, u32[]{:S(2)}, u32[]{:S(2)}) collective-permute-start(bf16[272,256]{1,0:T(8,128)(2,1)S(1)} %get-tuple-element.30.refs_4_), channel_id=1, source_target_pairs={{0,2},{2,0},{1,3},{3,1},{4,6},{6,4},{5,7},{7,5},{8,10},{10,8},{9,1... | collective-permute-start | bytes 417800 | tf_op jit(solution)/shard_map/ppermute | solution.py:600
  20.2 6.7 %collective-permute-start.1 = (bf16[272,256]{1,0:T(8,128)(2,1)S(1)}, bf16[272,256]{1,0:T(8,128)(2,1)S(1)}, u32[]{:S(2)}, u32[]{:S(2)}) collective-permute-start(bf16[272,256]{1,0:T(8,128)(2,1)S(1)} %get-tuple-element.25.after_any.refs_4_), channel_id=1, source_target_pairs={{0,2},{2,0},{1,3},{3,1},{4,6},{6,4},{5,7},{7,5},{8,10},{10,8},{9,1... | collective-permute-start | bytes 417800 | tf_op jit(solution)/shard_map/ppermute | solution.py:600
  30.2 1.6 %collective-permute-start.3 = (f32[520,128]{1,0:T(8,128)S(1)}, f32[520,128]{1,0:T(8,128)S(1)}, u32[]{:S(2)}, u32[]{:S(2)}) collective-permute-start(f32[520,128]{1,0:T(8,128)S(1)} %get-tuple-element.35), channel_id=1, source_target_pairs={{0,1},{1,0},{2,3},{3,2},{4,5},{5,4},{6,7},{7,6},{8,9},{9,8},{10,11... | collective-permute-start | bytes 798728 | tf_op jit(solution)/shard_map/ppermute | solution.py:638

commit v20 on v18

--- a/solution.py
+++ b/solution.py
@@ -476,13 +476,9 @@
     )(block_count, *in_hbm(earnings.T, starts.reshape(-1, HB), lengths.reshape(-1, HB)))
     packed, later_logits = lax.optimization_barrier((packed, trans_logits))
     other_logits = lax.ppermute(later_logits, "st", swap)
-    along = group // sides
-    centre = along // 2
-    outward = sorted(range(along), key=lambda z: (abs(z - centre), -z))
-    listed = [z * sides + x for z in outward for x in reversed(range(sides))]
     gathered = lax.all_to_all(
         packed, ("hh", "per", "st"), split_axis=0, concat_axis=0,
-        axis_index_groups=[[n * cores + c for n in listed] for c in range(cores)], tiled=True,
+        axis_index_groups=[[n * cores + c for n in reversed(range(group))] for c in range(cores)], tiled=True,
     )
     mat_shape = shaped((steps, states, 2 * states), BF16)
     first_mat, consts = pl.pallas_call(

time: 31.4 us -> 32.1 us (1.022)
  starting transfers between devices: 10.7 us -> 11.8 us
    all_to_all x1, starting transfers between devices: 7.84 us -> 8.86 us  [per_device(): lax.all_to_all(packed, ('hh', 'per', 'st'), split_axis=0, concat_axis=0,...]
    all_to_all x1, waiting for transfers between devices: 1.74 us -> 1.36 us  [per_device(): lax.all_to_all(packed, ('hh', 'per', 'st'), split_axis=0, concat_axis=0,...]
  transfers between devices with their start and end apart: 5 -> 5, of which waited for: 2 -> 3; matrix products, arithmetic and copies ran while one was open for 0% -> 0% of each run, Pallas kernels for 28% -> 27%
where the time goes in v20:
time: 32.1 us; the launch traced here: 31.8 us
  Pallas kernels  15.5 us (48%)
  starting transfers between devices  11.8 us (37%)
  waiting for transfers between devices  2.99 us (9%)
  between operations  1.53 us (5%)
    all_to_all x1, starting transfers between devices, per_device(): lax.all_to_all(packed, ('hh', 'per', 'st'), split_axis=0, concat_axis=0,...  8.86 us
    pallas_call x2, Pallas kernels, second_pass(): pl.pallas_call(functools.partial(second_kernel, resume, last, extend, gri...  5.32 us
    pallas_call x2, Pallas kernels, first_pass(): pl.pallas_call(functools.partial(first_kernel, resume, grids, index), gri...  4.03 us
    ppermute x2, starting transfers between devices, hand_over(): return lax.ppermute(state, 'per', moves)  2.32 us
    pallas_call x1, Pallas kernels, per_device(): pl.pallas_call(prep_own_kernel, out_shape=[pltpu.VMEM(mat_shape.shape, BF...  1.81 us
    ppermute x1, waiting for transfers between devices, per_device(): received = lax.ppermute(other, 'st', swap)  1.53 us
    pallas_call x1, Pallas kernels, per_device(): pl.pallas_call(pack_kernel, out_shape=pltpu.VMEM((group, periods // 2, sl...  1.49 us
    pallas_call x1, Pallas kernels, prep_second(): pl.pallas_call(prep_second_kernel, out_shape=[mat_shape, shaped((steps, r...  1.42 us
  transfers between devices with their start and end apart: 5, of which 3 were waited for; matrix products, arithmetic and copies ran while one was open for 0% of the time, Pallas kernels for 27%

profile of v20, /device:TPU:0, one launch (start us, length us, event | category | flops | bytes accessed | tf_op | source)
XLA Modules:
  0.0 31.8 jit_solution(9180921686568904104)
XLA Ops:
  1.3 1.5 %pack.1 = f32[8,8,384]{2,1,0:T(8,128)} custom-call(s32[1]{0:T(128)S(6)} %copy.12.count_ref, f32[16,384]{1,0:T(8,128)} %bitcast.7, s32[3,128]{1,0:T(4,128)} %bitcast.8, s32[3,128]{1,0:T(4,128)} %bitcast.9), custom_call_target="tpu_custom_call" | custom-call | tf_op jit(solution)/shard_map/pack/pallas_call | solution.py:468
  2.8 0.5 %collective-permute-start = (bf16[4,256,256]{2,1,0:T(8,128)(2,1)}, bf16[4,256,256]{2,1,0:T(8,128)(2,1)S(1)}, u32[]{:S(2)}, u32[]{:S(2)}) collective-permute-start(bf16[4,256,256]{2,1,0:T(8,128)(2,1)} %own_ref.1), channel_id=1, source_target_pairs={{0,1},{1,0},{2,3},{3,2},{4,5},{5,4},{6,7},{7,6},{8,9},{9,8},{10,11... | collective-permute-start | bytes 1572872 | tf_op jit(solution)/shard_map/ppermute | solution.py:478
  3.3 8.9 %all-to-all-start = ((f32[8,8,384]{2,1,0:T(8,128)}), f32[8,8,384]{2,1,0:T(8,128)S(1)}, u32[]{:S(2)}, u32[]{:S(2)}) async-start(f32[8,8,384]{2,1,0:T(8,128)} %pack.1), calls=%async_computation | async-start | bytes 196608 | tf_op jit(solution)/shard_map/all_to_all | solution.py:479
  12.2 1.8 %prep_own.1 = (bf16[8,256,512]{2,1,0:T(8,128)(2,1)S(1)}, f32[4,256,128]{2,1,0:T(8,128)S(1)}) custom-call(bf16[4,256,256]{2,1,0:T(8,128)(2,1)} %own_ref.1, f32[1,256]{1,0:T(1,128)} %bitcast.10, f32[1,256]{1,0:T(1,128)} %bitcast.11, f32[1,256]{1,0:T(1,128)} %bitcast.12), custom_call_target="tpu_custom_call" | custom-call | tf_op jit(solution)/shard_map/prep_own/pallas_call | solution.py:484
  14.0 0.0 collective-permute-done.other_ref
  14.0 0.7 %prep_other.1.mat = bf16[8,256,512]{2,1,0:T(8,128)(2,1)S(1)} custom-call(bf16[4,256,256]{2,1,0:T(8,128)(2,1)S(1)} %collective-permute-done.other_ref, bf16[8,256,512]{2,1,0:T(8,128)(2,1)S(1)} %get-tuple-element.22.mat_in), custom_call_target="tpu_custom_call", output_to_operand_aliasing={{}: (1, {})} | custom-call | tf_op jit(solution)/shard_map/prep_other/pallas_call | solution.py:498
  14.7 1.4 %all-to-all-done.rows_ref = f32[8,8,384]{2,1,0:T(8,128)S(1)} async-done(((f32[8,8,384]{2,1,0:T(8,128)}), f32[8,8,384]{2,1,0:T(8,128)S(1)}, u32[]{:S(2)}, u32[]{:S(2)}) %all-to-all-start) | async-done | bytes 98336 | tf_op jit(solution)/shard_map/all_to_all | solution.py:479
  16.0 0.0 copy-start
  16.0 2.0 %first_pass.3 = (bf16[8,256,256]{2,1,0:T(8,128)(2,1)S(1)}, bf16[272,256]{1,0:T(8,128)(2,1)S(1)}, f32[3,16,8,256]{3,2,1,0:T(8,128)S(1)}) custom-call(f32[8,8,384]{2,1,0:T(8,128)S(1)} %all-to-all-done.rows_ref, bf16[8,256,512]{2,1,0:T(8,128)(2,1)S(1)} %prep_other.1.mat, f32[4,256,128]{2,1,0:T(8,128)S(1)} %get-tuple-element.23.consts.refs_2_), custom_call_target="tpu_custom_call" | custom-call | tf_op jit(solution)/shard_map/first_pass/pallas_call | solution.py:540
  18.1 0.9 %collective-permute-start.2 = (bf16[272,256]{1,0:T(8,128)(2,1)S(1)}, bf16[272,256]{1,0:T(8,128)(2,1)S(1)}, u32[]{:S(2)}, u32[]{:S(2)}) collective-permute-start(bf16[272,256]{1,0:T(8,128)(2,1)S(1)} %get-tuple-element.30.refs_4_), channel_id=1, source_target_pairs={{0,2},{2,0},{1,3},{3,1},{4,6},{6,4},{5,7},{7,5},{8,10},{10,8},{9,1... | collective-permute-start | bytes 417800 | tf_op jit(solution)/shard_map/ppermute | solution.py:587
  19.0 2.0 %first_pass.2 = (bf16[8,256,256]{2,1,0:T(8,128)(2,1)S(1)}, bf16[272,256]{1,0:T(8,128)(2,1)S(1)}, f32[3,16,8,256]{3,2,1,0:T(8,128)S(1)}) custom-call(f32[8,8,384]{2,1,0:T(8,128)S(1)} %all-to-all-done.rows_ref, bf16[8,256,512]{2,1,0:T(8,128)(2,1)S(1)} %prep_other.1.mat, f32[4,256,128]{2,1,0:T(8,128)S(1)} %get-tuple-element.23.consts.refs_2_), custom_call_target="tpu_custom_call" | custom-call | tf_op jit(solution)/shard_map/first_pass/pallas_call | solution.py:540
  21.0 1.4 %collective-permute-start.1 = (bf16[272,256]{1,0:T(8,128)(2,1)S(1)}, bf16[272,256]{1,0:T(8,128)(2,1)S(1)}, u32[]{:S(2)}, u32[]{:S(2)}) collective-permute-start(bf16[272,256]{1,0:T(8,128)(2,1)S(1)} %get-tuple-element.25.after_any.refs_4_), channel_id=1, source_target_pairs={{0,2},{2,0},{1,3},{3,1},{4,6},{6,4},{5,7},{7,5},{8,10},{10,8},{9,1... | collective-permute-start | bytes 417800 | tf_op jit(solution)/shard_map/ppermute | solution.py:587
  22.4 0.0 copy-done
  22.4 1.4 %prep_second.1 = (bf16[8,256,512]{2,1,0:T(8,128)(2,1)S(1)}, f32[8,64,256]{2,1,0:T(8,128)S(1)}) custom-call(bf16[4,256,256]{2,1,0:T(8,128)(2,1)S(1)} %copy-done, bf16[4,256,256]{2,1,0:T(8,128)(2,1)S(1)} %collective-permute-done.other_ref, bf16[272,256]{1,0:T(8,128)(2,1)S(1)} %get-tuple-element.25.after_any.refs_4_), custom_call_target="tpu_custom_call" | custom-call | tf_op jit(solution)/shard_map/prep_second/pallas_call | solution.py:509
  23.8 0.1 collective-permute-done.2.refs_5_
  23.9 2.7 %second_pass.2 = (f32[8,64,256]{2,1,0:T(8,128)S(1)}, f32[8,128]{1,0:T(8,128)S(1)}) custom-call(f32[3,16,8,256]{3,2,1,0:T(8,128)S(1)} %get-tuple-element.28.refs_0_, bf16[8,256,512]{2,1,0:T(8,128)(2,1)S(1)} %get-tuple-element.26.refs_1_, f32[4,256,128]{2,1,0:T(8,128)S(1)} %get-tuple-element.23.consts.refs_2_, ...), custom_call_target="tpu_custom_call" | custom-call | tf_op jit(solution)/shard_map/second_pass/pallas_call | solution.py:568
  26.6 0.0 collective-permute-done.1.refs_5_
  26.6 2.7 %second_pass.3 = (f32[520,128]{1,0:T(8,128)S(1)}, f32[520,128]{1,0:T(8,128)S(1)}) custom-call(f32[3,16,8,256]{3,2,1,0:T(8,128)S(1)} %get-tuple-element.24.refs_0_, bf16[8,256,512]{2,1,0:T(8,128)(2,1)S(1)} %get-tuple-element.26.refs_1_, f32[4,256,128]{2,1,0:T(8,128)S(1)} %get-tuple-element.23.consts.refs_2_, ...), custom_call_target="tpu_custom_call" | custom-call | tf_op jit(solution)/shard_map/second_pass/pallas_call | solution.py:568
  29.3 0.1 collective-permute-start.3
  29.4 1.5 %collective-permute-done.3.other_ref = f32[520,128]{1,0:T(8,128)S(1)} collective-permute-done((f32[520,128]{1,0:T(8,128)S(1)}, f32[520,128]{1,0:T(8,128)S(1)}, u32[]{:S(2)}, u32[]{:S(2)}) %collective-permute-start.3) | collective-permute-done | bytes 266272 | tf_op jit(solution)/shard_map/ppermute | solution.py:625
  30.9 0.8 %finish.1 = (f32[512,128]{1,0:T(8,128)}, f32[1]{0:T(128)}) custom-call(f32[520,128]{1,0:T(8,128)S(1)} %get-tuple-element.34.mine_ref, f32[520,128]{1,0:T(8,128)S(1)} %collective-permute-done.3.other_ref), custom_call_target="tpu_custom_call" | custom-call | tf_op jit(solution)/shard_map/finish/pallas_call | solution.py:626
Async XLA Ops:
  2.8 11.2 %collective-permute-start = (bf16[4,256,256]{2,1,0:T(8,128)(2,1)}, bf16[4,256,256]{2,1,0:T(8,128)(2,1)S(1)}, u32[]{:S(2)}, u32[]{:S(2)}) collective-permute-start(bf16[4,256,256]{2,1,0:T(8,128)(2,1)} %own_ref.1), channel_id=1, source_target_pairs={{0,1},{1,0},{2,3},{3,2},{4,5},{5,4},{6,7},{7,6},{8,9},{9,8},{10,11... | collective-permute-start | bytes 1572872 | tf_op jit(solution)/shard_map/ppermute | solution.py:478
  3.3 12.7 %all-to-all-start = ((f32[8,8,384]{2,1,0:T(8,128)}), f32[8,8,384]{2,1,0:T(8,128)S(1)}, u32[]{:S(2)}, u32[]{:S(2)}) async-start(f32[8,8,384]{2,1,0:T(8,128)} %pack.1), calls=%async_computation | async-start | bytes 196608 | tf_op jit(solution)/shard_map/all_to_all | solution.py:479
  16.0 6.4 %copy-start = (bf16[4,256,256]{2,1,0:T(8,128)(2,1)S(1)}, bf16[4,256,256]{2,1,0:T(8,128)(2,1)}, u32[]{:S(2)}) copy-start(bf16[4,256,256]{2,1,0:T(8,128)(2,1)} %own_ref.1) | copy-start | bytes 1572868
  18.1 5.9 %collective-permute-start.2 = (bf16[272,256]{1,0:T(8,128)(2,1)S(1)}, bf16[272,256]{1,0:T(8,128)(2,1)S(1)}, u32[]{:S(2)}, u32[]{:S(2)}) collective-permute-start(bf16[272,256]{1,0:T(8,128)(2,1)S(1)} %get-tuple-element.30.refs_4_), channel_id=1, source_target_pairs={{0,2},{2,0},{1,3},{3,1},{4,6},{6,4},{5,7},{7,5},{8,10},{10,8},{9,1... | collective-permute-start | bytes 417800 | tf_op jit(solution)/shard_map/ppermute | solution.py:587
  21.0 5.6 %collective-permute-start.1 = (bf16[272,256]{1,0:T(8,128)(2,1)S(1)}, bf16[272,256]{1,0:T(8,128)(2,1)S(1)}, u32[]{:S(2)}, u32[]{:S(2)}) collective-permute-start(bf16[272,256]{1,0:T(8,128)(2,1)S(1)} %get-tuple-element.25.after_any.refs_4_), channel_id=1, source_target_pairs={{0,2},{2,0},{1,3},{3,1},{4,6},{6,4},{5,7},{7,5},{8,10},{10,8},{9,1... | collective-permute-start | bytes 417800 | tf_op jit(solution)/shard_map/ppermute | solution.py:587
  29.3 1.6 %collective-permute-start.3 = (f32[520,128]{1,0:T(8,128)S(1)}, f32[520,128]{1,0:T(8,128)S(1)}, u32[]{:S(2)}, u32[]{:S(2)}) collective-permute-start(f32[520,128]{1,0:T(8,128)S(1)} %get-tuple-element.35), channel_id=1, source_target_pairs={{0,1},{1,0},{2,3},{3,2},{4,5},{5,4},{6,7},{7,6},{8,9},{9,8},{10,11... | collective-permute-start | bytes 798728 | tf_op jit(solution)/shard_map/ppermute | solution.py:625

commit v21 on v18

--- a/solution.py
+++ b/solution.py
@@ -146,6 +146,10 @@
     return jnp.exp2(power if less is None else power - less)
 
 
+def first_row(lead):
+    return 0 if lax.axis_size("per") == 2 else lead
+
+
 def is_moving(sel_ref, step_now, cols):
     return sel_ref[1, step_now, :1, cols] > 0.5
 
@@ -169,18 +173,21 @@
 def run_forward(lead, mat, hist, sel_ref, consts, ab_ref, logs, second=None, fresh=False):
     steps, states, width = hist.shape
     cuts = tiles(width)
-    inverse = [1.0 / column_sum(ab_ref[:, cols].astype(F32)) for cols in cuts]
+    here = hist.at[0] if second is None else ab_ref
+    inverse = [1.0 / column_sum(here[:, cols].astype(F32)) for cols in cuts]
     for k in range(steps):
-        step_now = lead + k
+        step_now = first_row(lead) + k
+        here = there = ab_ref
         if second is None:
-            hist[k] = ab_ref[...]
+            here = hist.at[k]
+            there = hist.at[k + 1] if k + 1 < steps else ab_ref
         else:
             weights_ref, row_begin, add_counts = second
             own_alpha = ab_ref[own_rows(row_begin, weights_ref.shape[0]), :].astype(F32)
         for q, cols in enumerate(cuts):
             begins = fresh and k == 0
             if not begins:
-                moved = both_halves(mat[k], ab_ref[:, cols]) * inverse[q]
+                moved = both_halves(mat[k], here[:, cols]) * inverse[q]
                 moving = is_moving(sel_ref, step_now, cols)
             if second is not None:
                 total = column_sum(moved * hist[k, :, cols].astype(F32))
@@ -193,7 +200,7 @@
                 seen = is_seen(sel_ref, step_now, cols)
                 logs[q] = logs[q] + jnp.where(seen, jnp.log2(scale), 0.0)
             inverse[q] = 1.0 / scale
-            ab_ref[:, cols] = joint.astype(BF16)
+            there[:, cols] = joint.astype(BF16)
         if second is not None:
             add_counts(k, outer_sum(weights_ref, hist[k]))
     return logs
@@ -206,12 +213,13 @@
     size = [jnp.zeros((1, LANES), F32) for _ in cuts]
 
     def step(k):
-        step_now = lead + k
+        step_now = first_row(lead) + k
+        here = hist.at[k] if second is None else ub_ref
         grown = []
         for q, cols in enumerate(cuts):
             emit = emission(sel_ref, consts, step_now, cols, size[q] if second is None else None)
             carried = emit * state[q]
-            ub_ref[:, cols] = carried.astype(BF16)
+            here[:, cols] = carried.astype(BF16)
             whole = column_sum(carried)
             grown.append(whole)
             if second is None:
@@ -220,13 +228,11 @@
                 logs[q] = logs[q] + jnp.where(seen, size[q], 0.0)
                 begun = column_sum(carried * consts[0]) / whole
                 rest[q] = jnp.where(seen, begun, rest[q])
-        if second is None:
-            hist[k] = ub_ref[...]
-        else:
+        if second is not None:
             weights_ref, row_begin, add_counts = second
             own_alpha = hist[k, own_rows(row_begin, weights_ref.shape[0]), :].astype(F32)
         for q, cols in enumerate(cuts):
-            product = both_halves(mat[k], ub_ref[:, cols])
+            product = both_halves(mat[k], here[:, cols])
             moving = is_moving(sel_ref, step_now, cols)
             if second is None:
                 state[q] = jnp.where(moving, product, rest[q] * grown[q])
@@ -306,34 +312,42 @@
     else:
         carry = lax.fori_loop(0, group, scan_source, carry)
     low_lane = lax.broadcasted_iota(jnp.int32, (half_periods, HB), 1) < HALF
-    for q, cols in enumerate(cuts):
-        left, right = carry[1][2 * q], carry[1][2 * q + 1]
-        before = jnp.zeros((1, HB), F32)
-        for late in range(2):
-            value = (
-                jnp.where(low_lane, pltpu.roll(left, HALF, 1), right)
-                if late
-                else jnp.where(low_lane, left, pltpu.roll(right, HALF, 1))
+    local = lax.axis_size("per") == 2
+
+    def lay_out(parts):
+        for q, cols in enumerate(cuts):
+            left, right = carry[1][2 * q], carry[1][2 * q + 1]
+            values = (
+                jnp.where(low_lane, left, pltpu.roll(right, HALF, 1)),
+                jnp.where(low_lane, pltpu.roll(left, HALF, 1), right),
             )
-            seen = value > 0.5 * SEEN
-            earn = jnp.where(seen, value - SEEN, value)
-            seen = seen.astype(F32)
-            for i in range(half_periods):
-                at = late * half_periods + i
-                now = seen[i : i + 1]
-                sel_ref[0, at, :, cols] = jnp.broadcast_to(earn[i : i + 1], (8, HB))
-                sel_ref[1, at, :, cols] = jnp.broadcast_to(now * before, (8, HB))
-                sel_ref[2, at, :, cols] = jnp.broadcast_to(now, (8, HB))
-                before = now
+            flags = [(value > 0.5 * SEEN).astype(F32) for value in values]
+            for late in parts:
+                earn = jnp.where(flags[late] > 0.5, values[late] - SEEN, values[late])
+                before = flags[0][half_periods - 1 :] if late else jnp.zeros((1, HB), F32)
+                for i in range(half_periods):
+                    at = i if local else late * half_periods + i
+                    now = flags[late][i : i + 1]
+                    sel_ref[0, at, :, cols] = jnp.broadcast_to(earn[i : i + 1], (8, HB))
+                    sel_ref[1, at, :, cols] = jnp.broadcast_to(now * before, (8, HB))
+                    sel_ref[2, at, :, cols] = jnp.broadcast_to(now, (8, HB))
+                    before = now
+            years = column_sum(flags[0] + flags[1])
+            sel_ref[2, sel_ref.shape[1] - 1, :, cols] = jnp.broadcast_to(years, (8, HB))
+
+    if not local:
+        lay_out((0, 1))
     zeros = [jnp.zeros((1, LANES), F32) for _ in cuts]
 
     @pl.when(forward_first)
     def _():
+        if local:
+            lay_out((0,))
         if resume:
-            ab_ref[...] = state_in[:states, :]
+            hist[0] = state_in[:states, :]
         else:
             for cols in cuts:
-                ab_ref[:, cols] = consts[0].astype(BF16)
+                hist[0, :, cols] = consts[0].astype(BF16)
         logs = state_logs(state_in) if resume else list(zeros)
         fresh = lax.axis_size("per") == 2
         run_forward(lead, mat, hist, sel_ref, consts, ab_ref, logs, fresh=fresh)
@@ -341,6 +355,8 @@
 
     @pl.when(jnp.logical_not(forward_first))
     def _():
+        if local:
+            lay_out((1,))
         state = [
             state_in[:states, cols].astype(F32) if resume else jnp.ones((states, LANES), F32) for cols in cuts
         ]
@@ -401,7 +417,7 @@
             alpha = alpha_ref[:states, cols].astype(F32)
             meet = column_sum(alpha * other_state[:states, cols].astype(F32))
             total += (here + there + jnp.log2(meet / column_sum(alpha))) * LN2
-            years += jnp.sum(sel_ref[2, :, :, cols], axis=0)
+            years += sel_ref[2, sel_ref.shape[1] - 1, :, cols]
         total = jnp.broadcast_to(jnp.sum(total, axis=1, keepdims=True), (1, LANES))
         years = jnp.broadcast_to(jnp.sum(years[:1], axis=1, keepdims=True), (1, LANES))
         row = lax.broadcasted_iota(jnp.int32, (8, LANES), 0)
@@ -532,11 +548,12 @@
     grid = (grids,) if grids > 1 else ()
     hist_shape = shaped((steps, states, share), BF16)
     state_shape = shaped((states + EXTRA, share), BF16)
-    sel_shape = shaped((3, periods, 8, share), F32)
+    laid = (steps if sides == 2 else periods) + 1
+    sel_shape = shaped((3, laid, 8, share), F32)
     swap_shape = shaped((steps * rows + 8, LANES), F32)
     counts_shape = shaped((steps, rows, states), F32)
     sums_shape = shaped((8, LANES), F32)
-    hist_spec, state_spec, sel_spec = lanes(steps, states), lanes(states + EXTRA), lanes(3, periods, 8)
+    hist_spec, state_spec, sel_spec = lanes(steps, states), lanes(states + EXTRA), lanes(3, laid, 8)
     const_spec = whole(4, states, LANES)
 
     def first_pass(index, state_in):

time: 31.4 us -> 31.4 us (level)
  transfers between devices with their start and end apart: 5 -> 5, of which waited for: 2 -> 3; matrix products, arithmetic and copies ran while one was open for 0% -> 0% of each run, Pallas kernels for 28% -> 27%
where the time goes in v21:
time: 31.4 us; the launch traced here: 31.1 us
  Pallas kernels  15.4 us (49%)
  starting transfers between devices  10.8 us (34%)
  waiting for transfers between devices  3.43 us (11%)
  between operations  1.53 us (5%)
    all_to_all x1, starting transfers between devices, per_device(): lax.all_to_all(packed, ('hh', 'per', 'st'), split_axis=0, concat_axis=0,...  7.84 us
    pallas_call x2, Pallas kernels, second_pass(): pl.pallas_call(functools.partial(second_kernel, resume, last, extend, gri...  5.31 us
    pallas_call x2, Pallas kernels, first_pass(): pl.pallas_call(functools.partial(first_kernel, resume, grids, index), gri...  3.9 us
    ppermute x2, starting transfers between devices, hand_over(): return lax.ppermute(state, 'per', moves)  2.34 us
    pallas_call x1, Pallas kernels, per_device(): pl.pallas_call(prep_own_kernel, out_shape=[pltpu.VMEM(mat_shape.shape, BF...  1.81 us
    all_to_all x1, waiting for transfers between devices, per_device(): lax.all_to_all(packed, ('hh', 'per', 'st'), split_axis=0, concat_axis=0,...  1.74 us
    ppermute x1, waiting for transfers between devices, per_device(): received = lax.ppermute(other, 'st', swap)  1.53 us
    pallas_call x1, Pallas kernels, per_device(): pl.pallas_call(pack_kernel, out_shape=pltpu.VMEM((group, periods // 2, sl...  1.49 us
  transfers between devices with their start and end apart: 5, of which 3 were waited for; matrix products, arithmetic and copies ran while one was open for 0% of the time, Pallas kernels for 27%

profile of v21, /device:TPU:0, one launch (start us, length us, event | category | flops | bytes accessed | tf_op | source)
XLA Modules:
  0.0 31.1 jit_solution(16958034851262811840)
XLA Ops:
  1.3 1.5 %pack.1 = f32[8,8,384]{2,1,0:T(8,128)} custom-call(s32[1]{0:T(128)S(6)} %copy.12.count_ref, f32[16,384]{1,0:T(8,128)} %bitcast.7, s32[3,128]{1,0:T(4,128)} %bitcast.8, s32[3,128]{1,0:T(4,128)} %bitcast.9), custom_call_target="tpu_custom_call" | custom-call | tf_op jit(solution)/shard_map/pack/pallas_call | solution.py:484
  2.8 0.5 %collective-permute-start = (bf16[4,256,256]{2,1,0:T(8,128)(2,1)}, bf16[4,256,256]{2,1,0:T(8,128)(2,1)S(1)}, u32[]{:S(2)}, u32[]{:S(2)}) collective-permute-start(bf16[4,256,256]{2,1,0:T(8,128)(2,1)} %own_ref.1), channel_id=1, source_target_pairs={{0,1},{1,0},{2,3},{3,2},{4,5},{5,4},{6,7},{7,6},{8,9},{9,8},{10,11... | collective-permute-start | bytes 1572872 | tf_op jit(solution)/shard_map/ppermute | solution.py:494
  3.3 7.8 %all-to-all-start = ((f32[8,8,384]{2,1,0:T(8,128)}), f32[8,8,384]{2,1,0:T(8,128)S(1)}, u32[]{:S(2)}, u32[]{:S(2)}) async-start(f32[8,8,384]{2,1,0:T(8,128)} %pack.1), calls=%async_computation | async-start | bytes 196608 | tf_op jit(solution)/shard_map/all_to_all | solution.py:499
  11.1 1.8 %prep_own.1 = (bf16[8,256,512]{2,1,0:T(8,128)(2,1)S(1)}, f32[4,256,128]{2,1,0:T(8,128)S(1)}) custom-call(bf16[4,256,256]{2,1,0:T(8,128)(2,1)} %own_ref.1, f32[1,256]{1,0:T(1,128)} %bitcast.10, f32[1,256]{1,0:T(1,128)} %bitcast.11, f32[1,256]{1,0:T(1,128)} %bitcast.12), custom_call_target="tpu_custom_call" | custom-call | tf_op jit(solution)/shard_map/prep_own/pallas_call | solution.py:504
  13.0 0.0 collective-permute-done.other_ref
  13.0 0.7 %prep_other.1.mat = bf16[8,256,512]{2,1,0:T(8,128)(2,1)S(1)} custom-call(bf16[4,256,256]{2,1,0:T(8,128)(2,1)S(1)} %collective-permute-done.other_ref, bf16[8,256,512]{2,1,0:T(8,128)(2,1)S(1)} %get-tuple-element.22.mat_in), custom_call_target="tpu_custom_call", output_to_operand_aliasing={{}: (1, {})} | custom-call | tf_op jit(solution)/shard_map/prep_other/pallas_call | solution.py:518
  13.7 1.7 %all-to-all-done.rows_ref = f32[8,8,384]{2,1,0:T(8,128)S(1)} async-done(((f32[8,8,384]{2,1,0:T(8,128)}), f32[8,8,384]{2,1,0:T(8,128)S(1)}, u32[]{:S(2)}, u32[]{:S(2)}) %all-to-all-start) | async-done | bytes 98336 | tf_op jit(solution)/shard_map/all_to_all | solution.py:499
  15.4 0.0 copy-start
  15.4 2.0 %first_pass.3 = (bf16[8,256,256]{2,1,0:T(8,128)(2,1)S(1)}, bf16[272,256]{1,0:T(8,128)(2,1)S(1)}, f32[3,9,8,256]{3,2,1,0:T(8,128)S(1)}) custom-call(f32[8,8,384]{2,1,0:T(8,128)S(1)} %all-to-all-done.rows_ref, bf16[8,256,512]{2,1,0:T(8,128)(2,1)S(1)} %prep_other.1.mat, f32[4,256,128]{2,1,0:T(8,128)S(1)} %get-tuple-element.23.consts.refs_2_), custom_call_target="tpu_custom_call" | custom-call | tf_op jit(solution)/shard_map/first_pass/pallas_call | solution.py:561
  17.4 0.8 %collective-permute-start.2 = (bf16[272,256]{1,0:T(8,128)(2,1)S(1)}, bf16[272,256]{1,0:T(8,128)(2,1)S(1)}, u32[]{:S(2)}, u32[]{:S(2)}) collective-permute-start(bf16[272,256]{1,0:T(8,128)(2,1)S(1)} %get-tuple-element.30.refs_4_), channel_id=1, source_target_pairs={{0,2},{2,0},{1,3},{3,1},{4,6},{6,4},{5,7},{7,5},{8,10},{10,8},{9,1... | collective-permute-start | bytes 417800 | tf_op jit(solution)/shard_map/ppermute | solution.py:608
  18.2 1.9 %first_pass.2 = (bf16[8,256,256]{2,1,0:T(8,128)(2,1)S(1)}, bf16[272,256]{1,0:T(8,128)(2,1)S(1)}, f32[3,9,8,256]{3,2,1,0:T(8,128)S(1)}) custom-call(f32[8,8,384]{2,1,0:T(8,128)S(1)} %all-to-all-done.rows_ref, bf16[8,256,512]{2,1,0:T(8,128)(2,1)S(1)} %prep_other.1.mat, f32[4,256,128]{2,1,0:T(8,128)S(1)} %get-tuple-element.23.consts.refs_2_), custom_call_target="tpu_custom_call" | custom-call | tf_op jit(solution)/shard_map/first_pass/pallas_call | solution.py:561
  20.1 1.6 %collective-permute-start.1 = (bf16[272,256]{1,0:T(8,128)(2,1)S(1)}, bf16[272,256]{1,0:T(8,128)(2,1)S(1)}, u32[]{:S(2)}, u32[]{:S(2)}) collective-permute-start(bf16[272,256]{1,0:T(8,128)(2,1)S(1)} %get-tuple-element.25.after_any.refs_4_), channel_id=1, source_target_pairs={{0,2},{2,0},{1,3},{3,1},{4,6},{6,4},{5,7},{7,5},{8,10},{10,8},{9,1... | collective-permute-start | bytes 417800 | tf_op jit(solution)/shard_map/ppermute | solution.py:608
  21.7 0.0 copy-done
  21.7 1.4 %prep_second.1 = (bf16[8,256,512]{2,1,0:T(8,128)(2,1)S(1)}, f32[8,64,256]{2,1,0:T(8,128)S(1)}) custom-call(bf16[4,256,256]{2,1,0:T(8,128)(2,1)S(1)} %copy-done, bf16[4,256,256]{2,1,0:T(8,128)(2,1)S(1)} %collective-permute-done.other_ref, bf16[272,256]{1,0:T(8,128)(2,1)S(1)} %get-tuple-element.25.after_any.refs_4_), custom_call_target="tpu_custom_call" | custom-call | tf_op jit(solution)/shard_map/prep_second/pallas_call | solution.py:529
  23.1 0.2 collective-permute-done.2.refs_5_
  23.3 2.7 %second_pass.2 = (f32[8,64,256]{2,1,0:T(8,128)S(1)}, f32[8,128]{1,0:T(8,128)S(1)}) custom-call(f32[3,9,8,256]{3,2,1,0:T(8,128)S(1)} %get-tuple-element.28.refs_0_, bf16[8,256,512]{2,1,0:T(8,128)(2,1)S(1)} %get-tuple-element.26.refs_1_, f32[4,256,128]{2,1,0:T(8,128)S(1)} %get-tuple-element.23.consts.refs_2_, ...), custom_call_target="tpu_custom_call" | custom-call | tf_op jit(solution)/shard_map/second_pass/pallas_call | solution.py:589
  25.9 0.0 collective-permute-done.1.refs_5_
  25.9 2.7 %second_pass.3 = (f32[520,128]{1,0:T(8,128)S(1)}, f32[520,128]{1,0:T(8,128)S(1)}) custom-call(f32[3,9,8,256]{3,2,1,0:T(8,128)S(1)} %get-tuple-element.24.refs_0_, bf16[8,256,512]{2,1,0:T(8,128)(2,1)S(1)} %get-tuple-element.26.refs_1_, f32[4,256,128]{2,1,0:T(8,128)S(1)} %get-tuple-element.23.consts.refs_2_, ...), custom_call_target="tpu_custom_call" | custom-call | tf_op jit(solution)/shard_map/second_pass/pallas_call | solution.py:589
  28.6 0.1 collective-permute-start.3
  28.7 1.5 %collective-permute-done.3.other_ref = f32[520,128]{1,0:T(8,128)S(1)} collective-permute-done((f32[520,128]{1,0:T(8,128)S(1)}, f32[520,128]{1,0:T(8,128)S(1)}, u32[]{:S(2)}, u32[]{:S(2)}) %collective-permute-start.3) | collective-permute-done | bytes 266272 | tf_op jit(solution)/shard_map/ppermute | solution.py:646
  30.2 0.8 %finish.1 = (f32[512,128]{1,0:T(8,128)}, f32[1]{0:T(128)}) custom-call(f32[520,128]{1,0:T(8,128)S(1)} %get-tuple-element.34.mine_ref, f32[520,128]{1,0:T(8,128)S(1)} %collective-permute-done.3.other_ref), custom_call_target="tpu_custom_call" | custom-call | tf_op jit(solution)/shard_map/finish/pallas_call | solution.py:647
Async XLA Ops:
  2.8 10.2 %collective-permute-start = (bf16[4,256,256]{2,1,0:T(8,128)(2,1)}, bf16[4,256,256]{2,1,0:T(8,128)(2,1)S(1)}, u32[]{:S(2)}, u32[]{:S(2)}) collective-permute-start(bf16[4,256,256]{2,1,0:T(8,128)(2,1)} %own_ref.1), channel_id=1, source_target_pairs={{0,1},{1,0},{2,3},{3,2},{4,5},{5,4},{6,7},{7,6},{8,9},{9,8},{10,11... | collective-permute-start | bytes 1572872 | tf_op jit(solution)/shard_map/ppermute | solution.py:494
  3.3 12.1 %all-to-all-start = ((f32[8,8,384]{2,1,0:T(8,128)}), f32[8,8,384]{2,1,0:T(8,128)S(1)}, u32[]{:S(2)}, u32[]{:S(2)}) async-start(f32[8,8,384]{2,1,0:T(8,128)} %pack.1), calls=%async_computation | async-start | bytes 196608 | tf_op jit(solution)/shard_map/all_to_all | solution.py:499
  15.4 6.3 %copy-start = (bf16[4,256,256]{2,1,0:T(8,128)(2,1)S(1)}, bf16[4,256,256]{2,1,0:T(8,128)(2,1)}, u32[]{:S(2)}) copy-start(bf16[4,256,256]{2,1,0:T(8,128)(2,1)} %own_ref.1) | copy-start | bytes 1572868
  17.4 5.9 %collective-permute-start.2 = (bf16[272,256]{1,0:T(8,128)(2,1)S(1)}, bf16[272,256]{1,0:T(8,128)(2,1)S(1)}, u32[]{:S(2)}, u32[]{:S(2)}) collective-permute-start(bf16[272,256]{1,0:T(8,128)(2,1)S(1)} %get-tuple-element.30.refs_4_), channel_id=1, source_target_pairs={{0,2},{2,0},{1,3},{3,1},{4,6},{6,4},{5,7},{7,5},{8,10},{10,8},{9,1... | collective-permute-start | bytes 417800 | tf_op jit(solution)/shard_map/ppermute | solution.py:608
  20.1 5.8 %collective-permute-start.1 = (bf16[272,256]{1,0:T(8,128)(2,1)S(1)}, bf16[272,256]{1,0:T(8,128)(2,1)S(1)}, u32[]{:S(2)}, u32[]{:S(2)}) collective-permute-start(bf16[272,256]{1,0:T(8,128)(2,1)S(1)} %get-tuple-element.25.after_any.refs_4_), channel_id=1, source_target_pairs={{0,2},{2,0},{1,3},{3,1},{4,6},{6,4},{5,7},{7,5},{8,10},{10,8},{9,1... | collective-permute-start | bytes 417800 | tf_op jit(solution)/shard_map/ppermute | solution.py:608
  28.6 1.6 %collective-permute-start.3 = (f32[520,128]{1,0:T(8,128)S(1)}, f32[520,128]{1,0:T(8,128)S(1)}, u32[]{:S(2)}, u32[]{:S(2)}) collective-permute-start(f32[520,128]{1,0:T(8,128)S(1)} %get-tuple-element.35), channel_id=1, source_target_pairs={{0,1},{1,0},{2,3},{3,2},{4,5},{5,4},{6,7},{7,6},{8,9},{9,8},{10,11... | collective-permute-start | bytes 798728 | tf_op jit(solution)/shard_map/ppermute | solution.py:646

commit v22 on v21

--- a/solution.py
+++ b/solution.py
@@ -15,7 +15,6 @@
 BF16 = jnp.bfloat16
 LOG2E = 1.4426950408889634
 LN2 = 0.6931471805599453
-EXTRA = 16
 
 
 def vmem():
@@ -174,6 +173,7 @@
     steps, states, width = hist.shape
     cuts = tiles(width)
     here = hist.at[0] if second is None else ab_ref
+    last = [None] * len(cuts)
     inverse = [1.0 / column_sum(here[:, cols].astype(F32)) for cols in cuts]
     for k in range(steps):
         step_now = first_row(lead) + k
@@ -201,9 +201,10 @@
                 logs[q] = logs[q] + jnp.where(seen, jnp.log2(scale), 0.0)
             inverse[q] = 1.0 / scale
             there[:, cols] = joint.astype(BF16)
+            last[q] = joint
         if second is not None:
             add_counts(k, outer_sum(weights_ref, hist[k]))
-    return logs
+    return last
 
 
 def run_backward(lead, mat, hist, sel_ref, consts, state, ub_ref, logs, leave, second=None, between=None):
@@ -267,22 +268,22 @@
         second[2](0, jnp.zeros((second[0].shape[0], states), F32))
 
 
-def put_state(state_out, values, logs):
-    states = state_out.shape[0] - EXTRA
-    row = lax.broadcasted_iota(jnp.int32, (EXTRA, LANES), 0)
+def put_state(state_out, values, logs, spread):
     for q, cols in enumerate(tiles(state_out.shape[1])):
-        state_out[:states, cols] = values[q].astype(BF16)
-        high = logs[q].astype(BF16).astype(F32)
-        middle = (logs[q] - high).astype(BF16).astype(F32)
-        piece = jnp.where(
-            row == 0, high, jnp.where(row == 1, middle, jnp.where(row == 2, logs[q] - high - middle, 0.0))
-        )
-        state_out[states:, cols] = piece.astype(BF16)
-
-
-def state_logs(state_ref):
-    states = state_ref.shape[0] - EXTRA
-    return [column_sum(state_ref[states:, cols].astype(F32)) for cols in tiles(state_ref.shape[1])]
+        factor = jnp.exp2(logs[q] * (1.0 / spread)) / column_sum(values[q])
+        state_out[:, cols] = (values[q] * factor).astype(BF16)
+
+
+def state_sums(state_ref):
+    return [column_sum(state_ref[:, cols].astype(F32)) for cols in tiles(state_ref.shape[1])]
+
+
+def state_logs(sums, spread):
+    return [jnp.log2(x) * spread for x in sums]
+
+
+def unit_state(state_ref, sums):
+    return [state_ref[:, cols].astype(F32) * (1.0 / x) for cols, x in zip(tiles(state_ref.shape[1]), sums)]
 
 
 def first_kernel(resume, grids, part, rows_ref, mat, consts, *refs):
@@ -344,28 +345,31 @@
         if local:
             lay_out((0,))
         if resume:
-            hist[0] = state_in[:states, :]
+            hist[0] = state_in[...]
         else:
             for cols in cuts:
                 hist[0, :, cols] = consts[0].astype(BF16)
-        logs = state_logs(state_in) if resume else list(zeros)
+        logs = state_logs(state_sums(state_in), half_periods) if resume else list(zeros)
         fresh = lax.axis_size("per") == 2
-        run_forward(lead, mat, hist, sel_ref, consts, ab_ref, logs, fresh=fresh)
-        put_state(state_out, [ab_ref[:, cols] for cols in cuts], logs)
+        last = run_forward(lead, mat, hist, sel_ref, consts, ab_ref, logs, fresh=fresh)
+        put_state(state_out, last, logs, half_periods)
 
     @pl.when(jnp.logical_not(forward_first))
     def _():
         if local:
             lay_out((1,))
-        state = [
-            state_in[:states, cols].astype(F32) if resume else jnp.ones((states, LANES), F32) for cols in cuts
-        ]
-        logs = state_logs(state_in) if resume else list(zeros)
-        leave = lambda values: put_state(state_out, values, logs)
+        sums = state_sums(state_in) if resume else None
+        state = unit_state(state_in, sums) if resume else [jnp.ones((states, LANES), F32) for _ in cuts]
+        logs = state_logs(sums, half_periods) if resume else list(zeros)
+
+        def leave(values):
+            grown = [old + jnp.log2(column_sum(x)) for old, x in zip(logs, values)]
+            put_state(state_out, values, grown, half_periods)
+
         run_backward(lead, mat, hist, sel_ref, consts, state, ab_ref, logs, leave)
 
 
-def second_kernel(resume, last, extend, grids, *refs):
+def second_kernel(resume, last, extend, grids, spread, *refs):
     refs = list(refs)
     sel_ref, mat, consts, hist, own_state, state_in = (refs.pop(0) for _ in range(6))
     counts_in, sums_in = (refs.pop(0), refs.pop(0)) if resume else (None, None)
@@ -413,10 +417,10 @@
     def add_sums(alpha_ref, other_state):
         total = jnp.zeros((1, LANES), F32)
         years = jnp.zeros((8, LANES), F32)
-        for cols, here, there in zip(tiles(width), state_logs(alpha_ref), state_logs(other_state)):
-            alpha = alpha_ref[:states, cols].astype(F32)
-            meet = column_sum(alpha * other_state[:states, cols].astype(F32))
-            total += (here + there + jnp.log2(meet / column_sum(alpha))) * LN2
+        for cols, here, there in zip(tiles(width), state_sums(alpha_ref), state_sums(other_state)):
+            meet = column_sum(alpha_ref[:, cols].astype(F32) * (1.0 / here) * other_state[:, cols].astype(F32))
+            scales = (jnp.log2(here) + jnp.log2(there)) * spread
+            total += (scales + jnp.log2(meet / there)) * LN2
             years += sel_ref[2, sel_ref.shape[1] - 1, :, cols]
         total = jnp.broadcast_to(jnp.sum(total, axis=1, keepdims=True), (1, LANES))
         years = jnp.broadcast_to(jnp.sum(years[:1], axis=1, keepdims=True), (1, LANES))
@@ -427,16 +431,16 @@
 
     @pl.when(jnp.logical_not(forward_first))
     def _():
-        ab_ref[...] = state_in[:states, :]
-        run_forward(lead, mat, hist, sel_ref, consts, ab_ref, list(zeros), second)
+        ab_ref[...] = state_in[...]
+        values = run_forward(lead, mat, hist, sel_ref, consts, ab_ref, list(zeros), second)
         add_sums(state_in, own_state)
         if extend:
-            put_state(state_out, [ab_ref[:, cols] for cols in tiles(width)], zeros)
+            put_state(state_out, values, zeros, spread)
 
     @pl.when(forward_first)
     def _():
-        state = [state_in[:states, cols].astype(F32) for cols in tiles(width)]
-        leave = lambda values: put_state(state_out, values, zeros) if extend else None
+        state = unit_state(state_in, state_sums(state_in))
+        leave = lambda values: put_state(state_out, values, zeros, spread) if extend else None
         run_backward(lead, mat, hist, sel_ref, consts, state, ab_ref, list(zeros), leave, second, lambda: add_sums(own_state, state_in))
 
     if last:
@@ -547,13 +551,13 @@
 
     grid = (grids,) if grids > 1 else ()
     hist_shape = shaped((steps, states, share), BF16)
-    state_shape = shaped((states + EXTRA, share), BF16)
+    state_shape = shaped((states, share), BF16)
     laid = (steps if sides == 2 else periods) + 1
     sel_shape = shaped((3, laid, 8, share), F32)
     swap_shape = shaped((steps * rows + 8, LANES), F32)
     counts_shape = shaped((steps, rows, states), F32)
     sums_shape = shaped((8, LANES), F32)
-    hist_spec, state_spec, sel_spec = lanes(steps, states), lanes(states + EXTRA), lanes(3, laid, 8)
+    hist_spec, state_spec, sel_spec = lanes(steps, states), lanes(states), lanes(3, laid, 8)
     const_spec = whole(4, states, LANES)
 
     def first_pass(index, state_in):
@@ -587,7 +591,7 @@
         if extend:
             out_shape, out_specs = out_shape + [state_shape], out_specs + [state_spec]
         return pl.pallas_call(
-            functools.partial(second_kernel, resume, last, extend, grids),
+            functools.partial(second_kernel, resume, last, extend, grids, periods // 2),
             grid=grid,
             out_shape=out_shape,
             in_specs=[sel_spec, whole(*second_mat.shape), const_spec, hist_spec, state_spec, state_spec]

time: 31.4 us -> 31.4 us (level)
  transfers between devices with their start and end apart: 5 -> 5, of which waited for: 3 -> 2; matrix products, arithmetic and copies ran while one was open for 0% -> 0% of each run, Pallas kernels for 27% -> 28%
where the time goes in v22:
time: 31.4 us; the launch traced here: 31.1 us
  Pallas kernels  15.4 us (49%)
  starting transfers between devices  10.8 us (34%)
  waiting for transfers between devices  3.28 us (10%)
  between operations  1.54 us (5%)
    all_to_all x1, starting transfers between devices, per_device(): lax.all_to_all(packed, ('hh', 'per', 'st'), split_axis=0, concat_axis=0,...  7.84 us
    pallas_call x2, Pallas kernels, second_pass(): pl.pallas_call(functools.partial(second_kernel, resume, last, extend, gri...  5.42 us
    pallas_call x2, Pallas kernels, first_pass(): pl.pallas_call(functools.partial(first_kernel, resume, grids, index), gri...  3.83 us
    ppermute x2, starting transfers between devices, hand_over(): return lax.ppermute(state, 'per', moves)  2.4 us
    pallas_call x1, Pallas kernels, per_device(): pl.pallas_call(prep_own_kernel, out_shape=[pltpu.VMEM(mat_shape.shape, BF...  1.81 us
    all_to_all x1, waiting for transfers between devices, per_device(): lax.all_to_all(packed, ('hh', 'per', 'st'), split_axis=0, concat_axis=0,...  1.74 us
    ppermute x1, waiting for transfers between devices, per_device(): received = lax.ppermute(other, 'st', swap)  1.53 us
    pallas_call x1, Pallas kernels, per_device(): pl.pallas_call(pack_kernel, out_shape=pltpu.VMEM((group, periods // 2, sl...  1.49 us
  transfers between devices with their start and end apart: 5, of which 2 were waited for; matrix products, arithmetic and copies ran while one was open for 0% of the time, Pallas kernels for 28%

profile of v22, /device:TPU:0, one launch (start us, length us, event | category | flops | bytes accessed | tf_op | source)
XLA Modules:
  0.0 31.1 jit_solution(3992332733373986549)
XLA Ops:
  1.3 1.5 %pack.1 = f32[8,8,384]{2,1,0:T(8,128)} custom-call(s32[1]{0:T(128)S(6)} %copy.12.count_ref, f32[16,384]{1,0:T(8,128)} %bitcast.7, s32[3,128]{1,0:T(4,128)} %bitcast.8, s32[3,128]{1,0:T(4,128)} %bitcast.9), custom_call_target="tpu_custom_call" | custom-call | tf_op jit(solution)/shard_map/pack/pallas_call | solution.py:488
  2.8 0.5 %collective-permute-start = (bf16[4,256,256]{2,1,0:T(8,128)(2,1)}, bf16[4,256,256]{2,1,0:T(8,128)(2,1)S(1)}, u32[]{:S(2)}, u32[]{:S(2)}) collective-permute-start(bf16[4,256,256]{2,1,0:T(8,128)(2,1)} %own_ref.1), channel_id=1, source_target_pairs={{0,1},{1,0},{2,3},{3,2},{4,5},{5,4},{6,7},{7,6},{8,9},{9,8},{10,11... | collective-permute-start | bytes 1572872 | tf_op jit(solution)/shard_map/ppermute | solution.py:498
  3.3 7.8 %all-to-all-start = ((f32[8,8,384]{2,1,0:T(8,128)}), f32[8,8,384]{2,1,0:T(8,128)S(1)}, u32[]{:S(2)}, u32[]{:S(2)}) async-start(f32[8,8,384]{2,1,0:T(8,128)} %pack.1), calls=%async_computation | async-start | bytes 196608 | tf_op jit(solution)/shard_map/all_to_all | solution.py:503
  11.1 1.8 %prep_own.1 = (bf16[8,256,512]{2,1,0:T(8,128)(2,1)S(1)}, f32[4,256,128]{2,1,0:T(8,128)S(1)}) custom-call(bf16[4,256,256]{2,1,0:T(8,128)(2,1)} %own_ref.1, f32[1,256]{1,0:T(1,128)} %bitcast.10, f32[1,256]{1,0:T(1,128)} %bitcast.11, f32[1,256]{1,0:T(1,128)} %bitcast.12), custom_call_target="tpu_custom_call" | custom-call | tf_op jit(solution)/shard_map/prep_own/pallas_call | solution.py:508
  13.0 0.0 collective-permute-done.other_ref
  13.0 0.7 %prep_other.1.mat = bf16[8,256,512]{2,1,0:T(8,128)(2,1)S(1)} custom-call(bf16[4,256,256]{2,1,0:T(8,128)(2,1)S(1)} %collective-permute-done.other_ref, bf16[8,256,512]{2,1,0:T(8,128)(2,1)S(1)} %get-tuple-element.22.mat_in), custom_call_target="tpu_custom_call", output_to_operand_aliasing={{}: (1, {})} | custom-call | tf_op jit(solution)/shard_map/prep_other/pallas_call | solution.py:522
  13.7 1.7 %all-to-all-done.rows_ref = f32[8,8,384]{2,1,0:T(8,128)S(1)} async-done(((f32[8,8,384]{2,1,0:T(8,128)}), f32[8,8,384]{2,1,0:T(8,128)S(1)}, u32[]{:S(2)}, u32[]{:S(2)}) %all-to-all-start) | async-done | bytes 98336 | tf_op jit(solution)/shard_map/all_to_all | solution.py:503
  15.4 0.0 copy-start
  15.4 1.9 %first_pass.3 = (bf16[8,256,256]{2,1,0:T(8,128)(2,1)S(1)}, bf16[256,256]{1,0:T(8,128)(2,1)S(1)}, f32[3,9,8,256]{3,2,1,0:T(8,128)S(1)}) custom-call(f32[8,8,384]{2,1,0:T(8,128)S(1)} %all-to-all-done.rows_ref, bf16[8,256,512]{2,1,0:T(8,128)(2,1)S(1)} %prep_other.1.mat, f32[4,256,128]{2,1,0:T(8,128)S(1)} %get-tuple-element.23.consts.refs_2_), custom_call_target="tpu_custom_call" | custom-call | tf_op jit(solution)/shard_map/first_pass/pallas_call | solution.py:565
  17.3 0.9 %collective-permute-start.2 = (bf16[256,256]{1,0:T(8,128)(2,1)S(1)}, bf16[256,256]{1,0:T(8,128)(2,1)S(1)}, u32[]{:S(2)}, u32[]{:S(2)}) collective-permute-start(bf16[256,256]{1,0:T(8,128)(2,1)S(1)} %get-tuple-element.30.refs_4_), channel_id=1, source_target_pairs={{0,2},{2,0},{1,3},{3,1},{4,6},{6,4},{5,7},{7,5},{8,10},{10,8},{9,1... | collective-permute-start | bytes 393224 | tf_op jit(solution)/shard_map/ppermute | solution.py:612
  18.2 1.9 %first_pass.2 = (bf16[8,256,256]{2,1,0:T(8,128)(2,1)S(1)}, bf16[256,256]{1,0:T(8,128)(2,1)S(1)}, f32[3,9,8,256]{3,2,1,0:T(8,128)S(1)}) custom-call(f32[8,8,384]{2,1,0:T(8,128)S(1)} %all-to-all-done.rows_ref, bf16[8,256,512]{2,1,0:T(8,128)(2,1)S(1)} %prep_other.1.mat, f32[4,256,128]{2,1,0:T(8,128)S(1)} %get-tuple-element.23.consts.refs_2_), custom_call_target="tpu_custom_call" | custom-call | tf_op jit(solution)/shard_map/first_pass/pallas_call | solution.py:565
  20.1 1.5 %collective-permute-start.1 = (bf16[256,256]{1,0:T(8,128)(2,1)S(1)}, bf16[256,256]{1,0:T(8,128)(2,1)S(1)}, u32[]{:S(2)}, u32[]{:S(2)}) collective-permute-start(bf16[256,256]{1,0:T(8,128)(2,1)S(1)} %get-tuple-element.25.after_any.refs_4_), channel_id=1, source_target_pairs={{0,2},{2,0},{1,3},{3,1},{4,6},{6,4},{5,7},{7,5},{8,10},{10,8},{9,1... | collective-permute-start | bytes 393224 | tf_op jit(solution)/shard_map/ppermute | solution.py:612
  21.7 0.0 copy-done
  21.7 1.4 %prep_second.1 = (bf16[8,256,512]{2,1,0:T(8,128)(2,1)S(1)}, f32[8,64,256]{2,1,0:T(8,128)S(1)}) custom-call(bf16[4,256,256]{2,1,0:T(8,128)(2,1)S(1)} %copy-done, bf16[4,256,256]{2,1,0:T(8,128)(2,1)S(1)} %collective-permute-done.other_ref, bf16[256,256]{1,0:T(8,128)(2,1)S(1)} %get-tuple-element.25.after_any.refs_4_), custom_call_target="tpu_custom_call" | custom-call | tf_op jit(solution)/shard_map/prep_second/pallas_call | solution.py:533
  23.1 0.0 collective-permute-done.2.refs_5_
  23.1 2.7 %second_pass.2 = (f32[8,64,256]{2,1,0:T(8,128)S(1)}, f32[8,128]{1,0:T(8,128)S(1)}) custom-call(f32[3,9,8,256]{3,2,1,0:T(8,128)S(1)} %get-tuple-element.28.refs_0_, bf16[8,256,512]{2,1,0:T(8,128)(2,1)S(1)} %get-tuple-element.26.refs_1_, f32[4,256,128]{2,1,0:T(8,128)S(1)} %get-tuple-element.23.consts.refs_2_, ...), custom_call_target="tpu_custom_call" | custom-call | tf_op jit(solution)/shard_map/second_pass/pallas_call | solution.py:593
  25.8 0.0 collective-permute-done.1.refs_5_
  25.8 2.7 %second_pass.3 = (f32[520,128]{1,0:T(8,128)S(1)}, f32[520,128]{1,0:T(8,128)S(1)}) custom-call(f32[3,9,8,256]{3,2,1,0:T(8,128)S(1)} %get-tuple-element.24.refs_0_, bf16[8,256,512]{2,1,0:T(8,128)(2,1)S(1)} %get-tuple-element.26.refs_1_, f32[4,256,128]{2,1,0:T(8,128)S(1)} %get-tuple-element.23.consts.refs_2_, ...), custom_call_target="tpu_custom_call" | custom-call | tf_op jit(solution)/shard_map/second_pass/pallas_call | solution.py:593
  28.5 0.1 collective-permute-start.3
  28.6 1.5 %collective-permute-done.3.other_ref = f32[520,128]{1,0:T(8,128)S(1)} collective-permute-done((f32[520,128]{1,0:T(8,128)S(1)}, f32[520,128]{1,0:T(8,128)S(1)}, u32[]{:S(2)}, u32[]{:S(2)}) %collective-permute-start.3) | collective-permute-done | bytes 266272 | tf_op jit(solution)/shard_map/ppermute | solution.py:650
  30.2 0.8 %finish.1 = (f32[512,128]{1,0:T(8,128)}, f32[1]{0:T(128)}) custom-call(f32[520,128]{1,0:T(8,128)S(1)} %get-tuple-element.34.mine_ref, f32[520,128]{1,0:T(8,128)S(1)} %collective-permute-done.3.other_ref), custom_call_target="tpu_custom_call" | custom-call | tf_op jit(solution)/shard_map/finish/pallas_call | solution.py:651
Async XLA Ops:
  2.8 10.2 %collective-permute-start = (bf16[4,256,256]{2,1,0:T(8,128)(2,1)}, bf16[4,256,256]{2,1,0:T(8,128)(2,1)S(1)}, u32[]{:S(2)}, u32[]{:S(2)}) collective-permute-start(bf16[4,256,256]{2,1,0:T(8,128)(2,1)} %own_ref.1), channel_id=1, source_target_pairs={{0,1},{1,0},{2,3},{3,2},{4,5},{5,4},{6,7},{7,6},{8,9},{9,8},{10,11... | collective-permute-start | bytes 1572872 | tf_op jit(solution)/shard_map/ppermute | solution.py:498
  3.3 12.1 %all-to-all-start = ((f32[8,8,384]{2,1,0:T(8,128)}), f32[8,8,384]{2,1,0:T(8,128)S(1)}, u32[]{:S(2)}, u32[]{:S(2)}) async-start(f32[8,8,384]{2,1,0:T(8,128)} %pack.1), calls=%async_computation | async-start | bytes 196608 | tf_op jit(solution)/shard_map/all_to_all | solution.py:503
  15.4 6.2 %copy-start = (bf16[4,256,256]{2,1,0:T(8,128)(2,1)S(1)}, bf16[4,256,256]{2,1,0:T(8,128)(2,1)}, u32[]{:S(2)}) copy-start(bf16[4,256,256]{2,1,0:T(8,128)(2,1)} %own_ref.1) | copy-start | bytes 1572868
  17.3 5.7 %collective-permute-start.2 = (bf16[256,256]{1,0:T(8,128)(2,1)S(1)}, bf16[256,256]{1,0:T(8,128)(2,1)S(1)}, u32[]{:S(2)}, u32[]{:S(2)}) collective-permute-start(bf16[256,256]{1,0:T(8,128)(2,1)S(1)} %get-tuple-element.30.refs_4_), channel_id=1, source_target_pairs={{0,2},{2,0},{1,3},{3,1},{4,6},{6,4},{5,7},{7,5},{8,10},{10,8},{9,1... | collective-permute-start | bytes 393224 | tf_op jit(solution)/shard_map/ppermute | solution.py:612
  20.1 5.7 %collective-permute-start.1 = (bf16[256,256]{1,0:T(8,128)(2,1)S(1)}, bf16[256,256]{1,0:T(8,128)(2,1)S(1)}, u32[]{:S(2)}, u32[]{:S(2)}) collective-permute-start(bf16[256,256]{1,0:T(8,128)(2,1)S(1)} %get-tuple-element.25.after_any.refs_4_), channel_id=1, source_target_pairs={{0,2},{2,0},{1,3},{3,1},{4,6},{6,4},{5,7},{7,5},{8,10},{10,8},{9,1... | collective-permute-start | bytes 393224 | tf_op jit(solution)/shard_map/ppermute | solution.py:612
  28.5 1.6 %collective-permute-start.3 = (f32[520,128]{1,0:T(8,128)S(1)}, f32[520,128]{1,0:T(8,128)S(1)}, u32[]{:S(2)}, u32[]{:S(2)}) collective-permute-start(f32[520,128]{1,0:T(8,128)S(1)} %get-tuple-element.35), channel_id=1, source_target_pairs={{0,1},{1,0},{2,3},{3,2},{4,5},{5,4},{6,7},{7,6},{8,9},{9,8},{10,11... | collective-permute-start | bytes 798728 | tf_op jit(solution)/shard_map/ppermute | solution.py:650

commit v23 on v22

--- a/solution.py
+++ b/solution.py
@@ -90,10 +90,10 @@
     return high + jnp.dot(mat[:, states:], state, preferred_element_type=F32)
 
 
-def fill_periods(mat, turned_pass, source, ref):
-    @pl.loop(0, ref.shape[0])
+def fill_periods(mat, turned_pass, lead, ref, begin, end):
+    @pl.loop(begin, end)
     def _(i):
-        at = source * ref.shape[0] + i
+        at = lead + i
 
         @pl.when(turned_pass)
         def _():
@@ -107,8 +107,9 @@
 
 
 def prep_own_kernel(
-    own_any, init_any, mean_any, sd_any, mat, consts, own_ref, init_ref, mean_ref, sd_ref, sem, sems
+    own_any, init_any, mean_any, sd_any, mat, consts, early, own_ref, init_ref, mean_ref, sd_ref, sem, sems
 ):
+    part = own_ref.shape[0]
     copy = pltpu.make_async_copy(own_any, own_ref, sem)
     copy.start()
     fetch(((init_any, init_ref), (mean_any, mean_ref), (sd_any, sd_ref)), sems)
@@ -122,21 +123,28 @@
     for i, row in enumerate(rows):
         consts[i] = jnp.broadcast_to(row, (LANES, own_ref.shape[1])).T
     copy.wait()
-    fill_periods(mat, is_forward_first(), core_index(), own_ref)
+    fill_periods(mat, is_forward_first(), core_index() * part, own_ref, 0, part)
+    fill_periods(early, jnp.logical_not(is_forward_first()), 0, own_ref, 0, early.shape[0])
 
 
 def prep_other_kernel(other_ref, mat_in, mat):
-    fill_periods(mat, is_forward_first(), 1 - core_index(), other_ref)
-
-
-def prep_second_kernel(own_ref, other_ref, after_any, mat, row_probs):
+    part = other_ref.shape[0]
+    fill_periods(mat, is_forward_first(), (1 - core_index()) * part, other_ref, 0, part)
+
+
+def prep_second_kernel(own_ref, other_ref, early, after_any, mat, row_probs):
     rows = row_probs.shape[1]
+    part = own_ref.shape[0]
     here = own_rows(lax.axis_index("hh") * rows, rows)
-    for source, ref in ((core_index(), own_ref), (1 - core_index(), other_ref)):
-        for i in range(ref.shape[0]):
+    turned_pass = jnp.logical_not(is_forward_first())
+    own_lead = core_index() * part
+    for i in range(early.shape[0]):
+        mat[own_lead + i] = early[i]
+    for lead, ref, begin in ((own_lead, own_ref, early.shape[0]), (part - own_lead, other_ref, 0)):
+        for i in range(part):
             lifted = jnp.exp(ref[i, here, :].astype(F32))
-            row_probs[source * ref.shape[0] + i] = lifted * (1.0 / jnp.sum(lifted, axis=1, keepdims=True))
-        fill_periods(mat, jnp.logical_not(is_forward_first()), source, ref)
+            row_probs[lead + i] = lifted * (1.0 / jnp.sum(lifted, axis=1, keepdims=True))
+        fill_periods(mat, turned_pass, lead, ref, begin, part)
 
 
 def emission(sel_ref, consts, step_now, cols, less=None):
@@ -505,11 +513,15 @@
         axis_index_groups=[[n * cores + c for n in listed] for c in range(cores)], tiled=True,
     )
     mat_shape = shaped((steps, states, 2 * states), BF16)
-    first_mat, consts = pl.pallas_call(
+    first_mat, consts, early_mat = pl.pallas_call(
         prep_own_kernel,
-        out_shape=[pltpu.VMEM(mat_shape.shape, BF16), pltpu.VMEM((4, states, LANES), F32)],
+        out_shape=[
+            pltpu.VMEM(mat_shape.shape, BF16),
+            pltpu.VMEM((4, states, LANES), F32),
+            pltpu.VMEM((max(part - 1, 1),) + mat_shape.shape[1:], BF16),
+        ],
         in_specs=[hbm()] * 4,
-        out_specs=[vmem(), vmem()],
+        out_specs=[vmem()] * 3,
         scratch_shapes=[pltpu.VMEM(trans_logits.shape, BF16), vec_row, vec_row, vec_row, dma, dma((3,))],
         compiler_params=params(4),
         name="prep_own",
@@ -533,11 +545,11 @@
         return pl.pallas_call(
             prep_second_kernel,
             out_shape=[mat_shape, shaped((steps, rows, states), F32)],
-            in_specs=[vmem(), vmem(), hbm()],
+            in_specs=[vmem(), vmem(), vmem(), hbm()],
             out_specs=[vmem(), vmem()],
             compiler_params=params(4),
             name="prep_second",
-        )(trans_logits, other_logits, after)
+        )(trans_logits, other_logits, early_mat, after)
 
     def whole(*shape):
         if grids == 1:

time: 31.4 us -> 31.3 us (level)
  waiting for transfers between devices: 3.28 us -> 2.26 us
  local copies, waits for them, and re-layouts: 0.01 us -> 0.91 us
    all_to_all x1, waiting for transfers between devices: 1.74 us -> 0.42 us  [per_device(): lax.all_to_all(packed, ('hh', 'per', 'st'), split_axis=0, concat_axis=0,...]
    unnamed x2 -> x6, local copies, waits for them, and re-layouts: 0.01 us -> 0.91 us
    pallas_call x1, Pallas kernels: 1.81 us -> 2.25 us  [per_device(): pl.pallas_call(prep_own_kernel, out_shape=[pltpu.VMEM(mat_shape.shape, BF...]
    pallas_call x1, Pallas kernels: 1.42 us -> 1.03 us  [prep_second(): pl.pallas_call(prep_second_kernel, out_shape=[mat_shape, shaped((steps, r...]
  transfers between devices with their start and end apart: 5 -> 5, of which waited for: 2 -> 3; matrix products, arithmetic and copies ran while one was open for 0% -> 0% of each run, Pallas kernels for 28% -> 28%
where the time goes in v23:
time: 31.3 us; the launch traced here: 31 us
  Pallas kernels  15.4 us (49%)
  starting transfers between devices  10.8 us (35%)
  waiting for transfers between devices  2.26 us (7%)
  between operations  1.53 us (5%)
  local copies, waits for them, and re-layouts  0.91 us (3%)
    all_to_all x1, starting transfers between devices, per_device(): lax.all_to_all(packed, ('hh', 'per', 'st'), split_axis=0, concat_axis=0,...  7.84 us
    pallas_call x2, Pallas kernels, second_pass(): pl.pallas_call(functools.partial(second_kernel, resume, last, extend, gri...  5.39 us
    pallas_call x2, Pallas kernels, first_pass(): pl.pallas_call(functools.partial(first_kernel, resume, grids, index), gri...  3.83 us
    ppermute x2, starting transfers between devices, hand_over(): return lax.ppermute(state, 'per', moves)  2.4 us
    pallas_call x1, Pallas kernels, per_device(): pl.pallas_call(prep_own_kernel, out_shape=[pltpu.VMEM(mat_shape.shape, BF...  2.25 us
    ppermute x1, waiting for transfers between devices, per_device(): received = lax.ppermute(other, 'st', swap)  1.53 us
    pallas_call x1, Pallas kernels, per_device(): pl.pallas_call(pack_kernel, out_shape=pltpu.VMEM((group, periods // 2, sl...  1.49 us
    pallas_call x1, Pallas kernels, prep_second(): pl.pallas_call(prep_second_kernel, out_shape=[mat_shape, shaped((steps, r...  1.03 us
  transfers between devices with their start and end apart: 5, of which 3 were waited for; matrix products, arithmetic and copies ran while one was open for 0% of the time, Pallas kernels for 28%

profile of v23, /device:TPU:0, one launch (start us, length us, event | category | flops | bytes accessed | tf_op | source)
XLA Modules:
  0.0 31.0 jit_solution(5184469230165496658)
XLA Ops:
  1.3 1.5 %pack.1 = f32[8,8,384]{2,1,0:T(8,128)} custom-call(s32[1]{0:T(128)S(6)} %copy.12.count_ref, f32[16,384]{1,0:T(8,128)} %bitcast.7, s32[3,128]{1,0:T(4,128)} %bitcast.8, s32[3,128]{1,0:T(4,128)} %bitcast.9), custom_call_target="tpu_custom_call" | custom-call | tf_op jit(solution)/shard_map/pack/pallas_call | solution.py:496
  2.8 0.5 %collective-permute-start = (bf16[4,256,256]{2,1,0:T(8,128)(2,1)}, bf16[4,256,256]{2,1,0:T(8,128)(2,1)S(1)}, u32[]{:S(2)}, u32[]{:S(2)}) collective-permute-start(bf16[4,256,256]{2,1,0:T(8,128)(2,1)} %own_ref.1), channel_id=1, source_target_pairs={{0,1},{1,0},{2,3},{3,2},{4,5},{5,4},{6,7},{7,6},{8,9},{9,8},{10,11... | collective-permute-start | bytes 1572872 | tf_op jit(solution)/shard_map/ppermute | solution.py:506
  3.3 7.8 %all-to-all-start = ((f32[8,8,384]{2,1,0:T(8,128)}), f32[8,8,384]{2,1,0:T(8,128)S(1)}, u32[]{:S(2)}, u32[]{:S(2)}) async-start(f32[8,8,384]{2,1,0:T(8,128)} %pack.1), calls=%async_computation | async-start | bytes 196608 | tf_op jit(solution)/shard_map/all_to_all | solution.py:511
  11.1 2.3 %prep_own.1 = (bf16[8,256,512]{2,1,0:T(8,128)(2,1)S(1)}, f32[4,256,128]{2,1,0:T(8,128)S(1)}, bf16[3,256,512]{2,1,0:T(8,128)(2,1)S(1)}) custom-call(bf16[4,256,256]{2,1,0:T(8,128)(2,1)} %own_ref.1, f32[1,256]{1,0:T(1,128)} %bitcast.10, f32[1,256]{1,0:T(1,128)} %bitcast.11, f32[1,256]{1,0:T(1,128)} %bitcast.12), custom_call_target="tpu_custom_call" | custom-call | tf_op jit(solution)/shard_map/prep_own/pallas_call | solution.py:516
  13.4 0.0 copy-start.1
  13.4 0.9 %copy-done.1 = bf16[3,256,512]{2,1,0:T(8,128)(2,1)} copy-done((bf16[3,256,512]{2,1,0:T(8,128)(2,1)}, bf16[3,256,512]{2,1,0:T(8,128)(2,1)S(1)}, u32[]{:S(2)}) %copy-start.1) | copy-done | bytes 786456
  14.3 0.0 collective-permute-done.other_ref
  14.3 0.7 %prep_other.1.mat = bf16[8,256,512]{2,1,0:T(8,128)(2,1)S(1)} custom-call(bf16[4,256,256]{2,1,0:T(8,128)(2,1)S(1)} %collective-permute-done.other_ref, bf16[8,256,512]{2,1,0:T(8,128)(2,1)S(1)} %get-tuple-element.23.mat_in), custom_call_target="tpu_custom_call", output_to_operand_aliasing={{}: (1, {})} | custom-call | tf_op jit(solution)/shard_map/prep_other/pallas_call | solution.py:534
  15.0 0.4 %all-to-all-done.rows_ref = f32[8,8,384]{2,1,0:T(8,128)S(1)} async-done(((f32[8,8,384]{2,1,0:T(8,128)}), f32[8,8,384]{2,1,0:T(8,128)S(1)}, u32[]{:S(2)}, u32[]{:S(2)}) %all-to-all-start) | async-done | bytes 98336 | tf_op jit(solution)/shard_map/all_to_all | solution.py:511
  15.4 0.0 copy-start
  15.4 0.0 copy-start.2
  15.4 1.9 %first_pass.3 = (bf16[8,256,256]{2,1,0:T(8,128)(2,1)S(1)}, bf16[256,256]{1,0:T(8,128)(2,1)S(1)}, f32[3,9,8,256]{3,2,1,0:T(8,128)S(1)}) custom-call(f32[8,8,384]{2,1,0:T(8,128)S(1)} %all-to-all-done.rows_ref, bf16[8,256,512]{2,1,0:T(8,128)(2,1)S(1)} %prep_other.1.mat, f32[4,256,128]{2,1,0:T(8,128)S(1)} %get-tuple-element.24.consts.refs_2_), custom_call_target="tpu_custom_call" | custom-call | tf_op jit(solution)/shard_map/first_pass/pallas_call | solution.py:577
  17.3 0.9 %collective-permute-start.2 = (bf16[256,256]{1,0:T(8,128)(2,1)S(1)}, bf16[256,256]{1,0:T(8,128)(2,1)S(1)}, u32[]{:S(2)}, u32[]{:S(2)}) collective-permute-start(bf16[256,256]{1,0:T(8,128)(2,1)S(1)} %get-tuple-element.32.refs_4_), channel_id=1, source_target_pairs={{0,2},{2,0},{1,3},{3,1},{4,6},{6,4},{5,7},{7,5},{8,10},{10,8},{9,1... | collective-permute-start | bytes 393224 | tf_op jit(solution)/shard_map/ppermute | solution.py:624
  18.2 1.9 %first_pass.2 = (bf16[8,256,256]{2,1,0:T(8,128)(2,1)S(1)}, bf16[256,256]{1,0:T(8,128)(2,1)S(1)}, f32[3,9,8,256]{3,2,1,0:T(8,128)S(1)}) custom-call(f32[8,8,384]{2,1,0:T(8,128)S(1)} %all-to-all-done.rows_ref, bf16[8,256,512]{2,1,0:T(8,128)(2,1)S(1)} %prep_other.1.mat, f32[4,256,128]{2,1,0:T(8,128)S(1)} %get-tuple-element.24.consts.refs_2_), custom_call_target="tpu_custom_call" | custom-call | tf_op jit(solution)/shard_map/first_pass/pallas_call | solution.py:577
  20.1 1.5 %collective-permute-start.1 = (bf16[256,256]{1,0:T(8,128)(2,1)S(1)}, bf16[256,256]{1,0:T(8,128)(2,1)S(1)}, u32[]{:S(2)}, u32[]{:S(2)}) collective-permute-start(bf16[256,256]{1,0:T(8,128)(2,1)S(1)} %get-tuple-element.27.after_any.refs_4_), channel_id=1, source_target_pairs={{0,2},{2,0},{1,3},{3,1},{4,6},{6,4},{5,7},{7,5},{8,10},{10,8},{9,1... | collective-permute-start | bytes 393224 | tf_op jit(solution)/shard_map/ppermute | solution.py:624
  21.7 0.0 copy-done
  21.7 0.0 copy-done.2
  21.7 1.0 %prep_second.1 = (bf16[8,256,512]{2,1,0:T(8,128)(2,1)S(1)}, f32[8,64,256]{2,1,0:T(8,128)S(1)}) custom-call(bf16[4,256,256]{2,1,0:T(8,128)(2,1)S(1)} %copy-done, bf16[4,256,256]{2,1,0:T(8,128)(2,1)S(1)} %collective-permute-done.other_ref, bf16[3,256,512]{2,1,0:T(8,128)(2,1)S(1)} %copy-done.2, bf16[256,256]{1,0:T(8,128)(2,1)S(1)} %get-tuple-element.27.after_any.refs_4_), custom_call_target="tpu_custom_call" | custom-call | tf_op jit(solution)/shard_map/prep_second/pallas_call | solution.py:545
  22.7 0.3 collective-permute-done.2.refs_5_
  23.0 2.7 %second_pass.2 = (f32[8,64,256]{2,1,0:T(8,128)S(1)}, f32[8,128]{1,0:T(8,128)S(1)}) custom-call(f32[3,9,8,256]{3,2,1,0:T(8,128)S(1)} %get-tuple-element.30.refs_0_, bf16[8,256,512]{2,1,0:T(8,128)(2,1)S(1)} %get-tuple-element.28.refs_1_, f32[4,256,128]{2,1,0:T(8,128)S(1)} %get-tuple-element.24.consts.refs_2_, ...), custom_call_target="tpu_custom_call" | custom-call | tf_op jit(solution)/shard_map/second_pass/pallas_call | solution.py:605
  25.7 0.0 collective-permute-done.1.refs_5_
  25.7 2.7 %second_pass.3 = (f32[520,128]{1,0:T(8,128)S(1)}, f32[520,128]{1,0:T(8,128)S(1)}) custom-call(f32[3,9,8,256]{3,2,1,0:T(8,128)S(1)} %get-tuple-element.25.refs_0_, bf16[8,256,512]{2,1,0:T(8,128)(2,1)S(1)} %get-tuple-element.28.refs_1_, f32[4,256,128]{2,1,0:T(8,128)S(1)} %get-tuple-element.24.consts.refs_2_, ...), custom_call_target="tpu_custom_call" | custom-call | tf_op jit(solution)/shard_map/second_pass/pallas_call | solution.py:605
  28.4 0.1 collective-permute-start.3
  28.5 1.5 %collective-permute-done.3.other_ref = f32[520,128]{1,0:T(8,128)S(1)} collective-permute-done((f32[520,128]{1,0:T(8,128)S(1)}, f32[520,128]{1,0:T(8,128)S(1)}, u32[]{:S(2)}, u32[]{:S(2)}) %collective-permute-start.3) | collective-permute-done | bytes 266272 | tf_op jit(solution)/shard_map/ppermute | solution.py:662
  30.0 0.8 %finish.1 = (f32[512,128]{1,0:T(8,128)}, f32[1]{0:T(128)}) custom-call(f32[520,128]{1,0:T(8,128)S(1)} %get-tuple-element.36.mine_ref, f32[520,128]{1,0:T(8,128)S(1)} %collective-permute-done.3.other_ref), custom_call_target="tpu_custom_call" | custom-call | tf_op jit(solution)/shard_map/finish/pallas_call | solution.py:663
Async XLA Ops:
  2.8 11.5 %collective-permute-start = (bf16[4,256,256]{2,1,0:T(8,128)(2,1)}, bf16[4,256,256]{2,1,0:T(8,128)(2,1)S(1)}, u32[]{:S(2)}, u32[]{:S(2)}) collective-permute-start(bf16[4,256,256]{2,1,0:T(8,128)(2,1)} %own_ref.1), channel_id=1, source_target_pairs={{0,1},{1,0},{2,3},{3,2},{4,5},{5,4},{6,7},{7,6},{8,9},{9,8},{10,11... | collective-permute-start | bytes 1572872 | tf_op jit(solution)/shard_map/ppermute | solution.py:506
  3.3 12.1 %all-to-all-start = ((f32[8,8,384]{2,1,0:T(8,128)}), f32[8,8,384]{2,1,0:T(8,128)S(1)}, u32[]{:S(2)}, u32[]{:S(2)}) async-start(f32[8,8,384]{2,1,0:T(8,128)} %pack.1), calls=%async_computation | async-start | bytes 196608 | tf_op jit(solution)/shard_map/all_to_all | solution.py:511
  13.4 0.9 %copy-start.1 = (bf16[3,256,512]{2,1,0:T(8,128)(2,1)}, bf16[3,256,512]{2,1,0:T(8,128)(2,1)S(1)}, u32[]{:S(2)}) copy-start(bf16[3,256,512]{2,1,0:T(8,128)(2,1)S(1)} %get-tuple-element.26.early) | copy-start | bytes 2359300
  15.4 6.2 %copy-start = (bf16[4,256,256]{2,1,0:T(8,128)(2,1)S(1)}, bf16[4,256,256]{2,1,0:T(8,128)(2,1)}, u32[]{:S(2)}) copy-start(bf16[4,256,256]{2,1,0:T(8,128)(2,1)} %own_ref.1) | copy-start | bytes 1572868
  15.4 6.2 %copy-start.2 = (bf16[3,256,512]{2,1,0:T(8,128)(2,1)S(1)}, bf16[3,256,512]{2,1,0:T(8,128)(2,1)}, u32[]{:S(2)}) copy-start(bf16[3,256,512]{2,1,0:T(8,128)(2,1)} %copy-done.1) | copy-start | bytes 2359300
  17.3 5.7 %collective-permute-start.2 = (bf16[256,256]{1,0:T(8,128)(2,1)S(1)}, bf16[256,256]{1,0:T(8,128)(2,1)S(1)}, u32[]{:S(2)}, u32[]{:S(2)}) collective-permute-start(bf16[256,256]{1,0:T(8,128)(2,1)S(1)} %get-tuple-element.32.refs_4_), channel_id=1, source_target_pairs={{0,2},{2,0},{1,3},{3,1},{4,6},{6,4},{5,7},{7,5},{8,10},{10,8},{9,1... | collective-permute-start | bytes 393224 | tf_op jit(solution)/shard_map/ppermute | solution.py:624
  20.1 5.6 %collective-permute-start.1 = (bf16[256,256]{1,0:T(8,128)(2,1)S(1)}, bf16[256,256]{1,0:T(8,128)(2,1)S(1)}, u32[]{:S(2)}, u32[]{:S(2)}) collective-permute-start(bf16[256,256]{1,0:T(8,128)(2,1)S(1)} %get-tuple-element.27.after_any.refs_4_), channel_id=1, source_target_pairs={{0,2},{2,0},{1,3},{3,1},{4,6},{6,4},{5,7},{7,5},{8,10},{10,8},{9,1... | collective-permute-start | bytes 393224 | tf_op jit(solution)/shard_map/ppermute | solution.py:624
  28.4 1.6 %collective-permute-start.3 = (f32[520,128]{1,0:T(8,128)S(1)}, f32[520,128]{1,0:T(8,128)S(1)}, u32[]{:S(2)}, u32[]{:S(2)}) collective-permute-start(f32[520,128]{1,0:T(8,128)S(1)} %get-tuple-element.37), channel_id=1, source_target_pairs={{0,1},{1,0},{2,3},{3,2},{4,5},{5,4},{6,7},{7,6},{8,9},{9,8},{10,11... | collective-permute-start | bytes 798728 | tf_op jit(solution)/shard_map/ppermute | solution.py:662

commit v24 on v23

--- a/solution.py
+++ b/solution.py
@@ -518,7 +518,7 @@
         out_shape=[
             pltpu.VMEM(mat_shape.shape, BF16),
             pltpu.VMEM((4, states, LANES), F32),
-            pltpu.VMEM((max(part - 1, 1),) + mat_shape.shape[1:], BF16),
+            pltpu.VMEM((max(part // 2, 1),) + mat_shape.shape[1:], BF16),
         ],
         in_specs=[hbm()] * 4,
         out_specs=[vmem()] * 3,

time: 31.3 us -> 31.1 us (level)
  transfers between devices with their start and end apart: 5 -> 5, of which waited for: 3 -> 2; matrix products, arithmetic and copies ran while one was open for 0% -> 0% of each run, Pallas kernels for 28% -> 28%
where the time goes in v24:
time: 31.1 us; the launch traced here: 30.8 us
  Pallas kernels  15.5 us (50%)
  starting transfers between devices  10.8 us (35%)
  waiting for transfers between devices  2.22 us (7%)
  between operations  1.54 us (5%)
  local copies, waits for them, and re-layouts  0.79 us (3%)
    all_to_all x1, starting transfers between devices, per_device(): lax.all_to_all(packed, ('hh', 'per', 'st'), split_axis=0, concat_axis=0,...  7.84 us
    pallas_call x2, Pallas kernels, second_pass(): pl.pallas_call(functools.partial(second_kernel, resume, last, extend, gri...  5.43 us
    pallas_call x2, Pallas kernels, first_pass(): pl.pallas_call(functools.partial(first_kernel, resume, grids, index), gri...  3.83 us
    ppermute x2, starting transfers between devices, hand_over(): return lax.ppermute(state, 'per', moves)  2.4 us
    pallas_call x1, Pallas kernels, per_device(): pl.pallas_call(prep_own_kernel, out_shape=[pltpu.VMEM(mat_shape.shape, BF...  2.1 us
    ppermute x1, waiting for transfers between devices, per_device(): received = lax.ppermute(other, 'st', swap)  1.53 us
    pallas_call x1, Pallas kernels, per_device(): pl.pallas_call(pack_kernel, out_shape=pltpu.VMEM((group, periods // 2, sl...  1.49 us
    pallas_call x1, Pallas kernels, prep_second(): pl.pallas_call(prep_second_kernel, out_shape=[mat_shape, shaped((steps, r...  1.17 us
  transfers between devices with their start and end apart: 5, of which 2 were waited for; matrix products, arithmetic and copies ran while one was open for 0% of the time, Pallas kernels for 28%

profile of v24, /device:TPU:0, one launch (start us, length us, event | category | flops | bytes accessed | tf_op | source)
XLA Modules:
  0.0 30.8 jit_solution(10333308580614190716)
XLA Ops:
  1.3 1.5 %pack.1 = f32[8,8,384]{2,1,0:T(8,128)} custom-call(s32[1]{0:T(128)S(6)} %copy.12.count_ref, f32[16,384]{1,0:T(8,128)} %bitcast.7, s32[3,128]{1,0:T(4,128)} %bitcast.8, s32[3,128]{1,0:T(4,128)} %bitcast.9), custom_call_target="tpu_custom_call" | custom-call | tf_op jit(solution)/shard_map/pack/pallas_call | solution.py:496
  2.8 0.5 %collective-permute-start = (bf16[4,256,256]{2,1,0:T(8,128)(2,1)}, bf16[4,256,256]{2,1,0:T(8,128)(2,1)S(1)}, u32[]{:S(2)}, u32[]{:S(2)}) collective-permute-start(bf16[4,256,256]{2,1,0:T(8,128)(2,1)} %own_ref.1), channel_id=1, source_target_pairs={{0,1},{1,0},{2,3},{3,2},{4,5},{5,4},{6,7},{7,6},{8,9},{9,8},{10,11... | collective-permute-start | bytes 1572872 | tf_op jit(solution)/shard_map/ppermute | solution.py:506
  3.3 7.8 %all-to-all-start = ((f32[8,8,384]{2,1,0:T(8,128)}), f32[8,8,384]{2,1,0:T(8,128)S(1)}, u32[]{:S(2)}, u32[]{:S(2)}) async-start(f32[8,8,384]{2,1,0:T(8,128)} %pack.1), calls=%async_computation | async-start | bytes 196608 | tf_op jit(solution)/shard_map/all_to_all | solution.py:511
  11.1 2.1 %prep_own.1 = (bf16[8,256,512]{2,1,0:T(8,128)(2,1)S(1)}, f32[4,256,128]{2,1,0:T(8,128)S(1)}, bf16[2,256,512]{2,1,0:T(8,128)(2,1)S(1)}) custom-call(bf16[4,256,256]{2,1,0:T(8,128)(2,1)} %own_ref.1, f32[1,256]{1,0:T(1,128)} %bitcast.10, f32[1,256]{1,0:T(1,128)} %bitcast.11, f32[1,256]{1,0:T(1,128)} %bitcast.12), custom_call_target="tpu_custom_call" | custom-call | tf_op jit(solution)/shard_map/prep_own/pallas_call | solution.py:516
  13.2 0.0 copy-start.1
  13.3 0.8 %copy-done.1 = bf16[2,256,512]{2,1,0:T(8,128)(2,1)} copy-done((bf16[2,256,512]{2,1,0:T(8,128)(2,1)}, bf16[2,256,512]{2,1,0:T(8,128)(2,1)S(1)}, u32[]{:S(2)}) %copy-start.1) | copy-done | bytes 524312
  14.0 0.0 collective-permute-done.other_ref
  14.0 0.7 %prep_other.1.mat = bf16[8,256,512]{2,1,0:T(8,128)(2,1)S(1)} custom-call(bf16[4,256,256]{2,1,0:T(8,128)(2,1)S(1)} %collective-permute-done.other_ref, bf16[8,256,512]{2,1,0:T(8,128)(2,1)S(1)} %get-tuple-element.23.mat_in), custom_call_target="tpu_custom_call", output_to_operand_aliasing={{}: (1, {})} | custom-call | tf_op jit(solution)/shard_map/prep_other/pallas_call | solution.py:534
  14.7 0.7 %all-to-all-done.rows_ref = f32[8,8,384]{2,1,0:T(8,128)S(1)} async-done(((f32[8,8,384]{2,1,0:T(8,128)}), f32[8,8,384]{2,1,0:T(8,128)S(1)}, u32[]{:S(2)}, u32[]{:S(2)}) %all-to-all-start) | async-done | bytes 98336 | tf_op jit(solution)/shard_map/all_to_all | solution.py:511
  15.4 0.0 copy-start
  15.4 0.0 copy-start.2
  15.4 1.9 %first_pass.3 = (bf16[8,256,256]{2,1,0:T(8,128)(2,1)S(1)}, bf16[256,256]{1,0:T(8,128)(2,1)S(1)}, f32[3,9,8,256]{3,2,1,0:T(8,128)S(1)}) custom-call(f32[8,8,384]{2,1,0:T(8,128)S(1)} %all-to-all-done.rows_ref, bf16[8,256,512]{2,1,0:T(8,128)(2,1)S(1)} %prep_other.1.mat, f32[4,256,128]{2,1,0:T(8,128)S(1)} %get-tuple-element.24.consts.refs_2_), custom_call_target="tpu_custom_call" | custom-call | tf_op jit(solution)/shard_map/first_pass/pallas_call | solution.py:577
  17.3 0.9 %collective-permute-start.2 = (bf16[256,256]{1,0:T(8,128)(2,1)S(1)}, bf16[256,256]{1,0:T(8,128)(2,1)S(1)}, u32[]{:S(2)}, u32[]{:S(2)}) collective-permute-start(bf16[256,256]{1,0:T(8,128)(2,1)S(1)} %get-tuple-element.32.refs_4_), channel_id=1, source_target_pairs={{0,2},{2,0},{1,3},{3,1},{4,6},{6,4},{5,7},{7,5},{8,10},{10,8},{9,1... | collective-permute-start | bytes 393224 | tf_op jit(solution)/shard_map/ppermute | solution.py:624
  18.2 1.9 %first_pass.2 = (bf16[8,256,256]{2,1,0:T(8,128)(2,1)S(1)}, bf16[256,256]{1,0:T(8,128)(2,1)S(1)}, f32[3,9,8,256]{3,2,1,0:T(8,128)S(1)}) custom-call(f32[8,8,384]{2,1,0:T(8,128)S(1)} %all-to-all-done.rows_ref, bf16[8,256,512]{2,1,0:T(8,128)(2,1)S(1)} %prep_other.1.mat, f32[4,256,128]{2,1,0:T(8,128)S(1)} %get-tuple-element.24.consts.refs_2_), custom_call_target="tpu_custom_call" | custom-call | tf_op jit(solution)/shard_map/first_pass/pallas_call | solution.py:577
  20.1 1.5 %collective-permute-start.1 = (bf16[256,256]{1,0:T(8,128)(2,1)S(1)}, bf16[256,256]{1,0:T(8,128)(2,1)S(1)}, u32[]{:S(2)}, u32[]{:S(2)}) collective-permute-start(bf16[256,256]{1,0:T(8,128)(2,1)S(1)} %get-tuple-element.27.after_any.refs_4_), channel_id=1, source_target_pairs={{0,2},{2,0},{1,3},{3,1},{4,6},{6,4},{5,7},{7,5},{8,10},{10,8},{9,1... | collective-permute-start | bytes 393224 | tf_op jit(solution)/shard_map/ppermute | solution.py:624
  21.7 0.0 copy-done
  21.7 0.0 copy-done.2
  21.7 1.2 %prep_second.1 = (bf16[8,256,512]{2,1,0:T(8,128)(2,1)S(1)}, f32[8,64,256]{2,1,0:T(8,128)S(1)}) custom-call(bf16[4,256,256]{2,1,0:T(8,128)(2,1)S(1)} %copy-done, bf16[4,256,256]{2,1,0:T(8,128)(2,1)S(1)} %collective-permute-done.other_ref, bf16[2,256,512]{2,1,0:T(8,128)(2,1)S(1)} %copy-done.2, bf16[256,256]{1,0:T(8,128)(2,1)S(1)} %get-tuple-element.27.after_any.refs_4_), custom_call_target="tpu_custom_call" | custom-call | tf_op jit(solution)/shard_map/prep_second/pallas_call | solution.py:545
  22.8 0.0 collective-permute-done.2.refs_5_
  22.8 2.7 %second_pass.2 = (f32[8,64,256]{2,1,0:T(8,128)S(1)}, f32[8,128]{1,0:T(8,128)S(1)}) custom-call(f32[3,9,8,256]{3,2,1,0:T(8,128)S(1)} %get-tuple-element.30.refs_0_, bf16[8,256,512]{2,1,0:T(8,128)(2,1)S(1)} %get-tuple-element.28.refs_1_, f32[4,256,128]{2,1,0:T(8,128)S(1)} %get-tuple-element.24.consts.refs_2_, ...), custom_call_target="tpu_custom_call" | custom-call | tf_op jit(solution)/shard_map/second_pass/pallas_call | solution.py:605
  25.6 0.0 collective-permute-done.1.refs_5_
  25.6 2.7 %second_pass.3 = (f32[520,128]{1,0:T(8,128)S(1)}, f32[520,128]{1,0:T(8,128)S(1)}) custom-call(f32[3,9,8,256]{3,2,1,0:T(8,128)S(1)} %get-tuple-element.25.refs_0_, bf16[8,256,512]{2,1,0:T(8,128)(2,1)S(1)} %get-tuple-element.28.refs_1_, f32[4,256,128]{2,1,0:T(8,128)S(1)} %get-tuple-element.24.consts.refs_2_, ...), custom_call_target="tpu_custom_call" | custom-call | tf_op jit(solution)/shard_map/second_pass/pallas_call | solution.py:605
  28.3 0.1 collective-permute-start.3
  28.4 1.5 %collective-permute-done.3.other_ref = f32[520,128]{1,0:T(8,128)S(1)} collective-permute-done((f32[520,128]{1,0:T(8,128)S(1)}, f32[520,128]{1,0:T(8,128)S(1)}, u32[]{:S(2)}, u32[]{:S(2)}) %collective-permute-start.3) | collective-permute-done | bytes 266272 | tf_op jit(solution)/shard_map/ppermute | solution.py:662
  29.9 0.8 %finish.1 = (f32[512,128]{1,0:T(8,128)}, f32[1]{0:T(128)}) custom-call(f32[520,128]{1,0:T(8,128)S(1)} %get-tuple-element.36.mine_ref, f32[520,128]{1,0:T(8,128)S(1)} %collective-permute-done.3.other_ref), custom_call_target="tpu_custom_call" | custom-call | tf_op jit(solution)/shard_map/finish/pallas_call | solution.py:663
Async XLA Ops:
  2.8 11.3 %collective-permute-start = (bf16[4,256,256]{2,1,0:T(8,128)(2,1)}, bf16[4,256,256]{2,1,0:T(8,128)(2,1)S(1)}, u32[]{:S(2)}, u32[]{:S(2)}) collective-permute-start(bf16[4,256,256]{2,1,0:T(8,128)(2,1)} %own_ref.1), channel_id=1, source_target_pairs={{0,1},{1,0},{2,3},{3,2},{4,5},{5,4},{6,7},{7,6},{8,9},{9,8},{10,11... | collective-permute-start | bytes 1572872 | tf_op jit(solution)/shard_map/ppermute | solution.py:506
  3.3 12.1 %all-to-all-start = ((f32[8,8,384]{2,1,0:T(8,128)}), f32[8,8,384]{2,1,0:T(8,128)S(1)}, u32[]{:S(2)}, u32[]{:S(2)}) async-start(f32[8,8,384]{2,1,0:T(8,128)} %pack.1), calls=%async_computation | async-start | bytes 196608 | tf_op jit(solution)/shard_map/all_to_all | solution.py:511
  13.2 0.8 %copy-start.1 = (bf16[2,256,512]{2,1,0:T(8,128)(2,1)}, bf16[2,256,512]{2,1,0:T(8,128)(2,1)S(1)}, u32[]{:S(2)}) copy-start(bf16[2,256,512]{2,1,0:T(8,128)(2,1)S(1)} %get-tuple-element.26.early) | copy-start | bytes 1572868
  15.4 6.2 %copy-start = (bf16[4,256,256]{2,1,0:T(8,128)(2,1)S(1)}, bf16[4,256,256]{2,1,0:T(8,128)(2,1)}, u32[]{:S(2)}) copy-start(bf16[4,256,256]{2,1,0:T(8,128)(2,1)} %own_ref.1) | copy-start | bytes 1572868
  15.4 6.2 %copy-start.2 = (bf16[2,256,512]{2,1,0:T(8,128)(2,1)S(1)}, bf16[2,256,512]{2,1,0:T(8,128)(2,1)}, u32[]{:S(2)}) copy-start(bf16[2,256,512]{2,1,0:T(8,128)(2,1)} %copy-done.1) | copy-start | bytes 1572868
  17.3 5.5 %collective-permute-start.2 = (bf16[256,256]{1,0:T(8,128)(2,1)S(1)}, bf16[256,256]{1,0:T(8,128)(2,1)S(1)}, u32[]{:S(2)}, u32[]{:S(2)}) collective-permute-start(bf16[256,256]{1,0:T(8,128)(2,1)S(1)} %get-tuple-element.32.refs_4_), channel_id=1, source_target_pairs={{0,2},{2,0},{1,3},{3,1},{4,6},{6,4},{5,7},{7,5},{8,10},{10,8},{9,1... | collective-permute-start | bytes 393224 | tf_op jit(solution)/shard_map/ppermute | solution.py:624
  20.1 5.5 %collective-permute-start.1 = (bf16[256,256]{1,0:T(8,128)(2,1)S(1)}, bf16[256,256]{1,0:T(8,128)(2,1)S(1)}, u32[]{:S(2)}, u32[]{:S(2)}) collective-permute-start(bf16[256,256]{1,0:T(8,128)(2,1)S(1)} %get-tuple-element.27.after_any.refs_4_), channel_id=1, source_target_pairs={{0,2},{2,0},{1,3},{3,1},{4,6},{6,4},{5,7},{7,5},{8,10},{10,8},{9,1... | collective-permute-start | bytes 393224 | tf_op jit(solution)/shard_map/ppermute | solution.py:624
  28.3 1.6 %collective-permute-start.3 = (f32[520,128]{1,0:T(8,128)S(1)}, f32[520,128]{1,0:T(8,128)S(1)}, u32[]{:S(2)}, u32[]{:S(2)}) collective-permute-start(f32[520,128]{1,0:T(8,128)S(1)} %get-tuple-element.37), channel_id=1, source_target_pairs={{0,1},{1,0},{2,3},{3,2},{4,5},{5,4},{6,7},{7,6},{8,9},{9,8},{10,11... | collective-permute-start | bytes 798728 | tf_op jit(solution)/shard_map/ppermute | solution.py:662

commit v25 on v24

--- a/solution.py
+++ b/solution.py
@@ -177,7 +177,7 @@
     return lax.dot_general(weights_ref[...], carried, (((1,), (1,)), ((), ())), preferred_element_type=F32)
 
 
-def run_forward(lead, mat, hist, sel_ref, consts, ab_ref, logs, second=None, fresh=False):
+def run_forward(lead, mat, hist, sel_ref, consts, ab_ref, logs, second=None, fresh=False, extend=True):
     steps, states, width = hist.shape
     cuts = tiles(width)
     here = hist.at[0] if second is None else ab_ref
@@ -201,6 +201,8 @@
                 total = column_sum(moved * hist[k, :, cols].astype(F32))
                 weight = jnp.where(moving, 1.0 / total, 0.0)
                 weights_ref[:, cols] = (own_alpha[:, cols] * inverse[q] * weight).astype(BF16)
+                if k + 1 == steps and not extend:
+                    continue
             emit = emission(sel_ref, consts, step_now, cols)
             joint = (consts[0] if begins else jnp.where(moving, moved, consts[0])) * emit
             scale = column_sum(joint)
@@ -219,6 +221,7 @@
     steps, states, width = hist.shape
     cuts = tiles(width)
     rest = [x[:1] for x in state]
+    at_edge = lax.axis_size("per") == 2
     size = [jnp.zeros((1, LANES), F32) for _ in cuts]
 
     def step(k):
@@ -251,7 +254,8 @@
                 total = column_sum(product * hist[k, :, cols].astype(F32))
                 weight = jnp.where(moving, 1.0 / total, 0.0)
                 weights_ref[:, cols] = (own_alpha[:, cols] * weight * shrink).astype(BF16)
-                state[q] = jnp.where(moving, product, rest[q])
+                if k > 1 or not at_edge:
+                    state[q] = jnp.where(moving, product, rest[q])
         if second is not None:
             add_counts(k, outer_sum(weights_ref, ub_ref[...]))
 
@@ -265,6 +269,10 @@
         leave(left())
         return
     between()
+    nothing = jnp.zeros((second[0].shape[0], states), F32)
+    if at_edge:
+        second[2](0, nothing)
+        return
 
     @pl.when(lead > 0)
     def _():
@@ -273,7 +281,7 @@
 
     @pl.when(lead == 0)
     def _():
-        second[2](0, jnp.zeros((second[0].shape[0], states), F32))
+        second[2](0, nothing)
 
 
 def put_state(state_out, values, logs, spread):
@@ -440,7 +448,7 @@
     @pl.when(jnp.logical_not(forward_first))
     def _():
         ab_ref[...] = state_in[...]
-        values = run_forward(lead, mat, hist, sel_ref, consts, ab_ref, list(zeros), second)
+        values = run_forward(lead, mat, hist, sel_ref, consts, ab_ref, list(zeros), second, extend=extend)
         add_sums(state_in, own_state)
         if extend:
             put_state(state_out, values, zeros, spread)

time: 31.1 us -> 31 us (level)
  no operation moved by 1% of the time
where the time goes in v25:
time: 31 us; the launch traced here: 30.7 us
  Pallas kernels  15.4 us (50%)
  starting transfers between devices  10.8 us (35%)
  waiting for transfers between devices  2.23 us (7%)
  between operations  1.53 us (5%)
  local copies, waits for them, and re-layouts  0.79 us (3%)
    all_to_all x1, starting transfers between devices, per_device(): lax.all_to_all(packed, ('hh', 'per', 'st'), split_axis=0, concat_axis=0,...  7.84 us
    pallas_call x2, Pallas kernels, second_pass(): pl.pallas_call(functools.partial(second_kernel, resume, last, extend, gri...  5.34 us
    pallas_call x2, Pallas kernels, first_pass(): pl.pallas_call(functools.partial(first_kernel, resume, grids, index), gri...  3.83 us
    ppermute x2, starting transfers between devices, hand_over(): return lax.ppermute(state, 'per', moves)  2.4 us
    pallas_call x1, Pallas kernels, per_device(): pl.pallas_call(prep_own_kernel, out_shape=[pltpu.VMEM(mat_shape.shape, BF...  2.1 us
    ppermute x1, waiting for transfers between devices, per_device(): received = lax.ppermute(other, 'st', swap)  1.53 us
    pallas_call x1, Pallas kernels, per_device(): pl.pallas_call(pack_kernel, out_shape=pltpu.VMEM((group, periods // 2, sl...  1.49 us
    pallas_call x1, Pallas kernels, prep_second(): pl.pallas_call(prep_second_kernel, out_shape=[mat_shape, shaped((steps, r...  1.17 us
  transfers between devices with their start and end apart: 5, of which 2 were waited for; matrix products, arithmetic and copies ran while one was open for 0% of the time, Pallas kernels for 28%

profile of v25, /device:TPU:0, one launch (start us, length us, event | category | flops | bytes accessed | tf_op | source)
XLA Modules:
  0.0 30.7 jit_solution(10922837217715954145)
XLA Ops:
  1.3 1.5 %pack.1 = f32[8,8,384]{2,1,0:T(8,128)} custom-call(s32[1]{0:T(128)S(6)} %copy.12.count_ref, f32[16,384]{1,0:T(8,128)} %bitcast.7, s32[3,128]{1,0:T(4,128)} %bitcast.8, s32[3,128]{1,0:T(4,128)} %bitcast.9), custom_call_target="tpu_custom_call" | custom-call | tf_op jit(solution)/shard_map/pack/pallas_call | solution.py:504
  2.8 0.5 %collective-permute-start = (bf16[4,256,256]{2,1,0:T(8,128)(2,1)}, bf16[4,256,256]{2,1,0:T(8,128)(2,1)S(1)}, u32[]{:S(2)}, u32[]{:S(2)}) collective-permute-start(bf16[4,256,256]{2,1,0:T(8,128)(2,1)} %own_ref.1), channel_id=1, source_target_pairs={{0,1},{1,0},{2,3},{3,2},{4,5},{5,4},{6,7},{7,6},{8,9},{9,8},{10,11... | collective-permute-start | bytes 1572872 | tf_op jit(solution)/shard_map/ppermute | solution.py:514
  3.3 7.8 %all-to-all-start = ((f32[8,8,384]{2,1,0:T(8,128)}), f32[8,8,384]{2,1,0:T(8,128)S(1)}, u32[]{:S(2)}, u32[]{:S(2)}) async-start(f32[8,8,384]{2,1,0:T(8,128)} %pack.1), calls=%async_computation | async-start | bytes 196608 | tf_op jit(solution)/shard_map/all_to_all | solution.py:519
  11.1 2.1 %prep_own.1 = (bf16[8,256,512]{2,1,0:T(8,128)(2,1)S(1)}, f32[4,256,128]{2,1,0:T(8,128)S(1)}, bf16[2,256,512]{2,1,0:T(8,128)(2,1)S(1)}) custom-call(bf16[4,256,256]{2,1,0:T(8,128)(2,1)} %own_ref.1, f32[1,256]{1,0:T(1,128)} %bitcast.10, f32[1,256]{1,0:T(1,128)} %bitcast.11, f32[1,256]{1,0:T(1,128)} %bitcast.12), custom_call_target="tpu_custom_call" | custom-call | tf_op jit(solution)/shard_map/prep_own/pallas_call | solution.py:524
  13.2 0.0 copy-start.1
  13.3 0.8 %copy-done.1 = bf16[2,256,512]{2,1,0:T(8,128)(2,1)} copy-done((bf16[2,256,512]{2,1,0:T(8,128)(2,1)}, bf16[2,256,512]{2,1,0:T(8,128)(2,1)S(1)}, u32[]{:S(2)}) %copy-start.1) | copy-done | bytes 524312
  14.0 0.0 collective-permute-done.other_ref
  14.0 0.7 %prep_other.1.mat = bf16[8,256,512]{2,1,0:T(8,128)(2,1)S(1)} custom-call(bf16[4,256,256]{2,1,0:T(8,128)(2,1)S(1)} %collective-permute-done.other_ref, bf16[8,256,512]{2,1,0:T(8,128)(2,1)S(1)} %get-tuple-element.23.mat_in), custom_call_target="tpu_custom_call", output_to_operand_aliasing={{}: (1, {})} | custom-call | tf_op jit(solution)/shard_map/prep_other/pallas_call | solution.py:542
  14.7 0.7 %all-to-all-done.rows_ref = f32[8,8,384]{2,1,0:T(8,128)S(1)} async-done(((f32[8,8,384]{2,1,0:T(8,128)}), f32[8,8,384]{2,1,0:T(8,128)S(1)}, u32[]{:S(2)}, u32[]{:S(2)}) %all-to-all-start) | async-done | bytes 98336 | tf_op jit(solution)/shard_map/all_to_all | solution.py:519
  15.4 0.0 copy-start
  15.4 0.0 copy-start.2
  15.4 1.9 %first_pass.3 = (bf16[8,256,256]{2,1,0:T(8,128)(2,1)S(1)}, bf16[256,256]{1,0:T(8,128)(2,1)S(1)}, f32[3,9,8,256]{3,2,1,0:T(8,128)S(1)}) custom-call(f32[8,8,384]{2,1,0:T(8,128)S(1)} %all-to-all-done.rows_ref, bf16[8,256,512]{2,1,0:T(8,128)(2,1)S(1)} %prep_other.1.mat, f32[4,256,128]{2,1,0:T(8,128)S(1)} %get-tuple-element.24.consts.refs_2_), custom_call_target="tpu_custom_call" | custom-call | tf_op jit(solution)/shard_map/first_pass/pallas_call | solution.py:585
  17.3 0.9 %collective-permute-start.2 = (bf16[256,256]{1,0:T(8,128)(2,1)S(1)}, bf16[256,256]{1,0:T(8,128)(2,1)S(1)}, u32[]{:S(2)}, u32[]{:S(2)}) collective-permute-start(bf16[256,256]{1,0:T(8,128)(2,1)S(1)} %get-tuple-element.32.refs_4_), channel_id=1, source_target_pairs={{0,2},{2,0},{1,3},{3,1},{4,6},{6,4},{5,7},{7,5},{8,10},{10,8},{9,1... | collective-permute-start | bytes 393224 | tf_op jit(solution)/shard_map/ppermute | solution.py:632
  18.2 1.9 %first_pass.2 = (bf16[8,256,256]{2,1,0:T(8,128)(2,1)S(1)}, bf16[256,256]{1,0:T(8,128)(2,1)S(1)}, f32[3,9,8,256]{3,2,1,0:T(8,128)S(1)}) custom-call(f32[8,8,384]{2,1,0:T(8,128)S(1)} %all-to-all-done.rows_ref, bf16[8,256,512]{2,1,0:T(8,128)(2,1)S(1)} %prep_other.1.mat, f32[4,256,128]{2,1,0:T(8,128)S(1)} %get-tuple-element.24.consts.refs_2_), custom_call_target="tpu_custom_call" | custom-call | tf_op jit(solution)/shard_map/first_pass/pallas_call | solution.py:585
  20.1 1.5 %collective-permute-start.1 = (bf16[256,256]{1,0:T(8,128)(2,1)S(1)}, bf16[256,256]{1,0:T(8,128)(2,1)S(1)}, u32[]{:S(2)}, u32[]{:S(2)}) collective-permute-start(bf16[256,256]{1,0:T(8,128)(2,1)S(1)} %get-tuple-element.27.after_any.refs_4_), channel_id=1, source_target_pairs={{0,2},{2,0},{1,3},{3,1},{4,6},{6,4},{5,7},{7,5},{8,10},{10,8},{9,1... | collective-permute-start | bytes 393224 | tf_op jit(solution)/shard_map/ppermute | solution.py:632
  21.7 0.0 copy-done
  21.7 0.0 copy-done.2
  21.7 1.2 %prep_second.1 = (bf16[8,256,512]{2,1,0:T(8,128)(2,1)S(1)}, f32[8,64,256]{2,1,0:T(8,128)S(1)}) custom-call(bf16[4,256,256]{2,1,0:T(8,128)(2,1)S(1)} %copy-done, bf16[4,256,256]{2,1,0:T(8,128)(2,1)S(1)} %collective-permute-done.other_ref, bf16[2,256,512]{2,1,0:T(8,128)(2,1)S(1)} %copy-done.2, bf16[256,256]{1,0:T(8,128)(2,1)S(1)} %get-tuple-element.27.after_any.refs_4_), custom_call_target="tpu_custom_call" | custom-call | tf_op jit(solution)/shard_map/prep_second/pallas_call | solution.py:553
  22.8 0.0 collective-permute-done.2.refs_5_
  22.8 2.7 %second_pass.2 = (f32[8,64,256]{2,1,0:T(8,128)S(1)}, f32[8,128]{1,0:T(8,128)S(1)}) custom-call(f32[3,9,8,256]{3,2,1,0:T(8,128)S(1)} %get-tuple-element.30.refs_0_, bf16[8,256,512]{2,1,0:T(8,128)(2,1)S(1)} %get-tuple-element.28.refs_1_, f32[4,256,128]{2,1,0:T(8,128)S(1)} %get-tuple-element.24.consts.refs_2_, ...), custom_call_target="tpu_custom_call" | custom-call | tf_op jit(solution)/shard_map/second_pass/pallas_call | solution.py:613
  25.6 0.0 collective-permute-done.1.refs_5_
  25.6 2.6 %second_pass.3 = (f32[520,128]{1,0:T(8,128)S(1)}, f32[520,128]{1,0:T(8,128)S(1)}) custom-call(f32[3,9,8,256]{3,2,1,0:T(8,128)S(1)} %get-tuple-element.25.refs_0_, bf16[8,256,512]{2,1,0:T(8,128)(2,1)S(1)} %get-tuple-element.28.refs_1_, f32[4,256,128]{2,1,0:T(8,128)S(1)} %get-tuple-element.24.consts.refs_2_, ...), custom_call_target="tpu_custom_call" | custom-call | tf_op jit(solution)/shard_map/second_pass/pallas_call | solution.py:613
  28.2 0.1 collective-permute-start.3
  28.3 1.5 %collective-permute-done.3.other_ref = f32[520,128]{1,0:T(8,128)S(1)} collective-permute-done((f32[520,128]{1,0:T(8,128)S(1)}, f32[520,128]{1,0:T(8,128)S(1)}, u32[]{:S(2)}, u32[]{:S(2)}) %collective-permute-start.3) | collective-permute-done | bytes 266272 | tf_op jit(solution)/shard_map/ppermute | solution.py:670
  29.8 0.8 %finish.1 = (f32[512,128]{1,0:T(8,128)}, f32[1]{0:T(128)}) custom-call(f32[520,128]{1,0:T(8,128)S(1)} %get-tuple-element.36.mine_ref, f32[520,128]{1,0:T(8,128)S(1)} %collective-permute-done.3.other_ref), custom_call_target="tpu_custom_call" | custom-call | tf_op jit(solution)/shard_map/finish/pallas_call | solution.py:671
Async XLA Ops:
  2.8 11.3 %collective-permute-start = (bf16[4,256,256]{2,1,0:T(8,128)(2,1)}, bf16[4,256,256]{2,1,0:T(8,128)(2,1)S(1)}, u32[]{:S(2)}, u32[]{:S(2)}) collective-permute-start(bf16[4,256,256]{2,1,0:T(8,128)(2,1)} %own_ref.1), channel_id=1, source_target_pairs={{0,1},{1,0},{2,3},{3,2},{4,5},{5,4},{6,7},{7,6},{8,9},{9,8},{10,11... | collective-permute-start | bytes 1572872 | tf_op jit(solution)/shard_map/ppermute | solution.py:514
  3.3 12.1 %all-to-all-start = ((f32[8,8,384]{2,1,0:T(8,128)}), f32[8,8,384]{2,1,0:T(8,128)S(1)}, u32[]{:S(2)}, u32[]{:S(2)}) async-start(f32[8,8,384]{2,1,0:T(8,128)} %pack.1), calls=%async_computation | async-start | bytes 196608 | tf_op jit(solution)/shard_map/all_to_all | solution.py:519
  13.2 0.8 %copy-start.1 = (bf16[2,256,512]{2,1,0:T(8,128)(2,1)}, bf16[2,256,512]{2,1,0:T(8,128)(2,1)S(1)}, u32[]{:S(2)}) copy-start(bf16[2,256,512]{2,1,0:T(8,128)(2,1)S(1)} %get-tuple-element.26.early) | copy-start | bytes 1572868
  15.4 6.2 %copy-start = (bf16[4,256,256]{2,1,0:T(8,128)(2,1)S(1)}, bf16[4,256,256]{2,1,0:T(8,128)(2,1)}, u32[]{:S(2)}) copy-start(bf16[4,256,256]{2,1,0:T(8,128)(2,1)} %own_ref.1) | copy-start | bytes 1572868
  15.4 6.2 %copy-start.2 = (bf16[2,256,512]{2,1,0:T(8,128)(2,1)S(1)}, bf16[2,256,512]{2,1,0:T(8,128)(2,1)}, u32[]{:S(2)}) copy-start(bf16[2,256,512]{2,1,0:T(8,128)(2,1)} %copy-done.1) | copy-start | bytes 1572868
  17.3 5.5 %collective-permute-start.2 = (bf16[256,256]{1,0:T(8,128)(2,1)S(1)}, bf16[256,256]{1,0:T(8,128)(2,1)S(1)}, u32[]{:S(2)}, u32[]{:S(2)}) collective-permute-start(bf16[256,256]{1,0:T(8,128)(2,1)S(1)} %get-tuple-element.32.refs_4_), channel_id=1, source_target_pairs={{0,2},{2,0},{1,3},{3,1},{4,6},{6,4},{5,7},{7,5},{8,10},{10,8},{9,1... | collective-permute-start | bytes 393224 | tf_op jit(solution)/shard_map/ppermute | solution.py:632
  20.1 5.5 %collective-permute-start.1 = (bf16[256,256]{1,0:T(8,128)(2,1)S(1)}, bf16[256,256]{1,0:T(8,128)(2,1)S(1)}, u32[]{:S(2)}, u32[]{:S(2)}) collective-permute-start(bf16[256,256]{1,0:T(8,128)(2,1)S(1)} %get-tuple-element.27.after_any.refs_4_), channel_id=1, source_target_pairs={{0,2},{2,0},{1,3},{3,1},{4,6},{6,4},{5,7},{7,5},{8,10},{10,8},{9,1... | collective-permute-start | bytes 393224 | tf_op jit(solution)/shard_map/ppermute | solution.py:632
  28.2 1.6 %collective-permute-start.3 = (f32[520,128]{1,0:T(8,128)S(1)}, f32[520,128]{1,0:T(8,128)S(1)}, u32[]{:S(2)}, u32[]{:S(2)}) collective-permute-start(f32[520,128]{1,0:T(8,128)S(1)} %get-tuple-element.37), channel_id=1, source_target_pairs={{0,1},{1,0},{2,3},{3,2},{4,5},{5,4},{6,7},{7,6},{8,9},{9,8},{10,11... | collective-permute-start | bytes 798728 | tf_op jit(solution)/shard_map/ppermute | solution.py:670

commit v26 on v25

--- a/solution.py
+++ b/solution.py
@@ -84,10 +84,17 @@
     ref[at, :states, states:] = (value - high.astype(F32)).astype(BF16)
 
 
+def split(x):
+    high = x.astype(BF16)
+    return high, (x - high.astype(F32)).astype(BF16)
+
+
 def both_halves(mat, state):
     states = mat.shape[0]
-    high = jnp.dot(mat[:, :states], state, preferred_element_type=F32)
-    return high + jnp.dot(mat[:, states:], state, preferred_element_type=F32)
+    high, low = split(state)
+    result = jnp.dot(mat[:, states:], high, preferred_element_type=F32)
+    result += jnp.dot(mat[:, :states], low, preferred_element_type=F32)
+    return result + jnp.dot(mat[:, :states], high, preferred_element_type=F32)
 
 
 def fill_periods(mat, turned_pass, lead, ref, begin, end):
@@ -174,7 +181,12 @@
 
 
 def outer_sum(weights_ref, carried):
-    return lax.dot_general(weights_ref[...], carried, (((1,), (1,)), ((), ())), preferred_element_type=F32)
+    def turned(x, y):
+        return lax.dot_general(x, y, (((1,), (1,)), ((), ())), preferred_element_type=F32)
+
+    high, low = split(weights_ref[...])
+    carried_high, carried_low = split(carried)
+    return turned(low, carried_high) + turned(high, carried_low) + turned(high, carried_high)
 
 
 def run_forward(lead, mat, hist, sel_ref, consts, ab_ref, logs, second=None, fresh=False, extend=True):
@@ -200,7 +212,7 @@
             if second is not None:
                 total = column_sum(moved * hist[k, :, cols].astype(F32))
                 weight = jnp.where(moving, 1.0 / total, 0.0)
-                weights_ref[:, cols] = (own_alpha[:, cols] * inverse[q] * weight).astype(BF16)
+                weights_ref[:, cols] = own_alpha[:, cols] * inverse[q] * weight
                 if k + 1 == steps and not extend:
                     continue
             emit = emission(sel_ref, consts, step_now, cols)
@@ -210,7 +222,7 @@
                 seen = is_seen(sel_ref, step_now, cols)
                 logs[q] = logs[q] + jnp.where(seen, jnp.log2(scale), 0.0)
             inverse[q] = 1.0 / scale
-            there[:, cols] = joint.astype(BF16)
+            there[:, cols] = joint
             last[q] = joint
         if second is not None:
             add_counts(k, outer_sum(weights_ref, hist[k]))
@@ -231,7 +243,7 @@
         for q, cols in enumerate(cuts):
             emit = emission(sel_ref, consts, step_now, cols, size[q] if second is None else None)
             carried = emit * state[q]
-            here[:, cols] = carried.astype(BF16)
+            here[:, cols] = carried
             whole = column_sum(carried)
             grown.append(whole)
             if second is None:
@@ -253,7 +265,7 @@
                 product = product * shrink
                 total = column_sum(product * hist[k, :, cols].astype(F32))
                 weight = jnp.where(moving, 1.0 / total, 0.0)
-                weights_ref[:, cols] = (own_alpha[:, cols] * weight * shrink).astype(BF16)
+                weights_ref[:, cols] = own_alpha[:, cols] * weight * shrink
                 if k > 1 or not at_edge:
                     state[q] = jnp.where(moving, product, rest[q])
         if second is not None:
@@ -287,7 +299,7 @@
 def put_state(state_out, values, logs, spread):
     for q, cols in enumerate(tiles(state_out.shape[1])):
         factor = jnp.exp2(logs[q] * (1.0 / spread)) / column_sum(values[q])
-        state_out[:, cols] = (values[q] * factor).astype(BF16)
+        state_out[:, cols] = values[q] * factor
 
 
 def state_sums(state_ref):
@@ -364,7 +376,7 @@
             hist[0] = state_in[...]
         else:
             for cols in cuts:
-                hist[0, :, cols] = consts[0].astype(BF16)
+                hist[0, :, cols] = consts[0]
         logs = state_logs(state_sums(state_in), half_periods) if resume else list(zeros)
         fresh = lax.axis_size("per") == 2
         last = run_forward(lead, mat, hist, sel_ref, consts, ab_ref, logs, fresh=fresh)
@@ -570,8 +582,8 @@
         return pl.BlockSpec(lead + (width,), lambda g: (0,) * len(lead) + (g,))
 
     grid = (grids,) if grids > 1 else ()
-    hist_shape = shaped((steps, states, share), BF16)
-    state_shape = shaped((states, share), BF16)
+    hist_shape = shaped((steps, states, share), F32)
+    state_shape = shaped((states, share), F32)
     laid = (steps if sides == 2 else periods) + 1
     sel_shape = shaped((3, laid, 8, share), F32)
     swap_shape = shaped((steps * rows + 8, LANES), F32)
@@ -589,8 +601,8 @@
             in_specs=[whole(*gathered.shape), whole(*first_mat.shape), const_spec]
             + [state_spec] * resume,
             out_specs=[hist_spec, state_spec, sel_spec],
-            scratch_shapes=[pltpu.VMEM((states, width), BF16)],
-            compiler_params=params(8 if grids == 1 else 32),
+            scratch_shapes=[pltpu.VMEM((states, width), F32)],
+            compiler_params=params(16 if grids == 1 else 40),
             name="first_pass",
         )(gathered, first_mat, consts, *([state_in] if resume else []))
 
@@ -598,8 +610,8 @@
         hist, own_state, sel = kept
         resume = sums_in is not None
         scratch = [
-            pltpu.VMEM((states, width), BF16),
-            pltpu.VMEM((rows, width), BF16),
+            pltpu.VMEM((states, width), F32),
+            pltpu.VMEM((rows, width), F32),
         ]
         counts_spec, sums_spec = whole(*counts_shape.shape), whole(*sums_shape.shape)
         if last:
@@ -619,7 +631,7 @@
             + [whole(*row_probs.shape)] * last,
             out_specs=out_specs,
             scratch_shapes=scratch,
-            compiler_params=params(8 if grids == 1 else 32),
+            compiler_params=params(16 if grids == 1 else 40),
             name="second_pass",
         )(
             sel, second_mat, consts, hist, own_state, state_in,

time: 31 us -> 37.8 us (1.22)
  waiting for transfers between devices: 2.23 us -> 6.3 us
  Pallas kernels: 15.4 us -> 18 us
    ppermute x2, waiting for transfers between devices: 0.01 us -> 4.09 us  [hand_over(): return lax.ppermute(state, 'per', moves)]
    pallas_call x2, Pallas kernels: 5.34 us -> 7.23 us  [second_pass(): pl.pallas_call(functools.partial(second_kernel, resume, last, extend, gri...]
    pallas_call x2, Pallas kernels: 3.83 us -> 4.58 us  [first_pass(): pl.pallas_call(functools.partial(first_kernel, resume, grids, index), gri...]
  transfers between devices with their start and end apart: 5 -> 5, of which waited for: 2 -> 4; matrix products, arithmetic and copies ran while one was open for 0% -> 0% of each run, Pallas kernels for 28% -> 26%
where the time goes in v26:
time: 37.8 us; the launch traced here: 37.5 us
  Pallas kernels  18 us (48%)
  starting transfers between devices  10.9 us (29%)
  waiting for transfers between devices  6.3 us (17%)
  between operations  1.54 us (4%)
  local copies, waits for them, and re-layouts  0.79 us (2%)
    all_to_all x1, starting transfers between devices, per_device(): lax.all_to_all(packed, ('hh', 'per', 'st'), split_axis=0, concat_axis=0,...  7.84 us
    pallas_call x2, Pallas kernels, second_pass(): pl.pallas_call(functools.partial(second_kernel, resume, last, extend, gri...  7.23 us
    pallas_call x2, Pallas kernels, first_pass(): pl.pallas_call(functools.partial(first_kernel, resume, grids, index), gri...  4.58 us
    ppermute x2, waiting for transfers between devices, hand_over(): return lax.ppermute(state, 'per', moves)  4.09 us
    ppermute x2, starting transfers between devices, hand_over(): return lax.ppermute(state, 'per', moves)  2.45 us
    pallas_call x1, Pallas kernels, per_device(): pl.pallas_call(prep_own_kernel, out_shape=[pltpu.VMEM(mat_shape.shape, BF...  2.1 us
    ppermute x1, waiting for transfers between devices, per_device(): received = lax.ppermute(other, 'st', swap)  1.53 us
    pallas_call x1, Pallas kernels, per_device(): pl.pallas_call(pack_kernel, out_shape=pltpu.VMEM((group, periods // 2, sl...  1.49 us
  transfers between devices with their start and end apart: 5, of which 4 were waited for; matrix products, arithmetic and copies ran while one was open for 0% of the time, Pallas kernels for 26%

profile of v26, /device:TPU:0, one launch (start us, length us, event | category | flops | bytes accessed | tf_op | source)
XLA Modules:
  0.0 37.5 jit_solution(15133121085443834878)
XLA Ops:
  1.3 1.5 %pack.1 = f32[8,8,384]{2,1,0:T(8,128)} custom-call(s32[1]{0:T(128)S(6)} %copy.12.count_ref, f32[16,384]{1,0:T(8,128)} %bitcast.7, s32[3,128]{1,0:T(4,128)} %bitcast.8, s32[3,128]{1,0:T(4,128)} %bitcast.9), custom_call_target="tpu_custom_call" | custom-call | tf_op jit(solution)/shard_map/pack/pallas_call | solution.py:516
  2.8 0.5 %collective-permute-start = (bf16[4,256,256]{2,1,0:T(8,128)(2,1)}, bf16[4,256,256]{2,1,0:T(8,128)(2,1)S(1)}, u32[]{:S(2)}, u32[]{:S(2)}) collective-permute-start(bf16[4,256,256]{2,1,0:T(8,128)(2,1)} %own_ref.1), channel_id=1, source_target_pairs={{0,1},{1,0},{2,3},{3,2},{4,5},{5,4},{6,7},{7,6},{8,9},{9,8},{10,11... | collective-permute-start | bytes 1572872 | tf_op jit(solution)/shard_map/ppermute | solution.py:526
  3.3 7.8 %all-to-all-start = ((f32[8,8,384]{2,1,0:T(8,128)}), f32[8,8,384]{2,1,0:T(8,128)S(1)}, u32[]{:S(2)}, u32[]{:S(2)}) async-start(f32[8,8,384]{2,1,0:T(8,128)} %pack.1), calls=%async_computation | async-start | bytes 196608 | tf_op jit(solution)/shard_map/all_to_all | solution.py:531
  11.1 2.1 %prep_own.1 = (bf16[8,256,512]{2,1,0:T(8,128)(2,1)S(1)}, f32[4,256,128]{2,1,0:T(8,128)S(1)}, bf16[2,256,512]{2,1,0:T(8,128)(2,1)S(1)}) custom-call(bf16[4,256,256]{2,1,0:T(8,128)(2,1)} %own_ref.1, f32[1,256]{1,0:T(1,128)} %bitcast.10, f32[1,256]{1,0:T(1,128)} %bitcast.11, f32[1,256]{1,0:T(1,128)} %bitcast.12), custom_call_target="tpu_custom_call" | custom-call | tf_op jit(solution)/shard_map/prep_own/pallas_call | solution.py:536
  13.2 0.0 copy-start.1
  13.3 0.8 %copy-done.1 = bf16[2,256,512]{2,1,0:T(8,128)(2,1)} copy-done((bf16[2,256,512]{2,1,0:T(8,128)(2,1)}, bf16[2,256,512]{2,1,0:T(8,128)(2,1)S(1)}, u32[]{:S(2)}) %copy-start.1) | copy-done | bytes 524312
  14.0 0.0 collective-permute-done.other_ref
  14.0 0.7 %prep_other.1.mat = bf16[8,256,512]{2,1,0:T(8,128)(2,1)S(1)} custom-call(bf16[4,256,256]{2,1,0:T(8,128)(2,1)S(1)} %collective-permute-done.other_ref, bf16[8,256,512]{2,1,0:T(8,128)(2,1)S(1)} %get-tuple-element.23.mat_in), custom_call_target="tpu_custom_call", output_to_operand_aliasing={{}: (1, {})} | custom-call | tf_op jit(solution)/shard_map/prep_other/pallas_call | solution.py:554
  14.7 0.7 %all-to-all-done.rows_ref = f32[8,8,384]{2,1,0:T(8,128)S(1)} async-done(((f32[8,8,384]{2,1,0:T(8,128)}), f32[8,8,384]{2,1,0:T(8,128)S(1)}, u32[]{:S(2)}, u32[]{:S(2)}) %all-to-all-start) | async-done | bytes 98336 | tf_op jit(solution)/shard_map/all_to_all | solution.py:531
  15.4 0.0 copy-start
  15.4 0.0 copy-start.2
  15.4 2.3 %first_pass.3 = (f32[8,256,256]{2,1,0:T(8,128)S(1)}, f32[256,256]{1,0:T(8,128)S(1)}, f32[3,9,8,256]{3,2,1,0:T(8,128)S(1)}) custom-call(f32[8,8,384]{2,1,0:T(8,128)S(1)} %all-to-all-done.rows_ref, bf16[8,256,512]{2,1,0:T(8,128)(2,1)S(1)} %prep_other.1.mat, f32[4,256,128]{2,1,0:T(8,128)S(1)} %get-tuple-element.24.consts.refs_2_), custom_call_target="tpu_custom_call" | custom-call | tf_op jit(solution)/shard_map/first_pass/pallas_call | solution.py:597
  17.7 0.9 %collective-permute-start.2 = (f32[256,256]{1,0:T(8,128)S(1)}, f32[256,256]{1,0:T(8,128)S(1)}, u32[]{:S(2)}, u32[]{:S(2)}) collective-permute-start(f32[256,256]{1,0:T(8,128)S(1)} %get-tuple-element.32.refs_4_), channel_id=1, source_target_pairs={{0,2},{2,0},{1,3},{3,1},{4,6},{6,4},{5,7},{7,5},{8,10},{10,8},{9,1... | collective-permute-start | bytes 786440 | tf_op jit(solution)/shard_map/ppermute | solution.py:644
  18.6 2.3 %first_pass.2 = (f32[8,256,256]{2,1,0:T(8,128)S(1)}, f32[256,256]{1,0:T(8,128)S(1)}, f32[3,9,8,256]{3,2,1,0:T(8,128)S(1)}) custom-call(f32[8,8,384]{2,1,0:T(8,128)S(1)} %all-to-all-done.rows_ref, bf16[8,256,512]{2,1,0:T(8,128)(2,1)S(1)} %prep_other.1.mat, f32[4,256,128]{2,1,0:T(8,128)S(1)} %get-tuple-element.24.consts.refs_2_), custom_call_target="tpu_custom_call" | custom-call | tf_op jit(solution)/shard_map/first_pass/pallas_call | solution.py:597
  20.9 1.5 %collective-permute-start.1 = (f32[256,256]{1,0:T(8,128)S(1)}, f32[256,256]{1,0:T(8,128)S(1)}, u32[]{:S(2)}, u32[]{:S(2)}) collective-permute-start(f32[256,256]{1,0:T(8,128)S(1)} %get-tuple-element.27.after_any.refs_4_), channel_id=1, source_target_pairs={{0,2},{2,0},{1,3},{3,1},{4,6},{6,4},{5,7},{7,5},{8,10},{10,8},{9,1... | collective-permute-start | bytes 786440 | tf_op jit(solution)/shard_map/ppermute | solution.py:644
  22.5 0.0 copy-done
  22.5 0.0 copy-done.2
  22.5 1.2 %prep_second.1 = (bf16[8,256,512]{2,1,0:T(8,128)(2,1)S(1)}, f32[8,64,256]{2,1,0:T(8,128)S(1)}) custom-call(bf16[4,256,256]{2,1,0:T(8,128)(2,1)S(1)} %copy-done, bf16[4,256,256]{2,1,0:T(8,128)(2,1)S(1)} %collective-permute-done.other_ref, bf16[2,256,512]{2,1,0:T(8,128)(2,1)S(1)} %copy-done.2, f32[256,256]{1,0:T(8,128)S(1)} %get-tuple-element.27.after_any.refs_4_), custom_call_target="tpu_custom_call" | custom-call | tf_op jit(solution)/shard_map/prep_second/pallas_call | solution.py:565
  23.6 3.4 %collective-permute-done.2.refs_5_ = f32[256,256]{1,0:T(8,128)S(1)} collective-permute-done((f32[256,256]{1,0:T(8,128)S(1)}, f32[256,256]{1,0:T(8,128)S(1)}, u32[]{:S(2)}, u32[]{:S(2)}) %collective-permute-start.2) | collective-permute-done | bytes 262176 | tf_op jit(solution)/shard_map/ppermute | solution.py:644
  27.0 3.6 %second_pass.2 = (f32[8,64,256]{2,1,0:T(8,128)S(1)}, f32[8,128]{1,0:T(8,128)S(1)}) custom-call(f32[3,9,8,256]{3,2,1,0:T(8,128)S(1)} %get-tuple-element.30.refs_0_, bf16[8,256,512]{2,1,0:T(8,128)(2,1)S(1)} %get-tuple-element.28.refs_1_, f32[4,256,128]{2,1,0:T(8,128)S(1)} %get-tuple-element.24.consts.refs_2_, f32[8,256,256]{2,1,0:T(8,128)S(1)} %get-tuple-element.31.refs_3_, ...), custom_call_target="tpu_custom_call" | custom-call | tf_op jit(solution)/shard_map/second_pass/pallas_call | solution.py:625
  30.6 0.7 %collective-permute-done.1.refs_5_ = f32[256,256]{1,0:T(8,128)S(1)} collective-permute-done((f32[256,256]{1,0:T(8,128)S(1)}, f32[256,256]{1,0:T(8,128)S(1)}, u32[]{:S(2)}, u32[]{:S(2)}) %collective-permute-start.1) | collective-permute-done | bytes 262176 | tf_op jit(solution)/shard_map/ppermute | solution.py:644
  31.3 3.6 %second_pass.3 = (f32[520,128]{1,0:T(8,128)S(1)}, f32[520,128]{1,0:T(8,128)S(1)}) custom-call(f32[3,9,8,256]{3,2,1,0:T(8,128)S(1)} %get-tuple-element.25.refs_0_, bf16[8,256,512]{2,1,0:T(8,128)(2,1)S(1)} %get-tuple-element.28.refs_1_, f32[4,256,128]{2,1,0:T(8,128)S(1)} %get-tuple-element.24.consts.refs_2_, f32[8,256,256]{2,1,0:T(8,128)S(1)} %get-tuple-element.29.refs_3_, ...), custom_call_target="tpu_custom_call" | custom-call | tf_op jit(solution)/shard_map/second_pass/pallas_call | solution.py:625
  35.0 0.1 collective-permute-start.3
  35.0 1.5 %collective-permute-done.3.other_ref = f32[520,128]{1,0:T(8,128)S(1)} collective-permute-done((f32[520,128]{1,0:T(8,128)S(1)}, f32[520,128]{1,0:T(8,128)S(1)}, u32[]{:S(2)}, u32[]{:S(2)}) %collective-permute-start.3) | collective-permute-done | bytes 266272 | tf_op jit(solution)/shard_map/ppermute | solution.py:682
  36.6 0.8 %finish.1 = (f32[512,128]{1,0:T(8,128)}, f32[1]{0:T(128)}) custom-call(f32[520,128]{1,0:T(8,128)S(1)} %get-tuple-element.36.mine_ref, f32[520,128]{1,0:T(8,128)S(1)} %collective-permute-done.3.other_ref), custom_call_target="tpu_custom_call" | custom-call | tf_op jit(solution)/shard_map/finish/pallas_call | solution.py:683
Async XLA Ops:
  2.8 11.3 %collective-permute-start = (bf16[4,256,256]{2,1,0:T(8,128)(2,1)}, bf16[4,256,256]{2,1,0:T(8,128)(2,1)S(1)}, u32[]{:S(2)}, u32[]{:S(2)}) collective-permute-start(bf16[4,256,256]{2,1,0:T(8,128)(2,1)} %own_ref.1), channel_id=1, source_target_pairs={{0,1},{1,0},{2,3},{3,2},{4,5},{5,4},{6,7},{7,6},{8,9},{9,8},{10,11... | collective-permute-start | bytes 1572872 | tf_op jit(solution)/shard_map/ppermute | solution.py:526
  3.3 12.1 %all-to-all-start = ((f32[8,8,384]{2,1,0:T(8,128)}), f32[8,8,384]{2,1,0:T(8,128)S(1)}, u32[]{:S(2)}, u32[]{:S(2)}) async-start(f32[8,8,384]{2,1,0:T(8,128)} %pack.1), calls=%async_computation | async-start | bytes 196608 | tf_op jit(solution)/shard_map/all_to_all | solution.py:531
  13.2 0.8 %copy-start.1 = (bf16[2,256,512]{2,1,0:T(8,128)(2,1)}, bf16[2,256,512]{2,1,0:T(8,128)(2,1)S(1)}, u32[]{:S(2)}) copy-start(bf16[2,256,512]{2,1,0:T(8,128)(2,1)S(1)} %get-tuple-element.26.early) | copy-start | bytes 1572868
  15.4 7.1 %copy-start = (bf16[4,256,256]{2,1,0:T(8,128)(2,1)S(1)}, bf16[4,256,256]{2,1,0:T(8,128)(2,1)}, u32[]{:S(2)}) copy-start(bf16[4,256,256]{2,1,0:T(8,128)(2,1)} %own_ref.1) | copy-start | bytes 1572868
  15.4 7.1 %copy-start.2 = (bf16[2,256,512]{2,1,0:T(8,128)(2,1)S(1)}, bf16[2,256,512]{2,1,0:T(8,128)(2,1)}, u32[]{:S(2)}) copy-start(bf16[2,256,512]{2,1,0:T(8,128)(2,1)} %copy-done.1) | copy-start | bytes 1572868
  17.7 9.3 %collective-permute-start.2 = (f32[256,256]{1,0:T(8,128)S(1)}, f32[256,256]{1,0:T(8,128)S(1)}, u32[]{:S(2)}, u32[]{:S(2)}) collective-permute-start(f32[256,256]{1,0:T(8,128)S(1)} %get-tuple-element.32.refs_4_), channel_id=1, source_target_pairs={{0,2},{2,0},{1,3},{3,1},{4,6},{6,4},{5,7},{7,5},{8,10},{10,8},{9,1... | collective-permute-start | bytes 786440 | tf_op jit(solution)/shard_map/ppermute | solution.py:644
  20.9 10.4 %collective-permute-start.1 = (f32[256,256]{1,0:T(8,128)S(1)}, f32[256,256]{1,0:T(8,128)S(1)}, u32[]{:S(2)}, u32[]{:S(2)}) collective-permute-start(f32[256,256]{1,0:T(8,128)S(1)} %get-tuple-element.27.after_any.refs_4_), channel_id=1, source_target_pairs={{0,2},{2,0},{1,3},{3,1},{4,6},{6,4},{5,7},{7,5},{8,10},{10,8},{9,1... | collective-permute-start | bytes 786440 | tf_op jit(solution)/shard_map/ppermute | solution.py:644
  35.0 1.6 %collective-permute-start.3 = (f32[520,128]{1,0:T(8,128)S(1)}, f32[520,128]{1,0:T(8,128)S(1)}, u32[]{:S(2)}, u32[]{:S(2)}) collective-permute-start(f32[520,128]{1,0:T(8,128)S(1)} %get-tuple-element.37), channel_id=1, source_target_pairs={{0,1},{1,0},{2,3},{3,2},{4,5},{5,4},{6,7},{7,6},{8,9},{9,8},{10,11... | collective-permute-start | bytes 798728 | tf_op jit(solution)/shard_map/ppermute | solution.py:682

commit v27 on v26

--- a/solution.py
+++ b/solution.py
@@ -299,7 +299,7 @@
 def put_state(state_out, values, logs, spread):
     for q, cols in enumerate(tiles(state_out.shape[1])):
         factor = jnp.exp2(logs[q] * (1.0 / spread)) / column_sum(values[q])
-        state_out[:, cols] = values[q] * factor
+        state_out[:, cols] = (values[q] * factor).astype(BF16)
 
 
 def state_sums(state_ref):
@@ -373,7 +373,7 @@
         if local:
             lay_out((0,))
         if resume:
-            hist[0] = state_in[...]
+            hist[0] = state_in[...].astype(F32)
         else:
             for cols in cuts:
                 hist[0, :, cols] = consts[0]
@@ -459,7 +459,7 @@
 
     @pl.when(jnp.logical_not(forward_first))
     def _():
-        ab_ref[...] = state_in[...]
+        ab_ref[...] = state_in[...].astype(F32)
         values = run_forward(lead, mat, hist, sel_ref, consts, ab_ref, list(zeros), second, extend=extend)
         add_sums(state_in, own_state)
         if extend:
@@ -583,7 +583,7 @@
 
     grid = (grids,) if grids > 1 else ()
     hist_shape = shaped((steps, states, share), F32)
-    state_shape = shaped((states, share), F32)
+    state_shape = shaped((states, share), BF16)
     laid = (steps if sides == 2 else periods) + 1
     sel_shape = shaped((3, laid, 8, share), F32)
     swap_shape = shaped((steps * rows + 8, LANES), F32)

time: 37.8 us -> 34.2 us (0.905)
  waiting for transfers between devices: 6.3 us -> 2.22 us
  Pallas kernels: 18 us -> 18.5 us
    ppermute x2, waiting for transfers between devices: 4.09 us -> 0.01 us  [hand_over(): return lax.ppermute(state, 'per', moves)]
    pallas_call x2, Pallas kernels: 7.23 us -> 7.7 us  [second_pass(): pl.pallas_call(functools.partial(second_kernel, resume, last, extend, gri...]
  transfers between devices with their start and end apart: 5 -> 5, of which waited for: 4 -> 2; matrix products, arithmetic and copies ran while one was open for 0% -> 0% of each run, Pallas kernels for 26% -> 29%
where the time goes in v27:
time: 34.2 us; the launch traced here: 33.9 us
  Pallas kernels  18.5 us (54%)
  starting transfers between devices  10.9 us (32%)
  waiting for transfers between devices  2.22 us (6%)
  between operations  1.54 us (5%)
  local copies, waits for them, and re-layouts  0.79 us (2%)
    all_to_all x1, starting transfers between devices, per_device(): lax.all_to_all(packed, ('hh', 'per', 'st'), split_axis=0, concat_axis=0,...  7.84 us
    pallas_call x2, Pallas kernels, second_pass(): pl.pallas_call(functools.partial(second_kernel, resume, last, extend, gri...  7.7 us
    pallas_call x2, Pallas kernels, first_pass(): pl.pallas_call(functools.partial(first_kernel, resume, grids, index), gri...  4.58 us
    ppermute x2, starting transfers between devices, hand_over(): return lax.ppermute(state, 'per', moves)  2.44 us
    pallas_call x1, Pallas kernels, per_device(): pl.pallas_call(prep_own_kernel, out_shape=[pltpu.VMEM(mat_shape.shape, BF...  2.1 us
    ppermute x1, waiting for transfers between devices, per_device(): received = lax.ppermute(other, 'st', swap)  1.53 us
    pallas_call x1, Pallas kernels, per_device(): pl.pallas_call(pack_kernel, out_shape=pltpu.VMEM((group, periods // 2, sl...  1.49 us
    pallas_call x1, Pallas kernels, prep_second(): pl.pallas_call(prep_second_kernel, out_shape=[mat_shape, shaped((steps, r...  1.17 us
  transfers between devices with their start and end apart: 5, of which 2 were waited for; matrix products, arithmetic and copies ran while one was open for 0% of the time, Pallas kernels for 29%

profile of v27, /device:TPU:0, one launch (start us, length us, event | category | flops | bytes accessed | tf_op | source)
XLA Modules:
  0.0 33.9 jit_solution(4849767978210639282)
XLA Ops:
  1.3 1.5 %pack.1 = f32[8,8,384]{2,1,0:T(8,128)} custom-call(s32[1]{0:T(128)S(6)} %copy.12.count_ref, f32[16,384]{1,0:T(8,128)} %bitcast.7, s32[3,128]{1,0:T(4,128)} %bitcast.8, s32[3,128]{1,0:T(4,128)} %bitcast.9), custom_call_target="tpu_custom_call" | custom-call | tf_op jit(solution)/shard_map/pack/pallas_call | solution.py:516
  2.8 0.5 %collective-permute-start = (bf16[4,256,256]{2,1,0:T(8,128)(2,1)}, bf16[4,256,256]{2,1,0:T(8,128)(2,1)S(1)}, u32[]{:S(2)}, u32[]{:S(2)}) collective-permute-start(bf16[4,256,256]{2,1,0:T(8,128)(2,1)} %own_ref.1), channel_id=1, source_target_pairs={{0,1},{1,0},{2,3},{3,2},{4,5},{5,4},{6,7},{7,6},{8,9},{9,8},{10,11... | collective-permute-start | bytes 1572872 | tf_op jit(solution)/shard_map/ppermute | solution.py:526
  3.3 7.8 %all-to-all-start = ((f32[8,8,384]{2,1,0:T(8,128)}), f32[8,8,384]{2,1,0:T(8,128)S(1)}, u32[]{:S(2)}, u32[]{:S(2)}) async-start(f32[8,8,384]{2,1,0:T(8,128)} %pack.1), calls=%async_computation | async-start | bytes 196608 | tf_op jit(solution)/shard_map/all_to_all | solution.py:531
  11.1 2.1 %prep_own.1 = (bf16[8,256,512]{2,1,0:T(8,128)(2,1)S(1)}, f32[4,256,128]{2,1,0:T(8,128)S(1)}, bf16[2,256,512]{2,1,0:T(8,128)(2,1)S(1)}) custom-call(bf16[4,256,256]{2,1,0:T(8,128)(2,1)} %own_ref.1, f32[1,256]{1,0:T(1,128)} %bitcast.10, f32[1,256]{1,0:T(1,128)} %bitcast.11, f32[1,256]{1,0:T(1,128)} %bitcast.12), custom_call_target="tpu_custom_call" | custom-call | tf_op jit(solution)/shard_map/prep_own/pallas_call | solution.py:536
  13.2 0.0 copy-start.1
  13.3 0.8 %copy-done.1 = bf16[2,256,512]{2,1,0:T(8,128)(2,1)} copy-done((bf16[2,256,512]{2,1,0:T(8,128)(2,1)}, bf16[2,256,512]{2,1,0:T(8,128)(2,1)S(1)}, u32[]{:S(2)}) %copy-start.1) | copy-done | bytes 524312
  14.0 0.0 collective-permute-done.other_ref
  14.0 0.7 %prep_other.1.mat = bf16[8,256,512]{2,1,0:T(8,128)(2,1)S(1)} custom-call(bf16[4,256,256]{2,1,0:T(8,128)(2,1)S(1)} %collective-permute-done.other_ref, bf16[8,256,512]{2,1,0:T(8,128)(2,1)S(1)} %get-tuple-element.23.mat_in), custom_call_target="tpu_custom_call", output_to_operand_aliasing={{}: (1, {})} | custom-call | tf_op jit(solution)/shard_map/prep_other/pallas_call | solution.py:554
  14.7 0.7 %all-to-all-done.rows_ref = f32[8,8,384]{2,1,0:T(8,128)S(1)} async-done(((f32[8,8,384]{2,1,0:T(8,128)}), f32[8,8,384]{2,1,0:T(8,128)S(1)}, u32[]{:S(2)}, u32[]{:S(2)}) %all-to-all-start) | async-done | bytes 98336 | tf_op jit(solution)/shard_map/all_to_all | solution.py:531
  15.4 0.0 copy-start
  15.4 0.0 copy-start.2
  15.4 2.3 %first_pass.3 = (f32[8,256,256]{2,1,0:T(8,128)S(1)}, bf16[256,256]{1,0:T(8,128)(2,1)S(1)}, f32[3,9,8,256]{3,2,1,0:T(8,128)S(1)}) custom-call(f32[8,8,384]{2,1,0:T(8,128)S(1)} %all-to-all-done.rows_ref, bf16[8,256,512]{2,1,0:T(8,128)(2,1)S(1)} %prep_other.1.mat, f32[4,256,128]{2,1,0:T(8,128)S(1)} %get-tuple-element.24.consts.refs_2_), custom_call_target="tpu_custom_call" | custom-call | tf_op jit(solution)/shard_map/first_pass/pallas_call | solution.py:597
  17.7 0.9 %collective-permute-start.2 = (bf16[256,256]{1,0:T(8,128)(2,1)S(1)}, bf16[256,256]{1,0:T(8,128)(2,1)S(1)}, u32[]{:S(2)}, u32[]{:S(2)}) collective-permute-start(bf16[256,256]{1,0:T(8,128)(2,1)S(1)} %get-tuple-element.32.refs_4_), channel_id=1, source_target_pairs={{0,2},{2,0},{1,3},{3,1},{4,6},{6,4},{5,7},{7,5},{8,10},{10,8},{9,1... | collective-permute-start | bytes 393224 | tf_op jit(solution)/shard_map/ppermute | solution.py:644
  18.6 2.3 %first_pass.2 = (f32[8,256,256]{2,1,0:T(8,128)S(1)}, bf16[256,256]{1,0:T(8,128)(2,1)S(1)}, f32[3,9,8,256]{3,2,1,0:T(8,128)S(1)}) custom-call(f32[8,8,384]{2,1,0:T(8,128)S(1)} %all-to-all-done.rows_ref, bf16[8,256,512]{2,1,0:T(8,128)(2,1)S(1)} %prep_other.1.mat, f32[4,256,128]{2,1,0:T(8,128)S(1)} %get-tuple-element.24.consts.refs_2_), custom_call_target="tpu_custom_call" | custom-call | tf_op jit(solution)/shard_map/first_pass/pallas_call | solution.py:597
  20.9 1.5 %collective-permute-start.1 = (bf16[256,256]{1,0:T(8,128)(2,1)S(1)}, bf16[256,256]{1,0:T(8,128)(2,1)S(1)}, u32[]{:S(2)}, u32[]{:S(2)}) collective-permute-start(bf16[256,256]{1,0:T(8,128)(2,1)S(1)} %get-tuple-element.27.after_any.refs_4_), channel_id=1, source_target_pairs={{0,2},{2,0},{1,3},{3,1},{4,6},{6,4},{5,7},{7,5},{8,10},{10,8},{9,1... | collective-permute-start | bytes 393224 | tf_op jit(solution)/shard_map/ppermute | solution.py:644
  22.5 0.0 copy-done
  22.5 0.0 copy-done.2
  22.5 1.2 %prep_second.1 = (bf16[8,256,512]{2,1,0:T(8,128)(2,1)S(1)}, f32[8,64,256]{2,1,0:T(8,128)S(1)}) custom-call(bf16[4,256,256]{2,1,0:T(8,128)(2,1)S(1)} %copy-done, bf16[4,256,256]{2,1,0:T(8,128)(2,1)S(1)} %collective-permute-done.other_ref, bf16[2,256,512]{2,1,0:T(8,128)(2,1)S(1)} %copy-done.2, bf16[256,256]{1,0:T(8,128)(2,1)S(1)} %get-tuple-element.27.after_any.refs_4_), custom_call_target="tpu_custom_call" | custom-call | tf_op jit(solution)/shard_map/prep_second/pallas_call | solution.py:565
  23.6 0.0 collective-permute-done.2.refs_5_
  23.6 3.7 %second_pass.2 = (f32[8,64,256]{2,1,0:T(8,128)S(1)}, f32[8,128]{1,0:T(8,128)S(1)}) custom-call(f32[3,9,8,256]{3,2,1,0:T(8,128)S(1)} %get-tuple-element.30.refs_0_, bf16[8,256,512]{2,1,0:T(8,128)(2,1)S(1)} %get-tuple-element.28.refs_1_, f32[4,256,128]{2,1,0:T(8,128)S(1)} %get-tuple-element.24.consts.refs_2_, f32[8,256,256]{2,1,0:T(8,128)S(1)} %get-tuple-element.31.refs_3_, ...), custom_call_target="tpu_custom_call" | custom-call | tf_op jit(solution)/shard_map/second_pass/pallas_call | solution.py:625
  27.4 0.0 collective-permute-done.1.refs_5_
  27.4 4.0 %second_pass.3 = (f32[520,128]{1,0:T(8,128)S(1)}, f32[520,128]{1,0:T(8,128)S(1)}) custom-call(f32[3,9,8,256]{3,2,1,0:T(8,128)S(1)} %get-tuple-element.25.refs_0_, bf16[8,256,512]{2,1,0:T(8,128)(2,1)S(1)} %get-tuple-element.28.refs_1_, f32[4,256,128]{2,1,0:T(8,128)S(1)} %get-tuple-element.24.consts.refs_2_, f32[8,256,256]{2,1,0:T(8,128)S(1)} %get-tuple-element.29.refs_3_, ...), custom_call_target="tpu_custom_call" | custom-call | tf_op jit(solution)/shard_map/second_pass/pallas_call | solution.py:625
  31.4 0.1 collective-permute-start.3
  31.4 1.5 %collective-permute-done.3.other_ref = f32[520,128]{1,0:T(8,128)S(1)} collective-permute-done((f32[520,128]{1,0:T(8,128)S(1)}, f32[520,128]{1,0:T(8,128)S(1)}, u32[]{:S(2)}, u32[]{:S(2)}) %collective-permute-start.3) | collective-permute-done | bytes 266272 | tf_op jit(solution)/shard_map/ppermute | solution.py:682
  33.0 0.8 %finish.1 = (f32[512,128]{1,0:T(8,128)}, f32[1]{0:T(128)}) custom-call(f32[520,128]{1,0:T(8,128)S(1)} %get-tuple-element.36.mine_ref, f32[520,128]{1,0:T(8,128)S(1)} %collective-permute-done.3.other_ref), custom_call_target="tpu_custom_call" | custom-call | tf_op jit(solution)/shard_map/finish/pallas_call | solution.py:683
Async XLA Ops:
  2.8 11.3 %collective-permute-start = (bf16[4,256,256]{2,1,0:T(8,128)(2,1)}, bf16[4,256,256]{2,1,0:T(8,128)(2,1)S(1)}, u32[]{:S(2)}, u32[]{:S(2)}) collective-permute-start(bf16[4,256,256]{2,1,0:T(8,128)(2,1)} %own_ref.1), channel_id=1, source_target_pairs={{0,1},{1,0},{2,3},{3,2},{4,5},{5,4},{6,7},{7,6},{8,9},{9,8},{10,11... | collective-permute-start | bytes 1572872 | tf_op jit(solution)/shard_map/ppermute | solution.py:526
  3.3 12.1 %all-to-all-start = ((f32[8,8,384]{2,1,0:T(8,128)}), f32[8,8,384]{2,1,0:T(8,128)S(1)}, u32[]{:S(2)}, u32[]{:S(2)}) async-start(f32[8,8,384]{2,1,0:T(8,128)} %pack.1), calls=%async_computation | async-start | bytes 196608 | tf_op jit(solution)/shard_map/all_to_all | solution.py:531
  13.2 0.8 %copy-start.1 = (bf16[2,256,512]{2,1,0:T(8,128)(2,1)}, bf16[2,256,512]{2,1,0:T(8,128)(2,1)S(1)}, u32[]{:S(2)}) copy-start(bf16[2,256,512]{2,1,0:T(8,128)(2,1)S(1)} %get-tuple-element.26.early) | copy-start | bytes 1572868
  15.4 7.0 %copy-start = (bf16[4,256,256]{2,1,0:T(8,128)(2,1)S(1)}, bf16[4,256,256]{2,1,0:T(8,128)(2,1)}, u32[]{:S(2)}) copy-start(bf16[4,256,256]{2,1,0:T(8,128)(2,1)} %own_ref.1) | copy-start | bytes 1572868
  15.4 7.0 %copy-start.2 = (bf16[2,256,512]{2,1,0:T(8,128)(2,1)S(1)}, bf16[2,256,512]{2,1,0:T(8,128)(2,1)}, u32[]{:S(2)}) copy-start(bf16[2,256,512]{2,1,0:T(8,128)(2,1)} %copy-done.1) | copy-start | bytes 1572868
  17.7 5.9 %collective-permute-start.2 = (bf16[256,256]{1,0:T(8,128)(2,1)S(1)}, bf16[256,256]{1,0:T(8,128)(2,1)S(1)}, u32[]{:S(2)}, u32[]{:S(2)}) collective-permute-start(bf16[256,256]{1,0:T(8,128)(2,1)S(1)} %get-tuple-element.32.refs_4_), channel_id=1, source_target_pairs={{0,2},{2,0},{1,3},{3,1},{4,6},{6,4},{5,7},{7,5},{8,10},{10,8},{9,1... | collective-permute-start | bytes 393224 | tf_op jit(solution)/shard_map/ppermute | solution.py:644
  20.9 6.5 %collective-permute-start.1 = (bf16[256,256]{1,0:T(8,128)(2,1)S(1)}, bf16[256,256]{1,0:T(8,128)(2,1)S(1)}, u32[]{:S(2)}, u32[]{:S(2)}) collective-permute-start(bf16[256,256]{1,0:T(8,128)(2,1)S(1)} %get-tuple-element.27.after_any.refs_4_), channel_id=1, source_target_pairs={{0,2},{2,0},{1,3},{3,1},{4,6},{6,4},{5,7},{7,5},{8,10},{10,8},{9,1... | collective-permute-start | bytes 393224 | tf_op jit(solution)/shard_map/ppermute | solution.py:644
  31.4 1.6 %collective-permute-start.3 = (f32[520,128]{1,0:T(8,128)S(1)}, f32[520,128]{1,0:T(8,128)S(1)}, u32[]{:S(2)}, u32[]{:S(2)}) collective-permute-start(f32[520,128]{1,0:T(8,128)S(1)} %get-tuple-element.37), channel_id=1, source_target_pairs={{0,1},{1,0},{2,3},{3,2},{4,5},{5,4},{6,7},{7,6},{8,9},{9,8},{10,11... | collective-permute-start | bytes 798728 | tf_op jit(solution)/shard_map/ppermute | solution.py:682

commit v28 on v27

--- a/solution.py
+++ b/solution.py
@@ -186,7 +186,9 @@
 
     high, low = split(weights_ref[...])
     carried_high, carried_low = split(carried)
-    return turned(low, carried_high) + turned(high, carried_low) + turned(high, carried_high)
+    rows = high.shape[0]
+    both = turned(jnp.concatenate([high, low], axis=0), carried_high)
+    return both[rows:] + turned(high, carried_low) + both[:rows]
 
 
 def run_forward(lead, mat, hist, sel_ref, consts, ab_ref, logs, second=None, fresh=False, extend=True):

time: 34.2 us -> 33.6 us (0.982)
  Pallas kernels: 18.5 us -> 18 us
    pallas_call x2, Pallas kernels: 7.7 us -> 7.19 us  [second_pass(): pl.pallas_call(functools.partial(second_kernel, resume, last, extend, gri...]
where the time goes in v28:
time: 33.6 us; the launch traced here: 33.3 us
  Pallas kernels  18 us (54%)
  starting transfers between devices  10.8 us (32%)
  waiting for transfers between devices  2.22 us (7%)
  between operations  1.54 us (5%)
  local copies, waits for them, and re-layouts  0.79 us (2%)
    all_to_all x1, starting transfers between devices, per_device(): lax.all_to_all(packed, ('hh', 'per', 'st'), split_axis=0, concat_axis=0,...  7.84 us
    pallas_call x2, Pallas kernels, second_pass(): pl.pallas_call(functools.partial(second_kernel, resume, last, extend, gri...  7.19 us
    pallas_call x2, Pallas kernels, first_pass(): pl.pallas_call(functools.partial(first_kernel, resume, grids, index), gri...  4.58 us
    ppermute x2, starting transfers between devices, hand_over(): return lax.ppermute(state, 'per', moves)  2.44 us
    pallas_call x1, Pallas kernels, per_device(): pl.pallas_call(prep_own_kernel, out_shape=[pltpu.VMEM(mat_shape.shape, BF...  2.1 us
    ppermute x1, waiting for transfers between devices, per_device(): received = lax.ppermute(other, 'st', swap)  1.53 us
    pallas_call x1, Pallas kernels, per_device(): pl.pallas_call(pack_kernel, out_shape=pltpu.VMEM((group, periods // 2, sl...  1.49 us
    pallas_call x1, Pallas kernels, prep_second(): pl.pallas_call(prep_second_kernel, out_shape=[mat_shape, shaped((steps, r...  1.17 us
  transfers between devices with their start and end apart: 5, of which 2 were waited for; matrix products, arithmetic and copies ran while one was open for 0% of the time, Pallas kernels for 29%

profile of v28, /device:TPU:0, one launch (start us, length us, event | category | flops | bytes accessed | tf_op | source)
XLA Modules:
  0.0 33.3 jit_solution(16930645549482993572)
XLA Ops:
  1.3 1.5 %pack.1 = f32[8,8,384]{2,1,0:T(8,128)} custom-call(s32[1]{0:T(128)S(6)} %copy.12.count_ref, f32[16,384]{1,0:T(8,128)} %bitcast.7, s32[3,128]{1,0:T(4,128)} %bitcast.8, s32[3,128]{1,0:T(4,128)} %bitcast.9), custom_call_target="tpu_custom_call" | custom-call | tf_op jit(solution)/shard_map/pack/pallas_call | solution.py:518
  2.8 0.5 %collective-permute-start = (bf16[4,256,256]{2,1,0:T(8,128)(2,1)}, bf16[4,256,256]{2,1,0:T(8,128)(2,1)S(1)}, u32[]{:S(2)}, u32[]{:S(2)}) collective-permute-start(bf16[4,256,256]{2,1,0:T(8,128)(2,1)} %own_ref.1), channel_id=1, source_target_pairs={{0,1},{1,0},{2,3},{3,2},{4,5},{5,4},{6,7},{7,6},{8,9},{9,8},{10,11... | collective-permute-start | bytes 1572872 | tf_op jit(solution)/shard_map/ppermute | solution.py:528
  3.3 7.8 %all-to-all-start = ((f32[8,8,384]{2,1,0:T(8,128)}), f32[8,8,384]{2,1,0:T(8,128)S(1)}, u32[]{:S(2)}, u32[]{:S(2)}) async-start(f32[8,8,384]{2,1,0:T(8,128)} %pack.1), calls=%async_computation | async-start | bytes 196608 | tf_op jit(solution)/shard_map/all_to_all | solution.py:533
  11.1 2.1 %prep_own.1 = (bf16[8,256,512]{2,1,0:T(8,128)(2,1)S(1)}, f32[4,256,128]{2,1,0:T(8,128)S(1)}, bf16[2,256,512]{2,1,0:T(8,128)(2,1)S(1)}) custom-call(bf16[4,256,256]{2,1,0:T(8,128)(2,1)} %own_ref.1, f32[1,256]{1,0:T(1,128)} %bitcast.10, f32[1,256]{1,0:T(1,128)} %bitcast.11, f32[1,256]{1,0:T(1,128)} %bitcast.12), custom_call_target="tpu_custom_call" | custom-call | tf_op jit(solution)/shard_map/prep_own/pallas_call | solution.py:538
  13.2 0.0 copy-start.1
  13.3 0.8 %copy-done.1 = bf16[2,256,512]{2,1,0:T(8,128)(2,1)} copy-done((bf16[2,256,512]{2,1,0:T(8,128)(2,1)}, bf16[2,256,512]{2,1,0:T(8,128)(2,1)S(1)}, u32[]{:S(2)}) %copy-start.1) | copy-done | bytes 524312
  14.0 0.0 collective-permute-done.other_ref
  14.0 0.7 %prep_other.1.mat = bf16[8,256,512]{2,1,0:T(8,128)(2,1)S(1)} custom-call(bf16[4,256,256]{2,1,0:T(8,128)(2,1)S(1)} %collective-permute-done.other_ref, bf16[8,256,512]{2,1,0:T(8,128)(2,1)S(1)} %get-tuple-element.23.mat_in), custom_call_target="tpu_custom_call", output_to_operand_aliasing={{}: (1, {})} | custom-call | tf_op jit(solution)/shard_map/prep_other/pallas_call | solution.py:556
  14.7 0.7 %all-to-all-done.rows_ref = f32[8,8,384]{2,1,0:T(8,128)S(1)} async-done(((f32[8,8,384]{2,1,0:T(8,128)}), f32[8,8,384]{2,1,0:T(8,128)S(1)}, u32[]{:S(2)}, u32[]{:S(2)}) %all-to-all-start) | async-done | bytes 98336 | tf_op jit(solution)/shard_map/all_to_all | solution.py:533
  15.4 0.0 copy-start
  15.4 0.0 copy-start.2
  15.4 2.3 %first_pass.3 = (f32[8,256,256]{2,1,0:T(8,128)S(1)}, bf16[256,256]{1,0:T(8,128)(2,1)S(1)}, f32[3,9,8,256]{3,2,1,0:T(8,128)S(1)}) custom-call(f32[8,8,384]{2,1,0:T(8,128)S(1)} %all-to-all-done.rows_ref, bf16[8,256,512]{2,1,0:T(8,128)(2,1)S(1)} %prep_other.1.mat, f32[4,256,128]{2,1,0:T(8,128)S(1)} %get-tuple-element.24.consts.refs_2_), custom_call_target="tpu_custom_call" | custom-call | tf_op jit(solution)/shard_map/first_pass/pallas_call | solution.py:599
  17.7 0.9 %collective-permute-start.2 = (bf16[256,256]{1,0:T(8,128)(2,1)S(1)}, bf16[256,256]{1,0:T(8,128)(2,1)S(1)}, u32[]{:S(2)}, u32[]{:S(2)}) collective-permute-start(bf16[256,256]{1,0:T(8,128)(2,1)S(1)} %get-tuple-element.32.refs_4_), channel_id=1, source_target_pairs={{0,2},{2,0},{1,3},{3,1},{4,6},{6,4},{5,7},{7,5},{8,10},{10,8},{9,1... | collective-permute-start | bytes 393224 | tf_op jit(solution)/shard_map/ppermute | solution.py:646
  18.6 2.3 %first_pass.2 = (f32[8,256,256]{2,1,0:T(8,128)S(1)}, bf16[256,256]{1,0:T(8,128)(2,1)S(1)}, f32[3,9,8,256]{3,2,1,0:T(8,128)S(1)}) custom-call(f32[8,8,384]{2,1,0:T(8,128)S(1)} %all-to-all-done.rows_ref, bf16[8,256,512]{2,1,0:T(8,128)(2,1)S(1)} %prep_other.1.mat, f32[4,256,128]{2,1,0:T(8,128)S(1)} %get-tuple-element.24.consts.refs_2_), custom_call_target="tpu_custom_call" | custom-call | tf_op jit(solution)/shard_map/first_pass/pallas_call | solution.py:599
  20.9 1.5 %collective-permute-start.1 = (bf16[256,256]{1,0:T(8,128)(2,1)S(1)}, bf16[256,256]{1,0:T(8,128)(2,1)S(1)}, u32[]{:S(2)}, u32[]{:S(2)}) collective-permute-start(bf16[256,256]{1,0:T(8,128)(2,1)S(1)} %get-tuple-element.27.after_any.refs_4_), channel_id=1, source_target_pairs={{0,2},{2,0},{1,3},{3,1},{4,6},{6,4},{5,7},{7,5},{8,10},{10,8},{9,1... | collective-permute-start | bytes 393224 | tf_op jit(solution)/shard_map/ppermute | solution.py:646
  22.5 0.0 copy-done
  22.5 0.0 copy-done.2
  22.5 1.2 %prep_second.1 = (bf16[8,256,512]{2,1,0:T(8,128)(2,1)S(1)}, f32[8,64,256]{2,1,0:T(8,128)S(1)}) custom-call(bf16[4,256,256]{2,1,0:T(8,128)(2,1)S(1)} %copy-done, bf16[4,256,256]{2,1,0:T(8,128)(2,1)S(1)} %collective-permute-done.other_ref, bf16[2,256,512]{2,1,0:T(8,128)(2,1)S(1)} %copy-done.2, bf16[256,256]{1,0:T(8,128)(2,1)S(1)} %get-tuple-element.27.after_any.refs_4_), custom_call_target="tpu_custom_call" | custom-call | tf_op jit(solution)/shard_map/prep_second/pallas_call | solution.py:567
  23.6 0.0 collective-permute-done.2.refs_5_
  23.6 3.5 %second_pass.2 = (f32[8,64,256]{2,1,0:T(8,128)S(1)}, f32[8,128]{1,0:T(8,128)S(1)}) custom-call(f32[3,9,8,256]{3,2,1,0:T(8,128)S(1)} %get-tuple-element.30.refs_0_, bf16[8,256,512]{2,1,0:T(8,128)(2,1)S(1)} %get-tuple-element.28.refs_1_, f32[4,256,128]{2,1,0:T(8,128)S(1)} %get-tuple-element.24.consts.refs_2_, f32[8,256,256]{2,1,0:T(8,128)S(1)} %get-tuple-element.31.refs_3_, ...), custom_call_target="tpu_custom_call" | custom-call | tf_op jit(solution)/shard_map/second_pass/pallas_call | solution.py:627
  27.1 0.0 collective-permute-done.1.refs_5_
  27.1 3.7 %second_pass.3 = (f32[520,128]{1,0:T(8,128)S(1)}, f32[520,128]{1,0:T(8,128)S(1)}) custom-call(f32[3,9,8,256]{3,2,1,0:T(8,128)S(1)} %get-tuple-element.25.refs_0_, bf16[8,256,512]{2,1,0:T(8,128)(2,1)S(1)} %get-tuple-element.28.refs_1_, f32[4,256,128]{2,1,0:T(8,128)S(1)} %get-tuple-element.24.consts.refs_2_, f32[8,256,256]{2,1,0:T(8,128)S(1)} %get-tuple-element.29.refs_3_, ...), custom_call_target="tpu_custom_call" | custom-call | tf_op jit(solution)/shard_map/second_pass/pallas_call | solution.py:627
  30.8 0.0 collective-permute-start.3
  30.9 1.5 %collective-permute-done.3.other_ref = f32[520,128]{1,0:T(8,128)S(1)} collective-permute-done((f32[520,128]{1,0:T(8,128)S(1)}, f32[520,128]{1,0:T(8,128)S(1)}, u32[]{:S(2)}, u32[]{:S(2)}) %collective-permute-start.3) | collective-permute-done | bytes 266272 | tf_op jit(solution)/shard_map/ppermute | solution.py:684
  32.4 0.8 %finish.1 = (f32[512,128]{1,0:T(8,128)}, f32[1]{0:T(128)}) custom-call(f32[520,128]{1,0:T(8,128)S(1)} %get-tuple-element.36.mine_ref, f32[520,128]{1,0:T(8,128)S(1)} %collective-permute-done.3.other_ref), custom_call_target="tpu_custom_call" | custom-call | tf_op jit(solution)/shard_map/finish/pallas_call | solution.py:685
Async XLA Ops:
  2.8 11.3 %collective-permute-start = (bf16[4,256,256]{2,1,0:T(8,128)(2,1)}, bf16[4,256,256]{2,1,0:T(8,128)(2,1)S(1)}, u32[]{:S(2)}, u32[]{:S(2)}) collective-permute-start(bf16[4,256,256]{2,1,0:T(8,128)(2,1)} %own_ref.1), channel_id=1, source_target_pairs={{0,1},{1,0},{2,3},{3,2},{4,5},{5,4},{6,7},{7,6},{8,9},{9,8},{10,11... | collective-permute-start | bytes 1572872 | tf_op jit(solution)/shard_map/ppermute | solution.py:528
  3.3 12.1 %all-to-all-start = ((f32[8,8,384]{2,1,0:T(8,128)}), f32[8,8,384]{2,1,0:T(8,128)S(1)}, u32[]{:S(2)}, u32[]{:S(2)}) async-start(f32[8,8,384]{2,1,0:T(8,128)} %pack.1), calls=%async_computation | async-start | bytes 196608 | tf_op jit(solution)/shard_map/all_to_all | solution.py:533
  13.2 0.8 %copy-start.1 = (bf16[2,256,512]{2,1,0:T(8,128)(2,1)}, bf16[2,256,512]{2,1,0:T(8,128)(2,1)S(1)}, u32[]{:S(2)}) copy-start(bf16[2,256,512]{2,1,0:T(8,128)(2,1)S(1)} %get-tuple-element.26.early) | copy-start | bytes 1572868
  15.4 7.0 %copy-start = (bf16[4,256,256]{2,1,0:T(8,128)(2,1)S(1)}, bf16[4,256,256]{2,1,0:T(8,128)(2,1)}, u32[]{:S(2)}) copy-start(bf16[4,256,256]{2,1,0:T(8,128)(2,1)} %own_ref.1) | copy-start | bytes 1572868
  15.4 7.0 %copy-start.2 = (bf16[2,256,512]{2,1,0:T(8,128)(2,1)S(1)}, bf16[2,256,512]{2,1,0:T(8,128)(2,1)}, u32[]{:S(2)}) copy-start(bf16[2,256,512]{2,1,0:T(8,128)(2,1)} %copy-done.1) | copy-start | bytes 1572868
  17.7 5.9 %collective-permute-start.2 = (bf16[256,256]{1,0:T(8,128)(2,1)S(1)}, bf16[256,256]{1,0:T(8,128)(2,1)S(1)}, u32[]{:S(2)}, u32[]{:S(2)}) collective-permute-start(bf16[256,256]{1,0:T(8,128)(2,1)S(1)} %get-tuple-element.32.refs_4_), channel_id=1, source_target_pairs={{0,2},{2,0},{1,3},{3,1},{4,6},{6,4},{5,7},{7,5},{8,10},{10,8},{9,1... | collective-permute-start | bytes 393224 | tf_op jit(solution)/shard_map/ppermute | solution.py:646
  20.9 6.2 %collective-permute-start.1 = (bf16[256,256]{1,0:T(8,128)(2,1)S(1)}, bf16[256,256]{1,0:T(8,128)(2,1)S(1)}, u32[]{:S(2)}, u32[]{:S(2)}) collective-permute-start(bf16[256,256]{1,0:T(8,128)(2,1)S(1)} %get-tuple-element.27.after_any.refs_4_), channel_id=1, source_target_pairs={{0,2},{2,0},{1,3},{3,1},{4,6},{6,4},{5,7},{7,5},{8,10},{10,8},{9,1... | collective-permute-start | bytes 393224 | tf_op jit(solution)/shard_map/ppermute | solution.py:646
  30.8 1.5 %collective-permute-start.3 = (f32[520,128]{1,0:T(8,128)S(1)}, f32[520,128]{1,0:T(8,128)S(1)}, u32[]{:S(2)}, u32[]{:S(2)}) collective-permute-start(f32[520,128]{1,0:T(8,128)S(1)} %get-tuple-element.37), channel_id=1, source_target_pairs={{0,1},{1,0},{2,3},{3,2},{4,5},{5,4},{6,7},{7,6},{8,9},{9,8},{10,11... | collective-permute-start | bytes 798728 | tf_op jit(solution)/shard_map/ppermute | solution.py:684
